TPU v7x, 32 devices: a whole 2x2x4 slice. The times are simulated.
32 devices in a mesh: dp: 8 (over z, x), heads: 4 (over y, core).
Axes of the slice: x: 2, y: 2, z: 4, core: 2. Of those that a mesh axis runs over, the one named last changes fastest.
Arguments:
- noisy_mel: bfloat16 [16384, 100], P(('dp', 'heads')), may hold values from -6 to 6
- cond_mel: bfloat16 [16384, 100], P(('dp', 'heads')), may hold values from -6 to 6
- text_embed: bfloat16 [16384, 512], P(('dp', 'heads')), may hold values from -6 to 6
- time_embed: bfloat16 [32, 1024], P('dp'), may hold values from -6 to 6
- lengths: int32 [32], P('dp'), may hold values from 256 to 512, as said below
- spans: int32 [32, 2], P(('dp', 'heads')), may hold values from 0 to 512, as said below
- dw_kernel: float32 [7, 512], replicated, may hold values from -2 to 2
- text_bias: float32 [3, 512], replicated, may hold values from -1.8 to 1.8
- text_gain: float32 [512], replicated, may hold values from 0.1 to 1.9
- text_hidden: float32 [3, 1024], replicated, may hold values from -3 to 3
- pw_in: bfloat16 [512, 1024], replicated, may hold values from -0.25 to 0.25
- pw_out: bfloat16 [1024, 512], replicated, may hold values from -0.1875 to 0.1875
- in_proj: bfloat16 [712, 1024], replicated, may hold values from -0.21875 to 0.21875
- frame_bias: float32 [3, 1024], replicated, may hold values from -1.8 to 1.8
- mod_weight: bfloat16 [1024, 6144], P(None, 'heads'), may hold values from -0.1875 to 0.1875
- mod_bias: float32 [6144], P('heads'), may hold values from -4 to 4
- qkv_weight: bfloat16 [3, 1024, 1024], P(None, None, 'heads'), may hold values from -0.1875 to 0.1875
- qkv_bias: bfloat16 [3, 1024], P(None, 'heads'), may hold values from -1.796875 to 1.796875
- out_weight: bfloat16 [1024, 1024], P('heads'), may hold values from -0.75 to 0.75
- ff_in: bfloat16 [1024, 2048], P(None, 'heads'), may hold values from -0.1875 to 0.1875
- ff_in_bias: bfloat16 [2048], P('heads'), may hold values from -1.796875 to 1.796875
- ff_out: bfloat16 [2048, 1024], P('heads'), may hold values from -0.125 to 0.125
- cotangent: bfloat16 [16384, 1024], P(('dp', 'heads')), may hold values from -6 to 6
Outputs:
- output_frames: bfloat16 [16384, 1024], P(('dp', 'heads'))
- text_grad: float32 [16384, 512], P(('dp', 'heads'))
- time_grad: float32 [32, 1024], P('dp')
- dw_kernel_grad: float32 [7, 512], replicated
- text_bias_grad: float32 [3, 512], replicated
- text_gain_grad: float32 [512], replicated
- text_hidden_grad: float32 [3, 1024], replicated
- pw_in_grad: float32 [512, 1024], replicated
- pw_out_grad: float32 [1024, 512], replicated
- in_proj_grad: float32 [712, 1024], replicated
- frame_bias_grad: float32 [3, 1024], replicated
- mod_weight_grad: float32 [1024, 6144], P(None, 'heads')
- mod_bias_grad: float32 [6144], P('heads')
- qkv_weight_grad: float32 [3, 1024, 1024], P(None, None, 'heads')
- qkv_bias_grad: float32 [3, 1024], P(None, 'heads')
- out_weight_grad: float32 [1024, 1024], P('heads')
- ff_in_grad: float32 [1024, 2048], P(None, 'heads')
- ff_in_bias_grad: float32 [2048], P('heads')
- ff_out_grad: float32 [2048, 1024], P('heads')
Inputs may be any that keep to these rules, and one draw needn't show every extreme that they name: `lengths`: each utterance has 256 to 512 frames, and among the 4 utterances of every index of dp one has exactly 512. `spans`: start below end, end at most the utterance's length, the span covering 69 to 100 percent of that length.
All inputs are finite; a program needn't handle non-finite values.
Results may differ from a plain program's by a relative error of at most 0.029.
Values may be sent and summed in bfloat16 or wider, within the bound.
No kernel may reach another device: no remote copies, remote signals or barrier semaphores. Data moves between devices by JAX's collectives and lax.ppermute only.
A program may use at most 320 MiB of HBM per device.

v0:
```python
from functools import partial

import jax
import jax.numpy as jnp
from jax import lax
from jax.sharding import PartitionSpec as P

HD = 64


def layer_norm(values, epsilon):
    mean = jnp.mean(values, axis=-1, keepdims=True)
    centred = values - mean
    spread = jnp.mean(centred * centred, axis=-1, keepdims=True)
    return centred * lax.rsqrt(spread + epsilon)


def norm_mod(values, scale, shift):
    return layer_norm(values, 1e-06) * (1.0 + scale) + shift


def depthwise(rows_in, kernel):
    width = kernel.shape[0]
    margin = width // 2
    count = rows_in.shape[-2]
    widths = [(0, 0)] * (rows_in.ndim - 2) + [(margin, margin), (0, 0)]
    padded = jnp.pad(rows_in, widths)
    result = padded[..., 0:count, :] * kernel[0]
    for offset in range(1, width):
        result = result + padded[..., offset : offset + count, :] * kernel[offset]
    return result


def text_front(text_rows, kernel, conv_bias, gain, norm_bias):
    return layer_norm(depthwise(text_rows, kernel) + conv_bias, 1e-06) * gain + norm_bias


def grn_part(pre_act, gamma, beta):
    hidden = jax.nn.gelu(pre_act, approximate=False)
    energy = jnp.sqrt(jnp.sum(hidden * hidden, axis=-2, keepdims=True))
    ratio = energy / (jnp.mean(energy, axis=-1, keepdims=True) + 1e-06)
    return gamma * (hidden * ratio) + beta + hidden


def rope_tables(rows, width):
    half = width // 2
    inverse = 10000.0 ** (-2.0 * jnp.arange(half, dtype=jnp.float32) / width)
    angle = jnp.arange(rows, dtype=jnp.float32)[:, None] * inverse[None, :]
    return (jnp.cos(angle), jnp.sin(angle))


def rotate(values, cosine, sine):
    pairs = values.reshape(values.shape[:-1] + (values.shape[-1] // 2, 2))
    first = pairs[..., 0]
    second = pairs[..., 1]
    turned = jnp.stack([first * cosine - second * sine, second * cosine + first * sine], axis=-1)
    return turned.reshape(values.shape)


def inner_rows(left, right):
    return lax.dot_general(
        left, right, (((0,), (0,)), ((), ())), preferred_element_type=jnp.float32
    )


def inner_cols(left, right):
    return lax.dot_general(
        left, right, (((1,), (1,)), ((), ())), preferred_element_type=jnp.float32
    )


def to_items(values, units, rows):
    heads_here = values.shape[-1] // HD
    return (
        values.reshape(units, rows, heads_here, HD)
        .transpose(0, 2, 1, 3)
        .reshape(units * heads_here, rows, HD)
    )


def from_items(values, units, rows):
    heads_here = values.shape[0] // units
    return (
        values.reshape(units, heads_here, rows, HD)
        .transpose(0, 2, 1, 3)
        .reshape(units * rows, heads_here * HD)
    )


def masked_scores(query_block, key_block, count, scale):
    scores = inner_cols(query_block, key_block) * scale
    live = jnp.arange(key_block.shape[0], dtype=jnp.int32) < count
    return jnp.where(live[None, :], scores, -1e30)


def attend_forward(queries, key_rows, value_rows, item_lengths, scale):

    def per_item(args):
        query_block, key_block, value_block, count = args
        scores = masked_scores(query_block, key_block, count, scale)
        top = jnp.max(scores, axis=1, keepdims=True)
        expo = jnp.exp(scores - top)
        total = jnp.sum(expo, axis=1, keepdims=True)
        weights = (expo / total).astype(jnp.bfloat16)
        result = jnp.dot(weights, value_block, preferred_element_type=jnp.float32)
        return (result, (top + jnp.log(total))[:, 0])

    return lax.map(per_item, (queries, key_rows, value_rows, item_lengths))


def attend_backward(queries, key_rows, value_rows, item_lengths, log_totals, grad_out, scale):

    def per_item(args):
        query_block, key_block, value_block, count, log_total, grad_block = args
        scores = masked_scores(query_block, key_block, count, scale)
        weights = jnp.exp(scores - log_total[:, None])
        grad_weights = inner_cols(grad_block, value_block)
        grad_value = inner_rows(weights.astype(jnp.bfloat16), grad_block)
        grad_scores = weights * (
            grad_weights - jnp.sum(grad_weights * weights, axis=1, keepdims=True)
        )
        grad_low = grad_scores.astype(jnp.bfloat16)
        grad_query = jnp.dot(grad_low, key_block, preferred_element_type=jnp.float32) * scale
        grad_key = inner_rows(grad_low, query_block) * scale
        return (grad_query, grad_key, grad_value)

    return lax.map(per_item, (queries, key_rows, value_rows, item_lengths, log_totals, grad_out))


def on_device(
    noisy_mel,
    cond_mel,
    text_embed,
    time_embed,
    lengths,
    spans,
    dw_kernel,
    text_bias,
    text_gain,
    text_hidden,
    pw_in,
    pw_out,
    in_proj,
    frame_bias,
    mod_weight,
    mod_bias,
    qkv_weight,
    qkv_bias,
    out_weight,
    ff_in,
    ff_in_bias,
    ff_out,
    cotangent,
):
    group = lax.axis_size("heads")
    rows = text_embed.shape[0]
    model_width = in_proj.shape[1]
    position = jnp.arange(rows, dtype=jnp.int32)
    inside = (position >= spans[0, 0]) & (position < spans[0, 1])
    keep = jnp.where(inside, 0.0, 1.0).astype(jnp.float32)[:, None]
    cosine, sine = rope_tables(rows, HD)
    scale = HD ** (-0.5)
    text_rows = text_embed.astype(jnp.float32)
    normed_text, front_back = jax.vjp(
        text_front, text_rows, dw_kernel, text_bias[0], text_gain, text_bias[1]
    )
    normed_low = normed_text.astype(jnp.bfloat16)
    pre_act = jnp.dot(normed_low, pw_in, preferred_element_type=jnp.float32) + text_hidden[0]
    mixed_text, grn_back = jax.vjp(grn_part, pre_act, text_hidden[1], text_hidden[2])
    mixed_low = mixed_text.astype(jnp.bfloat16)
    refined = (
        text_rows + jnp.dot(mixed_low, pw_out, preferred_element_type=jnp.float32) + text_bias[2]
    )
    cond_low = (cond_mel.astype(jnp.float32) * keep).astype(jnp.bfloat16)
    frames_in = jnp.concatenate([noisy_mel, cond_low, refined.astype(jnp.bfloat16)], axis=1)
    state_zero = jnp.dot(frames_in, in_proj, preferred_element_type=jnp.float32) + frame_bias[0]
    time_rows = time_embed.astype(jnp.float32)
    activated, silu_back = jax.vjp(jax.nn.silu, time_rows)
    activated_low = activated.astype(jnp.bfloat16)
    modulation = (
        jnp.dot(activated_low, mod_weight, preferred_element_type=jnp.float32) + mod_bias
    ).astype(jnp.bfloat16)
    mod_row = lax.all_to_all(modulation, "heads", split_axis=0, concat_axis=1, tiled=True).astype(
        jnp.float32
    )
    shift_attn, scale_attn, gate_attn, shift_ffn, scale_ffn, gate_ffn = [
        mod_row[:, part * model_width : (part + 1) * model_width] for part in range(6)
    ]
    normed_attn, attn_norm_back = jax.vjp(norm_mod, state_zero, scale_attn, shift_attn)
    attn_in = normed_attn.astype(jnp.bfloat16)
    source = lax.all_gather(attn_in, "heads", axis=0, tiled=True)
    heads_here = qkv_weight.shape[2] // HD
    linear = [
        jnp.dot(source, qkv_weight[which], preferred_element_type=jnp.float32)
        + qkv_bias[which].astype(jnp.float32)
        for which in range(3)
    ]
    queries = rotate(to_items(linear[0], group, rows), cosine, sine).astype(jnp.bfloat16)
    key_rows = rotate(to_items(linear[1], group, rows), cosine, sine).astype(jnp.bfloat16)
    value_rows = to_items(linear[2], group, rows).astype(jnp.bfloat16)
    item_lengths = jnp.repeat(lengths, heads_here, total_repeat_length=group * heads_here)
    attended, log_totals = attend_forward(queries, key_rows, value_rows, item_lengths, scale)
    query_live = (position[None, :, None] < item_lengths[:, None, None]).astype(jnp.float32)
    attended_low = from_items(attended * query_live, group, rows).astype(jnp.bfloat16)
    projected = lax.psum_scatter(
        jnp.dot(attended_low, out_weight, preferred_element_type=jnp.float32).astype(jnp.bfloat16),
        "heads",
        scatter_dimension=0,
        tiled=True,
    ).astype(jnp.float32)
    attn_branch = projected + frame_bias[1]
    state_one = state_zero + gate_attn * attn_branch
    normed_ffn, ffn_norm_back = jax.vjp(norm_mod, state_one, scale_ffn, shift_ffn)
    ffn_in = normed_ffn.astype(jnp.bfloat16)
    ffn_source = lax.all_gather(ffn_in, "heads", axis=0, tiled=True)
    pre_ffn = jnp.dot(ffn_source, ff_in, preferred_element_type=jnp.float32) + ff_in_bias.astype(
        jnp.float32
    )
    hidden_ffn, gelu_back = jax.vjp(partial(jax.nn.gelu, approximate=True), pre_ffn)
    hidden_low = hidden_ffn.astype(jnp.bfloat16)
    lowered = lax.psum_scatter(
        jnp.dot(
            lax.slice_in_dim(hidden_low, 0, rows * lax.axis_size("heads"), axis=0),
            ff_out,
            preferred_element_type=jnp.float32,
        ).astype(jnp.bfloat16),
        "heads",
        scatter_dimension=0,
        tiled=True,
    ).astype(jnp.float32)
    ffn_branch = lowered + frame_bias[2]
    state_two = state_one + gate_ffn * ffn_branch
    grad_two = cotangent.astype(jnp.float32)
    grad_ffn = grad_two * gate_ffn
    grad_bias_ffn_out = jnp.sum(grad_ffn, axis=0)
    grad_gate_ffn = jnp.sum(grad_two * ffn_branch, axis=0, keepdims=True)
    grad_ffn_low = grad_ffn.astype(jnp.bfloat16)
    grad_ffn_rows = lax.all_gather(grad_ffn_low, "heads", axis=0, tiled=True)
    grad_hidden = inner_cols(grad_ffn_rows, ff_out)
    grad_weight_down = inner_rows(hidden_low, grad_ffn_rows)
    (grad_pre,) = gelu_back(grad_hidden)
    grad_bias_up = jnp.sum(grad_pre, axis=0)
    grad_pre_low = grad_pre.astype(jnp.bfloat16)
    grad_weight_up = inner_rows(ffn_source, grad_pre_low)
    grad_normed_ffn = lax.psum_scatter(
        inner_cols(grad_pre_low, ff_in).astype(jnp.bfloat16),
        "heads",
        scatter_dimension=0,
        tiled=True,
    ).astype(jnp.float32)
    grad_one_part, grad_scale_ffn, grad_shift_ffn = ffn_norm_back(grad_normed_ffn)
    grad_one = grad_two + grad_one_part
    grad_attn = grad_one * gate_attn
    grad_bias_attn_out = jnp.sum(grad_attn, axis=0)
    grad_gate_attn = jnp.sum(grad_one * attn_branch, axis=0, keepdims=True)
    grad_attn_low = grad_attn.astype(jnp.bfloat16)
    grad_attn_rows = lax.all_gather(grad_attn_low, "heads", axis=0, tiled=True)
    grad_attended = inner_cols(grad_attn_rows, out_weight)
    grad_weight_out = inner_rows(attended_low, grad_attn_rows)
    grad_items = (to_items(grad_attended, group, rows) * query_live).astype(jnp.bfloat16)
    grad_queries, grad_keys, grad_values = attend_backward(
        queries, key_rows, value_rows, item_lengths, log_totals, grad_items, scale
    )
    grad_linear = [
        from_items(rotate(grad_queries, cosine, -sine), group, rows),
        from_items(rotate(grad_keys, cosine, -sine), group, rows),
        from_items(grad_values, group, rows),
    ]
    grad_bias_qkv = jnp.stack([jnp.sum(member, axis=0) for member in grad_linear])
    grad_linear_low = [member.astype(jnp.bfloat16) for member in grad_linear]
    grad_weight_qkv = jnp.stack([inner_rows(source, member) for member in grad_linear_low])
    total = inner_cols(grad_linear_low[0], qkv_weight[0])
    for which in range(1, 3):
        total = total + inner_cols(
            lax.slice_in_dim(grad_linear_low[which], 0, rows * lax.axis_size("heads"), axis=0),
            qkv_weight[which],
        )
    grad_normed_attn = lax.psum_scatter(
        total.astype(jnp.bfloat16), "heads", scatter_dimension=0, tiled=True
    ).astype(jnp.float32)
    grad_zero_part, grad_scale_attn, grad_shift_attn = attn_norm_back(grad_normed_attn)
    grad_zero = grad_one + grad_zero_part
    grad_mod = jnp.concatenate(
        [
            grad_shift_attn,
            grad_scale_attn,
            grad_gate_attn,
            grad_shift_ffn,
            grad_scale_ffn,
            grad_gate_ffn,
        ],
        axis=1,
    ).astype(jnp.bfloat16)
    grad_mod_cols = lax.all_to_all(grad_mod, "heads", split_axis=1, concat_axis=0, tiled=True)
    grad_mod_weight = inner_rows(activated_low, grad_mod_cols)
    grad_mod_bias = jnp.sum(grad_mod_cols.astype(jnp.float32), axis=0)
    (grad_time_part,) = silu_back(inner_cols(grad_mod_cols, mod_weight))
    grad_zero_low = grad_zero.astype(jnp.bfloat16)
    grad_bias_in = jnp.sum(grad_zero, axis=0)
    grad_in_proj = inner_rows(frames_in, grad_zero_low)
    text_start = in_proj.shape[0] - text_rows.shape[1]
    grad_refined = inner_cols(grad_zero_low, in_proj[text_start:])
    grad_bias_pw_out = jnp.sum(grad_refined, axis=0)
    grad_refined_low = grad_refined.astype(jnp.bfloat16)
    grad_pw_out = inner_rows(mixed_low, grad_refined_low)
    grad_mixed = inner_cols(grad_refined_low, pw_out)
    grad_pre_act, grad_gamma, grad_beta = grn_back(grad_mixed)
    grad_bias_pw_in = jnp.sum(grad_pre_act, axis=0)
    grad_pre_act_low = grad_pre_act.astype(jnp.bfloat16)
    grad_pw_in = inner_rows(normed_low, grad_pre_act_low)
    grad_normed_text = inner_cols(grad_pre_act_low, pw_in)
    grad_text_conv, grad_kernel, grad_conv_bias, grad_gain, grad_norm_bias = front_back(
        grad_normed_text
    )
    grad_text = grad_refined + grad_text_conv
    replicated = (
        lax.psum(grad_time_part.astype(jnp.bfloat16), "heads").astype(jnp.float32),
        lax.psum(grad_kernel.astype(jnp.bfloat16), "heads").astype(jnp.float32),
        lax.psum(
            jnp.stack([grad_conv_bias, grad_norm_bias, grad_bias_pw_out]).astype(jnp.bfloat16),
            "heads",
        ).astype(jnp.float32),
        lax.psum(grad_gain.astype(jnp.bfloat16), "heads").astype(jnp.float32),
        lax.psum(
            jnp.stack([grad_bias_pw_in, grad_gamma, grad_beta]).astype(jnp.bfloat16), "heads"
        ).astype(jnp.float32),
        lax.psum(grad_pw_in.astype(jnp.bfloat16), "heads").astype(jnp.float32),
        lax.psum(grad_pw_out.astype(jnp.bfloat16), "heads").astype(jnp.float32),
        lax.psum(grad_in_proj.astype(jnp.bfloat16), "heads").astype(jnp.float32),
        lax.psum(
            jnp.stack([grad_bias_in, grad_bias_attn_out, grad_bias_ffn_out]).astype(jnp.bfloat16),
            "heads",
        ).astype(jnp.float32),
    )
    totals = (
        lax.psum(replicated[1].astype(jnp.bfloat16), "dp").astype(jnp.float32),
        lax.psum(replicated[2].astype(jnp.bfloat16), "dp").astype(jnp.float32),
        lax.psum(replicated[3].astype(jnp.bfloat16), "dp").astype(jnp.float32),
        lax.psum(replicated[4].astype(jnp.bfloat16), "dp").astype(jnp.float32),
        lax.psum(replicated[5].astype(jnp.bfloat16), "dp").astype(jnp.float32),
        lax.psum(replicated[6].astype(jnp.bfloat16), "dp").astype(jnp.float32),
        lax.psum(replicated[7].astype(jnp.bfloat16), "dp").astype(jnp.float32),
        lax.psum(replicated[8].astype(jnp.bfloat16), "dp").astype(jnp.float32),
        lax.psum(grad_mod_weight.astype(jnp.bfloat16), "dp").astype(jnp.float32),
        lax.psum(grad_mod_bias.astype(jnp.bfloat16), "dp").astype(jnp.float32),
        lax.psum(grad_weight_qkv.astype(jnp.bfloat16), "dp").astype(jnp.float32),
        lax.psum(grad_bias_qkv.astype(jnp.bfloat16), "dp").astype(jnp.float32),
        lax.psum(grad_weight_out.astype(jnp.bfloat16), "dp").astype(jnp.float32),
        lax.psum(grad_weight_up.astype(jnp.bfloat16), "dp").astype(jnp.float32),
        lax.psum(grad_bias_up.astype(jnp.bfloat16), "dp").astype(jnp.float32),
        lax.psum(grad_weight_down.astype(jnp.bfloat16), "dp").astype(jnp.float32),
    )
    return (
        state_two.astype(jnp.bfloat16),
        grad_text,
        replicated[0],
        totals[0],
        totals[1],
        totals[2],
        totals[3],
        totals[4],
        totals[5],
        totals[6],
        totals[7],
        totals[8],
        totals[9],
        totals[10],
        totals[11],
        totals[12],
        totals[13],
        totals[14],
        totals[15],
    )


def solution(mesh):
    in_specs = (
        P(("dp", "heads"), None),
        P(("dp", "heads"), None),
        P(("dp", "heads"), None),
        P("dp", None),
        P("dp"),
        P(("dp", "heads"), None),
        P(),
        P(),
        P(),
        P(),
        P(),
        P(),
        P(),
        P(),
        P(None, "heads"),
        P("heads"),
        P(None, None, "heads"),
        P(None, "heads"),
        P("heads", None),
        P(None, "heads"),
        P("heads"),
        P("heads", None),
        P(("dp", "heads"), None),
    )
    out_specs = (
        P(("dp", "heads"), None),
        P(("dp", "heads"), None),
        P("dp", None),
        P(),
        P(),
        P(),
        P(),
        P(),
        P(),
        P(),
        P(),
        P(None, "heads"),
        P("heads"),
        P(None, None, "heads"),
        P(None, "heads"),
        P("heads", None),
        P(None, "heads"),
        P("heads"),
        P("heads", None),
    )
    return jax.shard_map(
        on_device, mesh=mesh, in_specs=in_specs, out_specs=out_specs, check_vma=False
    )
```

profile of v0, /device:TPU:0, one launch (start us, length us, event | category | flops | bytes accessed | tf_op | source)
XLA Modules:
  0.0 1263.7 jit_solution(15688880503392613482)
XLA Ops:
  12.1 4.2 all-to-all-start
  23.3 7.2 multiply_reduce_fusion.6
  39.2 3.0 add_convert_fusion.3
  43.7 35.4 %all-gather.5.cloned.1.call-done = bf16[2048,1024]{1,0:T(8,128)(2,1)} async-done(((bf16[512,1024]{1,0:T(8,128)(2,1)}), bf16[2048,1024]{1,0:T(8,128)(2,1)}) %all-gather.5.cloned.1.call-update) | async-done | bytes 4194320 | tf_op jit(solution)/shard_map/all_gather | solution.py:191
  79.1 4.5 fusion.48
  88.5 4.0 copy.155
  92.5 4.9 convolution_add_fusion.1
  100.3 3.6 reshape.507
  103.9 3.6 copy.133
  107.5 3.4 reshape_reshape.13
  111.0 4.9 convolution_add_fusion.2
  118.7 3.6 reshape.506
  122.3 3.6 copy.130
  125.9 3.4 reshape_reshape.12
  129.4 7.7 subtract_convert_fusion
  137.1 6.0 pad_maximum_fusion.3
  144.9 3.1 copy.137
  148.0 3.1 copy.134
  151.1 3.1 copy.138
  155.8 95.5 %while.27 = (s32[]{:T(128)}, f32[16,512,64]{1,2,0:T(8,128)}, f32[16,512]{1,0:T(8,128)S(1)}, s32[16]{0:T(128)S(1)}, bf16[16,512,64]{2,1,0:T(8,128)(2,1)}, /*index...) while((s32[]{:T(128)}, f32[16,512,64]{1,2,0:T(8,128)}, ...), condition=%wide.region_9.10_spmd, body=%wide.region_6.9_spmd.sunk | while | flops 69206016 | bytes 7888021 | solution.py:108
  255.3 3.3 convolution_convert_fusion.3
  258.7 44.6 %reduce-scatter.5.cloned.1.call-done = bf16[512,1024]{1,0:T(8,128)(2,1)} async-done(((bf16[2048,1024]{1,0:T(8,128)(2,1)}), bf16[512,1024]{1,0:T(8,128)(2,1)}) %reduce-scatter.5.cloned.1.call-update) | async-done | bytes 1048592 | tf_op jit(solution)/shard_map/reduce_scatter | solution.py:205
  311.2 31.9 %all-gather.7.cloned.1.call-done = bf16[2048,1024]{1,0:T(8,128)(2,1)} async-done(((bf16[512,1024]{1,0:T(8,128)(2,1)}), bf16[2048,1024]{1,0:T(8,128)(2,1)}) %all-gather.7.cloned.1.call-update) | async-done | bytes 4194320 | tf_op jit(solution)/shard_map/all_gather | solution.py:215
  343.1 6.8 fusion.150
  350.0 29.7 %all-gather.9.cloned.1.call-done = bf16[2048,1024]{1,0:T(8,128)(2,1)} async-done(((bf16[512,1024]{1,0:T(8,128)(2,1)}), bf16[2048,1024]{1,0:T(8,128)(2,1)}) %all-gather.9.cloned.1.call-update) | async-done | bytes 4194320 | tf_op jit(solution)/shard_map/all_gather | solution.py:238
  379.7 9.0 fusion.133
  390.0 4.3 convolution_convert_fusion.1
  394.4 7.3 convolution_convert_fusion.2
  402.3 36.8 %reduce-scatter.9.cloned.1.call-done = bf16[512,1024]{1,0:T(8,128)(2,1)} async-done(((bf16[2048,1024]{1,0:T(8,128)(2,1)}), bf16[512,1024]{1,0:T(8,128)(2,1)}) %reduce-scatter.9.cloned.1.call-update) | async-done | bytes 1048592 | tf_op jit(solution)/shard_map/reduce_scatter | solution.py:245
  443.0 43.0 %reduce-scatter.7.cloned.1.call-done = bf16[512,1024]{1,0:T(8,128)(2,1)} async-done(((bf16[2048,1024]{1,0:T(8,128)(2,1)}), bf16[512,1024]{1,0:T(8,128)(2,1)}) %reduce-scatter.7.cloned.1.call-update) | async-done | bytes 1048592 | tf_op jit(solution)/shard_map/reduce_scatter | solution.py:221
  486.0 5.0 multiply_reduce_fusion.7
  493.6 34.6 %all-gather.11.cloned.1.call-done = bf16[2048,1024]{1,0:T(8,128)(2,1)} async-done(((bf16[512,1024]{1,0:T(8,128)(2,1)}), bf16[2048,1024]{1,0:T(8,128)(2,1)}) %all-gather.11.cloned.1.call-update) | async-done | bytes 4194320 | tf_op jit(solution)/shard_map/all_gather | solution.py:257
  528.2 4.9 fusion.151
  533.2 3.6 reshape.508
  545.1 151.8 %while.28 = (s32[]{:T(128)}, f32[16,512,64]{1,2,0:T(8,128)}, f32[16,512,64]{1,2,0:T(8,128)}, f32[16,512,64]{1,2,0:T(8,128)}, s32[16]{0:T(128)S(1)}, /*index=5*/b...) while((s32[]{:T(128)}, f32[16,512,64]{1,2,0:T(8,128)}, ...), condition=%wide.region_19.20_spmd, body=%wide.region_17.19_spmd.sunk | while | flops 170196992 | bytes 9060489 | solution.py:127
  696.9 2.9 copy.177
  701.1 3.5 reshape.510
  704.6 3.4 reshape.511
  708.0 8.5 multiply_subtract_fusion
  716.5 3.2 pad_maximum_fusion.1
  719.7 3.8 reshape_reshape.15
  723.6 3.1 copy.178
  728.0 3.2 pad_maximum_fusion
  731.2 3.6 reshape_reshape.14
  734.8 3.1 copy.179
  741.1 3.3 add_convert_fusion
  744.9 6.3 convolution_convert_fusion.8
  751.3 6.7 convolution_convert_fusion.7
  759.5 4.7 convolution_convert_fusion.9
  766.3 22.8 %reduce-scatter.11.cloned.1.call-done = bf16[512,1024]{1,0:T(8,128)(2,1)} async-done(((bf16[2048,1024]{1,0:T(8,128)(2,1)}), bf16[512,1024]{1,0:T(8,128)(2,1)}) %reduce-scatter.11.cloned.1.call-update) | async-done | bytes 1048592 | tf_op jit(solution)/shard_map/reduce_scatter | solution.py:278
  803.6 5.0 fusion.136
  811.4 4.7 fusion.72
  821.1 3.3 all-to-all-start.1
  831.0 56.3 %all-reduce.24.cloned.1.call-done = (bf16[512,1024]{1,0:T(8,128)(2,1)}, bf16[1024,512]{1,0:T(8,128)(2,1)}, bf16[712,1024]{1,0:T(8,128)(2,1)}) async-done(((bf16[512,1024]{1,0:T(8,128)(2,1)}, bf16[1024,512]{1,0:T(8,128)(2,1)}, bf16[712,1024]{1,0:T(8,128)(2,1)}), (bf16[512,1024]{1,0:T(8,128)(2,1)}, bf16[1024,512]{1,0:T(8,128)(2,1)}, bf16[712,1024]{1,0:T(8,128)(2,1)})) %all-reduce.24.cloned.1.call-update) | async-done | bytes 3555344 | tf_op jit(solution)/shard_map/psum | solution.py:327
  887.4 3.2 bitcast_reduce_fusion
  890.6 3.2 bitcast_reduce_fusion.1
  893.9 3.2 bitcast_reduce_fusion.2
  899.7 3.9 fusion.149
  909.7 3.1 multiply_reduce_fusion.15
  919.0 11.5 all-reduce.17
  931.2 40.4 %all-reduce.15 = (bf16[7,512]{1,0:T(8,128)(2,1)S(1)}, bf16[3,512]{1,0:T(4,128)(2,1)S(1)}, bf16[512]{0:T(512)(128)(2,1)S(1)}, bf16[3,1024]{1,0:T(4,128)(2,1)S(1)}...) all-reduce(bf16[7,512]{1,0:T(8,128)(2,1)S(1)} %get-tuple-element.36, ...), channel_id=1, replica_groups=mesh['dp'=8,'heads'=4] {'dp'}, use_global_device_ids=true, to_apply=%region_42.43 | all-reduce | flops 14592 | bytes 58368 | tf_op jit(solution)/shard_map/psum | solution.py:336
  976.3 262.7 %all-reduce.22.cloned.1.call-done = (bf16[512,1024]{1,0:T(8,128)(2,1)}, bf16[1024,512]{1,0:T(8,128)(2,1)}, bf16[712,1024]{1,0:T(8,128)(2,1)}, bf16[1024,1536]{1,...) async-done(((bf16[512,1024]{1,0:T(8,128)(2,1)}, ...) | async-done | bytes 10895376 | tf_op jit(solution)/shard_map/psum | solution.py:340
  1239.0 2.9 convert_element_type.361
  1253.0 3.6 convert_element_type.368
  (639 shorter events, 378.8 us)
Async XLA Ops:
  7.2 9.2 copy-start.81
  7.2 9.7 copy-start.77
  7.2 9.7 copy-start.73
  7.2 9.8 copy-start.74
  7.2 9.8 copy-start.72
  12.1 27.0 %all-to-all-start = ((bf16[4,2,768]{2,1,0:T(2,128)(2,1)}), bf16[4,2,768]{2,1,0:T(2,128)(2,1)S(1)}, u32[]{:S(2)}, u32[]{:S(2)}) async-start(bf16[4,2,768]{2,1,0:T(2,128)(2,1)} %reshape.536), calls=%async_computation | async-start | bytes 24576 | tf_op jit(solution)/shard_map/all_to_all | solution.py:183
  16.4 62.7 %all-gather.5.cloned.1.call-start = ((), (), s32[]{:S(2)}) async-start(), calls=%async_computation.6 | async-start | bytes 5242880 | tf_op jit(solution)/shard_map/all_gather | solution.py:191
  17.0 6.3 copy-start.82
  17.0 6.3 copy-start.70
  17.0 16.2 %copy-start.48 = (f32[1,1024]{1,0:T(1,128)}, f32[1,1024]{1,0:T(1,128)S(1)}, u32[]{:S(2)}) copy-start(f32[1,1024]{1,0:T(1,128)S(1)} %get-tuple-element.422) | copy-start | bytes 12292
  17.0 16.2 %copy-start.79 = (f32[1,1024]{1,0:T(1,128)}, f32[1,1024]{1,0:T(1,128)S(1)}, u32[]{:S(2)}) copy-start(f32[1,1024]{1,0:T(1,128)S(1)} %get-tuple-element.423) | copy-start | bytes 12292
  17.1 5.9 copy-start.52
  17.1 5.9 copy-start.54
  17.1 5.9 copy-start.56
  17.1 5.9 copy-start.58
  17.1 5.9 copy-start.60
  17.1 5.9 copy-start.62
  17.2 5.9 copy-start.64
  19.2 4.1 copy-start.75
  19.2 4.1 copy-start.92
  20.5 10.1 copy-start.14
  23.1 7.5 copy-start.10
  23.1 7.5 copy-start.50
  23.3 7.3 copy-start.66
  23.3 7.3 copy-start.68
  23.3 9.9 copy-start.40
  31.9 4.3 copy-start.46
  33.2 3.0 copy-start.41
  33.3 3.0 copy-start.89
  33.3 2.9 copy-start.93
  39.2 3.4 copy-start.85
  39.2 3.4 copy-start.1
  39.2 4.0 copy-start.78
  42.3 261.1 %reduce-scatter.5.cloned.1.call-start = ((), (), s32[]{:S(2)}) async-start(), calls=%async_computation.7 | async-start | bytes 5242880 | tf_op jit(solution)/shard_map/reduce_scatter | solution.py:205
  258.6 84.5 %all-gather.7.cloned.1.call-start = ((), (), s32[]{:S(2)}) async-start(), calls=%async_computation.8 | async-start | bytes 5242880 | tf_op jit(solution)/shard_map/all_gather | solution.py:215
  308.5 71.2 %all-gather.9.cloned.1.call-start = ((), (), s32[]{:S(2)}) async-start(), calls=%async_computation.10 | async-start | bytes 5242880 | tf_op jit(solution)/shard_map/all_gather | solution.py:238
  311.0 128.1 %reduce-scatter.9.cloned.1.call-start = ((), (), s32[]{:S(2)}) async-start(), calls=%async_computation.11 | async-start | bytes 5242880 | tf_op jit(solution)/shard_map/reduce_scatter | solution.py:245
  379.7 10.3 copy-start.91
  394.4 91.6 %reduce-scatter.7.cloned.1.call-start = ((), (), s32[]{:S(2)}) async-start(), calls=%async_computation.9 | async-start | bytes 5242880 | tf_op jit(solution)/shard_map/reduce_scatter | solution.py:221
  401.8 126.4 %all-gather.11.cloned.1.call-start = ((), (), s32[]{:S(2)}) async-start(), calls=%async_computation.12 | async-start | bytes 5242880 | tf_op jit(solution)/shard_map/all_gather | solution.py:257
  493.6 295.5 %reduce-scatter.11.cloned.1.call-start = ((), (), s32[]{:S(2)}) async-start(), calls=%async_computation.13 | async-start | bytes 5242880 | tf_op jit(solution)/shard_map/reduce_scatter | solution.py:278
  723.6 4.4 copy-start.27
  723.6 4.4 copy-start.28
  734.8 3.4 copy-start.30
  744.4 142.9 %all-reduce.24.cloned.1.call-start = ((), (), s32[]{:S(2)}) async-start(), calls=%async_computation.15 | async-start | bytes 7110656 | tf_op jit(solution)/shard_map/psum | solution.py:327
  744.9 6.4 copy-start.88
  759.4 4.7 copy-start.25
  759.4 4.7 copy-start.86
  799.9 3.7 copy-start.71
  803.6 6.0 copy-start.11
  803.6 6.0 copy-start.51
  803.6 6.0 copy-start.69
  803.6 6.0 copy-start.76
  803.6 6.0 copy-start.83
  811.4 4.8 copy-start.21
  811.4 4.8 copy-start.87
  818.3 10.0 copy-start.43
  821.1 7.2 all-to-all-start.1
  824.4 414.6 %all-reduce.22.cloned.1.call-start = ((), (), s32[]{:S(2)}) async-start(), calls=%async_computation.14 | async-start | bytes 21790720 | tf_op jit(solution)/shard_map/psum | solution.py:340
  903.6 4.7 copy-start.67
  909.6 3.1 copy-start.23
  1239.0 2.9 copy-start.39
  1239.0 4.0 copy-start.35
  1250.0 3.0 copy-start.29
  (61 other events, 91.4 us)
Sparse Core Ops, SparseCore 0:
  42.4 36.6 all-gather.4
  258.8 44.5 reduce-scatter.4
  308.6 34.4 all-gather.6
  345.2 34.4 all-gather.8
  394.5 44.5 reduce-scatter.8
  441.4 44.5 reduce-scatter.6
  493.7 34.4 all-gather.10
  744.5 44.5 reduce-scatter.10
  811.5 75.7 all-reduce.23
  894.6 344.3 all-reduce.21
where the time goes:
time: 1270 us; the launch traced here: 1260 us
  waiting for transfers between devices  599 us (47%)
  matrix products  294 us (23%)
  local copies, waits for them, and re-layouts  148 us (12%)
  other arithmetic  143 us (11%)
  blocking collectives  51.9 us (4%)
  between operations  17.1 us (1%)
    psum x1, waiting for transfers between devices, on_device(): lax.psum(replicated[5].astype(jnp.bfloat16), 'dp').astype(jnp.float32)  263 us
    dot_general x58, matrix products, inner_cols(): lax.dot_general(left, right, (((1,), (1,)), ((), ())), preferred_element_...  93.3 us
    dot_general x42, matrix products, inner_rows(): lax.dot_general(left, right, (((0,), (0,)), ((), ())), preferred_element_...  92.9 us
    psum x1, waiting for transfers between devices, on_device(): lax.psum(grad_pw_in.astype(jnp.bfloat16), 'heads').astype(jnp.float32)  56.3 us
    reduce_scatter x1, waiting for transfers between devices, on_device(): lax.psum_scatter(jnp.dot(attended_low, out_weight, preferred_element_type...  44.6 us
    reduce_scatter x1, waiting for transfers between devices, on_device(): lax.psum_scatter(jnp.dot(lax.slice_in_dim(hidden_low, 0, rows * lax.axis_...  43 us
    psum x1, blocking collectives, on_device(): lax.psum(replicated[1].astype(jnp.bfloat16), 'dp').astype(jnp.float32)  40.4 us
    reduce_scatter x1, waiting for transfers between devices, on_device(): lax.psum_scatter(inner_cols(grad_pre_low, ff_in).astype(jnp.bfloat16), 'h...  36.8 us
  transfers between devices with their start and end apart: 12, of which 11 were waited for; matrix products, arithmetic and copies ran while one was open for 9% of the time, Pallas kernels for 0%

commit v1 on v0

v1 whole, which is shorter than its diff:
```python
from functools import partial

import jax
import jax.numpy as jnp
from jax import lax
from jax.experimental import pallas as pl
from jax.experimental.pallas import tpu as pltpu
from jax.sharding import PartitionSpec as P

HD = 64


def inner_rows(left, right):
    return lax.dot_general(
        left, right, (((0,), (0,)), ((), ())), preferred_element_type=jnp.float32
    )


def inner_cols(left, right):
    return lax.dot_general(
        left, right, (((1,), (1,)), ((), ())), preferred_element_type=jnp.float32
    )


F32 = jnp.float32
BF16 = jnp.bfloat16
CHUNK = 64
SPAN = 256
VMEM = 60 * 1024 * 1024


def mm(left, right):
    return jnp.dot(left, right, preferred_element_type=F32)


def fold(values):
    return jnp.sum(values.reshape(values.shape[0] // 8, 8, values.shape[1]), axis=0)


def norm_parts(values):
    mean = jnp.mean(values, axis=-1, keepdims=True)
    centred = values - mean
    root = lax.rsqrt(jnp.mean(centred * centred, axis=-1, keepdims=True) + 1e-06)
    return centred * root, root


def norm_pull(grad, scale, xhat, root):
    entry = grad * (1.0 + scale)
    mean = jnp.mean(entry, axis=-1, keepdims=True)
    along = jnp.mean(entry * xhat, axis=-1, keepdims=True)
    return root * (entry - mean - xhat * along)


def swap_pairs(block):
    width = block.shape[1]
    lane = lax.broadcasted_iota(jnp.int32, block.shape, 1)
    if width % 128 == 0:
        after = pltpu.roll(block, width - 1, 1)
        before = pltpu.roll(block, 1, 1)
    else:
        after = jnp.concatenate([block[:, 1:], block[:, :1]], axis=1)
        before = jnp.concatenate([block[:, width - 1 :], block[:, : width - 1]], axis=1)
    return jnp.where(lane % 2 == 0, after, before)


def head_lanes(block, head):
    if block.shape[1] == HD:
        return block
    lane = lax.broadcasted_iota(jnp.int32, block.shape, 1)
    return jnp.where((lane >= head * HD) & (lane < (head + 1) * HD), block, jnp.zeros_like(block))


def slot_copies(pieces, target, sems, at, axis, half):
    if len(pieces) == 1:
        return [pltpu.make_async_copy(pieces[0], target.at[at], sems.at[at, 0])]
    copies = []
    for which, piece in enumerate(pieces):
        size = piece.shape[axis]
        start = pl.multiple_of((half if which == 0 else 1 - half) * size, size)
        index = (at,) + (slice(None),) * axis + (pl.ds(start, size),)
        copies.append(pltpu.make_async_copy(piece, target.at[index], sems.at[at, which]))
    return copies


def start_all(step, copies):
    @pl.when(step == 0)
    def _():
        for members in copies:
            for copy in members:
                copy.start()


def wait_own(step, copies):
    for at, members in enumerate(copies):

        @pl.when(step == at)
        def _(members=members):
            for copy in members:
                copy.wait()


def send_own(step, results):
    for at, members in enumerate(results):

        @pl.when(step == at)
        def _(members=members):
            for copy in members:
                copy.start()


def wait_all(step, results):
    @pl.when(step == len(results) - 1)
    def _():
        for members in results:
            for copy in members:
                copy.wait()


def attention_forward(pieces, first, last, *refs):
    parts = len(pieces)
    refs = list(refs)

    def take(count=1):
        taken = [refs.pop(0) for _ in range(count)]
        return taken[0] if count == 1 else taken

    count_ref, half_ref, state_ref, mod_ref, bias_ref, frame_ref, cosine_ref, sine_ref = take(8)
    weights = [[take() for _ in range(number)] for number in pieces]
    outs = [[take() for _ in range(number)] for number in pieces]
    if not first:
        normed_ref, before_ref = take(2)
    query_ref, key_ref, value_ref, attended_ref, log_ref = take(5)
    if first:
        normed_ref = take()
    if last:
        branch_ref, one_ref, ffn_ref = take(3)
    else:
        total_ref = take()
    weight_ref, out_ref, weight_sem, out_sem = take(4)
    if last:
        total_ref = take()
    step = pl.program_id(0)
    rows = state_ref.shape[0]
    width = weight_ref.shape[3]
    block = cosine_ref.shape[1]
    count = count_ref[0]
    half = half_ref[0]
    copies = [
        slot_copies(weights[at], weight_ref, weight_sem, at, 1, half)
        + slot_copies(outs[at], out_ref, out_sem, at, 0, half)
        for at in range(parts)
    ]
    start_all(step, copies)

    @pl.when(step == 0)
    def _():
        if first:

            def chunk(at, carry):
                here = pl.ds(at * CHUNK, CHUNK)
                xhat, _ = norm_parts(state_ref[here, :])
                normed_ref[here, :] = (xhat * (1.0 + mod_ref[1:2, :]) + mod_ref[0:1, :]).astype(
                    BF16
                )
                return carry

            lax.fori_loop(0, rows // CHUNK, chunk, 0)
            total_ref[...] = jnp.zeros_like(total_ref)
        else:
            total_ref[...] = before_ref[...]

    wait_own(step, copies)
    normed = normed_ref[...]
    cosine = cosine_ref[...]
    sine = sine_ref[...]
    logs = jnp.zeros((rows, 128), F32)
    lane = lax.broadcasted_iota(jnp.int32, (rows, 128), 1)
    query_lin = mm(normed, weight_ref[step, 0]) + bias_ref[0, 0:1, :]
    key_lin = mm(normed, weight_ref[step, 1]) + bias_ref[0, 1:2, :]
    value_ref[0] = (mm(normed, weight_ref[step, 2]) + bias_ref[0, 2:3, :]).astype(BF16)
    for at in range(width // block):
        cut = slice(at * block, (at + 1) * block)
        piece = query_lin[:, cut]
        turned = piece * cosine + swap_pairs(piece) * sine
        query_ref[0, :, cut] = (turned * HD**-0.5).astype(BF16)
        piece = key_lin[:, cut]
        key_ref[0, :, cut] = (piece * cosine + swap_pairs(piece) * sine).astype(BF16)
    live = lax.broadcasted_iota(jnp.int32, (1, rows), 1) < count
    for at in range(width // block):
        cut = slice(at * block, (at + 1) * block)
        keys = key_ref[0, :, cut]
        values = value_ref[0, :, cut]
        results = [None] * (rows // SPAN)
        pieces = [[] for _ in range(rows // SPAN)]
        for head in range(block // HD):
            own_values = head_lanes(values, head)
            for part in range(rows // SPAN):
                queries = head_lanes(query_ref[0, part * SPAN : (part + 1) * SPAN, cut], head)
                scores = jnp.where(live, inner_cols(queries, keys), -1e30)
                top = jnp.max(scores, axis=1, keepdims=True)
                expo = jnp.exp(scores - top)
                total = jnp.sum(expo, axis=1, keepdims=True)
                weights = (expo * (1.0 / total)).astype(BF16)
                result = mm(weights, own_values)
                results[part] = result if head == 0 else results[part] + result
                pieces[part].append(top + jnp.log(total))
        for head in range(block // HD):
            column = jnp.concatenate([pieces[part][head] for part in range(rows // SPAN)], axis=0)
            logs = jnp.where(lane == at * (block // HD) + head, column, logs)
        for part in range(rows // SPAN):
            place = part * SPAN + lax.broadcasted_iota(jnp.int32, (SPAN, block), 0)
            attended_ref[0, part * SPAN : (part + 1) * SPAN, cut] = jnp.where(
                place < count, results[part], 0.0
            ).astype(BF16)
    log_ref[0] = jnp.transpose(logs)[0:8, :]
    total_ref[...] += mm(attended_ref[0], out_ref[step])

    if last:

        @pl.when(step == parts - 1)
        def _():
            def chunk(at, carry):
                here = pl.ds(at * CHUNK, CHUNK)
                branch = total_ref[here, :] + frame_ref[1:2, :]
                branch_ref[here, :] = branch
                state_one = state_ref[here, :] + mod_ref[2:3, :] * branch
                one_ref[here, :] = state_one
                xhat, _ = norm_parts(state_one)
                ffn_ref[here, :] = (xhat * (1.0 + mod_ref[4:5, :]) + mod_ref[3:4, :]).astype(BF16)
                return carry

            lax.fori_loop(0, rows // CHUNK, chunk, 0)


def lay(target_ref, at, start, value):
    model, width = value.shape
    for block in range(model // width):
        target_ref[at, start : start + width, block * width : (block + 1) * width] = value[
            block * width : (block + 1) * width, :
        ]


def feed_forward(pieces, first, last, *refs):
    parts = len(pieces)
    refs = list(refs)

    def take(count=1):
        taken = [refs.pop(0) for _ in range(count)]
        return taken[0] if count == 1 else taken

    half_ref, cotangent_ref, one_ref, branch_ref, source_ref, mod_ref, bias_ref, frame_ref = take(8)
    ups = [[take() for _ in range(number)] for number in pieces]
    downs = [[take() for _ in range(number)] for number in pieces]
    if not first:
        grad_ref, total_in_ref, back_in_ref = take(3)
    grad_bias_ref, sums_ref = take(2)
    grads = [take() for _ in range(parts)]
    if first:
        grad_ref = take()
    if last:
        output_ref, grad_one_ref, grad_attn_ref = take(3)
    else:
        total_ref, back_ref = take(2)
    up_ref, down_ref, up_sem, down_sem = take(4)
    grads_ref, grads_sem = take(2)
    turned_ref, hidden_ref, pre_ref = take(3)
    if last:
        total_ref, back_ref = take(2)
    step = pl.program_id(0)
    rows, wide = one_ref.shape
    inner = 0.7978845608028654
    cubic = 0.044715
    half = half_ref[0]
    copies = [
        slot_copies(ups[at], up_ref, up_sem, at, 0, half)
        + slot_copies(downs[at], down_ref, down_sem, at, 0, half)
        for at in range(parts)
    ]
    results = [
        (pltpu.make_async_copy(grads_ref.at[at], grads[at], grads_sem.at[at]),)
        for at in range(parts)
    ]
    start_all(step, copies)

    @pl.when(step == 0)
    def _():
        if first:

            def chunk(at, carry):
                here = pl.ds(at * CHUNK, CHUNK)
                grad = cotangent_ref[here, :].astype(F32) * mod_ref[5:6, :]
                grad_ref[here, :] = grad.astype(BF16)
                return carry + fold(grad)

            lanes = lax.fori_loop(0, rows // CHUNK, chunk, jnp.zeros((8, wide), F32))
            sums_ref[0:1, :] = jnp.sum(lanes, axis=0, keepdims=True)
            total_ref[...] = jnp.zeros_like(total_ref)
            back_ref[...] = jnp.zeros_like(back_ref)
        else:
            total_ref[...] = total_in_ref[...]
            back_ref[...] = back_in_ref[...]
        turned_ref[...] = jnp.transpose(source_ref[...])

    wait_own(step, copies)
    up = up_ref[step]
    down = down_ref[step]
    lanes = jnp.zeros((8, up.shape[1]), F32)
    for part in range(rows // SPAN):
        here = slice(part * SPAN, (part + 1) * SPAN)
        pre = mm(source_ref[here, :], up) + bias_ref[0]
        grad_hidden = inner_cols(grad_ref[here, :], down)
        square = pre * pre
        bend = jnp.tanh(pre * (inner + inner * cubic * square))
        half = 0.5 * (1.0 + bend)
        hidden = (pre * half).astype(BF16)
        slope = half + 0.5 * pre * (1.0 - bend * bend) * (inner + 3.0 * inner * cubic * square)
        grad_pre = grad_hidden * slope
        lanes = lanes + fold(grad_pre)
        grad_pre = grad_pre.astype(BF16)
        hidden_ref[here, :] = hidden
        pre_ref[here, :] = grad_pre
        total_ref[here, :] += mm(hidden, down)
        back_ref[here, :] += inner_cols(grad_pre, up)
    grad_bias_ref[0] = jnp.sum(lanes, axis=0, keepdims=True)
    width = up_ref.shape[2]
    grads_ref[step, width:, :] = inner_rows(hidden_ref[...], grad_ref[...]).astype(BF16)
    lay(grads_ref, step, 0, mm(turned_ref[...], pre_ref[...]).astype(BF16))
    send_own(step, results)

    if last:

        @pl.when(step == parts - 1)
        def _():
            def chunk(at, carry):
                gate_ffn, scale_ffn, shift_ffn, bias_attn, gate_attn = carry
                here = pl.ds(at * CHUNK, CHUNK)
                branch = total_ref[here, :] + frame_ref[2:3, :]
                state_one = one_ref[here, :]
                output_ref[here, :] = (state_one + mod_ref[5:6, :] * branch).astype(BF16)
                cotangent = cotangent_ref[here, :].astype(F32)
                xhat, root = norm_parts(state_one)
                back = back_ref[here, :]
                grad_one = cotangent + norm_pull(back, mod_ref[4:5, :], xhat, root)
                grad_one_ref[here, :] = grad_one
                grad_attn = grad_one * mod_ref[2:3, :]
                grad_attn_ref[here, :] = grad_attn.astype(BF16)
                return (
                    gate_ffn + fold(cotangent * branch),
                    scale_ffn + fold(back * xhat),
                    shift_ffn + fold(back),
                    bias_attn + fold(grad_attn),
                    gate_attn + fold(grad_one * branch_ref[here, :]),
                )

            start = tuple(jnp.zeros((8, wide), F32) for _ in range(5))
            lanes = lax.fori_loop(0, rows // CHUNK, chunk, start)
            for at, member in enumerate(lanes):
                sums_ref[at + 1 : at + 2, :] = jnp.sum(member, axis=0, keepdims=True)

    wait_all(step, results)


def attention_backward(pieces, first, last, *refs):
    parts = len(pieces)
    refs = list(refs)

    def take(count=1):
        taken = [refs.pop(0) for _ in range(count)]
        return taken[0] if count == 1 else taken

    count_ref, half_ref, grad_attn_ref, normed_ref, mod_ref, cosine_ref, sine_ref = take(7)
    query_ref, key_ref, value_ref, attended_ref, log_ref = take(5)
    weights = [[take() for _ in range(number)] for number in pieces]
    outs = [[take() for _ in range(number)] for number in pieces]
    if not first:
        before_ref = take()
    if last:
        state_ref, grad_one_ref = take(2)
    grad_bias_ref = take()
    grads = [take() for _ in range(parts)]
    if last:
        grad_zero_ref, sums_ref = take(2)
    else:
        back_ref = take()
    weight_ref, out_ref, weight_sem, out_sem = take(4)
    grads_ref, grads_sem = take(2)
    turned_ref, item_ref = take(2)
    if last:
        back_ref = take()
    step = pl.program_id(0)
    rows, wide = normed_ref.shape
    width = weight_ref.shape[3]
    block = cosine_ref.shape[1]
    count = count_ref[0]
    half = half_ref[0]
    copies = [
        slot_copies(weights[at], weight_ref, weight_sem, at, 1, half)
        + slot_copies(outs[at], out_ref, out_sem, at, 0, half)
        for at in range(parts)
    ]
    results = [
        (pltpu.make_async_copy(grads_ref.at[at], grads[at], grads_sem.at[at]),)
        for at in range(parts)
    ]
    start_all(step, copies)

    @pl.when(step == 0)
    def _():
        turned_ref[...] = jnp.transpose(normed_ref[...])
        back_ref[...] = jnp.zeros_like(back_ref) if first else before_ref[...]

    wait_own(step, copies)
    grad_attn = grad_attn_ref[...]
    place = lax.broadcasted_iota(jnp.int32, (rows, width), 0)
    item_ref[...] = jnp.where(place < count, inner_cols(grad_attn, out_ref[step]), 0.0).astype(BF16)
    grads_ref[step, 3 * width :, :] = inner_rows(attended_ref[0], grad_attn).astype(BF16)
    cosine = cosine_ref[...]
    sine = sine_ref[...]
    live = lax.broadcasted_iota(jnp.int32, (rows, 1), 0) < count
    linear = [[], [], []]
    for at in range(width // block):
        cut = slice(at * block, (at + 1) * block)
        keys = key_ref[0, :, cut]
        values = value_ref[0, :, cut]
        keys_turned = jnp.transpose(keys)
        grad_keys = jnp.zeros((rows, block), F32)
        grad_values = jnp.zeros((rows, block), F32)
        grad_queries = [[] for _ in range(rows // SPAN)]
        for head in range(block // HD):
            index = at * (block // HD) + head
            for part in range(rows // SPAN):
                here = slice(part * SPAN, (part + 1) * SPAN)
                queries = head_lanes(query_ref[0, here, cut], head)
                items = head_lanes(item_ref[here, cut], head)
                scores = jnp.where(live, inner_cols(keys, queries), -1e30)
                weights = jnp.exp(scores - log_ref[0, index : index + 1, here])
                grad_weights = inner_cols(values, items)
                along = jnp.sum(grad_weights * weights, axis=0, keepdims=True)
                grad_scores = (weights * (grad_weights - along)).astype(BF16)
                grad_values = grad_values + mm(weights.astype(BF16), items)
                grad_keys = grad_keys + mm(grad_scores, queries)
                grad_queries[part].append(
                    mm(keys_turned[head * HD : (head + 1) * HD, :], grad_scores)
                )
        grad_query = jnp.concatenate(
            [jnp.concatenate(grad_queries[part], axis=0) for part in range(rows // SPAN)], axis=1
        )
        grad_query = jnp.transpose(grad_query) * HD**-0.5
        for which, member in enumerate((grad_query, grad_keys)):
            linear[which].append(member * cosine - swap_pairs(member) * sine)
        linear[2].append(grad_values)
    for which in range(3):
        member = jnp.concatenate(linear[which], axis=1) if width > block else linear[which][0]
        grad_bias_ref[0, which : which + 1, :] = jnp.sum(member, axis=0, keepdims=True)
        member = member.astype(BF16)
        lay(grads_ref, step, which * width, mm(turned_ref[...], member).astype(BF16))
        back_ref[...] += inner_cols(member, weight_ref[step, which])

    send_own(step, results)

    if last:

        @pl.when(step == parts - 1)
        def _():
            def chunk(at, carry):
                scale_attn, shift_attn, bias_in = carry
                here = pl.ds(at * CHUNK, CHUNK)
                xhat, root = norm_parts(state_ref[here, :])
                back = back_ref[here, :]
                grad_zero = grad_one_ref[here, :] + norm_pull(back, mod_ref[1:2, :], xhat, root)
                grad_zero_ref[here, :] = grad_zero.astype(BF16)
                return (
                    scale_attn + fold(back * xhat),
                    shift_attn + fold(back),
                    bias_in + fold(grad_zero),
                )

            start = tuple(jnp.zeros((8, wide), F32) for _ in range(3))
            lanes = lax.fori_loop(0, rows // CHUNK, chunk, start)
            for at, member in enumerate(lanes):
                sums_ref[at : at + 1, :] = jnp.sum(member, axis=0, keepdims=True)

    wait_all(step, results)


def total_of(refs):
    total = refs[0][...].astype(F32)
    for ref in refs[1:]:
        total = total + ref[...].astype(F32)
    return total.astype(BF16)


def sum_kernel(count, *refs):
    refs[count][...] = total_of(refs[:count])


def split_kernel(count, *refs):
    upper_kept = refs[0][0] == 1
    lower = total_of(refs[1 : 1 + count])
    upper = total_of(refs[1 + count : 1 + 2 * count])
    keep_ref, send_ref = refs[1 + 2 * count :]
    keep_ref[...] = jnp.where(upper_kept, upper, lower)
    send_ref[...] = jnp.where(upper_kept, lower, upper)


def bring(starts_ref, pieces, stack_ref, sems):
    size = pieces[0].shape[0]
    copies = []
    for at, piece in enumerate(pieces):
        start = pl.multiple_of(starts_ref[at], 16)
        copies.append(
            pltpu.make_async_copy(piece, stack_ref.at[pl.ds(start, size), :], sems.at[at])
        )
    for copy in copies:
        copy.start()
    for copy in copies:
        copy.wait()


def unlay(target, stack_ref, start, width):
    for block in range(target.shape[0] // width):
        target[block * width : (block + 1) * width, :] = stack_ref[
            start : start + width, block * width : (block + 1) * width
        ].astype(F32)


def ffn_unpack(count, starts_ref, *refs):
    pieces = refs[:count]
    up_ref, down_ref, stack_ref, sems = refs[count:]
    bring(starts_ref, pieces, stack_ref, sems)
    width = up_ref.shape[1]
    unlay(up_ref, stack_ref, 0, width)
    down_ref[...] = stack_ref[width:, :].astype(F32)


def attn_unpack(count, starts_ref, *refs):
    pieces = refs[:count]
    weight_ref, out_ref, stack_ref, sems = refs[count:]
    bring(starts_ref, pieces, stack_ref, sems)
    width = weight_ref.shape[2]
    for which in range(3):
        unlay(weight_ref.at[which], stack_ref, which * width, width)
    out_ref[...] = stack_ref[3 * width :, :].astype(F32)


def gelu_parts(pre):
    share = 0.5 * (1.0 + lax.erf(pre * 0.7071067811865476))
    slope = share + pre * (0.3989422804014327 * jnp.exp(-0.5 * pre * pre))
    return pre * share, slope


def fill_padded(padded_ref, text_ref):
    rows, wide = text_ref.shape
    edge = jnp.zeros((8, wide), F32)
    padded_ref[0:8, :] = edge
    padded_ref[rows + 8 : rows + 16, :] = edge
    for at in range(rows // CHUNK):
        here = slice(at * CHUNK, (at + 1) * CHUNK)
        padded_ref[at * CHUNK + 8 : (at + 1) * CHUNK + 8, :] = text_ref[here, :].astype(F32)


def text_forward(
    text_ref,
    mel_ref,
    kernel_ref,
    bias_ref,
    gain_ref,
    hidden_bias_ref,
    in_ref,
    out_ref,
    project_ref,
    frame_ref,
    normed_ref,
    pre_ref,
    energy_ref,
    mixed_ref,
    refined_ref,
    state_ref,
    padded_ref,
    hidden_ref,
):
    rows, wide = text_ref.shape
    taps = kernel_ref.shape[0]
    fill_padded(padded_ref, text_ref)

    def front(at, carry):
        start = pl.multiple_of(at * CHUNK, CHUNK)
        near = padded_ref[pl.ds(start, CHUNK + 16), :]
        conv = bias_ref[0:1, :]
        for tap in range(taps):
            shift = 8 + tap - taps // 2
            conv = conv + near[shift : shift + CHUNK, :] * kernel_ref[tap : tap + 1, :]
        xhat, _ = norm_parts(conv)
        normed_ref[pl.ds(start, CHUNK), :] = (xhat * gain_ref[...] + bias_ref[1:2, :]).astype(BF16)
        return carry

    lax.fori_loop(0, rows // CHUNK, front, 0)
    pre_ref[...] = mm(normed_ref[...], in_ref[...]) + hidden_bias_ref[0:1, :]

    def gelu(at, carry):
        here = pl.ds(at * CHUNK, CHUNK)
        hidden, _ = gelu_parts(pre_ref[here, :])
        hidden_ref[here, :] = hidden
        return carry + fold(hidden * hidden)

    squares = lax.fori_loop(0, rows // CHUNK, gelu, jnp.zeros((8, pre_ref.shape[1]), F32))
    energy = jnp.sqrt(jnp.sum(squares, axis=0, keepdims=True))
    energy_ref[0:1, :] = energy
    ratio = energy / (jnp.mean(energy, axis=1, keepdims=True) + 1e-06)

    def mix(at, carry):
        here = pl.ds(at * CHUNK, CHUNK)
        hidden = hidden_ref[here, :]
        mixed = hidden_bias_ref[1:2, :] * (hidden * ratio) + hidden_bias_ref[2:3, :] + hidden
        mixed_ref[here, :] = mixed.astype(BF16)
        return carry

    lax.fori_loop(0, rows // CHUNK, mix, 0)
    refined_ref[...] = (
        text_ref[...].astype(F32) + mm(mixed_ref[...], out_ref[...]) + bias_ref[2:3, :]
    ).astype(BF16)
    state_ref[...] = (
        mm(mel_ref[...], project_ref[0 : mel_ref.shape[1], :])
        + mm(refined_ref[...], project_ref[mel_ref.shape[1] :, :])
        + frame_ref[0:1, :]
    )


def full_line(members, wide):
    have = sum(member.shape[1] for member in members)
    return jnp.concatenate(list(members) + [jnp.zeros((1, wide - have), F32)], axis=1)


def small_rows(group):
    count = 12 + 2 * group
    return count + -count % 16


def text_backward(group, *refs):
    refs = list(refs)

    def take(count=1):
        taken = [refs.pop(0) for _ in range(count)]
        return taken[0] if count == 1 else taken

    own_ref, grad_zero_ref, text_ref, mel_ref, refined_ref, mixed_ref, normed_ref = take(7)
    pre_ref, energy_ref, kernel_ref, bias_ref, gain_ref, hidden_bias_ref = take(6)
    in_ref, out_ref, project_ref, attn_sums_ref, ffn_sums_ref = take(5)
    high_bias_ref, low_bias_ref, up_bias_ref = take(3)
    grad_text_ref, mods_ref = take(2)
    slots = [take() for _ in range(group)]
    stack_ref, sems, padded_ref, outer_ref, refined_grad_ref, low_ref, mixed_grad_ref = take(7)
    pre_low_ref, normed_grad_ref, lines_ref = take(3)
    small = small_rows(group)
    own = own_ref[0]
    rows, wide = text_ref.shape
    model = grad_zero_ref.shape[1]
    taps = kernel_ref.shape[0]
    mel_at = 3 * wide
    small_at = mel_at + mel_ref.shape[1] + (-(mel_at + mel_ref.shape[1])) % 16

    for at, (source, row) in enumerate(
        (
            (attn_sums_ref, 1),
            (attn_sums_ref, 0),
            (ffn_sums_ref, 5),
            (ffn_sums_ref, 3),
            (ffn_sums_ref, 2),
            (ffn_sums_ref, 1),
        )
    ):
        mods_ref[at : at + 1, :] = source[row : row + 1, :]

    grad_zero = grad_zero_ref[...]
    grad_refined = inner_cols(grad_zero, project_ref[mel_ref.shape[1] :, :])
    refined_grad_ref[...] = grad_refined
    low_ref[...] = grad_refined.astype(BF16)
    sum_out = jnp.sum(fold(grad_refined), axis=0, keepdims=True)
    mixed_grad_ref[...] = inner_cols(low_ref[...], out_ref[...])
    stack_ref[0:wide, :] = inner_rows(refined_ref[...], grad_zero).astype(BF16)
    spare = jnp.zeros((small_at - mel_at - mel_ref.shape[1], model), F32)
    grad_mel = inner_rows(mel_ref[...], grad_zero)
    stack_ref[mel_at:small_at, :] = jnp.concatenate([grad_mel, spare], axis=0).astype(BF16)
    rest = stack_ref.shape[0] - small_at - small
    if rest:
        stack_ref[small_at + small :, :] = jnp.zeros((rest, model), BF16)
    grad_out = inner_rows(mixed_ref[...], low_ref[...]).astype(BF16)
    stack_ref[2 * wide : 3 * wide, 0:wide] = grad_out[0:wide, :]
    stack_ref[2 * wide : 3 * wide, wide:] = grad_out[wide:, :]

    energy = energy_ref[0:1, :]
    mean = jnp.mean(energy, axis=1, keepdims=True) + 1e-06
    ratio = energy / mean

    def first_pass(at, carry):
        along, plain = carry
        here = pl.ds(at * CHUNK, CHUNK)
        hidden, _ = gelu_parts(pre_ref[here, :])
        grad = mixed_grad_ref[here, :]
        return along + fold(grad * hidden), plain + fold(grad)

    zero = jnp.zeros((8, model), F32)
    along, plain = lax.fori_loop(0, rows // CHUNK, first_pass, (zero, zero))
    along = jnp.sum(along, axis=0, keepdims=True)
    sum_beta = jnp.sum(plain, axis=0, keepdims=True)
    gamma = hidden_bias_ref[1:2, :]
    grad_ratio = gamma * along
    grad_mean = jnp.sum(grad_ratio * energy, axis=1, keepdims=True) / (mean * mean)
    grad_energy = grad_ratio / mean - grad_mean / model
    spread = grad_energy / energy
    factor = 1.0 + gamma * ratio

    def second_pass(at, carry):
        here = pl.ds(at * CHUNK, CHUNK)
        hidden, slope = gelu_parts(pre_ref[here, :])
        grad = (mixed_grad_ref[here, :] * factor + hidden * spread) * slope
        pre_low_ref[here, :] = grad.astype(BF16)
        return carry + fold(grad)

    sum_in = jnp.sum(lax.fori_loop(0, rows // CHUNK, second_pass, zero), axis=0, keepdims=True)
    normed_grad_ref[...] = inner_cols(pre_low_ref[...], in_ref[...])
    stack_ref[wide : 2 * wide, :] = inner_rows(normed_ref[...], pre_low_ref[...]).astype(BF16)

    fill_padded(padded_ref, text_ref)
    edge = jnp.zeros((8, wide), F32)
    outer_ref[0:8, :] = edge
    outer_ref[rows + 8 : rows + 16, :] = edge
    narrow = jnp.zeros((8, wide), F32)
    step = CHUNK // 2

    def conv_back(at, carry):
        sum_gain, sum_norm, sum_conv, sum_taps = carry
        start = pl.multiple_of(at * step, step)
        near = padded_ref[pl.ds(start, step + 16), :]
        conv = bias_ref[0:1, :]
        for tap in range(taps):
            shift = 8 + tap - taps // 2
            conv = conv + near[shift : shift + step, :] * kernel_ref[tap : tap + 1, :]
        xhat, root = norm_parts(conv)
        grad = normed_grad_ref[pl.ds(start, step), :]
        entry = grad * gain_ref[...]
        entry_mean = jnp.mean(entry, axis=-1, keepdims=True)
        entry_along = jnp.mean(entry * xhat, axis=-1, keepdims=True)
        grad_conv = root * (entry - entry_mean - xhat * entry_along)
        outer_ref[pl.ds(start + 8, step), :] = grad_conv
        sum_taps = tuple(
            member
            + fold(grad_conv * near[8 + tap - taps // 2 : 8 + tap - taps // 2 + step, :])
            for tap, member in enumerate(sum_taps)
        )
        return (
            sum_gain + fold(grad * xhat),
            sum_norm + fold(grad),
            sum_conv + fold(grad_conv),
            sum_taps,
        )

    sum_gain, sum_norm, sum_conv, sum_taps = lax.fori_loop(
        0, rows // step, conv_back, (narrow, narrow, narrow, (narrow,) * taps)
    )

    def text_grad(at, carry):
        start = pl.multiple_of(at * CHUNK, CHUNK)
        near = outer_ref[pl.ds(start, CHUNK + 16), :]
        total = refined_grad_ref[pl.ds(start, CHUNK), :]
        for tap in range(taps):
            shift = 8 + taps // 2 - tap
            total = total + near[shift : shift + CHUNK, :] * kernel_ref[tap : tap + 1, :]
        grad_text_ref[pl.ds(start, CHUNK), :] = total
        return carry

    lax.fori_loop(0, rows // CHUNK, text_grad, 0)

    def line(member):
        return jnp.sum(member, axis=0, keepdims=True)

    halves = [line(member) for member in sum_taps] + [line(sum_gain)]
    halves += [line(sum_conv), line(sum_norm), sum_out, jnp.zeros((1, wide), F32)]
    lines = [
        jnp.concatenate(halves[at : at + 2], axis=1) for at in range(0, len(halves), 2)
    ]
    lines += [sum_in, ratio * along, sum_beta]
    lines += [attn_sums_ref[2:3, :], ffn_sums_ref[4:5, :], ffn_sums_ref[0:1, :]]
    lines_ref[...] = jnp.zeros_like(lines_ref)
    for at, member in enumerate(lines):
        lines_ref[at : at + 1, :] = member
    parts = group // 2
    row = lax.broadcasted_iota(jnp.int32, lines_ref.shape, 0)
    total = lines_ref[...]
    for slot in range(group):
        source_ref = low_bias_ref if slot < parts else high_bias_ref
        owner = jnp.bitwise_xor(own, slot)
        members = [source_ref[slot % parts, which : which + 1, :] for which in range(3)]
        total = jnp.where(row == 12 + owner, full_line(members, model), total)
        total = jnp.where(row == 12 + group + owner, full_line([up_bias_ref[slot]], model), total)
    lines_ref[...] = total
    stack_ref[small_at : small_at + small, :] = lines_ref[...].astype(BF16)

    size = stack_ref.shape[0] // group
    copies = []
    for slot in range(group):
        start = pl.multiple_of(jnp.bitwise_xor(own, slot) * size, size)
        copies.append(
            pltpu.make_async_copy(stack_ref.at[pl.ds(start, size), :], slots[slot], sems.at[slot])
        )
    for copy in copies:
        copy.start()
    for copy in copies:
        copy.wait()


def text_unpack(count, group, starts_ref, own_ref, *refs):
    pieces = refs[:count]
    project_ref, in_ref, out_ref, taps_ref, bias_ref, gain_ref = refs[count : count + 6]
    hidden_ref, frame_ref, qkv_bias_ref, up_bias_ref, stack_ref, sems, lines_ref = refs[count + 6 :]
    bring(starts_ref, pieces, stack_ref, sems)
    own = own_ref[0]
    wide = in_ref.shape[0]
    taps = taps_ref.shape[0]
    mels = project_ref.shape[0] - wide
    mel_at = 3 * wide
    small_at = mel_at + mels + (-(mel_at + mels)) % 16
    project_ref[0:mels, :] = stack_ref[mel_at : mel_at + mels, :].astype(F32)
    project_ref[mels:, :] = stack_ref[0:wide, :].astype(F32)
    in_ref[...] = stack_ref[wide : 2 * wide, :].astype(F32)
    out_ref[0:wide, :] = stack_ref[2 * wide : 3 * wide, 0:wide].astype(F32)
    out_ref[wide:, :] = stack_ref[2 * wide : 3 * wide, wide:].astype(F32)
    lines_ref[...] = stack_ref[small_at : small_at + small_rows(group), :].astype(F32)

    def half(at):
        return lines_ref[at // 2 : at // 2 + 1, (at % 2) * wide : (at % 2 + 1) * wide]

    for tap in range(taps):
        taps_ref[tap : tap + 1, :] = half(tap)
    gain_ref[...] = half(taps)
    for at in range(3):
        bias_ref[at : at + 1, :] = half(taps + 1 + at)
    first = (taps + 5) // 2
    hidden_ref[...] = lines_ref[first : first + 3, :]
    frame_ref[...] = lines_ref[first + 3 : first + 6, :]
    row = lax.broadcasted_iota(jnp.int32, lines_ref.shape, 0)

    def pick(at):
        return jnp.sum(jnp.where(row == at, lines_ref[...], 0.0), axis=0, keepdims=True)

    line = pick(12 + own)
    width = qkv_bias_ref.shape[1]
    for which in range(3):
        qkv_bias_ref[which : which + 1, :] = line[:, which * width : (which + 1) * width]
    up_bias_ref[...] = pick(12 + group + own)[:, 0 : up_bias_ref.shape[1]]


ANY = pl.BlockSpec(memory_space=pl.ANY)
SMEM = pl.BlockSpec(memory_space=pltpu.SMEM)


def whole(shape):
    return pl.BlockSpec(shape, lambda g: (0,) * len(shape))


def held(shape, parts=None):
    if parts is None:
        return pl.BlockSpec((1,) + shape, lambda g: (g,) + (0,) * len(shape))
    return pl.BlockSpec((1,) + shape, lambda g: (parts - 1 - g,) + (0,) * len(shape))


def run_kernel(kernel, parts, inputs, outputs, scratch):
    return pl.pallas_call(
        kernel,
        grid=(parts,),
        in_specs=[spec for spec, _ in inputs],
        out_specs=[spec for spec, _, _ in outputs],
        out_shape=[jax.ShapeDtypeStruct(shape, kind) for _, shape, kind in outputs],
        scratch_shapes=scratch,
        compiler_params=pltpu.CompilerParams(vmem_limit_bytes=VMEM),
        cost_estimate=pl.CostEstimate(flops=1024, bytes_accessed=1024, transcendentals=0),
    )(*[array for _, array in inputs])


def after(arrays, *others):
    arrays = tuple(arrays)
    return lax.optimization_barrier(arrays + others)[: len(arrays)]


def swap(array, axis, bit):
    return lax.ppermute(array, axis, [(at, at ^ bit) for at in range(lax.axis_size(axis))])


def low_bit(slot):
    return slot & -slot


def tile_rows(rows):
    return next(size for size in (256, 224, 128, 112, 96, 80, 64, 48, 32, 16) if rows % size == 0)


def add_arrays(arrays):
    rows, wide = arrays[0].shape
    tile = tile_rows(rows)
    spec = pl.BlockSpec((tile, wide), lambda g: (g, 0))
    return run_kernel(
        partial(sum_kernel, len(arrays)),
        rows // tile,
        [(spec, array) for array in arrays],
        [(spec, (rows, wide), BF16)],
        [],
    )[0]


def add_and_split(arrays, upper):
    rows, wide = arrays[0].shape
    half = rows // 2
    tile = tile_rows(half)
    steps = half // tile
    spec = pl.BlockSpec((tile, wide), lambda g: (g, 0))
    high = pl.BlockSpec((tile, wide), lambda g: (g + steps, 0))
    return run_kernel(
        partial(split_kernel, len(arrays)),
        steps,
        [(SMEM, upper)]
        + [(spec, array) for array in arrays]
        + [(high, array) for array in arrays],
        [(spec, (half, wide), BF16)] * 2,
        [],
    )


class Fetch:
    def __init__(self, array, axis):
        size = array.shape[axis] // 2
        start = lax.axis_index("dp") % 2 * size
        self.half = lax.dynamic_slice_in_dim(array, start, size, axis=axis)
        self.group = lax.axis_size("heads")
        self.slots = {0: [array]}
        self.sent = {}

    def core(self, slot, *others):
        pieces = after(self.slots[slot], *others)
        self.slots[slot + 1] = [swap(piece, "heads", 1) for piece in pieces]

    def send(self, *others):
        (self.half,) = after([self.half], *others)
        for slot in range(2, self.group, 2):
            bit = low_bit(slot)
            if slot == bit:
                self.sent[slot] = swap(self.half, "heads", bit)

    def share(self, *others):
        for slot in range(2, self.group, 2):
            bit = low_bit(slot)
            if slot == bit:
                (came,) = after([self.sent[slot]], *others)
            else:
                came = swap(self.slots[slot - bit][0], "heads", bit)
            self.slots[slot] = [came, swap(came, "dp", 1)]

    def cores(self, first, last, *others):
        for slot in range(first, last, 2):
            self.core(slot, *others)

    def listed(self):
        return [self.slots[slot] for slot in range(self.group)]


def flat(slots):
    return [piece for pieces in slots for piece in pieces]


class GroupSum:
    def __init__(self):
        self.arrived = {}

    def put(self, slot, array, *others):
        arrays = [array] + self.arrived.pop(slot, [])
        if slot == 0:
            return arrays
        total = add_arrays(after(arrays, *others)) if len(arrays) > 1 else array
        bit = low_bit(slot)
        self.arrived.setdefault(slot - bit, []).append(swap(total, "heads", bit))
        return total


class DataSum:
    def __init__(self, arrays, bits):
        self.arrays = list(arrays)
        self.bits = list(bits)
        self.halved = []
        self.rows = arrays[0].shape[0]
        self.pieces = None

    def step(self, *others):
        arrays = after(self.arrays, *others)
        if not self.bits:
            total = add_arrays(arrays)
            self.gather(total)
            return total
        bit = self.bits.pop(0)
        if arrays[0].shape[0] % 32 == 0:
            upper = (lax.axis_index("dp") // bit % 2).astype(jnp.int32).reshape(1)
            keep, send = add_and_split(arrays, upper)
            self.halved.append(bit)
        else:
            keep = send = add_arrays(arrays)
        self.arrays = [keep, swap(send, "dp", bit)]
        return keep

    def gather(self, total):
        self.pieces = {0: total}
        for bit in self.halved[::-1]:
            for mask, piece in list(self.pieces.items()):
                self.pieces[mask | bit] = swap(piece, "dp", bit)

    def starts(self):
        own = lax.axis_index("dp")
        return [
            sum(
                (own ^ mask) // bit % 2 * (self.rows >> (at + 1))
                for at, bit in enumerate(self.halved)
            )
            for mask in self.pieces
        ]


def axis_bits(axis):
    size = lax.axis_size(axis)
    return [1 << at for at in range(size.bit_length() - 1)]


def on_device(
    noisy_mel,
    cond_mel,
    text_embed,
    time_embed,
    lengths,
    spans,
    dw_kernel,
    text_bias,
    text_gain,
    text_hidden,
    pw_in,
    pw_out,
    in_proj,
    frame_bias,
    mod_weight,
    mod_bias,
    qkv_weight,
    qkv_bias,
    out_weight,
    ff_in,
    ff_in_bias,
    ff_out,
    cotangent,
):
    group = lax.axis_size("heads")
    own = lax.axis_index("heads")
    own_data = lax.axis_index("dp")
    rows = text_embed.shape[0]
    model_width = in_proj.shape[1]
    width = qkv_weight.shape[2]
    units = ff_in.shape[1]
    block = min(128, width)
    parts = group // 2
    full = (rows, model_width)

    fetches = [Fetch(qkv_weight, 1), Fetch(out_weight, 0), Fetch(ff_in, 0), Fetch(ff_out, 0)]
    for fetch in fetches[:2]:
        fetch.send()
        fetch.core(0)

    time_rows = time_embed.astype(F32)
    activated, silu_back = jax.vjp(jax.nn.silu, time_rows)
    activated_low = activated.astype(BF16)
    modulation = (mm(activated_low, mod_weight) + mod_bias).astype(BF16)
    biases = jnp.concatenate([qkv_bias.reshape(-1), ff_in_bias])
    riders = jnp.broadcast_to(biases[None, :], (group, biases.size))
    sent = jnp.concatenate([modulation, riders], axis=1)
    came = lax.all_to_all(sent, "heads", split_axis=0, concat_axis=1, tiled=True)
    came = came.reshape(group, sent.shape[1]).astype(F32)
    mod_rows = came[:, : modulation.shape[1]].reshape(6, model_width)
    slot_owner = jnp.bitwise_xor(jnp.arange(group, dtype=jnp.int32), own)
    biases_all = jnp.take(came[:, modulation.shape[1] :], slot_owner, axis=0)
    qkv_bias_all = biases_all[:, : 3 * width].reshape(group, 3, width)
    up_bias_all = biases_all[:, 3 * width :].reshape(group, 1, units)

    position = jnp.arange(rows, dtype=jnp.int32)
    inside = (position >= spans[0, 0]) & (position < spans[0, 1])
    keep = jnp.where(inside, 0.0, 1.0).astype(F32)[:, None]
    count = lax.dynamic_slice_in_dim(lengths, own, 1)
    lane = jnp.arange(block, dtype=jnp.int32)
    pair = ((lane % HD) // 2).astype(F32)
    angle = position.astype(F32)[:, None] * (10000.0 ** (-2.0 * pair / HD))[None, :]
    cosine = jnp.cos(angle)
    sine = jnp.sin(angle) * jnp.where(lane % 2 == 0, -1.0, 1.0)[None, :]

    cond_low = (cond_mel.astype(F32) * keep).astype(BF16)
    mel = jnp.concatenate([noisy_mel, cond_low], axis=1)
    mels = mel.shape[1]
    text_width = text_embed.shape[1]
    gain = text_gain[None, :]

    def block_of(array):
        return (whole(array.shape), array)

    normed_text, pre_act, energy, mixed_text, refined, state_zero = run_kernel(
        text_forward,
        1,
        [
            block_of(member)
            for member in (
                text_embed,
                mel,
                dw_kernel,
                text_bias,
                gain,
                text_hidden,
                pw_in,
                pw_out,
                in_proj,
                frame_bias,
            )
        ],
        [
            (whole(shape), shape, kind)
            for shape, kind in (
                ((rows, text_width), BF16),
                ((rows, pw_in.shape[1]), F32),
                ((8, pw_in.shape[1]), F32),
                ((rows, pw_in.shape[1]), BF16),
                ((rows, text_width), BF16),
                (full, F32),
            )
        ],
        [pltpu.VMEM((rows + 16, text_width), F32), pltpu.VMEM((rows, pw_in.shape[1]), F32)],
    )

    def semaphores(number, pieces=2):
        shape = (number, pieces) if pieces > 1 else (number,)
        return pltpu.SemaphoreType.DMA(shape)

    def attn_buffers(number, pieces=2):
        return [
            pltpu.VMEM((number, 3, model_width, width), BF16),
            pltpu.VMEM((number, width, model_width), BF16),
            semaphores(number, pieces),
            semaphores(number, pieces),
        ]

    def ffn_buffers(number, pieces=2):
        return [
            pltpu.VMEM((number, model_width, units), BF16),
            pltpu.VMEM((number, units, model_width), BF16),
            semaphores(number, pieces),
            semaphores(number, pieces),
        ]

    half_index = (own_data % 2).astype(jnp.int32).reshape(1)

    def pieces_of(slots):
        return tuple(len(pieces) for pieces in slots)

    for fetch in fetches[2:]:
        fetch.send(state_zero)
    for fetch in fetches[:2]:
        fetch.share()
        fetch.cores(2, parts)
    kept = []
    for turn in range(2):
        first, last = turn == 0, turn == 1
        if last:
            for fetch in fetches[:2]:
                fetch.cores(parts, group, normed)
            for fetch in fetches[2:]:
                fetch.share(normed)
                fetch.core(0, normed)
            (before,) = after([before], *[fetch.slots[2][0] for fetch in fetches[2:]])
        chosen = range(turn * parts, (turn + 1) * parts)
        qkv_here = [fetches[0].slots[slot] for slot in chosen]
        out_here = [fetches[1].slots[slot] for slot in chosen]
        inputs = [
            (SMEM, count),
            (SMEM, half_index),
            (whole(full), state_zero),
            (whole((6, model_width)), mod_rows),
            (held((3, width)), qkv_bias_all[chosen[0] : chosen[-1] + 1]),
            (whole((3, model_width)), frame_bias),
            (whole((rows, block)), cosine),
            (whole((rows, block)), sine),
        ]
        inputs += [(ANY, member) for member in flat(qkv_here) + flat(out_here)]
        if not first:
            inputs += [(whole(full), normed), (whole(full), before)]
        outputs = [(held((rows, width)), (parts, rows, width), BF16)] * 4
        outputs += [(held((8, rows)), (parts, 8, rows), F32)]
        if first:
            outputs += [(whole(full), full, BF16)]
        outputs += [(whole(full), full, F32)]
        if last:
            outputs += [(whole(full), full, F32), (whole(full), full, BF16)]
        results = run_kernel(
            partial(attention_forward, pieces_of(qkv_here), first, last),
            parts,
            inputs,
            outputs,
            attn_buffers(parts) + ([pltpu.VMEM(full, F32)] if last else []),
        )
        kept.append(results[:5])
        if first:
            normed, before = results[5:]
        else:
            branch, state_one, ffn_in = results[5:]

    qkv_all, out_all = fetches[0].listed(), fetches[1].listed()
    fetches[2].cores(2, group, ffn_in)
    fetches[3].cores(2, group, ffn_in)
    up_all, down_all = fetches[2].listed()[::-1], fetches[3].listed()[::-1]
    inputs = [
        (SMEM, half_index),
        (whole(full), cotangent),
        (whole(full), state_one),
        (whole(full), branch),
        (whole(full), ffn_in),
        (whole((6, model_width)), mod_rows),
        (held((1, units), group), up_bias_all),
        (whole((3, model_width)), frame_bias),
    ]
    inputs += [(ANY, member) for member in flat(up_all) + flat(down_all)]
    merged = (2 * units, model_width)
    outputs = [(held((1, units), group), (group, 1, units), F32)]
    outputs += [(whole((8, model_width)), (8, model_width), F32)]
    outputs += [(ANY, merged, BF16)] * group
    outputs += [(whole(full), full, BF16)] * 2 + [(whole(full), full, F32)]
    outputs += [(whole(full), full, BF16)]
    results = run_kernel(
        partial(feed_forward, pieces_of(up_all), True, True),
        group,
        inputs,
        outputs,
        [
            pltpu.VMEM((group, model_width, units), BF16),
            pltpu.VMEM((group, units, model_width), BF16),
            semaphores(group),
            semaphores(group),
            pltpu.VMEM((group,) + merged, BF16),
            semaphores(group, 1),
            pltpu.VMEM((model_width, rows), BF16),
            pltpu.VMEM((rows, units), BF16),
            pltpu.VMEM((rows, units), BF16),
        ]
        + [pltpu.VMEM(full, F32)] * 2,
    )
    grad_up_bias, ffn_sums = results[:2]
    output, grad_one, grad_attn = results[3 + group :]
    ffn_grads = results[2 : 2 + group][::-1]

    attn_grads = []
    merged = (4 * width, model_width)
    qkv_bias_parts = []
    for turn in range(2):
        first, last = turn == 0, turn == 1
        chosen = [group - 1 - turn * parts - at for at in range(parts)]
        inputs = [
            (SMEM, count),
            (SMEM, half_index),
            (whole(full), grad_attn),
            (whole(full), normed),
            (whole((6, model_width)), mod_rows),
            (whole((rows, block)), cosine),
            (whole((rows, block)), sine),
        ]
        inputs += [(held((rows, width), parts), member) for member in kept[1 - turn][:4]]
        inputs += [(held((8, rows), parts), kept[1 - turn][4])]
        inputs += [(ANY, member) for member in flat([qkv_all[slot] for slot in chosen])]
        inputs += [(ANY, member) for member in flat([out_all[slot] for slot in chosen])]
        if not first:
            inputs += [(whole(full), back)]
        if last:
            inputs += [(whole(full), state_zero), (whole(full), grad_one)]
        outputs = [(held((3, width), parts), (parts, 3, width), F32)]
        outputs += [(ANY, merged, BF16)] * parts
        if last:
            outputs += [(whole(full), full, BF16), (whole((8, model_width)), (8, model_width), F32)]
        else:
            outputs += [(whole(full), full, F32)]
        results = run_kernel(
            partial(attention_backward, pieces_of([qkv_all[slot] for slot in chosen]), first, last),
            parts,
            inputs,
            outputs,
            attn_buffers(parts)
            + [pltpu.VMEM((parts,) + merged, BF16), semaphores(parts, 1)]
            + [pltpu.VMEM((model_width, rows), BF16), pltpu.VMEM((rows, width), BF16)]
            + ([pltpu.VMEM(full, F32)] if last else []),
        )
        qkv_bias_parts.append(results[0])
        attn_grads = list(results[1 : 1 + parts])[::-1] + attn_grads
        if first:
            back = results[1 + parts]
            ffn_sum = GroupSum()
            for slot in range(group - 1, 0, -1):
                token = ffn_sum.put(slot, ffn_grads[slot], back)
                if slot % 2 == 0:
                    (back,) = after([back], token)
        else:
            grad_zero, attn_sums = results[1 + parts :]
    attn_sum = GroupSum()
    for slot in range(group - 1, 0, -1):
        token = attn_sum.put(slot, attn_grads[slot], grad_zero)
        if slot % 2 == 0:
            (grad_zero,) = after([grad_zero], token)

    stack_rows = 3 * text_width + mels
    stack_rows += -stack_rows % 16 + small_rows(group)
    stack_rows += -stack_rows % (16 * group)
    own_index = own.astype(jnp.int32).reshape(1)
    results = run_kernel(
        partial(text_backward, group),
        1,
        [(SMEM, own_index)]
        + [
            block_of(member)
            for member in (
                grad_zero,
                text_embed,
                mel,
                refined,
                mixed_text,
                normed_text,
                pre_act,
                energy,
                dw_kernel,
                text_bias,
                gain,
                text_hidden,
                pw_in,
                pw_out,
                in_proj,
                attn_sums,
                ffn_sums,
                qkv_bias_parts[0],
                qkv_bias_parts[1],
                grad_up_bias,
            )
        ],
        [
            (whole((rows, text_width)), (rows, text_width), F32),
            (whole((6, model_width)), (6, model_width), F32),
        ]
        + [(ANY, (stack_rows // group, model_width), BF16)] * group,
        [
            pltpu.VMEM((stack_rows, model_width), BF16),
            semaphores(group, 1),
            pltpu.VMEM((rows + 16, text_width), F32),
            pltpu.VMEM((rows + 16, text_width), F32),
            pltpu.VMEM((rows, text_width), F32),
            pltpu.VMEM((rows, text_width), BF16),
            pltpu.VMEM((rows, pw_in.shape[1]), F32),
            pltpu.VMEM((rows, pw_in.shape[1]), BF16),
            pltpu.VMEM((rows, text_width), F32),
            pltpu.VMEM((small_rows(group), model_width), F32),
        ],
    )
    grad_text, grad_mod = results[:2]
    text_sum = GroupSum()
    bits = axis_bits("dp")
    ffn_data = DataSum(ffn_sum.put(0, ffn_grads[0]), bits)
    token = ffn_data.step(grad_mod)
    for slot in range(group - 1, 0, -1):
        total = text_sum.put(slot, results[2 + slot], token)
        if slot % 2 == 0:
            token = total
    attn_data = DataSum(attn_sum.put(0, attn_grads[0]), bits)
    text_data = DataSum(text_sum.put(0, results[2]), bits)
    (grad_mod,) = after([grad_mod], token)
    steps = [(at, ffn_data) for at in range(1, len(bits) + 1)]
    for at in range(len(bits) + 1):
        steps.append((at + 2.2 if at else 1.5, attn_data))
        steps.append((at + 2.25, text_data))
    for _, member in sorted(steps, key=lambda step: step[0]):
        token = member.step(token)
    text_pieces = [[text_data.pieces[mask] for mask in text_data.pieces]]
    for slot in range(1, group):
        bit = low_bit(slot)
        text_pieces.append([swap(piece, "heads", bit) for piece in text_pieces[slot - bit]])
    slot_rows = stack_rows // group
    text_starts = [
        slot_owner[slot] * slot_rows + start
        for slot in range(group)
        for start in text_data.starts()
    ]
    text_pieces = [piece for pieces in text_pieces for piece in pieces]
    unpacked = (
        in_proj.shape,
        pw_in.shape,
        pw_out.shape,
        dw_kernel.shape,
        text_bias.shape,
        gain.shape,
        text_hidden.shape,
        frame_bias.shape,
        (3, width),
        (1, units),
    )
    unpacked = run_kernel(
        partial(text_unpack, len(text_pieces), group),
        1,
        [(SMEM, jnp.stack(text_starts).astype(jnp.int32)), (SMEM, own_index)]
        + [(ANY, member) for member in text_pieces],
        [(whole(shape), shape, F32) for shape in unpacked],
        [
            pltpu.VMEM((stack_rows, model_width), BF16),
            semaphores(len(text_pieces), 1),
            pltpu.VMEM((small_rows(group), model_width), F32),
        ],
    )
    def unpack(data, kernel, first, second):
        pieces = list(data.pieces.values())
        return run_kernel(
            partial(kernel, len(pieces)),
            1,
            [(SMEM, jnp.stack(data.starts()).astype(jnp.int32))]
            + [(ANY, member) for member in pieces],
            [(whole(first.shape), first.shape, F32), (whole(second.shape), second.shape, F32)],
            [pltpu.VMEM((data.rows, model_width), BF16), semaphores(len(pieces), 1)],
        )

    weight_up, weight_down = unpack(ffn_data, ffn_unpack, ff_in, ff_out)
    weight_qkv, weight_out = unpack(attn_data, attn_unpack, qkv_weight, out_weight)

    grad_mod = grad_mod.astype(BF16).reshape(1, -1)
    grad_mod_cols = lax.all_to_all(grad_mod, "heads", split_axis=1, concat_axis=0, tiled=True)
    seen = jnp.concatenate([activated_low, grad_mod_cols], axis=1)
    for bit in bits:
        seen = jnp.concatenate([seen, swap(seen, "dp", bit)], axis=0)
    grad_mod_weight = inner_rows(seen[:, :model_width], seen[:, model_width:])
    grad_mod_bias = jnp.sum(seen[:, model_width:].astype(F32), axis=0)
    (grad_time,) = silu_back(inner_cols(grad_mod_cols, mod_weight))
    for bit in axis_bits("heads"):
        rounded = grad_time.astype(BF16)
        grad_time = rounded.astype(F32) + swap(rounded, "heads", bit).astype(F32)
    return (
        output,
        grad_text,
        grad_time,
        unpacked[3],
        unpacked[4],
        unpacked[5][0],
        unpacked[6],
        unpacked[1],
        unpacked[2],
        unpacked[0],
        unpacked[7],
        grad_mod_weight,
        grad_mod_bias,
        weight_qkv,
        unpacked[8],
        weight_out,
        weight_up,
        unpacked[9][0],
        weight_down,
    )


def solution(mesh):
    in_specs = (
        P(("dp", "heads"), None),
        P(("dp", "heads"), None),
        P(("dp", "heads"), None),
        P("dp", None),
        P("dp"),
        P(("dp", "heads"), None),
        P(),
        P(),
        P(),
        P(),
        P(),
        P(),
        P(),
        P(),
        P(None, "heads"),
        P("heads"),
        P(None, None, "heads"),
        P(None, "heads"),
        P("heads", None),
        P(None, "heads"),
        P("heads"),
        P("heads", None),
        P(("dp", "heads"), None),
    )
    out_specs = (
        P(("dp", "heads"), None),
        P(("dp", "heads"), None),
        P("dp", None),
        P(),
        P(),
        P(),
        P(),
        P(),
        P(),
        P(),
        P(),
        P(None, "heads"),
        P("heads"),
        P(None, None, "heads"),
        P(None, "heads"),
        P("heads", None),
        P(None, "heads"),
        P("heads"),
        P("heads", None),
    )
    return jax.shard_map(
        on_device, mesh=mesh, in_specs=in_specs, out_specs=out_specs, check_vma=False
    )
```

time: 1270 us -> 433 us (0.34)
  waiting for transfers between devices: 599 us -> 125 us
  matrix products: 294 us -> 7.22 us
  Pallas kernels: 0 us -> 189 us
  other arithmetic: 143 us -> 15.1 us
  local copies, waits for them, and re-layouts: 148 us -> 25.7 us
  blocking collectives: 51.9 us -> 0 us
  starting transfers between devices: 9.07 us -> 59.1 us
  between operations: 17.1 us -> 4.03 us
    psum x2 -> x0, waiting for transfers between devices: 319 us -> none  [the longest x1 263 us: on_device(): lax.psum(replicated[5].astype(jnp.bfloat16), 'dp').astype(jnp.float32)]
    pallas_call x0 -> x25, Pallas kernels: none -> 189 us  [run_kernel(): pl.pallas_call(kernel, grid=(parts,), in_specs=[spec for spec, _ in input...]
    reduce_scatter x4 -> x0, waiting for transfers between devices: 147 us -> none  [the longest x1 44.6 us: on_device(): lax.psum_scatter(jnp.dot(attended_low, out_weight, preferred_element_type...]
    all_gather x4 -> x0, waiting for transfers between devices: 132 us -> none  [the longest x1 35.4 us: on_device(): source = lax.all_gather(attn_in, 'heads', axis=0, tiled=True)]
    ppermute x0 -> x72, waiting for transfers between devices: none -> 118 us  [swap(): lax.ppermute(array, axis, [(at, at ^ bit) for at in range(lax.axis_size(a...]
    dot_general x42 -> x1, matrix products: 108 us -> 1.25 us  [mm(): return jnp.dot(left, right, preferred_element_type=F32)]
    dot_general x58 -> x1, matrix products: 93.3 us -> 1.53 us  [inner_cols(): lax.dot_general(left, right, (((1,), (1,)), ((), ())), preferred_element_...]
    dot_general x42 -> x1, matrix products: 92.9 us -> 4.44 us  [inner_rows(): lax.dot_general(left, right, (((0,), (0,)), ((), ())), preferred_element_...]
  transfers between devices with their start and end apart: 12 -> 74, of which waited for: 11 -> 28; matrix products, arithmetic and copies ran while one was open for 9% -> 9% of each run, Pallas kernels for 0% -> 37%
where the time goes in v1:
time: 433 us; the launch traced here: 425 us
  Pallas kernels  189 us (44%)
  waiting for transfers between devices  125 us (29%)
  starting transfers between devices  59.1 us (14%)
  local copies, waits for them, and re-layouts  25.7 us (6%)
  other arithmetic  15.1 us (3%)
  matrix products  7.22 us (2%)
    pallas_call x25, Pallas kernels, run_kernel(): pl.pallas_call(kernel, grid=(parts,), in_specs=[spec for spec, _ in input...  189 us
    ppermute x72, waiting for transfers between devices, swap(): lax.ppermute(array, axis, [(at, at ^ bit) for at in range(lax.axis_size(a...  118 us
    ppermute x72, starting transfers between devices, swap(): lax.ppermute(array, axis, [(at, at ^ bit) for at in range(lax.axis_size(a...  51.6 us
    unnamed x70, local copies, waits for them, and re-layouts  9.07 us
  transfers between devices with their start and end apart: 74, of which 28 were waited for; matrix products, arithmetic and copies ran while one was open for 9% of the time, Pallas kernels for 37%

profile of v1, /device:TPU:0, one launch (start us, length us, event | category | flops | bytes accessed | tf_op | source)
XLA Modules:
  0.0 424.9 jit_solution(5894912182058216094)
XLA Ops:
  5.7 4.2 all-to-all-start
  11.6 2.6 collective-permute-start.6
  14.2 2.1 constant_dynamic-slice_fusion.3
  19.8 1.9 constant_dynamic-slice_fusion.1
  24.1 1.8 pad_maximum_fusion.mel_ref.refs_3_
  25.9 9.7 %shard_map.366 = (bf16[512,512]{1,0:T(8,128)(2,1)}, f32[512,1024]{1,0:T(8,128)}, f32[8,1024]{1,0:T(8,128)}, bf16[512,1024]{1,0:T(8,128)(2,1)}, bf16[512,512]{1,0:T(8,128)(2,1)}, /*index=5*/f32[512,1024]{1,0:T(8,128)}) custom-call(bf16[512,512]{1,0:T(8,128)(2,1)} %refs_2_.1, bf16[512,200]{1,0:T(8,128)(2,1)} %pad_maximum_fusion.mel_ref.refs_3_, ...), custom_call_target="tpu_custom_call" | custom-call | flops 1024 | bytes 1024 | tf_op jit(solution)/shard_map/pallas_call | solution.py:868
  35.5 1.7 collective-permute-start.10
  37.3 1.9 constant_dynamic-slice_fusion
  39.2 1.8 fusion.1
  42.4 2.0 collective-permute-start.1
  46.6 14.3 %shard_map.367 = (bf16[2,512,256]{2,1,0:T(8,128)(2,1)}, bf16[2,512,256]{2,1,0:T(8,128)(2,1)}, bf16[2,512,256]{2,1,0:T(8,128)(2,1)}, bf16[2,512,256]{2,1,0:T(8,12...) custom-call(s32[1]{0:T(128)} %dynamic_slice.15.refs_0_, s32[1]{0:T(128)} %bitcast.refs_1_.refs_0_, ...), custom_call_target="tpu_custom_call" | custom-call | flops 1024 | bytes 1024 | tf_op jit(solution)/shard_map/pallas_call | solution.py:868
  62.4 1.8 collective-permute-start.7
  64.4 6.8 %collective-permute-done.7.refs_13_.refs_19_ = bf16[128,1024]{1,0:T(8,128)(2,1)S(1)} collective-permute-done((bf16[128,1024]{1,0:T(8,128)(2,1)S(1)}, bf16[128,1024]{1,0:T(8,128)(2,1)S(1)}, u32[]{:S(2)}, u32[]{:S(2)}) %collective-permute-start.7) | collective-permute-done | bytes 262176 | tf_op jit(solution)/shard_map/ppermute | solution.py:886
  71.7 2.1 collective-permute-done.8.refs_14_.refs_16_
  76.9 18.1 %shard_map.368 = (bf16[2,512,256]{2,1,0:T(8,128)(2,1)}, bf16[2,512,256]{2,1,0:T(8,128)(2,1)}, bf16[2,512,256]{2,1,0:T(8,128)(2,1)}, bf16[2,512,256]{2,1,0:T(8,12...) custom-call(s32[1]{0:T(128)} %dynamic_slice.15.refs_0_, ...), custom_call_target="tpu_custom_call" | custom-call | flops 1024 | bytes 1024 | tf_op jit(solution)/shard_map/pallas_call | solution.py:868
  95.0 4.3 %collective-permute-done.12.refs_11_ = bf16[512,512]{1,0:T(8,128)(2,1)} collective-permute-done((bf16[512,512]{1,0:T(8,128)(2,1)}, bf16[512,512]{1,0:T(8,128)(2,1)}, u32[]{:S(2)}, u32[]{:S(2)}) %collective-permute-start.12) | collective-permute-done | bytes 524320 | tf_op jit(solution)/shard_map/ppermute | solution.py:886
  103.8 25.0 %shard_map.369 = (f32[4,1,512]{2,1,0:T(1,128)}, f32[8,1024]{1,0:T(8,128)}, bf16[1024,1024]{1,0:T(8,128)(2,1)}, bf16[1024,1024]{1,0:T(8,128)(2,1)}, bf16[1024,102...) custom-call(s32[1]{0:T(128)} %bitcast.refs_1_.refs_0_, ...), custom_call_target="tpu_custom_call" | custom-call | flops 1024 | bytes 1024 | tf_op jit(solution)/shard_map/pallas_call | solution.py:868
  129.0 20.6 %shard_map.370 = (f32[2,3,256]{2,1,0:T(4,128)}, bf16[1024,1024]{1,0:T(8,128)(2,1)}, bf16[1024,1024]{1,0:T(8,128)(2,1)}, f32[512,1024]{1,0:T(8,128)}) custom-call(s32[1]{0:T(128)} %dynamic_slice.15.refs_0_, s32[1]{0:T(128)} %bitcast.refs_1_.refs_0_, bf16[512,1024]{1,0:T(8,128)(2,1)} %get-tuple-element.167.refs_2_, ...), custom_call_target="tpu_custom_call" | custom-call | flops 1024 | bytes 1024 | tf_op jit(solution)/shard_map/pallas_call | solution.py:868
  150.2 4.3 %shard_map.371 = bf16[1024,1024]{1,0:T(8,128)(2,1)} custom-call(bf16[1024,1024]{1,0:T(8,128)(2,1)} %get-tuple-element.181.refs_0_, bf16[1024,1024]{1,0:T(8,128)(2,1)} %collective-permute-done.20.refs_1_), custom_call_target="tpu_custom_call" | custom-call | flops 1024 | bytes 1024 | tf_op jit(solution)/shard_map/pallas_call | solution.py:868
  154.9 23.2 %shard_map.372 = (f32[2,3,256]{2,1,0:T(4,128)}, bf16[1024,1024]{1,0:T(8,128)(2,1)}, bf16[1024,1024]{1,0:T(8,128)(2,1)}, bf16[512,1024]{1,0:T(8,128)(2,1)}, f32[8,1024]{1,0:T(8,128)}) custom-call(s32[1]{0:T(128)} %dynamic_slice.15.refs_0_, s32[1]{0:T(128)} %bitcast.refs_1_.refs_0_, bf16[512,1024]{1,0:T(8,128)(2,1)} %get-tuple-element.167.refs_2_, ...), custom_call_target="tpu_custom_call" | custom-call | flops 1024 | bytes 1024 | tf_op jit(solution)/shard_map/pallas_call | solution.py:868
  178.3 4.3 %shard_map.373 = bf16[1024,1024]{1,0:T(8,128)(2,1)} custom-call(bf16[1024,1024]{1,0:T(8,128)(2,1)} %get-tuple-element.188.refs_0_, bf16[1024,1024]{1,0:T(8,128)(2,1)} %collective-permute-done.21.refs_1_), custom_call_target="tpu_custom_call" | custom-call | flops 1024 | bytes 1024 | tf_op jit(solution)/shard_map/pallas_call | solution.py:868
  184.2 21.2 %shard_map.374 = (f32[512,512]{1,0:T(8,128)}, f32[6,1024]{1,0:T(8,128)}, bf16[448,1024]{1,0:T(8,128)(2,1)}, bf16[448,1024]{1,0:T(8,128)(2,1)}, bf16[448,1024]{1,0:T(8,128)(2,1)}, /*index=5*/bf16[448,1024]{1,0:T(8,128)(2,1)}) custom-call(s32[1]{0:T(128)} %bitcast.8.refs_0_.own_ref, bf16[512,1024]{1,0:T(8,128)(2,1)} %get-tuple-element.190.refs_1_, ...), custom_call_target="tpu_custom_call" | custom-call | flops 1024 | bytes 1024 | tf_op jit(solution)/shard_map/pallas_call | solution.py:868
  205.7 4.2 shard_map.375
  209.9 1.7 collective-permute-start.29
  212.6 2.5 shard_map.376
  215.5 20.1 %collective-permute-done.29.refs_2_.refs_4_ = bf16[512,1024]{1,0:T(8,128)(2,1)} collective-permute-done((bf16[512,1024]{1,0:T(8,128)(2,1)}, bf16[512,1024]{1,0:T(8,128)(2,1)}, u32[]{:S(2)}, u32[]{:S(2)}) %collective-permute-start.29) | collective-permute-done | bytes 1048608 | tf_op jit(solution)/shard_map/ppermute | solution.py:886
  235.6 2.8 shard_map.377
  238.4 9.9 %collective-permute-done.31.refs_2_.refs_5_ = bf16[1024,1024]{1,0:T(8,128)(2,1)} collective-permute-done((bf16[1024,1024]{1,0:T(8,128)(2,1)}, bf16[1024,1024]{1,0:T(8,128)(2,1)}, u32[]{:S(2)}, u32[]{:S(2)}) %collective-permute-start.31) | collective-permute-done | bytes 2097184 | tf_op jit(solution)/shard_map/ppermute | solution.py:886
  248.3 4.2 shard_map.378
  252.5 1.7 collective-permute-start.34
  257.2 3.3 all-to-all-start.1
  260.5 7.0 %all-to-all-done.1 = bf16[4,2,768]{2,1,0:T(2,128)(2,1)S(1)} async-done(((bf16[4,2,768]{2,1,0:T(2,128)(2,1)}), bf16[4,2,768]{2,1,0:T(2,128)(2,1)S(1)}, u32[]{:S(2)}, u32[]{:S(2)}) %all-to-all-start.1) | async-done | bytes 12320 | tf_op jit(solution)/shard_map/all_to_all | solution.py:1430
  267.5 2.1 shard_map.379
  269.6 2.9 collective-permute-start.35
  272.5 3.0 shard_map.380
  278.5 6.4 %collective-permute-done.35.refs_1_ = bf16[128,1024]{1,0:T(8,128)(2,1)S(1)} collective-permute-done((bf16[128,1024]{1,0:T(8,128)(2,1)}, bf16[128,1024]{1,0:T(8,128)(2,1)S(1)}, u32[]{:S(2)}, u32[]{:S(2)}) %collective-permute-start.35) | collective-permute-done | bytes 262176 | tf_op jit(solution)/shard_map/ppermute | solution.py:886
  285.7 1.8 shard_map.381.refs_0_
  287.5 2.8 shard_map.382
  290.2 4.1 collective-permute-start.37
  297.9 2.2 shard_map.383
  303.0 8.4 %collective-permute-done.37.refs_2_.refs_4_ = bf16[256,1024]{1,0:T(8,128)(2,1)S(1)} collective-permute-done((bf16[256,1024]{1,0:T(8,128)(2,1)}, bf16[256,1024]{1,0:T(8,128)(2,1)S(1)}, u32[]{:S(2)}, u32[]{:S(2)}) %collective-permute-start.37) | collective-permute-done | bytes 524320 | tf_op jit(solution)/shard_map/ppermute | solution.py:886
  312.2 2.1 shard_map.384
  314.3 7.7 %collective-permute-done.36.refs_1_ = bf16[112,1024]{1,0:T(8,128)(2,1)} collective-permute-done((bf16[112,1024]{1,0:T(8,128)(2,1)}, bf16[112,1024]{1,0:T(8,128)(2,1)}, u32[]{:S(2)}, u32[]{:S(2)}) %collective-permute-start.36) | collective-permute-done | bytes 229408 | tf_op jit(solution)/shard_map/ppermute | solution.py:886
  322.1 1.8 shard_map.385.refs_0_
  325.9 3.4 collective-permute-done.26
  333.3 2.4 collective-permute-done.38.refs_1_
  337.8 12.6 %collective-permute-done.39.refs_1_ = bf16[128,1024]{1,0:T(8,128)(2,1)S(1)} collective-permute-done((bf16[128,1024]{1,0:T(8,128)(2,1)}, bf16[128,1024]{1,0:T(8,128)(2,1)S(1)}, u32[]{:S(2)}, u32[]{:S(2)}) %collective-permute-start.39) | collective-permute-done | bytes 262176 | tf_op jit(solution)/shard_map/ppermute | solution.py:886
  351.1 1.8 shard_map.386.refs_0_
  352.9 1.8 shard_map.387.refs_0_
  354.7 2.2 collective-permute-done.57
  359.4 2.5 collective-permute-start.40
  361.9 2.7 collective-permute-done.47.refs_8_
  365.4 7.3 %collective-permute-done.58.refs_1_ = bf16[128,1024]{1,0:T(8,128)(2,1)S(1)} collective-permute-done((bf16[128,1024]{1,0:T(8,128)(2,1)}, bf16[128,1024]{1,0:T(8,128)(2,1)S(1)}, u32[]{:S(2)}, u32[]{:S(2)}) %collective-permute-start.58) | collective-permute-done | bytes 262176 | tf_op jit(solution)/shard_map/ppermute | solution.py:886
  375.9 3.9 collective-permute-done.59.refs_2_
  380.0 1.9 collective-permute-start.62
  382.6 2.1 collective-permute-done.60.refs_3_
  388.5 1.8 collective-permute-start.48
  393.2 4.3 %collective-permute-done.48.refs_9_ = bf16[112,1024]{1,0:T(8,128)(2,1)} collective-permute-done((bf16[112,1024]{1,0:T(8,128)(2,1)}, bf16[112,1024]{1,0:T(8,128)(2,1)}, u32[]{:S(2)}, u32[]{:S(2)}) %collective-permute-start.48) | collective-permute-done | bytes 229408 | tf_op jit(solution)/shard_map/ppermute | solution.py:886
  397.4 2.4 collective-permute-done.63.refs_6_
  400.9 2.3 collective-permute-done.64.refs_7_
  403.2 4.4 %fusion.2 = f32[1024,1536]{1,0:T(8,128)} fusion(bf16[16,2560]{1,0:T(8,128)(2,1)S(1)} %collective-permute-done.57, bf16[8,2560]{1,0:T(8,128)(2,1)S(1)} %collective-permute-done.56, bf16[4,2560]{1,0:T(4,128)(2,1)} %collective-permute-done.55, bf16[4,1536]{1,0:T(4,128)(2,1)S(1)} %bitcast.56, bf16[4,1024]{1,0:T(4,128)(2,1)S(1)} %copy-done.12), kind=kOutput, calls=%fused_computation.14 | convolution fusion | flops 101482496 | bytes 6455296 | tf_op jit(solution)/shard_map/dot_general | solution.py:14
  409.0 4.4 %shard_map.390 = (f32[1024,512]{1,0:T(8,128)}, f32[512,1024]{1,0:T(8,128)}) custom-call(s32[8]{0:T(128)} %stack.112.starts_ref, bf16[128,1024]{1,0:T(8,128)(2,1)} %shard_map.381.refs_0_, bf16[128,1024]{1,0:T(8,128)(2,1)} %collective-permute-done.65.refs_1_, bf16[128,1024]{1,0:T(8,128)(2,1)} %collective-permute-done.66.refs_2_, ...), custom_call_target="tpu_custom_call" | custom-call | flops 1024 | bytes 1024 | tf_op jit(solution)/shard_map/pallas_call | solution.py:868
  413.4 4.5 %shard_map.389 = (f32[3,1024,256]{2,1,0:T(8,128)}, f32[256,1024]{1,0:T(8,128)}) custom-call(s32[8]{0:T(128)} %stack.112.starts_ref, bf16[128,1024]{1,0:T(8,128)(2,1)} %shard_map.386.refs_0_, bf16[128,1024]{1,0:T(8,128)(2,1)} %copy-done.14, bf16[128,1024]{1,0:T(8,128)(2,1)} %collective-permute-done.59.refs_2_, ...), custom_call_target="tpu_custom_call" | custom-call | flops 1024 | bytes 1024 | tf_op jit(solution)/shard_map/pallas_call | solution.py:868
  418.6 6.1 %shard_map.388 = (f32[712,1024]{1,0:T(8,128)}, f32[512,1024]{1,0:T(8,128)}, f32[1024,512]{1,0:T(8,128)}, f32[7,512]{1,0:T(8,128)}, f32[3,512]{1,0:T(4,128)}, /*i...) custom-call(s32[16]{0:T(128)} %stack.103.starts_ref, ...), custom_call_target="tpu_custom_call" | custom-call | flops 1024 | bytes 1024 | tf_op jit(solution)/shard_map/pallas_call | solution.py:868
  (227 shorter events, 68.0 us)
Async XLA Ops:
  5.7 35.9 %all-to-all-start = ((bf16[4,2,1408]{2,1,0:T(2,128)(2,1)}), bf16[4,2,1408]{2,1,0:T(2,128)(2,1)}, u32[]{:S(2)}, u32[]{:S(2)}) async-start(bf16[4,2,1408]{2,1,0:T(2,128)(2,1)} %reshape.184), calls=%async_computation | async-start | bytes 45056 | tf_op jit(solution)/shard_map/all_to_all | solution.py:1077
  11.6 50.8 %collective-permute-start.6 = (bf16[128,1024]{1,0:T(8,128)(2,1)}, bf16[128,1024]{1,0:T(8,128)(2,1)S(1)}, u32[]{:S(2)}, u32[]{:S(2)}) collective-permute-start(bf16[128,1024]{1,0:T(8,128)(2,1)} %constant_dynamic-slice_fusion.2), channel_id=1, source_target_pairs={{0,2},{1,3},{2,0},{3,1},{4,6},{5,7},{6,4},{7,5},{8,10},{9,11},{10,... | collective-permute-start | bytes 786440 | tf_op jit(solution)/shard_map/ppermute | solution.py:886
  14.2 32.1 %collective-permute-start.3 = (bf16[256,1024]{1,0:T(8,128)(2,1)}, bf16[256,1024]{1,0:T(8,128)(2,1)}, u32[]{:S(2)}, u32[]{:S(2)}) collective-permute-start(bf16[256,1024]{1,0:T(8,128)(2,1)} %refs_15_.2), channel_id=1, source_target_pairs={{0,1},{1,0},{2,3},{3,2},{4,5},{5,4},{6,7},{7,6},{8,9},{9,8},{10,11... | collective-permute-start | bytes 1572872 | tf_op jit(solution)/shard_map/ppermute | solution.py:886
  16.3 26.1 %collective-permute-start = (bf16[3,512,256]{2,1,0:T(8,128)(2,1)}, bf16[3,512,256]{2,1,0:T(8,128)(2,1)}, u32[]{:S(2)}, u32[]{:S(2)}) collective-permute-start(bf16[3,512,256]{2,1,0:T(8,128)(2,1)} %constant_dynamic-slice_fusion.3), channel_id=1, source_target_pairs={{0,2},{1,3},{2,0},{3,1},{4,6},{5,7},{6,4},{7,5},{8,10},{9,11},{10,... | collective-permute-start | bytes 2359304 | tf_op jit(solution)/shard_map/ppermute | solution.py:886
  16.3 30.3 %collective-permute-start.2 = (bf16[3,1024,256]{2,1,0:T(8,128)(2,1)}, bf16[3,1024,256]{2,1,0:T(8,128)(2,1)}, u32[]{:S(2)}, u32[]{:S(2)}) collective-permute-start(bf16[3,1024,256]{2,1,0:T(8,128)(2,1)} %refs_13_.4), channel_id=1, source_target_pairs={{0,1},{1,0},{2,3},{3,2},{4,5},{5,4},{6,7},{7,6},{8,9},{9,8},{10,11... | collective-permute-start | bytes 4718600 | tf_op jit(solution)/shard_map/ppermute | solution.py:886
  35.5 35.6 %collective-permute-start.10 = (bf16[512,512]{1,0:T(8,128)(2,1)}, bf16[512,512]{1,0:T(8,128)(2,1)}, u32[]{:S(2)}, u32[]{:S(2)}) collective-permute-start(bf16[512,512]{1,0:T(8,128)(2,1)} %constant_dynamic-slice_fusion.1), channel_id=1, source_target_pairs={{0,2},{1,3},{2,0},{3,1},{4,6},{5,7},{6,4},{7,5},{8,10},{9,11},{10,... | collective-permute-start | bytes 1572872 | tf_op jit(solution)/shard_map/ppermute | solution.py:886
  42.4 20.0 %collective-permute-start.1 = (bf16[3,512,256]{2,1,0:T(8,128)(2,1)}, bf16[3,512,256]{2,1,0:T(8,128)(2,1)}, u32[]{:S(2)}, u32[]{:S(2)}) collective-permute-start(bf16[3,512,256]{2,1,0:T(8,128)(2,1)} %collective-permute-done.refs_8_.refs_14_), channel_id=1, source_target_pairs={{0,4},{4,0},{8,12},{12,8},{16,20},{20,16},{24,28},{28,24},{1,5},{5... | collective-permute-start | bytes 2359304 | tf_op jit(solution)/shard_map/ppermute | solution.py:886
  46.3 25.3 %collective-permute-start.11 = (bf16[256,1024]{1,0:T(8,128)(2,1)}, bf16[256,1024]{1,0:T(8,128)(2,1)}, u32[]{:S(2)}, u32[]{:S(2)}) collective-permute-start(bf16[256,1024]{1,0:T(8,128)(2,1)} %constant_dynamic-slice_fusion), channel_id=1, source_target_pairs={{0,2},{1,3},{2,0},{3,1},{4,6},{5,7},{6,4},{7,5},{8,10},{9,11},{10,... | collective-permute-start | bytes 1572872 | tf_op jit(solution)/shard_map/ppermute | solution.py:886
  62.4 13.9 %collective-permute-start.4 = (bf16[3,512,256]{2,1,0:T(8,128)(2,1)}, bf16[3,512,256]{2,1,0:T(8,128)(2,1)}, u32[]{:S(2)}, u32[]{:S(2)}) collective-permute-start(bf16[3,512,256]{2,1,0:T(8,128)(2,1)} %collective-permute-done.refs_8_.refs_14_), channel_id=1, source_target_pairs={{0,1},{1,0},{2,3},{3,2},{4,5},{5,4},{6,7},{7,6},{8,9},{9,8},{10,11... | collective-permute-start | bytes 2359304 | tf_op jit(solution)/shard_map/ppermute | solution.py:886
  62.4 8.7 %collective-permute-start.7 = (bf16[128,1024]{1,0:T(8,128)(2,1)S(1)}, bf16[128,1024]{1,0:T(8,128)(2,1)S(1)}, u32[]{:S(2)}, u32[]{:S(2)}) collective-permute-start(bf16[128,1024]{1,0:T(8,128)(2,1)S(1)} %collective-permute-done.6.refs_12_.refs_18_), channel_id=1, source_target_pairs={{0,4},{4,0},{8,12},{12,8},{16,20},{20,16},{24,28},{28,24},{1,5},{5... | collective-permute-start | bytes 786440 | tf_op jit(solution)/shard_map/ppermute | solution.py:886
  64.2 35.6 %collective-permute-start.15 = (bf16[1024,512]{1,0:T(8,128)(2,1)}, bf16[1024,512]{1,0:T(8,128)(2,1)}, u32[]{:S(2)}, u32[]{:S(2)}) collective-permute-start(bf16[1024,512]{1,0:T(8,128)(2,1)} %refs_13_.3), channel_id=1, source_target_pairs={{0,1},{1,0},{2,3},{3,2},{4,5},{5,4},{6,7},{7,6},{8,9},{9,8},{10,11... | collective-permute-start | bytes 3145736 | tf_op jit(solution)/shard_map/ppermute | solution.py:886
  73.8 21.2 %collective-permute-start.16 = (bf16[256,1024]{1,0:T(8,128)(2,1)}, bf16[256,1024]{1,0:T(8,128)(2,1)}, u32[]{:S(2)}, u32[]{:S(2)}) collective-permute-start(bf16[256,1024]{1,0:T(8,128)(2,1)} %collective-permute-done.11.refs_16_), channel_id=1, source_target_pairs={{0,4},{4,0},{8,12},{12,8},{16,20},{20,16},{24,28},{28,24},{1,5},{5... | collective-permute-start | bytes 1572872 | tf_op jit(solution)/shard_map/ppermute | solution.py:886
  75.5 23.8 %collective-permute-start.12 = (bf16[512,512]{1,0:T(8,128)(2,1)}, bf16[512,512]{1,0:T(8,128)(2,1)}, u32[]{:S(2)}, u32[]{:S(2)}) collective-permute-start(bf16[512,512]{1,0:T(8,128)(2,1)} %collective-permute-done.10.refs_10_), channel_id=1, source_target_pairs={{0,4},{4,0},{8,12},{12,8},{16,20},{20,16},{24,28},{28,24},{1,5},{5... | collective-permute-start | bytes 1572872 | tf_op jit(solution)/shard_map/ppermute | solution.py:886
  76.3 24.7 %collective-permute-start.19 = (bf16[512,1024]{1,0:T(8,128)(2,1)}, bf16[512,1024]{1,0:T(8,128)(2,1)}, u32[]{:S(2)}, u32[]{:S(2)}) collective-permute-start(bf16[512,1024]{1,0:T(8,128)(2,1)} %refs_19_.1), channel_id=1, source_target_pairs={{0,1},{1,0},{2,3},{3,2},{4,5},{5,4},{6,7},{7,6},{8,9},{9,8},{10,11... | collective-permute-start | bytes 3145736 | tf_op jit(solution)/shard_map/ppermute | solution.py:886
  128.8 21.4 %collective-permute-start.20 = (bf16[1024,1024]{1,0:T(8,128)(2,1)}, bf16[1024,1024]{1,0:T(8,128)(2,1)}, u32[]{:S(2)}, u32[]{:S(2)}) collective-permute-start(bf16[1024,1024]{1,0:T(8,128)(2,1)} %get-tuple-element.180), channel_id=1, source_target_pairs={{0,1},{1,0},{2,3},{3,2},{4,5},{5,4},{6,7},{7,6},{8,9},{9,8},{10,11... | collective-permute-start | bytes 6291464 | tf_op jit(solution)/shard_map/ppermute | solution.py:886
  149.6 28.6 %collective-permute-start.21 = (bf16[1024,1024]{1,0:T(8,128)(2,1)}, bf16[1024,1024]{1,0:T(8,128)(2,1)}, u32[]{:S(2)}, u32[]{:S(2)}) collective-permute-start(bf16[1024,1024]{1,0:T(8,128)(2,1)} %get-tuple-element.187), channel_id=1, source_target_pairs={{0,1},{1,0},{2,3},{3,2},{4,5},{5,4},{6,7},{7,6},{8,9},{9,8},{10,11... | collective-permute-start | bytes 6291464 | tf_op jit(solution)/shard_map/ppermute | solution.py:886
  150.1 55.6 %collective-permute-start.24 = (bf16[1024,1024]{1,0:T(8,128)(2,1)}, bf16[1024,1024]{1,0:T(8,128)(2,1)}, u32[]{:S(2)}, u32[]{:S(2)}) collective-permute-start(bf16[1024,1024]{1,0:T(8,128)(2,1)} %get-tuple-element.206), channel_id=1, source_target_pairs={{0,1},{1,0},{2,3},{3,2},{4,5},{5,4},{6,7},{7,6},{8,9},{9,8},{10,11... | collective-permute-start | bytes 6291464 | tf_op jit(solution)/shard_map/ppermute | solution.py:886
  154.5 51.2 %collective-permute-start.23 = (bf16[1024,1024]{1,0:T(8,128)(2,1)}, bf16[1024,1024]{1,0:T(8,128)(2,1)}, u32[]{:S(2)}, u32[]{:S(2)}) collective-permute-start(bf16[1024,1024]{1,0:T(8,128)(2,1)} %shard_map.371), channel_id=1, source_target_pairs={{0,2},{1,3},{2,0},{3,1},{4,6},{5,7},{6,4},{7,5},{8,10},{9,11},{10,... | collective-permute-start | bytes 6291464 | tf_op jit(solution)/shard_map/ppermute | solution.py:886
  178.1 60.3 %collective-permute-start.32 = (bf16[1024,1024]{1,0:T(8,128)(2,1)}, bf16[1024,1024]{1,0:T(8,128)(2,1)}, u32[]{:S(2)}, u32[]{:S(2)}) collective-permute-start(bf16[1024,1024]{1,0:T(8,128)(2,1)} %get-tuple-element.222), channel_id=1, source_target_pairs={{0,1},{1,0},{2,3},{3,2},{4,5},{5,4},{6,7},{7,6},{8,9},{9,8},{10,11... | collective-permute-start | bytes 6291464 | tf_op jit(solution)/shard_map/ppermute | solution.py:886
  182.6 65.7 %collective-permute-start.31 = (bf16[1024,1024]{1,0:T(8,128)(2,1)}, bf16[1024,1024]{1,0:T(8,128)(2,1)}, u32[]{:S(2)}, u32[]{:S(2)}) collective-permute-start(bf16[1024,1024]{1,0:T(8,128)(2,1)} %shard_map.373), channel_id=1, source_target_pairs={{0,2},{1,3},{2,0},{3,1},{4,6},{5,7},{6,4},{7,5},{8,10},{9,11},{10,... | collective-permute-start | bytes 6291464 | tf_op jit(solution)/shard_map/ppermute | solution.py:886
  209.9 25.7 %collective-permute-start.29 = (bf16[512,1024]{1,0:T(8,128)(2,1)}, bf16[512,1024]{1,0:T(8,128)(2,1)}, u32[]{:S(2)}, u32[]{:S(2)}) collective-permute-start(bf16[512,1024]{1,0:T(8,128)(2,1)} %get-tuple-element.216), channel_id=1, source_target_pairs={{0,4},{4,0},{8,12},{12,8},{16,20},{20,16},{24,28},{28,24},{1,5},{5... | collective-permute-start | bytes 3145736 | tf_op jit(solution)/shard_map/ppermute | solution.py:886
  211.6 58.0 %collective-permute-start.28 = (bf16[448,1024]{1,0:T(8,128)(2,1)}, bf16[448,1024]{1,0:T(8,128)(2,1)}, u32[]{:S(2)}, u32[]{:S(2)}) collective-permute-start(bf16[448,1024]{1,0:T(8,128)(2,1)} %get-tuple-element.215), channel_id=1, source_target_pairs={{0,1},{1,0},{2,3},{3,2},{4,5},{5,4},{6,7},{7,6},{8,9},{9,8},{10,11... | collective-permute-start | bytes 2752520 | tf_op jit(solution)/shard_map/ppermute | solution.py:886
  215.1 54.5 %collective-permute-start.27 = (bf16[448,1024]{1,0:T(8,128)(2,1)}, bf16[448,1024]{1,0:T(8,128)(2,1)}, u32[]{:S(2)}, u32[]{:S(2)}) collective-permute-start(bf16[448,1024]{1,0:T(8,128)(2,1)} %shard_map.376), channel_id=1, source_target_pairs={{0,2},{1,3},{2,0},{3,1},{4,6},{5,7},{6,4},{7,5},{8,10},{9,11},{10,... | collective-permute-start | bytes 2752520 | tf_op jit(solution)/shard_map/ppermute | solution.py:886
  252.5 35.0 %collective-permute-start.34 = (bf16[512,1024]{1,0:T(8,128)(2,1)}, bf16[512,1024]{1,0:T(8,128)(2,1)}, u32[]{:S(2)}, u32[]{:S(2)}) collective-permute-start(bf16[512,1024]{1,0:T(8,128)(2,1)} %get-tuple-element.235), channel_id=1, source_target_pairs={{0,4},{4,0},{8,12},{12,8},{16,20},{20,16},{24,28},{28,24},{1,5},{5... | collective-permute-start | bytes 3145736 | tf_op jit(solution)/shard_map/ppermute | solution.py:886
  254.2 13.3 %collective-permute-start.30 = (bf16[256,1024]{1,0:T(8,128)(2,1)}, bf16[256,1024]{1,0:T(8,128)(2,1)}, u32[]{:S(2)}, u32[]{:S(2)}) collective-permute-start(bf16[256,1024]{1,0:T(8,128)(2,1)} %get-tuple-element.220), channel_id=1, source_target_pairs={{0,8},{4,12},{8,0},{12,4},{16,24},{20,28},{24,16},{28,20},{1,9},{5... | collective-permute-start | bytes 1572872 | tf_op jit(solution)/shard_map/ppermute | solution.py:886
  257.2 10.3 %all-to-all-start.1 = ((bf16[4,2,768]{2,1,0:T(2,128)(2,1)}), bf16[4,2,768]{2,1,0:T(2,128)(2,1)S(1)}, u32[]{:S(2)}, u32[]{:S(2)}) async-start(bf16[4,2,768]{2,1,0:T(2,128)(2,1)} %reshape.186), calls=%async_computation.1 | async-start | bytes 24576 | tf_op jit(solution)/shard_map/all_to_all | solution.py:1430
  269.6 15.3 %collective-permute-start.35 = (bf16[128,1024]{1,0:T(8,128)(2,1)}, bf16[128,1024]{1,0:T(8,128)(2,1)S(1)}, u32[]{:S(2)}, u32[]{:S(2)}) collective-permute-start(bf16[128,1024]{1,0:T(8,128)(2,1)} %get-tuple-element.236), channel_id=1, source_target_pairs={{0,16},{4,20},{8,24},{12,28},{16,0},{20,4},{24,8},{28,12},{1,17},{... | collective-permute-start | bytes 786440 | tf_op jit(solution)/shard_map/ppermute | solution.py:886
  275.5 21.6 %collective-permute-start.33 = (bf16[224,1024]{1,0:T(8,128)(2,1)}, bf16[224,1024]{1,0:T(8,128)(2,1)S(1)}, u32[]{:S(2)}, u32[]{:S(2)}) collective-permute-start(bf16[224,1024]{1,0:T(8,128)(2,1)} %get-tuple-element.234), channel_id=1, source_target_pairs={{0,4},{4,0},{8,12},{12,8},{16,20},{20,16},{24,28},{28,24},{1,5},{5... | collective-permute-start | bytes 1376264 | tf_op jit(solution)/shard_map/ppermute | solution.py:886
  287.5 14.7 %collective-permute-start.65 = (bf16[128,1024]{1,0:T(8,128)(2,1)}, bf16[128,1024]{1,0:T(8,128)(2,1)}, u32[]{:S(2)}, u32[]{:S(2)}) collective-permute-start(bf16[128,1024]{1,0:T(8,128)(2,1)} %shard_map.381.refs_0_), channel_id=1, source_target_pairs={{0,16},{4,20},{8,24},{12,28},{16,0},{20,4},{24,8},{28,12},{1,17},{... | collective-permute-start | bytes 786440 | tf_op jit(solution)/shard_map/ppermute | solution.py:886
  290.2 21.2 %collective-permute-start.37 = (bf16[256,1024]{1,0:T(8,128)(2,1)}, bf16[256,1024]{1,0:T(8,128)(2,1)S(1)}, u32[]{:S(2)}, u32[]{:S(2)}) collective-permute-start(bf16[256,1024]{1,0:T(8,128)(2,1)} %get-tuple-element.246), channel_id=1, source_target_pairs={{0,8},{4,12},{8,0},{12,4},{16,24},{20,28},{24,16},{28,20},{1,9},{5... | collective-permute-start | bytes 1572872 | tf_op jit(solution)/shard_map/ppermute | solution.py:886
  297.2 27.6 %collective-permute-start.25 = (bf16[4,1024]{1,0:T(4,128)(2,1)}, bf16[4,1024]{1,0:T(4,128)(2,1)}, u32[]{:S(2)}, u32[]{:S(2)}) collective-permute-start(bf16[4,1024]{1,0:T(4,128)(2,1)} %get-tuple-element.274), channel_id=1, source_target_pairs={{0,1},{1,0},{2,3},{3,2},{4,5},{5,4},{6,7},{7,6},{8,9},{9,8},{10,11... | collective-permute-start | bytes 24584 | tf_op jit(solution)/shard_map/ppermute | solution.py:886
  297.2 34.1 %collective-permute-start.66 = (bf16[128,1024]{1,0:T(8,128)(2,1)}, bf16[128,1024]{1,0:T(8,128)(2,1)}, u32[]{:S(2)}, u32[]{:S(2)}) collective-permute-start(bf16[128,1024]{1,0:T(8,128)(2,1)} %shard_map.381.refs_0_), channel_id=1, source_target_pairs={{0,8},{4,12},{8,0},{12,4},{16,24},{20,28},{24,16},{28,20},{1,9},{5... | collective-permute-start | bytes 786440 | tf_op jit(solution)/shard_map/ppermute | solution.py:886
  300.1 21.9 %collective-permute-start.36 = (bf16[112,1024]{1,0:T(8,128)(2,1)}, bf16[112,1024]{1,0:T(8,128)(2,1)}, u32[]{:S(2)}, u32[]{:S(2)}) collective-permute-start(bf16[112,1024]{1,0:T(8,128)(2,1)} %get-tuple-element.245), channel_id=1, source_target_pairs={{0,8},{4,12},{8,0},{12,4},{16,24},{20,28},{24,16},{28,20},{1,9},{5... | collective-permute-start | bytes 688136 | tf_op jit(solution)/shard_map/ppermute | solution.py:886
  302.2 30.6 %collective-permute-start.67 = (bf16[128,1024]{1,0:T(8,128)(2,1)}, bf16[128,1024]{1,0:T(8,128)(2,1)}, u32[]{:S(2)}, u32[]{:S(2)}) collective-permute-start(bf16[128,1024]{1,0:T(8,128)(2,1)} %collective-permute-done.65.refs_1_), channel_id=1, source_target_pairs={{0,8},{4,12},{8,0},{12,4},{16,24},{20,28},{24,16},{28,20},{1,9},{5... | collective-permute-start | bytes 786440 | tf_op jit(solution)/shard_map/ppermute | solution.py:886
  311.4 19.3 %collective-permute-start.56 = (bf16[8,2560]{1,0:T(8,128)(2,1)S(1)}, bf16[8,2560]{1,0:T(8,128)(2,1)S(1)}, u32[]{:S(2)}, u32[]{:S(2)}) collective-permute-start(bf16[8,2560]{1,0:T(8,128)(2,1)S(1)} %pad_maximum_fusion.6), channel_id=1, source_target_pairs={{0,8},{4,12},{8,0},{12,4},{16,24},{20,28},{24,16},{28,20},{1,9},{5... | collective-permute-start | bytes 122888 | tf_op jit(solution)/shard_map/ppermute | solution.py:886
  323.9 11.8 %collective-permute-start.38 = (bf16[112,1024]{1,0:T(8,128)(2,1)}, bf16[112,1024]{1,0:T(8,128)(2,1)S(1)}, u32[]{:S(2)}, u32[]{:S(2)}) collective-permute-start(bf16[112,1024]{1,0:T(8,128)(2,1)} %shard_map.385.refs_0_), channel_id=1, source_target_pairs={{0,16},{4,20},{8,24},{12,28},{16,0},{20,4},{24,8},{28,12},{1,17},{... | collective-permute-start | bytes 688136 | tf_op jit(solution)/shard_map/ppermute | solution.py:886
  329.2 27.7 %collective-permute-start.68 = (bf16[128,1024]{1,0:T(8,128)(2,1)S(1)}, bf16[128,1024]{1,0:T(8,128)(2,1)S(1)}, u32[]{:S(2)}, u32[]{:S(2)}) collective-permute-start(bf16[128,1024]{1,0:T(8,128)(2,1)S(1)} %copy-done.3), channel_id=1, source_target_pairs={{0,4},{4,0},{8,12},{12,8},{16,20},{20,16},{24,28},{28,24},{1,5},{5... | collective-permute-start | bytes 786440 | tf_op jit(solution)/shard_map/ppermute | solution.py:886
  330.7 27.2 %collective-permute-start.69 = (bf16[128,1024]{1,0:T(8,128)(2,1)}, bf16[128,1024]{1,0:T(8,128)(2,1)}, u32[]{:S(2)}, u32[]{:S(2)}) collective-permute-start(bf16[128,1024]{1,0:T(8,128)(2,1)} %collective-permute-done.65.refs_1_), channel_id=1, source_target_pairs={{0,4},{4,0},{8,12},{12,8},{16,20},{20,16},{24,28},{28,24},{1,5},{5... | collective-permute-start | bytes 786440 | tf_op jit(solution)/shard_map/ppermute | solution.py:886
  331.3 26.4 %collective-permute-start.70 = (bf16[128,1024]{1,0:T(8,128)(2,1)}, bf16[128,1024]{1,0:T(8,128)(2,1)}, u32[]{:S(2)}, u32[]{:S(2)}) collective-permute-start(bf16[128,1024]{1,0:T(8,128)(2,1)} %collective-permute-done.66.refs_2_), channel_id=1, source_target_pairs={{0,4},{4,0},{8,12},{12,8},{16,20},{20,16},{24,28},{28,24},{1,5},{5... | collective-permute-start | bytes 786440 | tf_op jit(solution)/shard_map/ppermute | solution.py:886
  332.8 26.7 %collective-permute-start.71 = (bf16[128,1024]{1,0:T(8,128)(2,1)}, bf16[128,1024]{1,0:T(8,128)(2,1)}, u32[]{:S(2)}, u32[]{:S(2)}) collective-permute-start(bf16[128,1024]{1,0:T(8,128)(2,1)} %collective-permute-done.67.refs_3_), channel_id=1, source_target_pairs={{0,4},{4,0},{8,12},{12,8},{16,20},{20,16},{24,28},{28,24},{1,5},{5... | collective-permute-start | bytes 786440 | tf_op jit(solution)/shard_map/ppermute | solution.py:886
  336.4 14.0 %collective-permute-start.39 = (bf16[128,1024]{1,0:T(8,128)(2,1)}, bf16[128,1024]{1,0:T(8,128)(2,1)S(1)}, u32[]{:S(2)}, u32[]{:S(2)}) collective-permute-start(bf16[128,1024]{1,0:T(8,128)(2,1)} %get-tuple-element.252), channel_id=1, source_target_pairs={{0,16},{4,20},{8,24},{12,28},{16,0},{20,4},{24,8},{28,12},{1,17},{... | collective-permute-start | bytes 786440 | tf_op jit(solution)/shard_map/ppermute | solution.py:886
  350.4 6.5 %collective-permute-start.57 = (bf16[16,2560]{1,0:T(8,128)(2,1)}, bf16[16,2560]{1,0:T(8,128)(2,1)S(1)}, u32[]{:S(2)}, u32[]{:S(2)}) collective-permute-start(bf16[16,2560]{1,0:T(8,128)(2,1)} %pad_maximum_fusion.5), channel_id=1, source_target_pairs={{0,16},{4,20},{8,24},{12,28},{16,0},{20,4},{24,8},{28,12},{1,17},{... | collective-permute-start | bytes 245768 | tf_op jit(solution)/shard_map/ppermute | solution.py:886
  356.9 7.7 %collective-permute-start.47 = (bf16[112,1024]{1,0:T(8,128)(2,1)}, bf16[112,1024]{1,0:T(8,128)(2,1)S(1)}, u32[]{:S(2)}, u32[]{:S(2)}) collective-permute-start(bf16[112,1024]{1,0:T(8,128)(2,1)} %shard_map.387.refs_0_), channel_id=1, source_target_pairs={{0,2},{1,3},{2,0},{3,1},{4,6},{5,7},{6,4},{7,5},{8,10},{9,11},{10,... | collective-permute-start | bytes 688136 | tf_op jit(solution)/shard_map/ppermute | solution.py:886
  357.6 7.8 %collective-permute-start.43 = (bf16[112,1024]{1,0:T(8,128)(2,1)}, bf16[112,1024]{1,0:T(8,128)(2,1)S(1)}, u32[]{:S(2)}, u32[]{:S(2)}) collective-permute-start(bf16[112,1024]{1,0:T(8,128)(2,1)} %shard_map.387.refs_0_), channel_id=1, source_target_pairs={{0,1},{1,0},{2,3},{3,2},{4,5},{5,4},{6,7},{7,6},{8,9},{9,8},{10,11... | collective-permute-start | bytes 688136 | tf_op jit(solution)/shard_map/ppermute | solution.py:886
  357.7 15.1 %collective-permute-start.58 = (bf16[128,1024]{1,0:T(8,128)(2,1)}, bf16[128,1024]{1,0:T(8,128)(2,1)S(1)}, u32[]{:S(2)}, u32[]{:S(2)}) collective-permute-start(bf16[128,1024]{1,0:T(8,128)(2,1)} %shard_map.386.refs_0_), channel_id=1, source_target_pairs={{0,16},{4,20},{8,24},{12,28},{16,0},{20,4},{24,8},{28,12},{1,17},{... | collective-permute-start | bytes 786440 | tf_op jit(solution)/shard_map/ppermute | solution.py:886
  357.9 14.8 %collective-permute-start.41 = (bf16[112,1024]{1,0:T(8,128)(2,1)}, bf16[112,1024]{1,0:T(8,128)(2,1)}, u32[]{:S(2)}, u32[]{:S(2)}) collective-permute-start(bf16[112,1024]{1,0:T(8,128)(2,1)} %shard_map.387.refs_0_), channel_id=1, source_target_pairs={{0,4},{4,0},{8,12},{12,8},{16,20},{20,16},{24,28},{28,24},{1,5},{5... | collective-permute-start | bytes 688136 | tf_op jit(solution)/shard_map/ppermute | solution.py:886
  359.4 14.7 %collective-permute-start.40 = (bf16[112,1024]{1,0:T(8,128)(2,1)}, bf16[112,1024]{1,0:T(8,128)(2,1)}, u32[]{:S(2)}, u32[]{:S(2)}) collective-permute-start(bf16[112,1024]{1,0:T(8,128)(2,1)} %shard_map.387.refs_0_), channel_id=1, source_target_pairs={{0,8},{4,12},{8,0},{12,4},{16,24},{20,28},{24,16},{28,20},{1,9},{5... | collective-permute-start | bytes 688136 | tf_op jit(solution)/shard_map/ppermute | solution.py:886
  364.6 11.3 %collective-permute-start.61 = (bf16[128,1024]{1,0:T(8,128)(2,1)}, bf16[128,1024]{1,0:T(8,128)(2,1)}, u32[]{:S(2)}, u32[]{:S(2)}) collective-permute-start(bf16[128,1024]{1,0:T(8,128)(2,1)} %shard_map.386.refs_0_), channel_id=1, source_target_pairs={{0,4},{4,0},{8,12},{12,8},{16,20},{20,16},{24,28},{28,24},{1,5},{5... | collective-permute-start | bytes 786440 | tf_op jit(solution)/shard_map/ppermute | solution.py:886
  365.4 14.4 %collective-permute-start.59 = (bf16[128,1024]{1,0:T(8,128)(2,1)}, bf16[128,1024]{1,0:T(8,128)(2,1)}, u32[]{:S(2)}, u32[]{:S(2)}) collective-permute-start(bf16[128,1024]{1,0:T(8,128)(2,1)} %shard_map.386.refs_0_), channel_id=1, source_target_pairs={{0,8},{4,12},{8,0},{12,4},{16,24},{20,28},{24,16},{28,20},{1,9},{5... | collective-permute-start | bytes 786440 | tf_op jit(solution)/shard_map/ppermute | solution.py:886
  372.7 12.0 %collective-permute-start.60 = (bf16[128,1024]{1,0:T(8,128)(2,1)S(1)}, bf16[128,1024]{1,0:T(8,128)(2,1)}, u32[]{:S(2)}, u32[]{:S(2)}) collective-permute-start(bf16[128,1024]{1,0:T(8,128)(2,1)S(1)} %collective-permute-done.58.refs_1_), channel_id=1, source_target_pairs={{0,8},{4,12},{8,0},{12,4},{16,24},{20,28},{24,16},{28,20},{1,9},{5... | collective-permute-start | bytes 786440 | tf_op jit(solution)/shard_map/ppermute | solution.py:886
  372.7 7.2 %collective-permute-start.51 = (bf16[112,1024]{1,0:T(8,128)(2,1)S(1)}, bf16[112,1024]{1,0:T(8,128)(2,1)S(1)}, u32[]{:S(2)}, u32[]{:S(2)}) collective-permute-start(bf16[112,1024]{1,0:T(8,128)(2,1)S(1)} %collective-permute-done.47.refs_8_), channel_id=1, source_target_pairs={{0,1},{1,0},{2,3},{3,2},{4,5},{5,4},{6,7},{7,6},{8,9},{9,8},{10,11... | collective-permute-start | bytes 688136 | tf_op jit(solution)/shard_map/ppermute | solution.py:886
  374.2 7.7 %collective-permute-start.49 = (bf16[112,1024]{1,0:T(8,128)(2,1)}, bf16[112,1024]{1,0:T(8,128)(2,1)S(1)}, u32[]{:S(2)}, u32[]{:S(2)}) collective-permute-start(bf16[112,1024]{1,0:T(8,128)(2,1)} %collective-permute-done.41.refs_2_), channel_id=1, source_target_pairs={{0,2},{1,3},{2,0},{3,1},{4,6},{5,7},{6,4},{7,5},{8,10},{9,11},{10,... | collective-permute-start | bytes 688136 | tf_op jit(solution)/shard_map/ppermute | solution.py:886
  375.9 12.6 %collective-permute-start.45 = (bf16[112,1024]{1,0:T(8,128)(2,1)}, bf16[112,1024]{1,0:T(8,128)(2,1)}, u32[]{:S(2)}, u32[]{:S(2)}) collective-permute-start(bf16[112,1024]{1,0:T(8,128)(2,1)} %collective-permute-done.41.refs_2_), channel_id=1, source_target_pairs={{0,1},{1,0},{2,3},{3,2},{4,5},{5,4},{6,7},{7,6},{8,9},{9,8},{10,11... | collective-permute-start | bytes 688136 | tf_op jit(solution)/shard_map/ppermute | solution.py:886
  379.8 10.5 %collective-permute-start.42 = (bf16[112,1024]{1,0:T(8,128)(2,1)}, bf16[112,1024]{1,0:T(8,128)(2,1)}, u32[]{:S(2)}, u32[]{:S(2)}) collective-permute-start(bf16[112,1024]{1,0:T(8,128)(2,1)} %collective-permute-done.40.refs_1_), channel_id=1, source_target_pairs={{0,4},{4,0},{8,12},{12,8},{16,20},{20,16},{24,28},{28,24},{1,5},{5... | collective-permute-start | bytes 688136 | tf_op jit(solution)/shard_map/ppermute | solution.py:886
  380.0 19.9 %collective-permute-start.62 = (bf16[128,1024]{1,0:T(8,128)(2,1)S(1)}, bf16[128,1024]{1,0:T(8,128)(2,1)}, u32[]{:S(2)}, u32[]{:S(2)}) collective-permute-start(bf16[128,1024]{1,0:T(8,128)(2,1)S(1)} %collective-permute-done.58.refs_1_), channel_id=1, source_target_pairs={{0,4},{4,0},{8,12},{12,8},{16,20},{20,16},{24,28},{28,24},{1,5},{5... | collective-permute-start | bytes 786440 | tf_op jit(solution)/shard_map/ppermute | solution.py:886
  381.9 18.0 %collective-permute-start.63 = (bf16[128,1024]{1,0:T(8,128)(2,1)}, bf16[128,1024]{1,0:T(8,128)(2,1)}, u32[]{:S(2)}, u32[]{:S(2)}) collective-permute-start(bf16[128,1024]{1,0:T(8,128)(2,1)} %collective-permute-done.59.refs_2_), channel_id=1, source_target_pairs={{0,4},{4,0},{8,12},{12,8},{16,20},{20,16},{24,28},{28,24},{1,5},{5... | collective-permute-start | bytes 786440 | tf_op jit(solution)/shard_map/ppermute | solution.py:886
  384.7 18.5 %collective-permute-start.64 = (bf16[128,1024]{1,0:T(8,128)(2,1)}, bf16[128,1024]{1,0:T(8,128)(2,1)}, u32[]{:S(2)}, u32[]{:S(2)}) collective-permute-start(bf16[128,1024]{1,0:T(8,128)(2,1)} %collective-permute-done.60.refs_3_), channel_id=1, source_target_pairs={{0,4},{4,0},{8,12},{12,8},{16,20},{20,16},{24,28},{28,24},{1,5},{5... | collective-permute-start | bytes 786440 | tf_op jit(solution)/shard_map/ppermute | solution.py:886
  388.5 8.9 %collective-permute-start.48 = (bf16[112,1024]{1,0:T(8,128)(2,1)}, bf16[112,1024]{1,0:T(8,128)(2,1)}, u32[]{:S(2)}, u32[]{:S(2)}) collective-permute-start(bf16[112,1024]{1,0:T(8,128)(2,1)} %collective-permute-done.40.refs_1_), channel_id=1, source_target_pairs={{0,2},{1,3},{2,0},{3,1},{4,6},{5,7},{6,4},{7,5},{8,10},{9,11},{10,... | collective-permute-start | bytes 688136 | tf_op jit(solution)/shard_map/ppermute | solution.py:886
  390.3 10.6 %collective-permute-start.50 = (bf16[112,1024]{1,0:T(8,128)(2,1)}, bf16[112,1024]{1,0:T(8,128)(2,1)}, u32[]{:S(2)}, u32[]{:S(2)}) collective-permute-start(bf16[112,1024]{1,0:T(8,128)(2,1)} %collective-permute-done.42.refs_3_), channel_id=1, source_target_pairs={{0,2},{1,3},{2,0},{3,1},{4,6},{5,7},{6,4},{7,5},{8,10},{9,11},{10,... | collective-permute-start | bytes 688136 | tf_op jit(solution)/shard_map/ppermute | solution.py:886
  397.4 20.4 %collective-permute-start.44 = (bf16[112,1024]{1,0:T(8,128)(2,1)}, bf16[112,1024]{1,0:T(8,128)(2,1)S(1)}, u32[]{:S(2)}, u32[]{:S(2)}) collective-permute-start(bf16[112,1024]{1,0:T(8,128)(2,1)} %collective-permute-done.40.refs_1_), channel_id=1, source_target_pairs={{0,1},{1,0},{2,3},{3,2},{4,5},{5,4},{6,7},{7,6},{8,9},{9,8},{10,11... | collective-permute-start | bytes 688136 | tf_op jit(solution)/shard_map/ppermute | solution.py:886
  399.9 18.0 %collective-permute-start.46 = (bf16[112,1024]{1,0:T(8,128)(2,1)}, bf16[112,1024]{1,0:T(8,128)(2,1)S(1)}, u32[]{:S(2)}, u32[]{:S(2)}) collective-permute-start(bf16[112,1024]{1,0:T(8,128)(2,1)} %collective-permute-done.42.refs_3_), channel_id=1, source_target_pairs={{0,1},{1,0},{2,3},{3,2},{4,5},{5,4},{6,7},{7,6},{8,9},{9,8},{10,11... | collective-permute-start | bytes 688136 | tf_op jit(solution)/shard_map/ppermute | solution.py:886
  399.9 18.0 %collective-permute-start.53 = (bf16[112,1024]{1,0:T(8,128)(2,1)}, bf16[112,1024]{1,0:T(8,128)(2,1)}, u32[]{:S(2)}, u32[]{:S(2)}) collective-permute-start(bf16[112,1024]{1,0:T(8,128)(2,1)} %copy-done.20), channel_id=1, source_target_pairs={{0,1},{1,0},{2,3},{3,2},{4,5},{5,4},{6,7},{7,6},{8,9},{9,8},{10,11... | collective-permute-start | bytes 688136 | tf_op jit(solution)/shard_map/ppermute | solution.py:886
  400.9 16.9 %collective-permute-start.52 = (bf16[112,1024]{1,0:T(8,128)(2,1)}, bf16[112,1024]{1,0:T(8,128)(2,1)}, u32[]{:S(2)}, u32[]{:S(2)}) collective-permute-start(bf16[112,1024]{1,0:T(8,128)(2,1)} %collective-permute-done.48.refs_9_), channel_id=1, source_target_pairs={{0,1},{1,0},{2,3},{3,2},{4,5},{5,4},{6,7},{7,6},{8,9},{9,8},{10,11... | collective-permute-start | bytes 688136 | tf_op jit(solution)/shard_map/ppermute | solution.py:886
  403.2 14.7 %collective-permute-start.54 = (bf16[112,1024]{1,0:T(8,128)(2,1)}, bf16[112,1024]{1,0:T(8,128)(2,1)}, u32[]{:S(2)}, u32[]{:S(2)}) collective-permute-start(bf16[112,1024]{1,0:T(8,128)(2,1)} %collective-permute-done.50.refs_11_), channel_id=1, source_target_pairs={{0,1},{1,0},{2,3},{3,2},{4,5},{5,4},{6,7},{7,6},{8,9},{9,8},{10,11... | collective-permute-start | bytes 688136 | tf_op jit(solution)/shard_map/ppermute | solution.py:886
  (42 other events, 402.0 us)

commit v2 on v1

--- a/solution.py
+++ b/solution.py
@@ -494,13 +494,18 @@
     refs[count][...] = total_of(refs[:count])
 
 
-def split_kernel(count, *refs):
-    upper_kept = refs[0][0] == 1
-    lower = total_of(refs[1 : 1 + count])
-    upper = total_of(refs[1 + count : 1 + 2 * count])
-    keep_ref, send_ref = refs[1 + 2 * count :]
-    keep_ref[...] = jnp.where(upper_kept, upper, lower)
-    send_ref[...] = jnp.where(upper_kept, lower, upper)
+def split_kernel(count, parts, *refs):
+    own = refs[0][0]
+    sums = [total_of(refs[1 + at * count : 1 + (at + 1) * count]) for at in range(parts)]
+    for mask, ref in enumerate(refs[1 + parts * count :]):
+        value = sums[mask]
+        for at in range(1, parts):
+            value = jnp.where(own == at, sums[at ^ mask], value)
+        ref[...] = value
+
+
+def merge_kernel(count, starts_ref, *refs):
+    bring(starts_ref, refs[:count], refs[count], refs[count + 1])
 
 
 def bring(starts_ref, pieces, stack_ref, sems):
@@ -646,7 +651,7 @@
     own_ref, grad_zero_ref, text_ref, mel_ref, refined_ref, mixed_ref, normed_ref = take(7)
     pre_ref, energy_ref, kernel_ref, bias_ref, gain_ref, hidden_bias_ref = take(6)
     in_ref, out_ref, project_ref, attn_sums_ref, ffn_sums_ref = take(5)
-    high_bias_ref, low_bias_ref, up_bias_ref = take(3)
+    high_bias_ref, low_bias_ref, up_bias_ref, active_ref = take(4)
     grad_text_ref, mods_ref = take(2)
     slots = [take() for _ in range(group)]
     stack_ref, sems, padded_ref, outer_ref, refined_grad_ref, low_ref, mixed_grad_ref = take(7)
@@ -659,17 +664,21 @@
     mel_at = 3 * wide
     small_at = mel_at + mel_ref.shape[1] + (-(mel_at + mel_ref.shape[1])) % 16
 
-    for at, (source, row) in enumerate(
-        (
-            (attn_sums_ref, 1),
-            (attn_sums_ref, 0),
-            (ffn_sums_ref, 5),
-            (ffn_sums_ref, 3),
-            (ffn_sums_ref, 2),
-            (ffn_sums_ref, 1),
-        )
-    ):
-        mods_ref[at : at + 1, :] = source[row : row + 1, :]
+    lines = [attn_sums_ref[1:2, :], attn_sums_ref[0:1, :]]
+    lines += [ffn_sums_ref[row : row + 1, :] for row in (5, 3, 2, 1)]
+    mods_at = small_at + small
+    stack_ref[mods_at:, :] = jnp.zeros((stack_ref.shape[0] - mods_at, model), BF16)
+    for at, member in enumerate(lines):
+        mods_ref[at : at + 1, :] = member.astype(BF16)
+    lines += [active_ref[...].astype(F32), jnp.zeros((1, model), F32)]
+    lines = jnp.concatenate(lines, axis=0)
+    empty = jnp.zeros_like(lines)
+    odd = own_ref[1] % 2 == 1
+    lines = jnp.where(
+        odd, jnp.concatenate([empty, lines], axis=0), jnp.concatenate([lines, empty], axis=0)
+    )
+    place = pl.multiple_of(mods_at + own_ref[1] // 2 * 16, 16)
+    stack_ref[pl.ds(place, 16), :] = lines.astype(BF16)
 
     grad_zero = grad_zero_ref[...]
     grad_refined = inner_cols(grad_zero, project_ref[mel_ref.shape[1] :, :])
@@ -681,9 +690,6 @@
     spare = jnp.zeros((small_at - mel_at - mel_ref.shape[1], model), F32)
     grad_mel = inner_rows(mel_ref[...], grad_zero)
     stack_ref[mel_at:small_at, :] = jnp.concatenate([grad_mel, spare], axis=0).astype(BF16)
-    rest = stack_ref.shape[0] - small_at - small
-    if rest:
-        stack_ref[small_at + small :, :] = jnp.zeros((rest, model), BF16)
     grad_out = inner_rows(mixed_ref[...], low_ref[...]).astype(BF16)
     stack_ref[2 * wide : 3 * wide, 0:wide] = grad_out[0:wide, :]
     stack_ref[2 * wide : 3 * wide, wide:] = grad_out[wide:, :]
@@ -812,7 +818,8 @@
 def text_unpack(count, group, starts_ref, own_ref, *refs):
     pieces = refs[:count]
     project_ref, in_ref, out_ref, taps_ref, bias_ref, gain_ref = refs[count : count + 6]
-    hidden_ref, frame_ref, qkv_bias_ref, up_bias_ref, stack_ref, sems, lines_ref = refs[count + 6 :]
+    hidden_ref, frame_ref, qkv_bias_ref, up_bias_ref, mods_ref = refs[count + 6 : count + 11]
+    stack_ref, sems, lines_ref = refs[count + 11 :]
     bring(starts_ref, pieces, stack_ref, sems)
     own = own_ref[0]
     wide = in_ref.shape[0]
@@ -826,6 +833,8 @@
     out_ref[0:wide, :] = stack_ref[2 * wide : 3 * wide, 0:wide].astype(F32)
     out_ref[wide:, :] = stack_ref[2 * wide : 3 * wide, wide:].astype(F32)
     lines_ref[...] = stack_ref[small_at : small_at + small_rows(group), :].astype(F32)
+    mods_at = small_at + small_rows(group)
+    mods_ref[...] = stack_ref[mods_at : mods_at + mods_ref.shape[0], :]
 
     def half(at):
         return lines_ref[at // 2 : at // 2 + 1, (at % 2) * wide : (at % 2 + 1) * wide]
@@ -907,22 +916,33 @@
     )[0]
 
 
-def add_and_split(arrays, upper):
+def add_and_split(arrays, own, parts):
     rows, wide = arrays[0].shape
-    half = rows // 2
-    tile = tile_rows(half)
-    steps = half // tile
-    spec = pl.BlockSpec((tile, wide), lambda g: (g, 0))
-    high = pl.BlockSpec((tile, wide), lambda g: (g + steps, 0))
+    size = rows // parts
+    tile = tile_rows(size)
+    steps = size // tile
+
+    def block_at(part):
+        return pl.BlockSpec((tile, wide), lambda g: (g + part * steps, 0))
+
     return run_kernel(
-        partial(split_kernel, len(arrays)),
+        partial(split_kernel, len(arrays), parts),
         steps,
-        [(SMEM, upper)]
-        + [(spec, array) for array in arrays]
-        + [(high, array) for array in arrays],
-        [(spec, (half, wide), BF16)] * 2,
+        [(SMEM, own.astype(jnp.int32).reshape(1))]
+        + [(block_at(part), array) for part in range(parts) for array in arrays],
+        [(block_at(0), (size, wide), BF16)] * parts,
         [],
     )
+
+
+def merge(pieces, starts, rows):
+    return run_kernel(
+        partial(merge_kernel, len(pieces)),
+        1,
+        [(SMEM, jnp.stack(starts).astype(jnp.int32))] + [(ANY, piece) for piece in pieces],
+        [(whole((rows, pieces[0].shape[1])), (rows, pieces[0].shape[1]), BF16)],
+        [pltpu.SemaphoreType.DMA((len(pieces),))],
+    )[0]
 
 
 class Fetch:
@@ -981,7 +1001,8 @@
 
 
 class DataSum:
-    def __init__(self, arrays, bits):
+    def __init__(self, arrays, bits, merged=False):
+        self.merged = merged
         self.arrays = list(arrays)
         self.bits = list(bits)
         self.halved = []
@@ -995,20 +1016,20 @@
             self.gather(total)
             return total
         bit = self.bits.pop(0)
-        if arrays[0].shape[0] % 32 == 0:
-            upper = (lax.axis_index("dp") // bit % 2).astype(jnp.int32).reshape(1)
-            keep, send = add_and_split(arrays, upper)
-            self.halved.append(bit)
-        else:
-            keep = send = add_arrays(arrays)
+        keep, send = add_and_split(arrays, lax.axis_index("dp") // bit % 2, 2)
+        self.halved.append(bit)
         self.arrays = [keep, swap(send, "dp", bit)]
         return keep
 
     def gather(self, total):
         self.pieces = {0: total}
-        for bit in self.halved[::-1]:
+        for bit in self.halved[: 0 if self.merged else None : -1]:
             for mask, piece in list(self.pieces.items()):
                 self.pieces[mask | bit] = swap(piece, "dp", bit)
+
+    def half(self, *others):
+        starts = [start % (self.rows // 2) for start in self.starts()]
+        return merge(after(self.pieces.values(), *others), starts, self.rows // 2)
 
     def starts(self):
         own = lax.axis_index("dp")
@@ -1067,21 +1088,6 @@
         fetch.send()
         fetch.core(0)
 
-    time_rows = time_embed.astype(F32)
-    activated, silu_back = jax.vjp(jax.nn.silu, time_rows)
-    activated_low = activated.astype(BF16)
-    modulation = (mm(activated_low, mod_weight) + mod_bias).astype(BF16)
-    biases = jnp.concatenate([qkv_bias.reshape(-1), ff_in_bias])
-    riders = jnp.broadcast_to(biases[None, :], (group, biases.size))
-    sent = jnp.concatenate([modulation, riders], axis=1)
-    came = lax.all_to_all(sent, "heads", split_axis=0, concat_axis=1, tiled=True)
-    came = came.reshape(group, sent.shape[1]).astype(F32)
-    mod_rows = came[:, : modulation.shape[1]].reshape(6, model_width)
-    slot_owner = jnp.bitwise_xor(jnp.arange(group, dtype=jnp.int32), own)
-    biases_all = jnp.take(came[:, modulation.shape[1] :], slot_owner, axis=0)
-    qkv_bias_all = biases_all[:, : 3 * width].reshape(group, 3, width)
-    up_bias_all = biases_all[:, 3 * width :].reshape(group, 1, units)
-
     position = jnp.arange(rows, dtype=jnp.int32)
     inside = (position >= spans[0, 0]) & (position < spans[0, 1])
     keep = jnp.where(inside, 0.0, 1.0).astype(F32)[:, None]
@@ -1158,11 +1164,28 @@
     def pieces_of(slots):
         return tuple(len(pieces) for pieces in slots)
 
+    (time_late,) = after([time_embed], state_zero)
+    time_rows = time_late.astype(F32)
+    activated, silu_back = jax.vjp(jax.nn.silu, time_rows)
+    activated_low = activated.astype(BF16)
+    modulation = (mm(activated_low, mod_weight) + mod_bias).astype(BF16)
+    biases = jnp.concatenate([qkv_bias.reshape(-1), ff_in_bias])
+    riders = jnp.broadcast_to(biases[None, :], (group, biases.size))
+    sent = jnp.concatenate([modulation, riders], axis=1)
+    came = lax.all_to_all(sent, "heads", split_axis=0, concat_axis=1, tiled=True)
+    came = came.reshape(group, sent.shape[1]).astype(F32)
+    mod_rows = came[:, : modulation.shape[1]].reshape(6, model_width)
+    slot_owner = jnp.bitwise_xor(jnp.arange(group, dtype=jnp.int32), own)
+    biases_all = jnp.take(came[:, modulation.shape[1] :], slot_owner, axis=0)
+    qkv_bias_all = biases_all[:, : 3 * width].reshape(group, 3, width)
+    up_bias_all = biases_all[:, 3 * width :].reshape(group, 1, units)
+
     for fetch in fetches[2:]:
-        fetch.send(state_zero)
+        fetch.send(came)
     for fetch in fetches[:2]:
         fetch.share()
         fetch.cores(2, parts)
+    (mod_rows,) = after([mod_rows], *[fetch.sent[2] for fetch in fetches[:2]])
     kept = []
     for turn in range(2):
         first, last = turn == 0, turn == 1
@@ -1296,22 +1319,28 @@
         if first:
             back = results[1 + parts]
             ffn_sum = GroupSum()
+            token = back
             for slot in range(group - 1, 0, -1):
-                token = ffn_sum.put(slot, ffn_grads[slot], back)
+                total = ffn_sum.put(slot, ffn_grads[slot], token)
                 if slot % 2 == 0:
-                    (back,) = after([back], token)
+                    token = total
+            (back,) = after([back], token)
         else:
             grad_zero, attn_sums = results[1 + parts :]
+    token = grad_zero
     attn_sum = GroupSum()
     for slot in range(group - 1, 0, -1):
-        token = attn_sum.put(slot, attn_grads[slot], grad_zero)
+        total = attn_sum.put(slot, attn_grads[slot], token)
         if slot % 2 == 0:
-            (grad_zero,) = after([grad_zero], token)
-
+            token = total
+    (grad_zero,) = after([grad_zero], token)
+
+    data = lax.axis_size("dp")
     stack_rows = 3 * text_width + mels
-    stack_rows += -stack_rows % 16 + small_rows(group)
-    stack_rows += -stack_rows % (16 * group)
-    own_index = own.astype(jnp.int32).reshape(1)
+    stack_rows += -stack_rows % 16 + small_rows(group) + 8 * group * data
+    stack_rows += -stack_rows % (16 * group * data)
+    own_index = jnp.stack([own, own_data * group + own]).astype(jnp.int32)
+    own_active = lax.dynamic_index_in_dim(activated_low, own, 0)
     results = run_kernel(
         partial(text_backward, group),
         1,
@@ -1339,11 +1368,12 @@
                 qkv_bias_parts[0],
                 qkv_bias_parts[1],
                 grad_up_bias,
+                own_active,
             )
         ],
         [
             (whole((rows, text_width)), (rows, text_width), F32),
-            (whole((6, model_width)), (6, model_width), F32),
+            (whole((6, model_width)), (6, model_width), BF16),
         ]
         + [(ANY, (stack_rows // group, model_width), BF16)] * group,
         [
@@ -1360,34 +1390,61 @@
         ],
     )
     grad_text, grad_mod = results[:2]
-    text_sum = GroupSum()
+    def unpack(kernel, data, first, second, *others):
+        pieces = after(data.pieces.values(), *others)
+        return run_kernel(
+            partial(kernel, len(pieces)),
+            1,
+            [(SMEM, jnp.stack(data.starts()).astype(jnp.int32))]
+            + [(ANY, member) for member in pieces],
+            [(whole(first.shape), first.shape, F32), (whole(second.shape), second.shape, F32)],
+            [pltpu.VMEM((data.rows, model_width), BF16), semaphores(len(pieces), 1)],
+        )
+
     bits = axis_bits("dp")
     ffn_data = DataSum(ffn_sum.put(0, ffn_grads[0]), bits)
     token = ffn_data.step(grad_mod)
+    text_sum = GroupSum()
     for slot in range(group - 1, 0, -1):
         total = text_sum.put(slot, results[2 + slot], token)
         if slot % 2 == 0:
             token = total
     attn_data = DataSum(attn_sum.put(0, attn_grads[0]), bits)
-    text_data = DataSum(text_sum.put(0, results[2]), bits)
-    (grad_mod,) = after([grad_mod], token)
+    text_data = DataSum(text_sum.put(0, results[2]), bits, merged=True)
     steps = [(at, ffn_data) for at in range(1, len(bits) + 1)]
     for at in range(len(bits) + 1):
         steps.append((at + 2.2 if at else 1.5, attn_data))
         steps.append((at + 2.25, text_data))
-    for _, member in sorted(steps, key=lambda step: step[0]):
+    for at, member in sorted(steps, key=lambda step: step[0]):
         token = member.step(token)
-    text_pieces = [[text_data.pieces[mask] for mask in text_data.pieces]]
-    for slot in range(1, group):
+
+    weight_up, weight_down = unpack(ffn_unpack, ffn_data, ff_in, ff_out, attn_data.pieces[0])
+    text_half = text_data.half(weight_up, *list(attn_data.pieces.values())[1:])
+    weight_qkv, weight_out = unpack(attn_unpack, attn_data, qkv_weight, out_weight, text_half)
+    text_halves = {0: [text_half]}
+    for slot in range(2, group, 2):
         bit = low_bit(slot)
-        text_pieces.append([swap(piece, "heads", bit) for piece in text_pieces[slot - bit]])
+        text_halves[slot] = [swap(text_halves[slot - bit][0], "heads", bit)]
+    for slot in range(0, group, 2):
+        text_halves[slot].append(swap(text_halves[slot][0], "dp", 1))
+        text_halves[slot + 1] = [swap(piece, "heads", 1) for piece in text_halves[slot]]
+    (grad_mod,) = after([grad_mod], text_halves[2][0])
+    columns = mod_weight.shape[1]
+    grad_mod = grad_mod.reshape(1, group * columns)
+    grad_mod_cols = lax.all_to_all(grad_mod, "heads", split_axis=1, concat_axis=0, tiled=True)
+    (grad_time,) = silu_back(inner_cols(grad_mod_cols, mod_weight))
+    grad_time = jnp.broadcast_to(grad_time.astype(BF16), (group,) + grad_time.shape)
+    grad_time = lax.all_to_all(grad_time, "heads", split_axis=0, concat_axis=0)
+    grad_time = jnp.sum(grad_time.astype(F32), axis=0)
+
     slot_rows = stack_rows // group
-    text_starts = [
-        slot_owner[slot] * slot_rows + start
-        for slot in range(group)
-        for start in text_data.starts()
-    ]
-    text_pieces = [piece for pieces in text_pieces for piece in pieces]
+    text_pieces, text_starts = [], []
+    for slot, pieces in text_halves.items():
+        for which, piece in enumerate(pieces):
+            text_pieces.append(piece)
+            text_starts.append(
+                slot_owner[slot] * slot_rows + ((own_data + which) % 2) * (slot_rows // 2)
+            )
     unpacked = (
         in_proj.shape,
         pw_in.shape,
@@ -1400,43 +1457,25 @@
         (3, width),
         (1, units),
     )
+    mods_shape = (8 * group * data, model_width)
     unpacked = run_kernel(
         partial(text_unpack, len(text_pieces), group),
         1,
         [(SMEM, jnp.stack(text_starts).astype(jnp.int32)), (SMEM, own_index)]
         + [(ANY, member) for member in text_pieces],
-        [(whole(shape), shape, F32) for shape in unpacked],
+        [(whole(shape), shape, F32) for shape in unpacked]
+        + [(whole(mods_shape), mods_shape, BF16)],
         [
             pltpu.VMEM((stack_rows, model_width), BF16),
             semaphores(len(text_pieces), 1),
             pltpu.VMEM((small_rows(group), model_width), F32),
         ],
     )
-    def unpack(data, kernel, first, second):
-        pieces = list(data.pieces.values())
-        return run_kernel(
-            partial(kernel, len(pieces)),
-            1,
-            [(SMEM, jnp.stack(data.starts()).astype(jnp.int32))]
-            + [(ANY, member) for member in pieces],
-            [(whole(first.shape), first.shape, F32), (whole(second.shape), second.shape, F32)],
-            [pltpu.VMEM((data.rows, model_width), BF16), semaphores(len(pieces), 1)],
-        )
-
-    weight_up, weight_down = unpack(ffn_data, ffn_unpack, ff_in, ff_out)
-    weight_qkv, weight_out = unpack(attn_data, attn_unpack, qkv_weight, out_weight)
-
-    grad_mod = grad_mod.astype(BF16).reshape(1, -1)
-    grad_mod_cols = lax.all_to_all(grad_mod, "heads", split_axis=1, concat_axis=0, tiled=True)
-    seen = jnp.concatenate([activated_low, grad_mod_cols], axis=1)
-    for bit in bits:
-        seen = jnp.concatenate([seen, swap(seen, "dp", bit)], axis=0)
-    grad_mod_weight = inner_rows(seen[:, :model_width], seen[:, model_width:])
-    grad_mod_bias = jnp.sum(seen[:, model_width:].astype(F32), axis=0)
-    (grad_time,) = silu_back(inner_cols(grad_mod_cols, mod_weight))
-    for bit in axis_bits("heads"):
-        rounded = grad_time.astype(BF16)
-        grad_time = rounded.astype(F32) + swap(rounded, "heads", bit).astype(F32)
+    seen = unpacked[10].reshape(group * data, 8, model_width)
+    grad_mod_all = seen[:, :6].reshape(group * data, 6 * model_width)
+    grad_mod_all = lax.dynamic_slice_in_dim(grad_mod_all, own * columns, columns, axis=1)
+    grad_mod_weight = inner_rows(seen[:, 6], grad_mod_all)
+    grad_mod_bias = jnp.sum(grad_mod_all.astype(F32), axis=0)
     return (
         output,
         grad_text,

time: 433 us -> 431 us (level)
  starting transfers between devices: 59.1 us -> 67.9 us
  other arithmetic: 15.1 us -> 9.95 us
    ppermute x72 -> x62, starting transfers between devices: 51.6 us -> 57.9 us  [swap(): lax.ppermute(array, axis, [(at, at ^ bit) for at in range(lax.axis_size(a...]
    pallas_call x25 -> x26, Pallas kernels: 189 us -> 192 us  [run_kernel(): pl.pallas_call(kernel, grid=(parts,), in_specs=[spec for spec, _ in input...]
    unnamed x70 -> x50, local copies, waits for them, and re-layouts: 9.07 us -> 6.49 us
    ppermute x72 -> x62, waiting for transfers between devices: 118 us -> 118 us  [swap(): lax.ppermute(array, axis, [(at, at ^ bit) for at in range(lax.axis_size(a...]
  transfers between devices with their start and end apart: 74 -> 65, of which waited for: 28 -> 22; matrix products, arithmetic and copies ran while one was open for 9% -> 7% of each run, Pallas kernels for 37% -> 37%
where the time goes in v2:
time: 431 us; the launch traced here: 424 us
  Pallas kernels  192 us (45%)
  waiting for transfers between devices  121 us (28%)
  starting transfers between devices  67.9 us (16%)
  local copies, waits for them, and re-layouts  24.7 us (6%)
  other arithmetic  9.95 us (2%)
  matrix products  5.13 us (1%)
    pallas_call x26, Pallas kernels, run_kernel(): pl.pallas_call(kernel, grid=(parts,), in_specs=[spec for spec, _ in input...  192 us
    ppermute x62, waiting for transfers between devices, swap(): lax.ppermute(array, axis, [(at, at ^ bit) for at in range(lax.axis_size(a...  118 us
    ppermute x62, starting transfers between devices, swap(): lax.ppermute(array, axis, [(at, at ^ bit) for at in range(lax.axis_size(a...  57.9 us
  transfers between devices with their start and end apart: 65, of which 22 were waited for; matrix products, arithmetic and copies ran while one was open for 7% of the time, Pallas kernels for 37%

profile of v2, /device:TPU:0, one launch (start us, length us, event | category | flops | bytes accessed | tf_op | source)
XLA Modules:
  0.0 423.9 jit_solution(7938654001870512708)
XLA Ops:
  0.7 2.2 constant_dynamic-slice_fusion.4
  2.9 3.0 collective-permute-start
  13.0 1.8 pad_maximum_fusion.mel_ref.refs_3_
  14.8 9.7 %shard_map.366 = (bf16[512,512]{1,0:T(8,128)(2,1)}, f32[512,1024]{1,0:T(8,128)}, f32[8,1024]{1,0:T(8,128)}, bf16[512,1024]{1,0:T(8,128)(2,1)}, bf16[512,512]{1,0:T(8,128)(2,1)}, /*index=5*/f32[512,1024]{1,0:T(8,128)}) custom-call(bf16[512,512]{1,0:T(8,128)(2,1)} %refs_2_.1, bf16[512,200]{1,0:T(8,128)(2,1)} %pad_maximum_fusion.mel_ref.refs_3_, ...), custom_call_target="tpu_custom_call" | custom-call | flops 1024 | bytes 1024 | tf_op jit(solution)/shard_map/pallas_call | solution.py:877
  26.9 3.5 all-to-all-start
  31.1 1.9 constant_dynamic-slice_fusion.2
  33.0 1.9 constant_dynamic-slice_fusion.1
  34.9 1.8 fusion.1
  37.3 2.0 collective-permute-start.2
  41.3 1.9 collective-permute-start.11
  43.3 14.3 %shard_map.367 = (bf16[2,512,256]{2,1,0:T(8,128)(2,1)}, bf16[2,512,256]{2,1,0:T(8,128)(2,1)}, bf16[2,512,256]{2,1,0:T(8,128)(2,1)}, bf16[2,512,256]{2,1,0:T(8,12...) custom-call(s32[1]{0:T(128)} %dynamic_slice.22.refs_0_, s32[1]{0:T(128)} %bitcast.refs_1_.refs_0_, ...), custom_call_target="tpu_custom_call" | custom-call | flops 1024 | bytes 1024 | tf_op jit(solution)/shard_map/pallas_call | solution.py:877
  57.8 1.8 collective-permute-start.7
  59.8 6.7 %collective-permute-done.7.refs_13_.refs_19_ = bf16[128,1024]{1,0:T(8,128)(2,1)S(1)} collective-permute-done((bf16[128,1024]{1,0:T(8,128)(2,1)S(1)}, bf16[128,1024]{1,0:T(8,128)(2,1)S(1)}, u32[]{:S(2)}, u32[]{:S(2)}) %collective-permute-start.7) | collective-permute-done | bytes 262176 | tf_op jit(solution)/shard_map/ppermute | solution.py:895
  67.1 2.1 collective-permute-done.8.refs_14_.refs_16_
  72.3 17.8 %shard_map.368 = (bf16[2,512,256]{2,1,0:T(8,128)(2,1)}, bf16[2,512,256]{2,1,0:T(8,128)(2,1)}, bf16[2,512,256]{2,1,0:T(8,128)(2,1)}, bf16[2,512,256]{2,1,0:T(8,12...) custom-call(s32[1]{0:T(128)} %dynamic_slice.22.refs_0_, ...), custom_call_target="tpu_custom_call" | custom-call | flops 1024 | bytes 1024 | tf_op jit(solution)/shard_map/pallas_call | solution.py:877
  90.7 4.0 collective-permute-done.12.refs_11_
  97.7 25.5 %shard_map.369 = (f32[4,1,512]{2,1,0:T(1,128)}, f32[8,1024]{1,0:T(8,128)}, bf16[1024,1024]{1,0:T(8,128)(2,1)}, bf16[1024,1024]{1,0:T(8,128)(2,1)}, bf16[1024,102...) custom-call(s32[1]{0:T(128)} %bitcast.refs_1_.refs_0_, ...), custom_call_target="tpu_custom_call" | custom-call | flops 1024 | bytes 1024 | tf_op jit(solution)/shard_map/pallas_call | solution.py:877
  123.4 20.1 %shard_map.370 = (f32[2,3,256]{2,1,0:T(4,128)}, bf16[1024,1024]{1,0:T(8,128)(2,1)}, bf16[1024,1024]{1,0:T(8,128)(2,1)}, f32[512,1024]{1,0:T(8,128)}) custom-call(s32[1]{0:T(128)} %dynamic_slice.22.refs_0_, s32[1]{0:T(128)} %bitcast.refs_1_.refs_0_, bf16[512,1024]{1,0:T(8,128)(2,1)} %get-tuple-element.194.refs_2_, ...), custom_call_target="tpu_custom_call" | custom-call | flops 1024 | bytes 1024 | tf_op jit(solution)/shard_map/pallas_call | solution.py:877
  144.1 4.3 %shard_map.371 = bf16[1024,1024]{1,0:T(8,128)(2,1)} custom-call(bf16[1024,1024]{1,0:T(8,128)(2,1)} %get-tuple-element.208.refs_0_, bf16[1024,1024]{1,0:T(8,128)(2,1)} %collective-permute-done.20.refs_1_), custom_call_target="tpu_custom_call" | custom-call | flops 1024 | bytes 1024 | tf_op jit(solution)/shard_map/pallas_call | solution.py:877
  148.4 1.9 collective-permute-start.23
  150.3 23.2 %shard_map.372 = (f32[2,3,256]{2,1,0:T(4,128)}, bf16[1024,1024]{1,0:T(8,128)(2,1)}, bf16[1024,1024]{1,0:T(8,128)(2,1)}, bf16[512,1024]{1,0:T(8,128)(2,1)}, f32[8,1024]{1,0:T(8,128)}) custom-call(s32[1]{0:T(128)} %dynamic_slice.22.refs_0_, s32[1]{0:T(128)} %bitcast.refs_1_.refs_0_, bf16[512,1024]{1,0:T(8,128)(2,1)} %get-tuple-element.194.refs_2_, ...), custom_call_target="tpu_custom_call" | custom-call | flops 1024 | bytes 1024 | tf_op jit(solution)/shard_map/pallas_call | solution.py:877
  173.5 4.3 %shard_map.373 = bf16[1024,1024]{1,0:T(8,128)(2,1)} custom-call(bf16[1024,1024]{1,0:T(8,128)(2,1)} %get-tuple-element.215.refs_0_, bf16[1024,1024]{1,0:T(8,128)(2,1)} %collective-permute-done.21.refs_1_), custom_call_target="tpu_custom_call" | custom-call | flops 1024 | bytes 1024 | tf_op jit(solution)/shard_map/pallas_call | solution.py:877
  179.2 21.4 %shard_map.374 = (f32[512,512]{1,0:T(8,128)}, bf16[6,1024]{1,0:T(8,128)(2,1)}, bf16[512,1024]{1,0:T(8,128)(2,1)}, bf16[512,1024]{1,0:T(8,128)(2,1)}, bf16[512,10...) custom-call(s32[2]{0:T(128)} %pad_add_fusion.refs_0_.own_ref, bf16[512,1024]{1,0:T(8,128)(2,1)} %get-tuple-element.217.refs_1_, ...), custom_call_target="tpu_custom_call" | custom-call | flops 1024 | bytes 1024 | tf_op jit(solution)/shard_map/pallas_call | solution.py:877
  201.2 4.2 shard_map.375
  207.1 2.6 shard_map.376
  211.5 19.3 %collective-permute-done.27.refs_2_.refs_4_ = bf16[512,1024]{1,0:T(8,128)(2,1)} collective-permute-done((bf16[512,1024]{1,0:T(8,128)(2,1)}, bf16[512,1024]{1,0:T(8,128)(2,1)}, u32[]{:S(2)}, u32[]{:S(2)}) %collective-permute-start.27) | collective-permute-done | bytes 1048608 | tf_op jit(solution)/shard_map/ppermute | solution.py:895
  230.8 2.8 shard_map.377
  233.6 8.5 %collective-permute-done.29.refs_2_.refs_5_ = bf16[1024,1024]{1,0:T(8,128)(2,1)} collective-permute-done((bf16[1024,1024]{1,0:T(8,128)(2,1)}, bf16[1024,1024]{1,0:T(8,128)(2,1)}, u32[]{:S(2)}, u32[]{:S(2)}) %collective-permute-start.29) | collective-permute-done | bytes 2097184 | tf_op jit(solution)/shard_map/ppermute | solution.py:895
  242.1 4.2 shard_map.378
  246.3 1.8 collective-permute-start.32
  249.7 11.3 %collective-permute-done.28.refs_2_.refs_4_ = bf16[256,1024]{1,0:T(8,128)(2,1)} collective-permute-done((bf16[256,1024]{1,0:T(8,128)(2,1)}, bf16[256,1024]{1,0:T(8,128)(2,1)}, u32[]{:S(2)}, u32[]{:S(2)}) %collective-permute-start.28) | collective-permute-done | bytes 524320 | tf_op jit(solution)/shard_map/ppermute | solution.py:895
  260.9 2.1 shard_map.379
  263.1 2.6 collective-permute-start.33
  265.7 3.2 shard_map.380
  269.4 6.4 %collective-permute-done.33.refs_1_ = bf16[128,1024]{1,0:T(8,128)(2,1)S(1)} collective-permute-done((bf16[128,1024]{1,0:T(8,128)(2,1)}, bf16[128,1024]{1,0:T(8,128)(2,1)S(1)}, u32[]{:S(2)}, u32[]{:S(2)}) %collective-permute-start.33) | collective-permute-done | bytes 262176 | tf_op jit(solution)/shard_map/ppermute | solution.py:895
  276.5 1.8 shard_map.381.refs_0_
  278.3 2.8 shard_map.382
  281.9 3.3 collective-permute-start.41
  286.0 2.1 shard_map.383
  288.1 13.7 %collective-permute-done.35.refs_2_.refs_4_ = bf16[256,1024]{1,0:T(8,128)(2,1)} collective-permute-done((bf16[256,1024]{1,0:T(8,128)(2,1)}, bf16[256,1024]{1,0:T(8,128)(2,1)}, u32[]{:S(2)}, u32[]{:S(2)}) %collective-permute-start.35) | collective-permute-done | bytes 524320 | tf_op jit(solution)/shard_map/ppermute | solution.py:895
  301.9 2.1 shard_map.384
  305.2 2.5 collective-permute-start.42
  309.4 1.9 shard_map.385
  311.3 6.8 %collective-permute-done.37.refs_1_ = bf16[128,1024]{1,0:T(8,128)(2,1)} collective-permute-done((bf16[128,1024]{1,0:T(8,128)(2,1)}, bf16[128,1024]{1,0:T(8,128)(2,1)}, u32[]{:S(2)}, u32[]{:S(2)}) %collective-permute-start.37) | collective-permute-done | bytes 262176 | tf_op jit(solution)/shard_map/ppermute | solution.py:895
  318.0 1.8 shard_map.386.refs_0_
  324.8 2.4 collective-permute-done.43.refs_3_
  328.3 8.4 %collective-permute-done.36.refs_1_ = bf16[64,1024]{1,0:T(8,128)(2,1)S(1)} collective-permute-done((bf16[64,1024]{1,0:T(8,128)(2,1)}, bf16[64,1024]{1,0:T(8,128)(2,1)S(1)}, u32[]{:S(2)}, u32[]{:S(2)}) %collective-permute-start.36) | collective-permute-done | bytes 131104 | tf_op jit(solution)/shard_map/ppermute | solution.py:895
  336.7 1.9 collective-permute-start.49
  340.4 3.2 collective-permute-start.38
  343.6 2.0 collective-permute-start.39
  346.1 7.9 %collective-permute-done.38.refs_1_ = bf16[64,1024]{1,0:T(8,128)(2,1)S(1)} collective-permute-done((bf16[64,1024]{1,0:T(8,128)(2,1)}, bf16[64,1024]{1,0:T(8,128)(2,1)S(1)}, u32[]{:S(2)}, u32[]{:S(2)}) %collective-permute-start.38) | collective-permute-done | bytes 131104 | tf_op jit(solution)/shard_map/ppermute | solution.py:895
  356.7 3.6 collective-permute-start.40
  361.6 4.4 %shard_map.388 = (f32[1024,512]{1,0:T(8,128)}, f32[512,1024]{1,0:T(8,128)}) custom-call(s32[8]{0:T(128)} %stack.103.starts_ref, bf16[128,1024]{1,0:T(8,128)(2,1)} %shard_map.381.refs_0_, bf16[128,1024]{1,0:T(8,128)(2,1)} %collective-permute-done.41.refs_1_, bf16[128,1024]{1,0:T(8,128)(2,1)} %copy-done.10, bf16[128,1024]{1,0:T(8,128)(2,1)} %collective-permute-done.43.refs_3_, ...), custom_call_target="tpu_custom_call" | custom-call | flops 1024 | bytes 1024 | tf_op jit(solution)/shard_map/pallas_call | solution.py:877
  366.0 2.3 collective-permute-done.53.refs_6_
  368.3 2.8 collective-permute-done.54.refs_7_
  371.1 2.6 shard_map.389.refs_0_
  376.0 8.3 %collective-permute-done.55.refs_2_ = bf16[256,1024]{1,0:T(8,128)(2,1)} collective-permute-done((bf16[256,1024]{1,0:T(8,128)(2,1)}, bf16[256,1024]{1,0:T(8,128)(2,1)}, u32[]{:S(2)}, u32[]{:S(2)}) %collective-permute-start.55) | collective-permute-done | bytes 524320 | tf_op jit(solution)/shard_map/ppermute | solution.py:895
  386.9 3.3 all-to-all-start.1
  391.2 2.8 all-to-all-done.1
  394.0 2.9 collective-permute-done.57.refs_3_
  398.5 3.3 all-to-all-start.2
  405.5 4.4 %shard_map.391 = (f32[3,1024,256]{2,1,0:T(8,128)}, f32[256,1024]{1,0:T(8,128)}) custom-call(s32[8]{0:T(128)} %stack.103.starts_ref, bf16[128,1024]{1,0:T(8,128)(2,1)} %shard_map.386.refs_0_, bf16[128,1024]{1,0:T(8,128)(2,1)} %collective-permute-done.48.refs_1_, bf16[128,1024]{1,0:T(8,128)(2,1)} %copy-done.9, ...), custom_call_target="tpu_custom_call" | custom-call | flops 1024 | bytes 1024 | tf_op jit(solution)/shard_map/pallas_call | solution.py:877
  410.7 6.2 %shard_map.390 = (f32[712,1024]{1,0:T(8,128)}, f32[512,1024]{1,0:T(8,128)}, f32[1024,512]{1,0:T(8,128)}, f32[7,512]{1,0:T(8,128)}, f32[3,512]{1,0:T(4,128)}, /*i...) custom-call(s32[8]{0:T(128)} %stack.112.starts_ref, ...), custom_call_target="tpu_custom_call" | custom-call | flops 1024 | bytes 1024 | tf_op jit(solution)/shard_map/pallas_call | solution.py:877
  420.0 3.7 fusion.2
  (191 shorter events, 58.7 us)
Async XLA Ops:
  2.9 34.4 %collective-permute-start = (bf16[3,512,256]{2,1,0:T(8,128)(2,1)}, bf16[3,512,256]{2,1,0:T(8,128)(2,1)}, u32[]{:S(2)}, u32[]{:S(2)}) collective-permute-start(bf16[3,512,256]{2,1,0:T(8,128)(2,1)} %constant_dynamic-slice_fusion.4), channel_id=1, source_target_pairs={{0,2},{1,3},{2,0},{3,1},{4,6},{5,7},{6,4},{7,5},{8,10},{9,11},{10,... | collective-permute-start | bytes 2359304 | tf_op jit(solution)/shard_map/ppermute | solution.py:895
  7.6 35.6 %collective-permute-start.1 = (bf16[128,1024]{1,0:T(8,128)(2,1)}, bf16[128,1024]{1,0:T(8,128)(2,1)S(1)}, u32[]{:S(2)}, u32[]{:S(2)}) collective-permute-start(bf16[128,1024]{1,0:T(8,128)(2,1)} %constant_dynamic-slice_fusion.3), channel_id=1, source_target_pairs={{0,2},{1,3},{2,0},{3,1},{4,6},{5,7},{6,4},{7,5},{8,10},{9,11},{10,... | collective-permute-start | bytes 786440 | tf_op jit(solution)/shard_map/ppermute | solution.py:895
  26.9 10.4 %all-to-all-start = ((bf16[4,2,1408]{2,1,0:T(2,128)(2,1)}), bf16[4,2,1408]{2,1,0:T(2,128)(2,1)S(1)}, u32[]{:S(2)}, u32[]{:S(2)}) async-start(bf16[4,2,1408]{2,1,0:T(2,128)(2,1)} %reshape.189), calls=%async_computation | async-start | bytes 45056 | tf_op jit(solution)/shard_map/all_to_all | solution.py:1175
  30.4 12.9 %collective-permute-start.3 = (bf16[3,1024,256]{2,1,0:T(8,128)(2,1)}, bf16[3,1024,256]{2,1,0:T(8,128)(2,1)}, u32[]{:S(2)}, u32[]{:S(2)}) collective-permute-start(bf16[3,1024,256]{2,1,0:T(8,128)(2,1)} %refs_13_.4), channel_id=1, source_target_pairs={{0,1},{1,0},{2,3},{3,2},{4,5},{5,4},{6,7},{7,6},{8,9},{9,8},{10,11... | collective-permute-start | bytes 4718600 | tf_op jit(solution)/shard_map/ppermute | solution.py:895
  31.0 12.3 %collective-permute-start.4 = (bf16[256,1024]{1,0:T(8,128)(2,1)}, bf16[256,1024]{1,0:T(8,128)(2,1)}, u32[]{:S(2)}, u32[]{:S(2)}) collective-permute-start(bf16[256,1024]{1,0:T(8,128)(2,1)} %refs_15_.2), channel_id=1, source_target_pairs={{0,1},{1,0},{2,3},{3,2},{4,5},{5,4},{6,7},{7,6},{8,9},{9,8},{10,11... | collective-permute-start | bytes 1572872 | tf_op jit(solution)/shard_map/ppermute | solution.py:895
  37.3 20.4 %collective-permute-start.2 = (bf16[3,512,256]{2,1,0:T(8,128)(2,1)}, bf16[3,512,256]{2,1,0:T(8,128)(2,1)}, u32[]{:S(2)}, u32[]{:S(2)}) collective-permute-start(bf16[3,512,256]{2,1,0:T(8,128)(2,1)} %collective-permute-done.refs_8_.refs_14_), channel_id=1, source_target_pairs={{0,4},{4,0},{8,12},{12,8},{16,20},{20,16},{24,28},{28,24},{1,5},{5... | collective-permute-start | bytes 2359304 | tf_op jit(solution)/shard_map/ppermute | solution.py:895
  41.3 25.3 %collective-permute-start.11 = (bf16[256,1024]{1,0:T(8,128)(2,1)}, bf16[256,1024]{1,0:T(8,128)(2,1)}, u32[]{:S(2)}, u32[]{:S(2)}) collective-permute-start(bf16[256,1024]{1,0:T(8,128)(2,1)} %constant_dynamic-slice_fusion.1), channel_id=1, source_target_pairs={{0,2},{1,3},{2,0},{3,1},{4,6},{5,7},{6,4},{7,5},{8,10},{9,11},{10,... | collective-permute-start | bytes 1572872 | tf_op jit(solution)/shard_map/ppermute | solution.py:895
  43.2 23.8 %collective-permute-start.10 = (bf16[512,512]{1,0:T(8,128)(2,1)}, bf16[512,512]{1,0:T(8,128)(2,1)}, u32[]{:S(2)}, u32[]{:S(2)}) collective-permute-start(bf16[512,512]{1,0:T(8,128)(2,1)} %constant_dynamic-slice_fusion.2), channel_id=1, source_target_pairs={{0,2},{1,3},{2,0},{3,1},{4,6},{5,7},{6,4},{7,5},{8,10},{9,11},{10,... | collective-permute-start | bytes 1572872 | tf_op jit(solution)/shard_map/ppermute | solution.py:895
  57.8 13.9 %collective-permute-start.5 = (bf16[3,512,256]{2,1,0:T(8,128)(2,1)}, bf16[3,512,256]{2,1,0:T(8,128)(2,1)}, u32[]{:S(2)}, u32[]{:S(2)}) collective-permute-start(bf16[3,512,256]{2,1,0:T(8,128)(2,1)} %collective-permute-done.refs_8_.refs_14_), channel_id=1, source_target_pairs={{0,1},{1,0},{2,3},{3,2},{4,5},{5,4},{6,7},{7,6},{8,9},{9,8},{10,11... | collective-permute-start | bytes 2359304 | tf_op jit(solution)/shard_map/ppermute | solution.py:895
  57.8 8.7 %collective-permute-start.7 = (bf16[128,1024]{1,0:T(8,128)(2,1)S(1)}, bf16[128,1024]{1,0:T(8,128)(2,1)S(1)}, u32[]{:S(2)}, u32[]{:S(2)}) collective-permute-start(bf16[128,1024]{1,0:T(8,128)(2,1)S(1)} %collective-permute-done.1.refs_12_.refs_18_), channel_id=1, source_target_pairs={{0,4},{4,0},{8,12},{12,8},{16,20},{20,16},{24,28},{28,24},{1,5},{5... | collective-permute-start | bytes 786440 | tf_op jit(solution)/shard_map/ppermute | solution.py:895
  59.5 35.2 %collective-permute-start.15 = (bf16[1024,512]{1,0:T(8,128)(2,1)}, bf16[1024,512]{1,0:T(8,128)(2,1)}, u32[]{:S(2)}, u32[]{:S(2)}) collective-permute-start(bf16[1024,512]{1,0:T(8,128)(2,1)} %refs_13_.3), channel_id=1, source_target_pairs={{0,1},{1,0},{2,3},{3,2},{4,5},{5,4},{6,7},{7,6},{8,9},{9,8},{10,11... | collective-permute-start | bytes 3145736 | tf_op jit(solution)/shard_map/ppermute | solution.py:895
  66.5 5.8 %collective-permute-start.6 = (bf16[3,512,256]{2,1,0:T(8,128)(2,1)}, bf16[3,512,256]{2,1,0:T(8,128)(2,1)}, u32[]{:S(2)}, u32[]{:S(2)}) collective-permute-start(bf16[3,512,256]{2,1,0:T(8,128)(2,1)} %collective-permute-done.2.refs_9_.refs_15_), channel_id=1, source_target_pairs={{0,1},{1,0},{2,3},{3,2},{4,5},{5,4},{6,7},{7,6},{8,9},{9,8},{10,11... | collective-permute-start | bytes 2359304 | tf_op jit(solution)/shard_map/ppermute | solution.py:895
  66.5 2.6 collective-permute-start.8
  67.0 3.9 collective-permute-start.9
  69.2 20.9 %collective-permute-start.16 = (bf16[256,1024]{1,0:T(8,128)(2,1)}, bf16[256,1024]{1,0:T(8,128)(2,1)}, u32[]{:S(2)}, u32[]{:S(2)}) collective-permute-start(bf16[256,1024]{1,0:T(8,128)(2,1)} %collective-permute-done.11.refs_16_), channel_id=1, source_target_pairs={{0,4},{4,0},{8,12},{12,8},{16,20},{20,16},{24,28},{28,24},{1,5},{5... | collective-permute-start | bytes 1572872 | tf_op jit(solution)/shard_map/ppermute | solution.py:895
  70.9 23.8 %collective-permute-start.12 = (bf16[512,512]{1,0:T(8,128)(2,1)}, bf16[512,512]{1,0:T(8,128)(2,1)}, u32[]{:S(2)}, u32[]{:S(2)}) collective-permute-start(bf16[512,512]{1,0:T(8,128)(2,1)} %collective-permute-done.10.refs_10_), channel_id=1, source_target_pairs={{0,4},{4,0},{8,12},{12,8},{16,20},{20,16},{24,28},{28,24},{1,5},{5... | collective-permute-start | bytes 1572872 | tf_op jit(solution)/shard_map/ppermute | solution.py:895
  71.7 24.2 %collective-permute-start.19 = (bf16[512,1024]{1,0:T(8,128)(2,1)}, bf16[512,1024]{1,0:T(8,128)(2,1)}, u32[]{:S(2)}, u32[]{:S(2)}) collective-permute-start(bf16[512,1024]{1,0:T(8,128)(2,1)} %refs_19_.1), channel_id=1, source_target_pairs={{0,1},{1,0},{2,3},{3,2},{4,5},{5,4},{6,7},{7,6},{8,9},{9,8},{10,11... | collective-permute-start | bytes 3145736 | tf_op jit(solution)/shard_map/ppermute | solution.py:895
  90.1 5.7 %collective-permute-start.17 = (bf16[256,1024]{1,0:T(8,128)(2,1)}, bf16[256,1024]{1,0:T(8,128)(2,1)S(1)}, u32[]{:S(2)}, u32[]{:S(2)}) collective-permute-start(bf16[256,1024]{1,0:T(8,128)(2,1)} %collective-permute-done.11.refs_16_), channel_id=1, source_target_pairs={{0,1},{1,0},{2,3},{3,2},{4,5},{5,4},{6,7},{7,6},{8,9},{9,8},{10,11... | collective-permute-start | bytes 1572872 | tf_op jit(solution)/shard_map/ppermute | solution.py:895
  90.7 5.2 %collective-permute-start.18 = (bf16[256,1024]{1,0:T(8,128)(2,1)}, bf16[256,1024]{1,0:T(8,128)(2,1)}, u32[]{:S(2)}, u32[]{:S(2)}) collective-permute-start(bf16[256,1024]{1,0:T(8,128)(2,1)} %collective-permute-done.16.refs_17_), channel_id=1, source_target_pairs={{0,1},{1,0},{2,3},{3,2},{4,5},{5,4},{6,7},{7,6},{8,9},{9,8},{10,11... | collective-permute-start | bytes 1572872 | tf_op jit(solution)/shard_map/ppermute | solution.py:895
  94.7 3.0 collective-permute-start.14
  123.2 20.9 %collective-permute-start.20 = (bf16[1024,1024]{1,0:T(8,128)(2,1)}, bf16[1024,1024]{1,0:T(8,128)(2,1)}, u32[]{:S(2)}, u32[]{:S(2)}) collective-permute-start(bf16[1024,1024]{1,0:T(8,128)(2,1)} %get-tuple-element.207), channel_id=1, source_target_pairs={{0,1},{1,0},{2,3},{3,2},{4,5},{5,4},{6,7},{7,6},{8,9},{9,8},{10,11... | collective-permute-start | bytes 6291464 | tf_op jit(solution)/shard_map/ppermute | solution.py:895
  143.5 30.0 %collective-permute-start.21 = (bf16[1024,1024]{1,0:T(8,128)(2,1)}, bf16[1024,1024]{1,0:T(8,128)(2,1)}, u32[]{:S(2)}, u32[]{:S(2)}) collective-permute-start(bf16[1024,1024]{1,0:T(8,128)(2,1)} %get-tuple-element.214), channel_id=1, source_target_pairs={{0,1},{1,0},{2,3},{3,2},{4,5},{5,4},{6,7},{7,6},{8,9},{9,8},{10,11... | collective-permute-start | bytes 6291464 | tf_op jit(solution)/shard_map/ppermute | solution.py:895
  143.9 57.3 %collective-permute-start.24 = (bf16[1024,1024]{1,0:T(8,128)(2,1)}, bf16[1024,1024]{1,0:T(8,128)(2,1)}, u32[]{:S(2)}, u32[]{:S(2)}) collective-permute-start(bf16[1024,1024]{1,0:T(8,128)(2,1)} %get-tuple-element.234), channel_id=1, source_target_pairs={{0,1},{1,0},{2,3},{3,2},{4,5},{5,4},{6,7},{7,6},{8,9},{9,8},{10,11... | collective-permute-start | bytes 6291464 | tf_op jit(solution)/shard_map/ppermute | solution.py:895
  148.4 52.8 %collective-permute-start.23 = (bf16[1024,1024]{1,0:T(8,128)(2,1)}, bf16[1024,1024]{1,0:T(8,128)(2,1)}, u32[]{:S(2)}, u32[]{:S(2)}) collective-permute-start(bf16[1024,1024]{1,0:T(8,128)(2,1)} %shard_map.371), channel_id=1, source_target_pairs={{0,2},{1,3},{2,0},{3,1},{4,6},{5,7},{6,4},{7,5},{8,10},{9,11},{10,... | collective-permute-start | bytes 6291464 | tf_op jit(solution)/shard_map/ppermute | solution.py:895
  177.8 64.3 %collective-permute-start.29 = (bf16[1024,1024]{1,0:T(8,128)(2,1)}, bf16[1024,1024]{1,0:T(8,128)(2,1)}, u32[]{:S(2)}, u32[]{:S(2)}) collective-permute-start(bf16[1024,1024]{1,0:T(8,128)(2,1)} %shard_map.373), channel_id=1, source_target_pairs={{0,2},{1,3},{2,0},{3,1},{4,6},{5,7},{6,4},{7,5},{8,10},{9,11},{10,... | collective-permute-start | bytes 6291464 | tf_op jit(solution)/shard_map/ppermute | solution.py:895
  178.0 64.1 %collective-permute-start.30 = (bf16[1024,1024]{1,0:T(8,128)(2,1)}, bf16[1024,1024]{1,0:T(8,128)(2,1)}, u32[]{:S(2)}, u32[]{:S(2)}) collective-permute-start(bf16[1024,1024]{1,0:T(8,128)(2,1)} %get-tuple-element.248), channel_id=1, source_target_pairs={{0,1},{1,0},{2,3},{3,2},{4,5},{5,4},{6,7},{7,6},{8,9},{9,8},{10,11... | collective-permute-start | bytes 6291464 | tf_op jit(solution)/shard_map/ppermute | solution.py:895
  200.6 6.5 %collective-permute-start.22 = (bf16[512,1024]{1,0:T(8,128)(2,1)}, bf16[512,1024]{1,0:T(8,128)(2,1)}, u32[]{:S(2)}, u32[]{:S(2)}) collective-permute-start(bf16[512,1024]{1,0:T(8,128)(2,1)} %get-tuple-element.232), channel_id=1, source_target_pairs={{0,1},{1,0},{2,3},{3,2},{4,5},{5,4},{6,7},{7,6},{8,9},{9,8},{10,11... | collective-permute-start | bytes 3145736 | tf_op jit(solution)/shard_map/ppermute | solution.py:895
  205.4 25.4 %collective-permute-start.27 = (bf16[512,1024]{1,0:T(8,128)(2,1)}, bf16[512,1024]{1,0:T(8,128)(2,1)}, u32[]{:S(2)}, u32[]{:S(2)}) collective-permute-start(bf16[512,1024]{1,0:T(8,128)(2,1)} %get-tuple-element.242), channel_id=1, source_target_pairs={{0,4},{4,0},{8,12},{12,8},{16,20},{20,16},{24,28},{28,24},{1,5},{5... | collective-permute-start | bytes 3145736 | tf_op jit(solution)/shard_map/ppermute | solution.py:895
  207.1 58.5 %collective-permute-start.26 = (bf16[512,1024]{1,0:T(8,128)(2,1)}, bf16[512,1024]{1,0:T(8,128)(2,1)}, u32[]{:S(2)}, u32[]{:S(2)}) collective-permute-start(bf16[512,1024]{1,0:T(8,128)(2,1)} %get-tuple-element.241), channel_id=1, source_target_pairs={{0,1},{1,0},{2,3},{3,2},{4,5},{5,4},{6,7},{7,6},{8,9},{9,8},{10,11... | collective-permute-start | bytes 3145736 | tf_op jit(solution)/shard_map/ppermute | solution.py:895
  209.8 55.9 %collective-permute-start.25 = (bf16[512,1024]{1,0:T(8,128)(2,1)}, bf16[512,1024]{1,0:T(8,128)(2,1)}, u32[]{:S(2)}, u32[]{:S(2)}) collective-permute-start(bf16[512,1024]{1,0:T(8,128)(2,1)} %shard_map.376), channel_id=1, source_target_pairs={{0,2},{1,3},{2,0},{3,1},{4,6},{5,7},{6,4},{7,5},{8,10},{9,11},{10,... | collective-permute-start | bytes 3145736 | tf_op jit(solution)/shard_map/ppermute | solution.py:895
  246.3 32.0 %collective-permute-start.32 = (bf16[512,1024]{1,0:T(8,128)(2,1)}, bf16[512,1024]{1,0:T(8,128)(2,1)}, u32[]{:S(2)}, u32[]{:S(2)}) collective-permute-start(bf16[512,1024]{1,0:T(8,128)(2,1)} %get-tuple-element.261), channel_id=1, source_target_pairs={{0,4},{4,0},{8,12},{12,8},{16,20},{20,16},{24,28},{28,24},{1,5},{5... | collective-permute-start | bytes 3145736 | tf_op jit(solution)/shard_map/ppermute | solution.py:895
  248.1 12.9 %collective-permute-start.28 = (bf16[256,1024]{1,0:T(8,128)(2,1)}, bf16[256,1024]{1,0:T(8,128)(2,1)}, u32[]{:S(2)}, u32[]{:S(2)}) collective-permute-start(bf16[256,1024]{1,0:T(8,128)(2,1)} %get-tuple-element.246), channel_id=1, source_target_pairs={{0,8},{4,12},{8,0},{12,4},{16,24},{20,28},{24,16},{28,20},{1,9},{5... | collective-permute-start | bytes 1572872 | tf_op jit(solution)/shard_map/ppermute | solution.py:895
  263.1 12.7 %collective-permute-start.33 = (bf16[128,1024]{1,0:T(8,128)(2,1)}, bf16[128,1024]{1,0:T(8,128)(2,1)S(1)}, u32[]{:S(2)}, u32[]{:S(2)}) collective-permute-start(bf16[128,1024]{1,0:T(8,128)(2,1)} %get-tuple-element.262), channel_id=1, source_target_pairs={{0,16},{4,20},{8,24},{12,28},{16,0},{20,4},{24,8},{28,12},{1,17},{... | collective-permute-start | bytes 786440 | tf_op jit(solution)/shard_map/ppermute | solution.py:895
  268.9 16.3 %collective-permute-start.31 = (bf16[256,1024]{1,0:T(8,128)(2,1)}, bf16[256,1024]{1,0:T(8,128)(2,1)S(1)}, u32[]{:S(2)}, u32[]{:S(2)}) collective-permute-start(bf16[256,1024]{1,0:T(8,128)(2,1)} %get-tuple-element.260), channel_id=1, source_target_pairs={{0,4},{4,0},{8,12},{12,8},{16,20},{20,16},{24,28},{28,24},{1,5},{5... | collective-permute-start | bytes 1572872 | tf_op jit(solution)/shard_map/ppermute | solution.py:895
  281.1 20.8 %collective-permute-start.35 = (bf16[256,1024]{1,0:T(8,128)(2,1)}, bf16[256,1024]{1,0:T(8,128)(2,1)}, u32[]{:S(2)}, u32[]{:S(2)}) collective-permute-start(bf16[256,1024]{1,0:T(8,128)(2,1)} %get-tuple-element.272), channel_id=1, source_target_pairs={{0,8},{4,12},{8,0},{12,4},{16,24},{20,28},{24,16},{28,20},{1,9},{5... | collective-permute-start | bytes 1572872 | tf_op jit(solution)/shard_map/ppermute | solution.py:895
  281.9 26.3 %collective-permute-start.41 = (bf16[128,1024]{1,0:T(8,128)(2,1)S(1)}, bf16[128,1024]{1,0:T(8,128)(2,1)}, u32[]{:S(2)}, u32[]{:S(2)}) collective-permute-start(bf16[128,1024]{1,0:T(8,128)(2,1)S(1)} %copy-done.2), channel_id=1, source_target_pairs={{0,16},{4,20},{8,24},{12,28},{16,0},{20,4},{24,8},{28,12},{1,17},{... | collective-permute-start | bytes 786440 | tf_op jit(solution)/shard_map/ppermute | solution.py:895
  288.1 20.6 %collective-permute-start.34 = (bf16[128,1024]{1,0:T(8,128)(2,1)}, bf16[128,1024]{1,0:T(8,128)(2,1)S(1)}, u32[]{:S(2)}, u32[]{:S(2)}) collective-permute-start(bf16[128,1024]{1,0:T(8,128)(2,1)} %get-tuple-element.271), channel_id=1, source_target_pairs={{0,8},{4,12},{8,0},{12,4},{16,24},{20,28},{24,16},{28,20},{1,9},{5... | collective-permute-start | bytes 786440 | tf_op jit(solution)/shard_map/ppermute | solution.py:895
  304.0 14.0 %collective-permute-start.37 = (bf16[128,1024]{1,0:T(8,128)(2,1)}, bf16[128,1024]{1,0:T(8,128)(2,1)}, u32[]{:S(2)}, u32[]{:S(2)}) collective-permute-start(bf16[128,1024]{1,0:T(8,128)(2,1)} %get-tuple-element.280), channel_id=1, source_target_pairs={{0,16},{4,20},{8,24},{12,28},{16,0},{20,4},{24,8},{28,12},{1,17},{... | collective-permute-start | bytes 786440 | tf_op jit(solution)/shard_map/ppermute | solution.py:895
  305.2 16.5 %collective-permute-start.42 = (bf16[128,1024]{1,0:T(8,128)(2,1)S(1)}, bf16[128,1024]{1,0:T(8,128)(2,1)S(1)}, u32[]{:S(2)}, u32[]{:S(2)}) collective-permute-start(bf16[128,1024]{1,0:T(8,128)(2,1)S(1)} %copy-done.2), channel_id=1, source_target_pairs={{0,8},{4,12},{8,0},{12,4},{16,24},{20,28},{24,16},{28,20},{1,9},{5... | collective-permute-start | bytes 786440 | tf_op jit(solution)/shard_map/ppermute | solution.py:895
  307.6 15.6 %collective-permute-start.44 = (bf16[128,1024]{1,0:T(8,128)(2,1)S(1)}, bf16[128,1024]{1,0:T(8,128)(2,1)}, u32[]{:S(2)}, u32[]{:S(2)}) collective-permute-start(bf16[128,1024]{1,0:T(8,128)(2,1)S(1)} %copy-done.2), channel_id=1, source_target_pairs={{0,4},{4,0},{8,12},{12,8},{16,20},{20,16},{24,28},{28,24},{1,5},{5... | collective-permute-start | bytes 786440 | tf_op jit(solution)/shard_map/ppermute | solution.py:895
  308.2 19.0 %collective-permute-start.43 = (bf16[128,1024]{1,0:T(8,128)(2,1)}, bf16[128,1024]{1,0:T(8,128)(2,1)}, u32[]{:S(2)}, u32[]{:S(2)}) collective-permute-start(bf16[128,1024]{1,0:T(8,128)(2,1)} %collective-permute-done.41.refs_1_), channel_id=1, source_target_pairs={{0,8},{4,12},{8,0},{12,4},{16,24},{20,28},{24,16},{28,20},{1,9},{5... | collective-permute-start | bytes 786440 | tf_op jit(solution)/shard_map/ppermute | solution.py:895
  319.8 18.8 %collective-permute-start.48 = (bf16[128,1024]{1,0:T(8,128)(2,1)}, bf16[128,1024]{1,0:T(8,128)(2,1)}, u32[]{:S(2)}, u32[]{:S(2)}) collective-permute-start(bf16[128,1024]{1,0:T(8,128)(2,1)} %shard_map.386.refs_0_), channel_id=1, source_target_pairs={{0,16},{4,20},{8,24},{12,28},{16,0},{20,4},{24,8},{28,12},{1,17},{... | collective-permute-start | bytes 786440 | tf_op jit(solution)/shard_map/ppermute | solution.py:895
  319.8 20.6 %collective-permute-start.45 = (bf16[128,1024]{1,0:T(8,128)(2,1)}, bf16[128,1024]{1,0:T(8,128)(2,1)S(1)}, u32[]{:S(2)}, u32[]{:S(2)}) collective-permute-start(bf16[128,1024]{1,0:T(8,128)(2,1)} %collective-permute-done.41.refs_1_), channel_id=1, source_target_pairs={{0,4},{4,0},{8,12},{12,8},{16,20},{20,16},{24,28},{28,24},{1,5},{5... | collective-permute-start | bytes 786440 | tf_op jit(solution)/shard_map/ppermute | solution.py:895
  321.7 15.0 %collective-permute-start.36 = (bf16[64,1024]{1,0:T(8,128)(2,1)}, bf16[64,1024]{1,0:T(8,128)(2,1)S(1)}, u32[]{:S(2)}, u32[]{:S(2)}) collective-permute-start(bf16[64,1024]{1,0:T(8,128)(2,1)} %get-tuple-element.279), channel_id=1, source_target_pairs={{0,16},{4,20},{8,24},{12,28},{16,0},{20,4},{24,8},{28,12},{1,17},{... | collective-permute-start | bytes 393224 | tf_op jit(solution)/shard_map/ppermute | solution.py:895
  323.2 20.4 %collective-permute-start.46 = (bf16[128,1024]{1,0:T(8,128)(2,1)S(1)}, bf16[128,1024]{1,0:T(8,128)(2,1)}, u32[]{:S(2)}, u32[]{:S(2)}) collective-permute-start(bf16[128,1024]{1,0:T(8,128)(2,1)S(1)} %collective-permute-done.42.refs_2_), channel_id=1, source_target_pairs={{0,4},{4,0},{8,12},{12,8},{16,20},{20,16},{24,28},{28,24},{1,5},{5... | collective-permute-start | bytes 786440 | tf_op jit(solution)/shard_map/ppermute | solution.py:895
  327.2 18.4 %collective-permute-start.47 = (bf16[128,1024]{1,0:T(8,128)(2,1)}, bf16[128,1024]{1,0:T(8,128)(2,1)}, u32[]{:S(2)}, u32[]{:S(2)}) collective-permute-start(bf16[128,1024]{1,0:T(8,128)(2,1)} %collective-permute-done.43.refs_3_), channel_id=1, source_target_pairs={{0,4},{4,0},{8,12},{12,8},{16,20},{20,16},{24,28},{28,24},{1,5},{5... | collective-permute-start | bytes 786440 | tf_op jit(solution)/shard_map/ppermute | solution.py:895
  336.7 17.9 %collective-permute-start.49 = (bf16[128,1024]{1,0:T(8,128)(2,1)}, bf16[128,1024]{1,0:T(8,128)(2,1)S(1)}, u32[]{:S(2)}, u32[]{:S(2)}) collective-permute-start(bf16[128,1024]{1,0:T(8,128)(2,1)} %shard_map.386.refs_0_), channel_id=1, source_target_pairs={{0,8},{4,12},{8,0},{12,4},{16,24},{20,28},{24,16},{28,20},{1,9},{5... | collective-permute-start | bytes 786440 | tf_op jit(solution)/shard_map/ppermute | solution.py:895
  338.6 17.6 %collective-permute-start.50 = (bf16[128,1024]{1,0:T(8,128)(2,1)}, bf16[128,1024]{1,0:T(8,128)(2,1)}, u32[]{:S(2)}, u32[]{:S(2)}) collective-permute-start(bf16[128,1024]{1,0:T(8,128)(2,1)} %collective-permute-done.48.refs_1_), channel_id=1, source_target_pairs={{0,8},{4,12},{8,0},{12,4},{16,24},{20,28},{24,16},{28,20},{1,9},{5... | collective-permute-start | bytes 786440 | tf_op jit(solution)/shard_map/ppermute | solution.py:895
  340.4 13.7 %collective-permute-start.38 = (bf16[64,1024]{1,0:T(8,128)(2,1)}, bf16[64,1024]{1,0:T(8,128)(2,1)S(1)}, u32[]{:S(2)}, u32[]{:S(2)}) collective-permute-start(bf16[64,1024]{1,0:T(8,128)(2,1)} %shard_map.387.refs_0_), channel_id=1, source_target_pairs={{0,16},{4,20},{8,24},{12,28},{16,0},{20,4},{24,8},{28,12},{1,17},{... | collective-permute-start | bytes 393224 | tf_op jit(solution)/shard_map/ppermute | solution.py:895
  343.6 13.1 %collective-permute-start.39 = (bf16[64,1024]{1,0:T(8,128)(2,1)}, bf16[64,1024]{1,0:T(8,128)(2,1)}, u32[]{:S(2)}, u32[]{:S(2)}) collective-permute-start(bf16[64,1024]{1,0:T(8,128)(2,1)} %shard_map.387.refs_0_), channel_id=1, source_target_pairs={{0,8},{4,12},{8,0},{12,4},{16,24},{20,28},{24,16},{28,20},{1,9},{5... | collective-permute-start | bytes 393224 | tf_op jit(solution)/shard_map/ppermute | solution.py:895
  345.6 20.4 %collective-permute-start.51 = (bf16[128,1024]{1,0:T(8,128)(2,1)}, bf16[128,1024]{1,0:T(8,128)(2,1)}, u32[]{:S(2)}, u32[]{:S(2)}) collective-permute-start(bf16[128,1024]{1,0:T(8,128)(2,1)} %shard_map.386.refs_0_), channel_id=1, source_target_pairs={{0,4},{4,0},{8,12},{12,8},{16,20},{20,16},{24,28},{28,24},{1,5},{5... | collective-permute-start | bytes 786440 | tf_op jit(solution)/shard_map/ppermute | solution.py:895
  354.1 11.9 %collective-permute-start.52 = (bf16[128,1024]{1,0:T(8,128)(2,1)}, bf16[128,1024]{1,0:T(8,128)(2,1)}, u32[]{:S(2)}, u32[]{:S(2)}) collective-permute-start(bf16[128,1024]{1,0:T(8,128)(2,1)} %collective-permute-done.48.refs_1_), channel_id=1, source_target_pairs={{0,4},{4,0},{8,12},{12,8},{16,20},{20,16},{24,28},{28,24},{1,5},{5... | collective-permute-start | bytes 786440 | tf_op jit(solution)/shard_map/ppermute | solution.py:895
  354.6 13.7 %collective-permute-start.53 = (bf16[128,1024]{1,0:T(8,128)(2,1)S(1)}, bf16[128,1024]{1,0:T(8,128)(2,1)}, u32[]{:S(2)}, u32[]{:S(2)}) collective-permute-start(bf16[128,1024]{1,0:T(8,128)(2,1)S(1)} %collective-permute-done.49.refs_2_), channel_id=1, source_target_pairs={{0,4},{4,0},{8,12},{12,8},{16,20},{20,16},{24,28},{28,24},{1,5},{5... | collective-permute-start | bytes 786440 | tf_op jit(solution)/shard_map/ppermute | solution.py:895
  356.2 14.9 %collective-permute-start.54 = (bf16[128,1024]{1,0:T(8,128)(2,1)}, bf16[128,1024]{1,0:T(8,128)(2,1)}, u32[]{:S(2)}, u32[]{:S(2)}) collective-permute-start(bf16[128,1024]{1,0:T(8,128)(2,1)} %collective-permute-done.50.refs_3_), channel_id=1, source_target_pairs={{0,4},{4,0},{8,12},{12,8},{16,20},{20,16},{24,28},{28,24},{1,5},{5... | collective-permute-start | bytes 786440 | tf_op jit(solution)/shard_map/ppermute | solution.py:895
  356.7 9.2 %collective-permute-start.40 = (bf16[64,1024]{1,0:T(8,128)(2,1)S(1)}, bf16[64,1024]{1,0:T(8,128)(2,1)}, u32[]{:S(2)}, u32[]{:S(2)}) collective-permute-start(bf16[64,1024]{1,0:T(8,128)(2,1)S(1)} %collective-permute-done.38.refs_1_), channel_id=1, source_target_pairs={{0,8},{4,12},{8,0},{12,4},{16,24},{20,28},{24,16},{28,20},{1,9},{5... | collective-permute-start | bytes 393224 | tf_op jit(solution)/shard_map/ppermute | solution.py:895
  373.7 10.6 %collective-permute-start.55 = (bf16[256,1024]{1,0:T(8,128)(2,1)}, bf16[256,1024]{1,0:T(8,128)(2,1)}, u32[]{:S(2)}, u32[]{:S(2)}) collective-permute-start(bf16[256,1024]{1,0:T(8,128)(2,1)} %shard_map.389.refs_0_), channel_id=1, source_target_pairs={{0,2},{1,3},{2,0},{3,1},{4,6},{5,7},{6,4},{7,5},{8,10},{9,11},{10,... | collective-permute-start | bytes 1572872 | tf_op jit(solution)/shard_map/ppermute | solution.py:895
  375.4 15.3 %collective-permute-start.56 = (bf16[256,1024]{1,0:T(8,128)(2,1)}, bf16[256,1024]{1,0:T(8,128)(2,1)}, u32[]{:S(2)}, u32[]{:S(2)}) collective-permute-start(bf16[256,1024]{1,0:T(8,128)(2,1)} %shard_map.389.refs_0_), channel_id=1, source_target_pairs={{0,4},{4,0},{8,12},{12,8},{16,20},{20,16},{24,28},{28,24},{1,5},{5... | collective-permute-start | bytes 1572872 | tf_op jit(solution)/shard_map/ppermute | solution.py:895
  384.3 12.6 %collective-permute-start.57 = (bf16[256,1024]{1,0:T(8,128)(2,1)}, bf16[256,1024]{1,0:T(8,128)(2,1)}, u32[]{:S(2)}, u32[]{:S(2)}) collective-permute-start(bf16[256,1024]{1,0:T(8,128)(2,1)} %collective-permute-done.55.refs_2_), channel_id=1, source_target_pairs={{0,4},{4,0},{8,12},{12,8},{16,20},{20,16},{24,28},{28,24},{1,5},{5... | collective-permute-start | bytes 1572872 | tf_op jit(solution)/shard_map/ppermute | solution.py:895
  386.9 7.1 %all-to-all-start.1 = ((bf16[4,2,768]{2,1,0:T(2,128)(2,1)}), bf16[4,2,768]{2,1,0:T(2,128)(2,1)S(1)}, u32[]{:S(2)}, u32[]{:S(2)}) async-start(bf16[4,2,768]{2,1,0:T(2,128)(2,1)} %reshape.191), calls=%async_computation.1 | async-start | bytes 24576 | tf_op jit(solution)/shard_map/all_to_all | solution.py:1434
  390.2 20.5 %collective-permute-start.58 = (bf16[256,1024]{1,0:T(8,128)(2,1)}, bf16[256,1024]{1,0:T(8,128)(2,1)}, u32[]{:S(2)}, u32[]{:S(2)}) collective-permute-start(bf16[256,1024]{1,0:T(8,128)(2,1)} %shard_map.389.refs_0_), channel_id=1, source_target_pairs={{0,1},{1,0},{2,3},{3,2},{4,5},{5,4},{6,7},{7,6},{8,9},{9,8},{10,11... | collective-permute-start | bytes 1572872 | tf_op jit(solution)/shard_map/ppermute | solution.py:895
  390.6 20.0 %collective-permute-start.60 = (bf16[256,1024]{1,0:T(8,128)(2,1)}, bf16[256,1024]{1,0:T(8,128)(2,1)}, u32[]{:S(2)}, u32[]{:S(2)}) collective-permute-start(bf16[256,1024]{1,0:T(8,128)(2,1)} %collective-permute-done.55.refs_2_), channel_id=1, source_target_pairs={{0,1},{1,0},{2,3},{3,2},{4,5},{5,4},{6,7},{7,6},{8,9},{9,8},{10,11... | collective-permute-start | bytes 1572872 | tf_op jit(solution)/shard_map/ppermute | solution.py:895
  390.8 19.9 %collective-permute-start.59 = (bf16[256,1024]{1,0:T(8,128)(2,1)}, bf16[256,1024]{1,0:T(8,128)(2,1)}, u32[]{:S(2)}, u32[]{:S(2)}) collective-permute-start(bf16[256,1024]{1,0:T(8,128)(2,1)} %collective-permute-done.56.refs_1_), channel_id=1, source_target_pairs={{0,1},{1,0},{2,3},{3,2},{4,5},{5,4},{6,7},{7,6},{8,9},{9,8},{10,11... | collective-permute-start | bytes 1572872 | tf_op jit(solution)/shard_map/ppermute | solution.py:895
  396.9 13.8 %collective-permute-start.61 = (bf16[256,1024]{1,0:T(8,128)(2,1)}, bf16[256,1024]{1,0:T(8,128)(2,1)}, u32[]{:S(2)}, u32[]{:S(2)}) collective-permute-start(bf16[256,1024]{1,0:T(8,128)(2,1)} %collective-permute-done.57.refs_3_), channel_id=1, source_target_pairs={{0,1},{1,0},{2,3},{3,2},{4,5},{5,4},{6,7},{7,6},{8,9},{9,8},{10,11... | collective-permute-start | bytes 1572872 | tf_op jit(solution)/shard_map/ppermute | solution.py:895
  398.5 11.5 %all-to-all-start.2 = ((bf16[4,4,1024]{2,1,0:T(4,128)(2,1)}), bf16[4,4,1024]{2,1,0:T(4,128)(2,1)S(1)}, u32[]{:S(2)}, u32[]{:S(2)}) async-start(bf16[4,4,1024]{2,1,0:T(4,128)(2,1)} %broadcast_in_dim.51), calls=%async_computation.2 | async-start | bytes 65536 | tf_op jit(solution)/shard_map/all_to_all | solution.py:1437
  (23 other events, 227.2 us)

commit v3 on v2

--- a/solution.py
+++ b/solution.py
@@ -1413,10 +1413,26 @@
     text_data = DataSum(text_sum.put(0, results[2]), bits, merged=True)
     steps = [(at, ffn_data) for at in range(1, len(bits) + 1)]
     for at in range(len(bits) + 1):
-        steps.append((at + 2.2 if at else 1.5, attn_data))
+        steps.append((at + 1.9 if at else 1.5, attn_data))
         steps.append((at + 2.25, text_data))
-    for at, member in sorted(steps, key=lambda step: step[0]):
-        token = member.step(token)
+    steps.sort(key=lambda step: step[0])
+    columns = mod_weight.shape[1]
+    grad_time = None
+    for at, member in steps:
+        if at > len(bits) and member is attn_data and grad_time is None:
+            (grad_mod,) = after([grad_mod], token)
+            grad_mod = grad_mod.reshape(1, group * columns)
+            grad_cols = lax.all_to_all(grad_mod, "heads", split_axis=1, concat_axis=0, tiled=True)
+            (grad_time,) = silu_back(inner_cols(grad_cols, mod_weight))
+            token = member.step(token, grad_time)
+        elif at == steps[-1][0]:
+            (grad_time,) = after([grad_time], token)
+            grad_time = jnp.broadcast_to(grad_time.astype(BF16), (group,) + grad_time.shape)
+            grad_time = lax.all_to_all(grad_time, "heads", split_axis=0, concat_axis=0)
+            grad_time = jnp.sum(grad_time.astype(F32), axis=0)
+            token = member.step(token, grad_time)
+        else:
+            token = member.step(token)
 
     weight_up, weight_down = unpack(ffn_unpack, ffn_data, ff_in, ff_out, attn_data.pieces[0])
     text_half = text_data.half(weight_up, *list(attn_data.pieces.values())[1:])
@@ -1425,18 +1441,10 @@
     for slot in range(2, group, 2):
         bit = low_bit(slot)
         text_halves[slot] = [swap(text_halves[slot - bit][0], "heads", bit)]
+        text_halves[slot] = list(after(text_halves[slot], weight_qkv))
     for slot in range(0, group, 2):
         text_halves[slot].append(swap(text_halves[slot][0], "dp", 1))
         text_halves[slot + 1] = [swap(piece, "heads", 1) for piece in text_halves[slot]]
-    (grad_mod,) = after([grad_mod], text_halves[2][0])
-    columns = mod_weight.shape[1]
-    grad_mod = grad_mod.reshape(1, group * columns)
-    grad_mod_cols = lax.all_to_all(grad_mod, "heads", split_axis=1, concat_axis=0, tiled=True)
-    (grad_time,) = silu_back(inner_cols(grad_mod_cols, mod_weight))
-    grad_time = jnp.broadcast_to(grad_time.astype(BF16), (group,) + grad_time.shape)
-    grad_time = lax.all_to_all(grad_time, "heads", split_axis=0, concat_axis=0)
-    grad_time = jnp.sum(grad_time.astype(F32), axis=0)
-
     slot_rows = stack_rows // group
     text_pieces, text_starts = [], []
     for slot, pieces in text_halves.items():

time: 431 us -> 425 us (0.986)
  waiting for transfers between devices: 121 us -> 116 us
  transfers between devices with their start and end apart: 65 -> 65, of which waited for: 22 -> 24; matrix products, arithmetic and copies ran while one was open for 7% -> 7% of each run, Pallas kernels for 37% -> 38%
where the time goes in v3:
time: 425 us; the launch traced here: 417 us
  Pallas kernels  191 us (45%)
  waiting for transfers between devices  116 us (27%)
  starting transfers between devices  64.5 us (15%)
  local copies, waits for them, and re-layouts  24.6 us (6%)
  other arithmetic  10.7 us (3%)
  matrix products  5.13 us (1%)
    pallas_call x26, Pallas kernels, run_kernel(): pl.pallas_call(kernel, grid=(parts,), in_specs=[spec for spec, _ in input...  191 us
    ppermute x62, waiting for transfers between devices, swap(): lax.ppermute(array, axis, [(at, at ^ bit) for at in range(lax.axis_size(a...  116 us
    ppermute x62, starting transfers between devices, swap(): lax.ppermute(array, axis, [(at, at ^ bit) for at in range(lax.axis_size(a...  53.9 us
  transfers between devices with their start and end apart: 65, of which 24 were waited for; matrix products, arithmetic and copies ran while one was open for 7% of the time, Pallas kernels for 38%

profile of v3, /device:TPU:0, one launch (start us, length us, event | category | flops | bytes accessed | tf_op | source)
XLA Modules:
  0.0 416.8 jit_solution(12358973918329976313)
XLA Ops:
  0.7 2.2 constant_dynamic-slice_fusion.4
  2.9 3.0 collective-permute-start
  13.0 1.8 pad_maximum_fusion.mel_ref.refs_3_
  14.8 9.7 %shard_map.366 = (bf16[512,512]{1,0:T(8,128)(2,1)}, f32[512,1024]{1,0:T(8,128)}, f32[8,1024]{1,0:T(8,128)}, bf16[512,1024]{1,0:T(8,128)(2,1)}, bf16[512,512]{1,0:T(8,128)(2,1)}, /*index=5*/f32[512,1024]{1,0:T(8,128)}) custom-call(bf16[512,512]{1,0:T(8,128)(2,1)} %refs_2_.1, bf16[512,200]{1,0:T(8,128)(2,1)} %pad_maximum_fusion.mel_ref.refs_3_, ...), custom_call_target="tpu_custom_call" | custom-call | flops 1024 | bytes 1024 | tf_op jit(solution)/shard_map/pallas_call | solution.py:877
  26.9 3.5 all-to-all-start
  31.1 1.9 constant_dynamic-slice_fusion.2
  33.0 1.9 constant_dynamic-slice_fusion.1
  34.9 1.8 fusion.1
  37.3 2.0 collective-permute-start.2
  41.3 1.9 collective-permute-start.11
  43.3 14.3 %shard_map.367 = (bf16[2,512,256]{2,1,0:T(8,128)(2,1)}, bf16[2,512,256]{2,1,0:T(8,128)(2,1)}, bf16[2,512,256]{2,1,0:T(8,128)(2,1)}, bf16[2,512,256]{2,1,0:T(8,12...) custom-call(s32[1]{0:T(128)} %dynamic_slice.22.refs_0_, s32[1]{0:T(128)} %bitcast.refs_1_.refs_0_, ...), custom_call_target="tpu_custom_call" | custom-call | flops 1024 | bytes 1024 | tf_op jit(solution)/shard_map/pallas_call | solution.py:877
  57.8 1.8 collective-permute-start.7
  59.8 6.7 %collective-permute-done.7.refs_13_.refs_19_ = bf16[128,1024]{1,0:T(8,128)(2,1)S(1)} collective-permute-done((bf16[128,1024]{1,0:T(8,128)(2,1)S(1)}, bf16[128,1024]{1,0:T(8,128)(2,1)S(1)}, u32[]{:S(2)}, u32[]{:S(2)}) %collective-permute-start.7) | collective-permute-done | bytes 262176 | tf_op jit(solution)/shard_map/ppermute | solution.py:895
  67.1 2.1 collective-permute-done.8.refs_14_.refs_16_
  69.2 1.7 collective-permute-start.16
  72.3 17.8 %shard_map.368 = (bf16[2,512,256]{2,1,0:T(8,128)(2,1)}, bf16[2,512,256]{2,1,0:T(8,128)(2,1)}, bf16[2,512,256]{2,1,0:T(8,128)(2,1)}, bf16[2,512,256]{2,1,0:T(8,12...) custom-call(s32[1]{0:T(128)} %dynamic_slice.22.refs_0_, ...), custom_call_target="tpu_custom_call" | custom-call | flops 1024 | bytes 1024 | tf_op jit(solution)/shard_map/pallas_call | solution.py:877
  90.7 4.0 collective-permute-done.12.refs_11_
  97.7 25.5 %shard_map.369 = (f32[4,1,512]{2,1,0:T(1,128)}, f32[8,1024]{1,0:T(8,128)}, bf16[1024,1024]{1,0:T(8,128)(2,1)}, bf16[1024,1024]{1,0:T(8,128)(2,1)}, bf16[1024,102...) custom-call(s32[1]{0:T(128)} %bitcast.refs_1_.refs_0_, ...), custom_call_target="tpu_custom_call" | custom-call | flops 1024 | bytes 1024 | tf_op jit(solution)/shard_map/pallas_call | solution.py:877
  123.4 20.1 %shard_map.370 = (f32[2,3,256]{2,1,0:T(4,128)}, bf16[1024,1024]{1,0:T(8,128)(2,1)}, bf16[1024,1024]{1,0:T(8,128)(2,1)}, f32[512,1024]{1,0:T(8,128)}) custom-call(s32[1]{0:T(128)} %dynamic_slice.22.refs_0_, s32[1]{0:T(128)} %bitcast.refs_1_.refs_0_, bf16[512,1024]{1,0:T(8,128)(2,1)} %get-tuple-element.196.refs_2_, ...), custom_call_target="tpu_custom_call" | custom-call | flops 1024 | bytes 1024 | tf_op jit(solution)/shard_map/pallas_call | solution.py:877
  144.1 4.3 %shard_map.371 = bf16[1024,1024]{1,0:T(8,128)(2,1)} custom-call(bf16[1024,1024]{1,0:T(8,128)(2,1)} %get-tuple-element.210.refs_0_, bf16[1024,1024]{1,0:T(8,128)(2,1)} %collective-permute-done.20.refs_1_), custom_call_target="tpu_custom_call" | custom-call | flops 1024 | bytes 1024 | tf_op jit(solution)/shard_map/pallas_call | solution.py:877
  148.4 1.9 collective-permute-start.23
  150.3 23.2 %shard_map.372 = (f32[2,3,256]{2,1,0:T(4,128)}, bf16[1024,1024]{1,0:T(8,128)(2,1)}, bf16[1024,1024]{1,0:T(8,128)(2,1)}, bf16[512,1024]{1,0:T(8,128)(2,1)}, f32[8,1024]{1,0:T(8,128)}) custom-call(s32[1]{0:T(128)} %dynamic_slice.22.refs_0_, s32[1]{0:T(128)} %bitcast.refs_1_.refs_0_, bf16[512,1024]{1,0:T(8,128)(2,1)} %get-tuple-element.196.refs_2_, ...), custom_call_target="tpu_custom_call" | custom-call | flops 1024 | bytes 1024 | tf_op jit(solution)/shard_map/pallas_call | solution.py:877
  173.5 4.3 %shard_map.373 = bf16[1024,1024]{1,0:T(8,128)(2,1)} custom-call(bf16[1024,1024]{1,0:T(8,128)(2,1)} %get-tuple-element.217.refs_0_, bf16[1024,1024]{1,0:T(8,128)(2,1)} %collective-permute-done.21.refs_1_), custom_call_target="tpu_custom_call" | custom-call | flops 1024 | bytes 1024 | tf_op jit(solution)/shard_map/pallas_call | solution.py:877
  179.2 21.4 %shard_map.374 = (f32[512,512]{1,0:T(8,128)}, bf16[6,1024]{1,0:T(8,128)(2,1)}, bf16[512,1024]{1,0:T(8,128)(2,1)}, bf16[512,1024]{1,0:T(8,128)(2,1)}, bf16[512,10...) custom-call(s32[2]{0:T(128)} %pad_add_fusion.refs_0_.own_ref, bf16[512,1024]{1,0:T(8,128)(2,1)} %get-tuple-element.219.refs_1_, ...), custom_call_target="tpu_custom_call" | custom-call | flops 1024 | bytes 1024 | tf_op jit(solution)/shard_map/pallas_call | solution.py:877
  201.2 4.2 %shard_map.375 = (bf16[512,1024]{1,0:T(8,128)(2,1)}, bf16[512,1024]{1,0:T(8,128)(2,1)}) custom-call(s32[1]{0:T(128)} %bitcast.refs_1_.refs_0_, bf16[1024,1024]{1,0:T(8,128)(2,1)} %get-tuple-element.237.refs_1_.refs_4_, bf16[1024,1024]{1,0:T(8,128)(2,1)} %collective-permute-done.23.refs_2_.refs_5_, ...), custom_call_target="tpu_custom_call" | custom-call | flops 1024 | bytes 1024 | tf_op jit(solution)/shard_map/pallas_call | solution.py:877
  205.4 1.7 collective-permute-start.27
  207.1 2.6 shard_map.376
  209.8 1.7 collective-permute-start.25
  211.5 19.3 %collective-permute-done.27.refs_2_.refs_4_ = bf16[512,1024]{1,0:T(8,128)(2,1)} collective-permute-done((bf16[512,1024]{1,0:T(8,128)(2,1)}, bf16[512,1024]{1,0:T(8,128)(2,1)}, u32[]{:S(2)}, u32[]{:S(2)}) %collective-permute-start.27) | collective-permute-done | bytes 1048608 | tf_op jit(solution)/shard_map/ppermute | solution.py:895
  230.8 2.8 shard_map.377
  233.6 8.5 %collective-permute-done.29.refs_2_.refs_5_ = bf16[1024,1024]{1,0:T(8,128)(2,1)} collective-permute-done((bf16[1024,1024]{1,0:T(8,128)(2,1)}, bf16[1024,1024]{1,0:T(8,128)(2,1)}, u32[]{:S(2)}, u32[]{:S(2)}) %collective-permute-start.29) | collective-permute-done | bytes 2097184 | tf_op jit(solution)/shard_map/ppermute | solution.py:895
  242.1 4.2 %shard_map.378 = (bf16[512,1024]{1,0:T(8,128)(2,1)}, bf16[512,1024]{1,0:T(8,128)(2,1)}) custom-call(s32[1]{0:T(128)} %bitcast.refs_1_.refs_0_, bf16[1024,1024]{1,0:T(8,128)(2,1)} %get-tuple-element.251.refs_1_.refs_4_, bf16[1024,1024]{1,0:T(8,128)(2,1)} %collective-permute-done.29.refs_2_.refs_5_, ...), custom_call_target="tpu_custom_call" | custom-call | flops 1024 | bytes 1024 | tf_op jit(solution)/shard_map/pallas_call | solution.py:877
  246.3 1.8 collective-permute-start.33
  249.7 11.3 %collective-permute-done.28.refs_2_.refs_4_ = bf16[256,1024]{1,0:T(8,128)(2,1)} collective-permute-done((bf16[256,1024]{1,0:T(8,128)(2,1)}, bf16[256,1024]{1,0:T(8,128)(2,1)}, u32[]{:S(2)}, u32[]{:S(2)}) %collective-permute-start.28) | collective-permute-done | bytes 524320 | tf_op jit(solution)/shard_map/ppermute | solution.py:895
  260.9 2.1 shard_map.379
  264.2 3.2 shard_map.380
  269.0 2.6 collective-permute-start.32
  271.9 2.8 shard_map.381
  276.2 7.1 %collective-permute-done.32.refs_1_ = bf16[128,1024]{1,0:T(8,128)(2,1)S(1)} collective-permute-done((bf16[128,1024]{1,0:T(8,128)(2,1)}, bf16[128,1024]{1,0:T(8,128)(2,1)S(1)}, u32[]{:S(2)}, u32[]{:S(2)}) %collective-permute-start.32) | collective-permute-done | bytes 262176 | tf_op jit(solution)/shard_map/ppermute | solution.py:895
  284.0 1.8 shard_map.382.refs_0_
  286.6 2.1 shard_map.383
  290.1 3.3 all-to-all-start.1
  293.4 4.0 collective-permute-start.36
  298.4 2.1 shard_map.384
  300.6 3.6 collective-permute-start.42
  304.8 4.4 %collective-permute-done.41.refs_1_ = bf16[128,1024]{1,0:T(8,128)(2,1)} collective-permute-done((bf16[128,1024]{1,0:T(8,128)(2,1)S(1)}, bf16[128,1024]{1,0:T(8,128)(2,1)}, u32[]{:S(2)}, u32[]{:S(2)}) %collective-permute-start.41) | collective-permute-done | bytes 262176 | tf_op jit(solution)/shard_map/ppermute | solution.py:895
  310.3 1.9 shard_map.385
  312.1 7.8 %collective-permute-done.35.refs_1_ = bf16[128,1024]{1,0:T(8,128)(2,1)S(1)} collective-permute-done((bf16[128,1024]{1,0:T(8,128)(2,1)}, bf16[128,1024]{1,0:T(8,128)(2,1)S(1)}, u32[]{:S(2)}, u32[]{:S(2)}) %collective-permute-start.35) | collective-permute-done | bytes 262176 | tf_op jit(solution)/shard_map/ppermute | solution.py:895
  320.7 1.8 shard_map.386.refs_0_
  323.7 2.9 collective-permute-start.37
  327.3 3.9 all-to-all-start.2
  333.3 9.3 %collective-permute-done.37.refs_1_ = bf16[64,1024]{1,0:T(8,128)(2,1)S(1)} collective-permute-done((bf16[64,1024]{1,0:T(8,128)(2,1)}, bf16[64,1024]{1,0:T(8,128)(2,1)S(1)}, u32[]{:S(2)}, u32[]{:S(2)}) %collective-permute-start.37) | collective-permute-done | bytes 131104 | tf_op jit(solution)/shard_map/ppermute | solution.py:895
  342.6 2.0 collective-permute-start.50
  348.3 1.7 collective-permute-start.39
  350.0 8.1 %collective-permute-done.38.refs_1_ = bf16[64,1024]{1,0:T(8,128)(2,1)S(1)} collective-permute-done((bf16[64,1024]{1,0:T(8,128)(2,1)}, bf16[64,1024]{1,0:T(8,128)(2,1)S(1)}, u32[]{:S(2)}, u32[]{:S(2)}) %collective-permute-start.38) | collective-permute-done | bytes 131104 | tf_op jit(solution)/shard_map/ppermute | solution.py:895
  363.9 4.4 %shard_map.388 = (f32[1024,512]{1,0:T(8,128)}, f32[512,1024]{1,0:T(8,128)}) custom-call(s32[8]{0:T(128)} %stack.112.starts_ref, bf16[128,1024]{1,0:T(8,128)(2,1)} %shard_map.382.refs_0_, bf16[128,1024]{1,0:T(8,128)(2,1)} %collective-permute-done.41.refs_1_, bf16[128,1024]{1,0:T(8,128)(2,1)} %copy-done.8, bf16[128,1024]{1,0:T(8,128)(2,1)} %collective-permute-done.43.refs_3_, ...), custom_call_target="tpu_custom_call" | custom-call | flops 1024 | bytes 1024 | tf_op jit(solution)/shard_map/pallas_call | solution.py:877
  368.3 4.1 collective-permute-done.53.refs_6_
  372.4 2.8 collective-permute-done.54.refs_7_
  375.2 2.6 shard_map.389.refs_0_
  379.0 4.4 %shard_map.390 = (f32[3,1024,256]{2,1,0:T(8,128)}, f32[256,1024]{1,0:T(8,128)}) custom-call(s32[8]{0:T(128)} %stack.112.starts_ref, bf16[128,1024]{1,0:T(8,128)(2,1)} %shard_map.386.refs_0_, bf16[128,1024]{1,0:T(8,128)(2,1)} %collective-permute-done.48.refs_1_, bf16[128,1024]{1,0:T(8,128)(2,1)} %copy-done.9, ...), custom_call_target="tpu_custom_call" | custom-call | flops 1024 | bytes 1024 | tf_op jit(solution)/shard_map/pallas_call | solution.py:877
  383.4 5.0 %collective-permute-done.56.refs_2_ = bf16[256,1024]{1,0:T(8,128)(2,1)} collective-permute-done((bf16[256,1024]{1,0:T(8,128)(2,1)}, bf16[256,1024]{1,0:T(8,128)(2,1)}, u32[]{:S(2)}, u32[]{:S(2)}) %collective-permute-start.56) | collective-permute-done | bytes 524320 | tf_op jit(solution)/shard_map/ppermute | solution.py:895
  390.1 9.6 %collective-permute-done.57.refs_3_ = bf16[256,1024]{1,0:T(8,128)(2,1)} collective-permute-done((bf16[256,1024]{1,0:T(8,128)(2,1)}, bf16[256,1024]{1,0:T(8,128)(2,1)}, u32[]{:S(2)}, u32[]{:S(2)}) %collective-permute-start.57) | collective-permute-done | bytes 524320 | tf_op jit(solution)/shard_map/ppermute | solution.py:895
  403.6 6.2 %shard_map.391 = (f32[712,1024]{1,0:T(8,128)}, f32[512,1024]{1,0:T(8,128)}, f32[1024,512]{1,0:T(8,128)}, f32[7,512]{1,0:T(8,128)}, f32[3,512]{1,0:T(4,128)}, /*i...) custom-call(s32[8]{0:T(128)} %stack.98.starts_ref, ...), custom_call_target="tpu_custom_call" | custom-call | flops 1024 | bytes 1024 | tf_op jit(solution)/shard_map/pallas_call | solution.py:877
  412.9 3.7 fusion.2
  (191 shorter events, 54.5 us)
Async XLA Ops:
  2.9 34.4 %collective-permute-start = (bf16[3,512,256]{2,1,0:T(8,128)(2,1)}, bf16[3,512,256]{2,1,0:T(8,128)(2,1)}, u32[]{:S(2)}, u32[]{:S(2)}) collective-permute-start(bf16[3,512,256]{2,1,0:T(8,128)(2,1)} %constant_dynamic-slice_fusion.4), channel_id=1, source_target_pairs={{0,2},{1,3},{2,0},{3,1},{4,6},{5,7},{6,4},{7,5},{8,10},{9,11},{10,... | collective-permute-start | bytes 2359304 | tf_op jit(solution)/shard_map/ppermute | solution.py:895
  7.6 35.6 %collective-permute-start.1 = (bf16[128,1024]{1,0:T(8,128)(2,1)}, bf16[128,1024]{1,0:T(8,128)(2,1)S(1)}, u32[]{:S(2)}, u32[]{:S(2)}) collective-permute-start(bf16[128,1024]{1,0:T(8,128)(2,1)} %constant_dynamic-slice_fusion.3), channel_id=1, source_target_pairs={{0,2},{1,3},{2,0},{3,1},{4,6},{5,7},{6,4},{7,5},{8,10},{9,11},{10,... | collective-permute-start | bytes 786440 | tf_op jit(solution)/shard_map/ppermute | solution.py:895
  26.9 10.4 %all-to-all-start = ((bf16[4,2,1408]{2,1,0:T(2,128)(2,1)}), bf16[4,2,1408]{2,1,0:T(2,128)(2,1)S(1)}, u32[]{:S(2)}, u32[]{:S(2)}) async-start(bf16[4,2,1408]{2,1,0:T(2,128)(2,1)} %reshape.189), calls=%async_computation | async-start | bytes 45056 | tf_op jit(solution)/shard_map/all_to_all | solution.py:1175
  30.4 12.9 %collective-permute-start.3 = (bf16[3,1024,256]{2,1,0:T(8,128)(2,1)}, bf16[3,1024,256]{2,1,0:T(8,128)(2,1)}, u32[]{:S(2)}, u32[]{:S(2)}) collective-permute-start(bf16[3,1024,256]{2,1,0:T(8,128)(2,1)} %refs_13_.4), channel_id=1, source_target_pairs={{0,1},{1,0},{2,3},{3,2},{4,5},{5,4},{6,7},{7,6},{8,9},{9,8},{10,11... | collective-permute-start | bytes 4718600 | tf_op jit(solution)/shard_map/ppermute | solution.py:895
  31.0 12.3 %collective-permute-start.4 = (bf16[256,1024]{1,0:T(8,128)(2,1)}, bf16[256,1024]{1,0:T(8,128)(2,1)}, u32[]{:S(2)}, u32[]{:S(2)}) collective-permute-start(bf16[256,1024]{1,0:T(8,128)(2,1)} %refs_15_.2), channel_id=1, source_target_pairs={{0,1},{1,0},{2,3},{3,2},{4,5},{5,4},{6,7},{7,6},{8,9},{9,8},{10,11... | collective-permute-start | bytes 1572872 | tf_op jit(solution)/shard_map/ppermute | solution.py:895
  37.3 20.4 %collective-permute-start.2 = (bf16[3,512,256]{2,1,0:T(8,128)(2,1)}, bf16[3,512,256]{2,1,0:T(8,128)(2,1)}, u32[]{:S(2)}, u32[]{:S(2)}) collective-permute-start(bf16[3,512,256]{2,1,0:T(8,128)(2,1)} %collective-permute-done.refs_8_.refs_14_), channel_id=1, source_target_pairs={{0,4},{4,0},{8,12},{12,8},{16,20},{20,16},{24,28},{28,24},{1,5},{5... | collective-permute-start | bytes 2359304 | tf_op jit(solution)/shard_map/ppermute | solution.py:895
  41.3 25.3 %collective-permute-start.11 = (bf16[256,1024]{1,0:T(8,128)(2,1)}, bf16[256,1024]{1,0:T(8,128)(2,1)}, u32[]{:S(2)}, u32[]{:S(2)}) collective-permute-start(bf16[256,1024]{1,0:T(8,128)(2,1)} %constant_dynamic-slice_fusion.1), channel_id=1, source_target_pairs={{0,2},{1,3},{2,0},{3,1},{4,6},{5,7},{6,4},{7,5},{8,10},{9,11},{10,... | collective-permute-start | bytes 1572872 | tf_op jit(solution)/shard_map/ppermute | solution.py:895
  43.2 23.8 %collective-permute-start.10 = (bf16[512,512]{1,0:T(8,128)(2,1)}, bf16[512,512]{1,0:T(8,128)(2,1)}, u32[]{:S(2)}, u32[]{:S(2)}) collective-permute-start(bf16[512,512]{1,0:T(8,128)(2,1)} %constant_dynamic-slice_fusion.2), channel_id=1, source_target_pairs={{0,2},{1,3},{2,0},{3,1},{4,6},{5,7},{6,4},{7,5},{8,10},{9,11},{10,... | collective-permute-start | bytes 1572872 | tf_op jit(solution)/shard_map/ppermute | solution.py:895
  57.8 13.9 %collective-permute-start.5 = (bf16[3,512,256]{2,1,0:T(8,128)(2,1)}, bf16[3,512,256]{2,1,0:T(8,128)(2,1)}, u32[]{:S(2)}, u32[]{:S(2)}) collective-permute-start(bf16[3,512,256]{2,1,0:T(8,128)(2,1)} %collective-permute-done.refs_8_.refs_14_), channel_id=1, source_target_pairs={{0,1},{1,0},{2,3},{3,2},{4,5},{5,4},{6,7},{7,6},{8,9},{9,8},{10,11... | collective-permute-start | bytes 2359304 | tf_op jit(solution)/shard_map/ppermute | solution.py:895
  57.8 8.7 %collective-permute-start.7 = (bf16[128,1024]{1,0:T(8,128)(2,1)S(1)}, bf16[128,1024]{1,0:T(8,128)(2,1)S(1)}, u32[]{:S(2)}, u32[]{:S(2)}) collective-permute-start(bf16[128,1024]{1,0:T(8,128)(2,1)S(1)} %collective-permute-done.1.refs_12_.refs_18_), channel_id=1, source_target_pairs={{0,4},{4,0},{8,12},{12,8},{16,20},{20,16},{24,28},{28,24},{1,5},{5... | collective-permute-start | bytes 786440 | tf_op jit(solution)/shard_map/ppermute | solution.py:895
  59.5 35.2 %collective-permute-start.15 = (bf16[1024,512]{1,0:T(8,128)(2,1)}, bf16[1024,512]{1,0:T(8,128)(2,1)}, u32[]{:S(2)}, u32[]{:S(2)}) collective-permute-start(bf16[1024,512]{1,0:T(8,128)(2,1)} %refs_13_.3), channel_id=1, source_target_pairs={{0,1},{1,0},{2,3},{3,2},{4,5},{5,4},{6,7},{7,6},{8,9},{9,8},{10,11... | collective-permute-start | bytes 3145736 | tf_op jit(solution)/shard_map/ppermute | solution.py:895
  66.5 5.8 %collective-permute-start.6 = (bf16[3,512,256]{2,1,0:T(8,128)(2,1)}, bf16[3,512,256]{2,1,0:T(8,128)(2,1)}, u32[]{:S(2)}, u32[]{:S(2)}) collective-permute-start(bf16[3,512,256]{2,1,0:T(8,128)(2,1)} %collective-permute-done.2.refs_9_.refs_15_), channel_id=1, source_target_pairs={{0,1},{1,0},{2,3},{3,2},{4,5},{5,4},{6,7},{7,6},{8,9},{9,8},{10,11... | collective-permute-start | bytes 2359304 | tf_op jit(solution)/shard_map/ppermute | solution.py:895
  66.5 2.6 collective-permute-start.8
  67.0 3.9 collective-permute-start.9
  69.2 20.9 %collective-permute-start.16 = (bf16[256,1024]{1,0:T(8,128)(2,1)}, bf16[256,1024]{1,0:T(8,128)(2,1)}, u32[]{:S(2)}, u32[]{:S(2)}) collective-permute-start(bf16[256,1024]{1,0:T(8,128)(2,1)} %collective-permute-done.11.refs_16_), channel_id=1, source_target_pairs={{0,4},{4,0},{8,12},{12,8},{16,20},{20,16},{24,28},{28,24},{1,5},{5... | collective-permute-start | bytes 1572872 | tf_op jit(solution)/shard_map/ppermute | solution.py:895
  70.9 23.8 %collective-permute-start.12 = (bf16[512,512]{1,0:T(8,128)(2,1)}, bf16[512,512]{1,0:T(8,128)(2,1)}, u32[]{:S(2)}, u32[]{:S(2)}) collective-permute-start(bf16[512,512]{1,0:T(8,128)(2,1)} %collective-permute-done.10.refs_10_), channel_id=1, source_target_pairs={{0,4},{4,0},{8,12},{12,8},{16,20},{20,16},{24,28},{28,24},{1,5},{5... | collective-permute-start | bytes 1572872 | tf_op jit(solution)/shard_map/ppermute | solution.py:895
  71.7 24.2 %collective-permute-start.19 = (bf16[512,1024]{1,0:T(8,128)(2,1)}, bf16[512,1024]{1,0:T(8,128)(2,1)}, u32[]{:S(2)}, u32[]{:S(2)}) collective-permute-start(bf16[512,1024]{1,0:T(8,128)(2,1)} %refs_19_.1), channel_id=1, source_target_pairs={{0,1},{1,0},{2,3},{3,2},{4,5},{5,4},{6,7},{7,6},{8,9},{9,8},{10,11... | collective-permute-start | bytes 3145736 | tf_op jit(solution)/shard_map/ppermute | solution.py:895
  90.1 5.7 %collective-permute-start.17 = (bf16[256,1024]{1,0:T(8,128)(2,1)}, bf16[256,1024]{1,0:T(8,128)(2,1)S(1)}, u32[]{:S(2)}, u32[]{:S(2)}) collective-permute-start(bf16[256,1024]{1,0:T(8,128)(2,1)} %collective-permute-done.11.refs_16_), channel_id=1, source_target_pairs={{0,1},{1,0},{2,3},{3,2},{4,5},{5,4},{6,7},{7,6},{8,9},{9,8},{10,11... | collective-permute-start | bytes 1572872 | tf_op jit(solution)/shard_map/ppermute | solution.py:895
  90.7 5.2 %collective-permute-start.18 = (bf16[256,1024]{1,0:T(8,128)(2,1)}, bf16[256,1024]{1,0:T(8,128)(2,1)}, u32[]{:S(2)}, u32[]{:S(2)}) collective-permute-start(bf16[256,1024]{1,0:T(8,128)(2,1)} %collective-permute-done.16.refs_17_), channel_id=1, source_target_pairs={{0,1},{1,0},{2,3},{3,2},{4,5},{5,4},{6,7},{7,6},{8,9},{9,8},{10,11... | collective-permute-start | bytes 1572872 | tf_op jit(solution)/shard_map/ppermute | solution.py:895
  94.7 3.0 collective-permute-start.14
  123.2 20.9 %collective-permute-start.20 = (bf16[1024,1024]{1,0:T(8,128)(2,1)}, bf16[1024,1024]{1,0:T(8,128)(2,1)}, u32[]{:S(2)}, u32[]{:S(2)}) collective-permute-start(bf16[1024,1024]{1,0:T(8,128)(2,1)} %get-tuple-element.209), channel_id=1, source_target_pairs={{0,1},{1,0},{2,3},{3,2},{4,5},{5,4},{6,7},{7,6},{8,9},{9,8},{10,11... | collective-permute-start | bytes 6291464 | tf_op jit(solution)/shard_map/ppermute | solution.py:895
  143.5 30.0 %collective-permute-start.21 = (bf16[1024,1024]{1,0:T(8,128)(2,1)}, bf16[1024,1024]{1,0:T(8,128)(2,1)}, u32[]{:S(2)}, u32[]{:S(2)}) collective-permute-start(bf16[1024,1024]{1,0:T(8,128)(2,1)} %get-tuple-element.216), channel_id=1, source_target_pairs={{0,1},{1,0},{2,3},{3,2},{4,5},{5,4},{6,7},{7,6},{8,9},{9,8},{10,11... | collective-permute-start | bytes 6291464 | tf_op jit(solution)/shard_map/ppermute | solution.py:895
  143.9 57.3 %collective-permute-start.24 = (bf16[1024,1024]{1,0:T(8,128)(2,1)}, bf16[1024,1024]{1,0:T(8,128)(2,1)}, u32[]{:S(2)}, u32[]{:S(2)}) collective-permute-start(bf16[1024,1024]{1,0:T(8,128)(2,1)} %get-tuple-element.236), channel_id=1, source_target_pairs={{0,1},{1,0},{2,3},{3,2},{4,5},{5,4},{6,7},{7,6},{8,9},{9,8},{10,11... | collective-permute-start | bytes 6291464 | tf_op jit(solution)/shard_map/ppermute | solution.py:895
  148.4 52.8 %collective-permute-start.23 = (bf16[1024,1024]{1,0:T(8,128)(2,1)}, bf16[1024,1024]{1,0:T(8,128)(2,1)}, u32[]{:S(2)}, u32[]{:S(2)}) collective-permute-start(bf16[1024,1024]{1,0:T(8,128)(2,1)} %shard_map.371), channel_id=1, source_target_pairs={{0,2},{1,3},{2,0},{3,1},{4,6},{5,7},{6,4},{7,5},{8,10},{9,11},{10,... | collective-permute-start | bytes 6291464 | tf_op jit(solution)/shard_map/ppermute | solution.py:895
  177.8 64.3 %collective-permute-start.29 = (bf16[1024,1024]{1,0:T(8,128)(2,1)}, bf16[1024,1024]{1,0:T(8,128)(2,1)}, u32[]{:S(2)}, u32[]{:S(2)}) collective-permute-start(bf16[1024,1024]{1,0:T(8,128)(2,1)} %shard_map.373), channel_id=1, source_target_pairs={{0,2},{1,3},{2,0},{3,1},{4,6},{5,7},{6,4},{7,5},{8,10},{9,11},{10,... | collective-permute-start | bytes 6291464 | tf_op jit(solution)/shard_map/ppermute | solution.py:895
  178.0 64.1 %collective-permute-start.30 = (bf16[1024,1024]{1,0:T(8,128)(2,1)}, bf16[1024,1024]{1,0:T(8,128)(2,1)}, u32[]{:S(2)}, u32[]{:S(2)}) collective-permute-start(bf16[1024,1024]{1,0:T(8,128)(2,1)} %get-tuple-element.250), channel_id=1, source_target_pairs={{0,1},{1,0},{2,3},{3,2},{4,5},{5,4},{6,7},{7,6},{8,9},{9,8},{10,11... | collective-permute-start | bytes 6291464 | tf_op jit(solution)/shard_map/ppermute | solution.py:895
  200.6 6.5 %collective-permute-start.22 = (bf16[512,1024]{1,0:T(8,128)(2,1)}, bf16[512,1024]{1,0:T(8,128)(2,1)}, u32[]{:S(2)}, u32[]{:S(2)}) collective-permute-start(bf16[512,1024]{1,0:T(8,128)(2,1)} %get-tuple-element.234), channel_id=1, source_target_pairs={{0,1},{1,0},{2,3},{3,2},{4,5},{5,4},{6,7},{7,6},{8,9},{9,8},{10,11... | collective-permute-start | bytes 3145736 | tf_op jit(solution)/shard_map/ppermute | solution.py:895
  205.4 25.4 %collective-permute-start.27 = (bf16[512,1024]{1,0:T(8,128)(2,1)}, bf16[512,1024]{1,0:T(8,128)(2,1)}, u32[]{:S(2)}, u32[]{:S(2)}) collective-permute-start(bf16[512,1024]{1,0:T(8,128)(2,1)} %get-tuple-element.244), channel_id=1, source_target_pairs={{0,4},{4,0},{8,12},{12,8},{16,20},{20,16},{24,28},{28,24},{1,5},{5... | collective-permute-start | bytes 3145736 | tf_op jit(solution)/shard_map/ppermute | solution.py:895
  207.1 55.9 %collective-permute-start.26 = (bf16[512,1024]{1,0:T(8,128)(2,1)}, bf16[512,1024]{1,0:T(8,128)(2,1)}, u32[]{:S(2)}, u32[]{:S(2)}) collective-permute-start(bf16[512,1024]{1,0:T(8,128)(2,1)} %get-tuple-element.243), channel_id=1, source_target_pairs={{0,1},{1,0},{2,3},{3,2},{4,5},{5,4},{6,7},{7,6},{8,9},{9,8},{10,11... | collective-permute-start | bytes 3145736 | tf_op jit(solution)/shard_map/ppermute | solution.py:895
  209.8 54.4 %collective-permute-start.25 = (bf16[512,1024]{1,0:T(8,128)(2,1)}, bf16[512,1024]{1,0:T(8,128)(2,1)}, u32[]{:S(2)}, u32[]{:S(2)}) collective-permute-start(bf16[512,1024]{1,0:T(8,128)(2,1)} %shard_map.376), channel_id=1, source_target_pairs={{0,2},{1,3},{2,0},{3,1},{4,6},{5,7},{6,4},{7,5},{8,10},{9,11},{10,... | collective-permute-start | bytes 3145736 | tf_op jit(solution)/shard_map/ppermute | solution.py:895
  246.3 25.6 %collective-permute-start.33 = (bf16[512,1024]{1,0:T(8,128)(2,1)}, bf16[512,1024]{1,0:T(8,128)(2,1)}, u32[]{:S(2)}, u32[]{:S(2)}) collective-permute-start(bf16[512,1024]{1,0:T(8,128)(2,1)} %get-tuple-element.264), channel_id=1, source_target_pairs={{0,4},{4,0},{8,12},{12,8},{16,20},{20,16},{24,28},{28,24},{1,5},{5... | collective-permute-start | bytes 3145736 | tf_op jit(solution)/shard_map/ppermute | solution.py:895
  248.1 12.9 %collective-permute-start.28 = (bf16[256,1024]{1,0:T(8,128)(2,1)}, bf16[256,1024]{1,0:T(8,128)(2,1)}, u32[]{:S(2)}, u32[]{:S(2)}) collective-permute-start(bf16[256,1024]{1,0:T(8,128)(2,1)} %get-tuple-element.248), channel_id=1, source_target_pairs={{0,8},{4,12},{8,0},{12,4},{16,24},{20,28},{24,16},{28,20},{1,9},{5... | collective-permute-start | bytes 1572872 | tf_op jit(solution)/shard_map/ppermute | solution.py:895
  267.4 18.4 %collective-permute-start.31 = (bf16[256,1024]{1,0:T(8,128)(2,1)}, bf16[256,1024]{1,0:T(8,128)(2,1)S(1)}, u32[]{:S(2)}, u32[]{:S(2)}) collective-permute-start(bf16[256,1024]{1,0:T(8,128)(2,1)} %get-tuple-element.262), channel_id=1, source_target_pairs={{0,4},{4,0},{8,12},{12,8},{16,20},{20,16},{24,28},{28,24},{1,5},{5... | collective-permute-start | bytes 1572872 | tf_op jit(solution)/shard_map/ppermute | solution.py:895
  269.0 14.3 %collective-permute-start.32 = (bf16[128,1024]{1,0:T(8,128)(2,1)}, bf16[128,1024]{1,0:T(8,128)(2,1)S(1)}, u32[]{:S(2)}, u32[]{:S(2)}) collective-permute-start(bf16[128,1024]{1,0:T(8,128)(2,1)} %get-tuple-element.263), channel_id=1, source_target_pairs={{0,16},{4,20},{8,24},{12,28},{16,0},{20,4},{24,8},{28,12},{1,17},{... | collective-permute-start | bytes 786440 | tf_op jit(solution)/shard_map/ppermute | solution.py:895
  274.7 23.8 %collective-permute-start.34 = (bf16[256,1024]{1,0:T(8,128)(2,1)}, bf16[256,1024]{1,0:T(8,128)(2,1)}, u32[]{:S(2)}, u32[]{:S(2)}) collective-permute-start(bf16[256,1024]{1,0:T(8,128)(2,1)} %get-tuple-element.274), channel_id=1, source_target_pairs={{0,8},{4,12},{8,0},{12,4},{16,24},{20,28},{24,16},{28,20},{1,9},{5... | collective-permute-start | bytes 1572872 | tf_op jit(solution)/shard_map/ppermute | solution.py:895
  290.1 7.4 %all-to-all-start.1 = ((bf16[4,2,768]{2,1,0:T(2,128)(2,1)}), bf16[4,2,768]{2,1,0:T(2,128)(2,1)S(1)}, u32[]{:S(2)}, u32[]{:S(2)}) async-start(bf16[4,2,768]{2,1,0:T(2,128)(2,1)} %reshape.191), calls=%async_computation.1 | async-start | bytes 24576 | tf_op jit(solution)/shard_map/all_to_all | solution.py:1425
  293.3 15.9 %collective-permute-start.41 = (bf16[128,1024]{1,0:T(8,128)(2,1)S(1)}, bf16[128,1024]{1,0:T(8,128)(2,1)}, u32[]{:S(2)}, u32[]{:S(2)}) collective-permute-start(bf16[128,1024]{1,0:T(8,128)(2,1)S(1)} %copy-done.2), channel_id=1, source_target_pairs={{0,16},{4,20},{8,24},{12,28},{16,0},{20,4},{24,8},{28,12},{1,17},{... | collective-permute-start | bytes 786440 | tf_op jit(solution)/shard_map/ppermute | solution.py:895
  293.4 16.8 %collective-permute-start.36 = (bf16[128,1024]{1,0:T(8,128)(2,1)}, bf16[128,1024]{1,0:T(8,128)(2,1)}, u32[]{:S(2)}, u32[]{:S(2)}) collective-permute-start(bf16[128,1024]{1,0:T(8,128)(2,1)} %get-tuple-element.279), channel_id=1, source_target_pairs={{0,8},{4,12},{8,0},{12,4},{16,24},{20,28},{24,16},{28,20},{1,9},{5... | collective-permute-start | bytes 786440 | tf_op jit(solution)/shard_map/ppermute | solution.py:895
  300.5 19.4 %collective-permute-start.35 = (bf16[128,1024]{1,0:T(8,128)(2,1)}, bf16[128,1024]{1,0:T(8,128)(2,1)S(1)}, u32[]{:S(2)}, u32[]{:S(2)}) collective-permute-start(bf16[128,1024]{1,0:T(8,128)(2,1)} %get-tuple-element.278), channel_id=1, source_target_pairs={{0,16},{4,20},{8,24},{12,28},{16,0},{20,4},{24,8},{28,12},{1,17},{... | collective-permute-start | bytes 786440 | tf_op jit(solution)/shard_map/ppermute | solution.py:895
  300.6 22.4 %collective-permute-start.42 = (bf16[128,1024]{1,0:T(8,128)(2,1)S(1)}, bf16[128,1024]{1,0:T(8,128)(2,1)S(1)}, u32[]{:S(2)}, u32[]{:S(2)}) collective-permute-start(bf16[128,1024]{1,0:T(8,128)(2,1)S(1)} %copy-done.2), channel_id=1, source_target_pairs={{0,8},{4,12},{8,0},{12,4},{16,24},{20,28},{24,16},{28,20},{1,9},{5... | collective-permute-start | bytes 786440 | tf_op jit(solution)/shard_map/ppermute | solution.py:895
  304.3 26.9 %collective-permute-start.44 = (bf16[128,1024]{1,0:T(8,128)(2,1)S(1)}, bf16[128,1024]{1,0:T(8,128)(2,1)}, u32[]{:S(2)}, u32[]{:S(2)}) collective-permute-start(bf16[128,1024]{1,0:T(8,128)(2,1)S(1)} %copy-done.2), channel_id=1, source_target_pairs={{0,4},{4,0},{8,12},{12,8},{16,20},{20,16},{24,28},{28,24},{1,5},{5... | collective-permute-start | bytes 786440 | tf_op jit(solution)/shard_map/ppermute | solution.py:895
  309.3 23.5 %collective-permute-start.43 = (bf16[128,1024]{1,0:T(8,128)(2,1)}, bf16[128,1024]{1,0:T(8,128)(2,1)}, u32[]{:S(2)}, u32[]{:S(2)}) collective-permute-start(bf16[128,1024]{1,0:T(8,128)(2,1)} %collective-permute-done.41.refs_1_), channel_id=1, source_target_pairs={{0,8},{4,12},{8,0},{12,4},{16,24},{20,28},{24,16},{28,20},{1,9},{5... | collective-permute-start | bytes 786440 | tf_op jit(solution)/shard_map/ppermute | solution.py:895
  322.5 20.1 %collective-permute-start.48 = (bf16[128,1024]{1,0:T(8,128)(2,1)}, bf16[128,1024]{1,0:T(8,128)(2,1)}, u32[]{:S(2)}, u32[]{:S(2)}) collective-permute-start(bf16[128,1024]{1,0:T(8,128)(2,1)} %shard_map.386.refs_0_), channel_id=1, source_target_pairs={{0,16},{4,20},{8,24},{12,28},{16,0},{20,4},{24,8},{28,12},{1,17},{... | collective-permute-start | bytes 786440 | tf_op jit(solution)/shard_map/ppermute | solution.py:895
  322.5 25.2 %collective-permute-start.45 = (bf16[128,1024]{1,0:T(8,128)(2,1)}, bf16[128,1024]{1,0:T(8,128)(2,1)}, u32[]{:S(2)}, u32[]{:S(2)}) collective-permute-start(bf16[128,1024]{1,0:T(8,128)(2,1)} %collective-permute-done.41.refs_1_), channel_id=1, source_target_pairs={{0,4},{4,0},{8,12},{12,8},{16,20},{20,16},{24,28},{28,24},{1,5},{5... | collective-permute-start | bytes 786440 | tf_op jit(solution)/shard_map/ppermute | solution.py:895
  323.7 18.9 %collective-permute-start.37 = (bf16[64,1024]{1,0:T(8,128)(2,1)}, bf16[64,1024]{1,0:T(8,128)(2,1)S(1)}, u32[]{:S(2)}, u32[]{:S(2)}) collective-permute-start(bf16[64,1024]{1,0:T(8,128)(2,1)} %get-tuple-element.286), channel_id=1, source_target_pairs={{0,16},{4,20},{8,24},{12,28},{16,0},{20,4},{24,8},{28,12},{1,17},{... | collective-permute-start | bytes 393224 | tf_op jit(solution)/shard_map/ppermute | solution.py:895
  327.3 17.4 %all-to-all-start.2 = ((bf16[4,4,1024]{2,1,0:T(4,128)(2,1)}), bf16[4,4,1024]{2,1,0:T(4,128)(2,1)}, u32[]{:S(2)}, u32[]{:S(2)}) async-start(bf16[4,4,1024]{2,1,0:T(4,128)(2,1)} %broadcast_in_dim.51), calls=%async_computation.2 | async-start | bytes 65536 | tf_op jit(solution)/shard_map/all_to_all | solution.py:1431
  331.1 16.5 %collective-permute-start.46 = (bf16[128,1024]{1,0:T(8,128)(2,1)}, bf16[128,1024]{1,0:T(8,128)(2,1)}, u32[]{:S(2)}, u32[]{:S(2)}) collective-permute-start(bf16[128,1024]{1,0:T(8,128)(2,1)} %copy-done.8), channel_id=1, source_target_pairs={{0,4},{4,0},{8,12},{12,8},{16,20},{20,16},{24,28},{28,24},{1,5},{5... | collective-permute-start | bytes 786440 | tf_op jit(solution)/shard_map/ppermute | solution.py:895
  332.7 15.6 %collective-permute-start.47 = (bf16[128,1024]{1,0:T(8,128)(2,1)}, bf16[128,1024]{1,0:T(8,128)(2,1)}, u32[]{:S(2)}, u32[]{:S(2)}) collective-permute-start(bf16[128,1024]{1,0:T(8,128)(2,1)} %collective-permute-done.43.refs_3_), channel_id=1, source_target_pairs={{0,4},{4,0},{8,12},{12,8},{16,20},{20,16},{24,28},{28,24},{1,5},{5... | collective-permute-start | bytes 786440 | tf_op jit(solution)/shard_map/ppermute | solution.py:895
  342.6 16.0 %collective-permute-start.49 = (bf16[128,1024]{1,0:T(8,128)(2,1)}, bf16[128,1024]{1,0:T(8,128)(2,1)S(1)}, u32[]{:S(2)}, u32[]{:S(2)}) collective-permute-start(bf16[128,1024]{1,0:T(8,128)(2,1)} %shard_map.386.refs_0_), channel_id=1, source_target_pairs={{0,8},{4,12},{8,0},{12,4},{16,24},{20,28},{24,16},{28,20},{1,9},{5... | collective-permute-start | bytes 786440 | tf_op jit(solution)/shard_map/ppermute | solution.py:895
  342.6 17.7 %collective-permute-start.50 = (bf16[128,1024]{1,0:T(8,128)(2,1)}, bf16[128,1024]{1,0:T(8,128)(2,1)}, u32[]{:S(2)}, u32[]{:S(2)}) collective-permute-start(bf16[128,1024]{1,0:T(8,128)(2,1)} %collective-permute-done.48.refs_1_), channel_id=1, source_target_pairs={{0,8},{4,12},{8,0},{12,4},{16,24},{20,28},{24,16},{28,20},{1,9},{5... | collective-permute-start | bytes 786440 | tf_op jit(solution)/shard_map/ppermute | solution.py:895
  347.7 10.4 %collective-permute-start.38 = (bf16[64,1024]{1,0:T(8,128)(2,1)}, bf16[64,1024]{1,0:T(8,128)(2,1)S(1)}, u32[]{:S(2)}, u32[]{:S(2)}) collective-permute-start(bf16[64,1024]{1,0:T(8,128)(2,1)} %shard_map.387.refs_0_), channel_id=1, source_target_pairs={{0,16},{4,20},{8,24},{12,28},{16,0},{20,4},{24,8},{28,12},{1,17},{... | collective-permute-start | bytes 393224 | tf_op jit(solution)/shard_map/ppermute | solution.py:895
  347.7 20.6 %collective-permute-start.51 = (bf16[128,1024]{1,0:T(8,128)(2,1)}, bf16[128,1024]{1,0:T(8,128)(2,1)}, u32[]{:S(2)}, u32[]{:S(2)}) collective-permute-start(bf16[128,1024]{1,0:T(8,128)(2,1)} %shard_map.386.refs_0_), channel_id=1, source_target_pairs={{0,4},{4,0},{8,12},{12,8},{16,20},{20,16},{24,28},{28,24},{1,5},{5... | collective-permute-start | bytes 786440 | tf_op jit(solution)/shard_map/ppermute | solution.py:895
  348.3 13.4 %collective-permute-start.39 = (bf16[64,1024]{1,0:T(8,128)(2,1)}, bf16[64,1024]{1,0:T(8,128)(2,1)}, u32[]{:S(2)}, u32[]{:S(2)}) collective-permute-start(bf16[64,1024]{1,0:T(8,128)(2,1)} %shard_map.387.refs_0_), channel_id=1, source_target_pairs={{0,8},{4,12},{8,0},{12,4},{16,24},{20,28},{24,16},{28,20},{1,9},{5... | collective-permute-start | bytes 393224 | tf_op jit(solution)/shard_map/ppermute | solution.py:895
  358.1 10.2 %collective-permute-start.52 = (bf16[128,1024]{1,0:T(8,128)(2,1)}, bf16[128,1024]{1,0:T(8,128)(2,1)}, u32[]{:S(2)}, u32[]{:S(2)}) collective-permute-start(bf16[128,1024]{1,0:T(8,128)(2,1)} %collective-permute-done.48.refs_1_), channel_id=1, source_target_pairs={{0,4},{4,0},{8,12},{12,8},{16,20},{20,16},{24,28},{28,24},{1,5},{5... | collective-permute-start | bytes 786440 | tf_op jit(solution)/shard_map/ppermute | solution.py:895
  358.6 13.8 %collective-permute-start.53 = (bf16[128,1024]{1,0:T(8,128)(2,1)S(1)}, bf16[128,1024]{1,0:T(8,128)(2,1)}, u32[]{:S(2)}, u32[]{:S(2)}) collective-permute-start(bf16[128,1024]{1,0:T(8,128)(2,1)S(1)} %collective-permute-done.49.refs_2_), channel_id=1, source_target_pairs={{0,4},{4,0},{8,12},{12,8},{16,20},{20,16},{24,28},{28,24},{1,5},{5... | collective-permute-start | bytes 786440 | tf_op jit(solution)/shard_map/ppermute | solution.py:895
  360.3 14.9 %collective-permute-start.54 = (bf16[128,1024]{1,0:T(8,128)(2,1)}, bf16[128,1024]{1,0:T(8,128)(2,1)}, u32[]{:S(2)}, u32[]{:S(2)}) collective-permute-start(bf16[128,1024]{1,0:T(8,128)(2,1)} %collective-permute-done.50.refs_3_), channel_id=1, source_target_pairs={{0,4},{4,0},{8,12},{12,8},{16,20},{20,16},{24,28},{28,24},{1,5},{5... | collective-permute-start | bytes 786440 | tf_op jit(solution)/shard_map/ppermute | solution.py:895
  361.7 6.6 %collective-permute-start.40 = (bf16[64,1024]{1,0:T(8,128)(2,1)S(1)}, bf16[64,1024]{1,0:T(8,128)(2,1)}, u32[]{:S(2)}, u32[]{:S(2)}) collective-permute-start(bf16[64,1024]{1,0:T(8,128)(2,1)S(1)} %collective-permute-done.38.refs_1_), channel_id=1, source_target_pairs={{0,8},{4,12},{8,0},{12,4},{16,24},{20,28},{24,16},{28,20},{1,9},{5... | collective-permute-start | bytes 393224 | tf_op jit(solution)/shard_map/ppermute | solution.py:895
  377.8 10.6 %collective-permute-start.56 = (bf16[256,1024]{1,0:T(8,128)(2,1)}, bf16[256,1024]{1,0:T(8,128)(2,1)}, u32[]{:S(2)}, u32[]{:S(2)}) collective-permute-start(bf16[256,1024]{1,0:T(8,128)(2,1)} %shard_map.389.refs_0_), channel_id=1, source_target_pairs={{0,2},{1,3},{2,0},{3,1},{4,6},{5,7},{6,4},{7,5},{8,10},{9,11},{10,... | collective-permute-start | bytes 1572872 | tf_op jit(solution)/shard_map/ppermute | solution.py:895
  378.4 11.7 %collective-permute-start.55 = (bf16[256,1024]{1,0:T(8,128)(2,1)}, bf16[256,1024]{1,0:T(8,128)(2,1)}, u32[]{:S(2)}, u32[]{:S(2)}) collective-permute-start(bf16[256,1024]{1,0:T(8,128)(2,1)} %shard_map.389.refs_0_), channel_id=1, source_target_pairs={{0,4},{4,0},{8,12},{12,8},{16,20},{20,16},{24,28},{28,24},{1,5},{5... | collective-permute-start | bytes 1572872 | tf_op jit(solution)/shard_map/ppermute | solution.py:895
  388.4 11.3 %collective-permute-start.57 = (bf16[256,1024]{1,0:T(8,128)(2,1)}, bf16[256,1024]{1,0:T(8,128)(2,1)}, u32[]{:S(2)}, u32[]{:S(2)}) collective-permute-start(bf16[256,1024]{1,0:T(8,128)(2,1)} %collective-permute-done.56.refs_2_), channel_id=1, source_target_pairs={{0,4},{4,0},{8,12},{12,8},{16,20},{20,16},{24,28},{28,24},{1,5},{5... | collective-permute-start | bytes 1572872 | tf_op jit(solution)/shard_map/ppermute | solution.py:895
  389.0 14.6 %collective-permute-start.58 = (bf16[256,1024]{1,0:T(8,128)(2,1)}, bf16[256,1024]{1,0:T(8,128)(2,1)}, u32[]{:S(2)}, u32[]{:S(2)}) collective-permute-start(bf16[256,1024]{1,0:T(8,128)(2,1)} %shard_map.389.refs_0_), channel_id=1, source_target_pairs={{0,1},{1,0},{2,3},{3,2},{4,5},{5,4},{6,7},{7,6},{8,9},{9,8},{10,11... | collective-permute-start | bytes 1572872 | tf_op jit(solution)/shard_map/ppermute | solution.py:895
  389.0 14.6 %collective-permute-start.60 = (bf16[256,1024]{1,0:T(8,128)(2,1)}, bf16[256,1024]{1,0:T(8,128)(2,1)}, u32[]{:S(2)}, u32[]{:S(2)}) collective-permute-start(bf16[256,1024]{1,0:T(8,128)(2,1)} %collective-permute-done.56.refs_2_), channel_id=1, source_target_pairs={{0,1},{1,0},{2,3},{3,2},{4,5},{5,4},{6,7},{7,6},{8,9},{9,8},{10,11... | collective-permute-start | bytes 1572872 | tf_op jit(solution)/shard_map/ppermute | solution.py:895
  390.1 13.5 %collective-permute-start.59 = (bf16[256,1024]{1,0:T(8,128)(2,1)}, bf16[256,1024]{1,0:T(8,128)(2,1)}, u32[]{:S(2)}, u32[]{:S(2)}) collective-permute-start(bf16[256,1024]{1,0:T(8,128)(2,1)} %collective-permute-done.55.refs_1_), channel_id=1, source_target_pairs={{0,1},{1,0},{2,3},{3,2},{4,5},{5,4},{6,7},{7,6},{8,9},{9,8},{10,11... | collective-permute-start | bytes 1572872 | tf_op jit(solution)/shard_map/ppermute | solution.py:895
  399.8 3.8 collective-permute-start.61
  (23 other events, 186.7 us)

commit v4 on v3

--- a/solution.py
+++ b/solution.py
@@ -1411,15 +1411,20 @@
             token = total
     attn_data = DataSum(attn_sum.put(0, attn_grads[0]), bits)
     text_data = DataSum(text_sum.put(0, results[2]), bits, merged=True)
-    steps = [(at, ffn_data) for at in range(1, len(bits) + 1)]
+    steps = [(1 + (at - 1) / len(bits), ffn_data) for at in range(1, len(bits))]
+    steps.append((2, ffn_data))
     for at in range(len(bits) + 1):
-        steps.append((at + 1.9 if at else 1.5, attn_data))
+        steps.append((at + 1.9 if at else 1.9 - 0.1, attn_data))
         steps.append((at + 2.25, text_data))
     steps.sort(key=lambda step: step[0])
     columns = mod_weight.shape[1]
     grad_time = None
+    last_attn = max(at for at, member in steps if member is attn_data)
     for at, member in steps:
-        if at > len(bits) and member is attn_data and grad_time is None:
+        if at == last_attn:
+            weight_up, weight_down = unpack(ffn_unpack, ffn_data, ff_in, ff_out, token)
+            token = member.step(token, weight_up)
+        elif at > len(bits) and member is attn_data and grad_time is None:
             (grad_mod,) = after([grad_mod], token)
             grad_mod = grad_mod.reshape(1, group * columns)
             grad_cols = lax.all_to_all(grad_mod, "heads", split_axis=1, concat_axis=0, tiled=True)
@@ -1434,7 +1439,6 @@
         else:
             token = member.step(token)
 
-    weight_up, weight_down = unpack(ffn_unpack, ffn_data, ff_in, ff_out, attn_data.pieces[0])
     text_half = text_data.half(weight_up, *list(attn_data.pieces.values())[1:])
     weight_qkv, weight_out = unpack(attn_unpack, attn_data, qkv_weight, out_weight, text_half)
     text_halves = {0: [text_half]}

time: 425 us -> 430 us (1.012)
  waiting for transfers between devices: 116 us -> 121 us
    ppermute x62, waiting for transfers between devices: 116 us -> 121 us  [swap(): lax.ppermute(array, axis, [(at, at ^ bit) for at in range(lax.axis_size(a...]
  transfers between devices with their start and end apart: 65 -> 65, of which waited for: 24 -> 25; matrix products, arithmetic and copies ran while one was open for 7% -> 7% of each run, Pallas kernels for 38% -> 37%
where the time goes in v4:
time: 430 us; the launch traced here: 423 us
  Pallas kernels  191 us (44%)
  waiting for transfers between devices  121 us (28%)
  starting transfers between devices  66.2 us (15%)
  local copies, waits for them, and re-layouts  24 us (6%)
  other arithmetic  10.7 us (2%)
  matrix products  5.13 us (1%)
    pallas_call x26, Pallas kernels, run_kernel(): pl.pallas_call(kernel, grid=(parts,), in_specs=[spec for spec, _ in input...  191 us
    ppermute x62, waiting for transfers between devices, swap(): lax.ppermute(array, axis, [(at, at ^ bit) for at in range(lax.axis_size(a...  121 us
    ppermute x62, starting transfers between devices, swap(): lax.ppermute(array, axis, [(at, at ^ bit) for at in range(lax.axis_size(a...  55.6 us
  transfers between devices with their start and end apart: 65, of which 25 were waited for; matrix products, arithmetic and copies ran while one was open for 7% of the time, Pallas kernels for 37%

profile of v4, /device:TPU:0, one launch (start us, length us, event | category | flops | bytes accessed | tf_op | source)
XLA Modules:
  0.0 422.9 jit_solution(9468541414309214994)
XLA Ops:
  0.7 2.2 constant_dynamic-slice_fusion.4
  2.9 3.0 collective-permute-start
  13.0 1.8 pad_maximum_fusion.mel_ref.refs_3_
  14.8 9.7 %shard_map.366 = (bf16[512,512]{1,0:T(8,128)(2,1)}, f32[512,1024]{1,0:T(8,128)}, f32[8,1024]{1,0:T(8,128)}, bf16[512,1024]{1,0:T(8,128)(2,1)}, bf16[512,512]{1,0:T(8,128)(2,1)}, /*index=5*/f32[512,1024]{1,0:T(8,128)}) custom-call(bf16[512,512]{1,0:T(8,128)(2,1)} %refs_2_.1, bf16[512,200]{1,0:T(8,128)(2,1)} %pad_maximum_fusion.mel_ref.refs_3_, ...), custom_call_target="tpu_custom_call" | custom-call | flops 1024 | bytes 1024 | tf_op jit(solution)/shard_map/pallas_call | solution.py:877
  26.9 3.5 all-to-all-start
  31.1 1.9 constant_dynamic-slice_fusion.2
  33.0 1.9 constant_dynamic-slice_fusion.1
  34.9 1.8 fusion.1
  37.3 2.0 collective-permute-start.2
  41.2 1.9 collective-permute-start.11
  43.3 14.3 %shard_map.367 = (bf16[2,512,256]{2,1,0:T(8,128)(2,1)}, bf16[2,512,256]{2,1,0:T(8,128)(2,1)}, bf16[2,512,256]{2,1,0:T(8,128)(2,1)}, bf16[2,512,256]{2,1,0:T(8,12...) custom-call(s32[1]{0:T(128)} %dynamic_slice.22.refs_0_, s32[1]{0:T(128)} %bitcast.refs_1_.refs_0_, ...), custom_call_target="tpu_custom_call" | custom-call | flops 1024 | bytes 1024 | tf_op jit(solution)/shard_map/pallas_call | solution.py:877
  57.8 1.8 collective-permute-start.7
  59.7 6.7 %collective-permute-done.7.refs_13_.refs_19_ = bf16[128,1024]{1,0:T(8,128)(2,1)S(1)} collective-permute-done((bf16[128,1024]{1,0:T(8,128)(2,1)S(1)}, bf16[128,1024]{1,0:T(8,128)(2,1)S(1)}, u32[]{:S(2)}, u32[]{:S(2)}) %collective-permute-start.7) | collective-permute-done | bytes 262176 | tf_op jit(solution)/shard_map/ppermute | solution.py:895
  67.1 2.1 collective-permute-done.8.refs_14_.refs_16_
  69.2 1.7 collective-permute-start.16
  72.2 17.8 %shard_map.368 = (bf16[2,512,256]{2,1,0:T(8,128)(2,1)}, bf16[2,512,256]{2,1,0:T(8,128)(2,1)}, bf16[2,512,256]{2,1,0:T(8,128)(2,1)}, bf16[2,512,256]{2,1,0:T(8,12...) custom-call(s32[1]{0:T(128)} %dynamic_slice.22.refs_0_, ...), custom_call_target="tpu_custom_call" | custom-call | flops 1024 | bytes 1024 | tf_op jit(solution)/shard_map/pallas_call | solution.py:877
  90.7 4.0 collective-permute-done.12.refs_11_
  97.7 25.5 %shard_map.369 = (f32[4,1,512]{2,1,0:T(1,128)}, f32[8,1024]{1,0:T(8,128)}, bf16[1024,1024]{1,0:T(8,128)(2,1)}, bf16[1024,1024]{1,0:T(8,128)(2,1)}, bf16[1024,102...) custom-call(s32[1]{0:T(128)} %bitcast.refs_1_.refs_0_, ...), custom_call_target="tpu_custom_call" | custom-call | flops 1024 | bytes 1024 | tf_op jit(solution)/shard_map/pallas_call | solution.py:877
  123.4 20.1 %shard_map.370 = (f32[2,3,256]{2,1,0:T(4,128)}, bf16[1024,1024]{1,0:T(8,128)(2,1)}, bf16[1024,1024]{1,0:T(8,128)(2,1)}, f32[512,1024]{1,0:T(8,128)}) custom-call(s32[1]{0:T(128)} %dynamic_slice.22.refs_0_, s32[1]{0:T(128)} %bitcast.refs_1_.refs_0_, bf16[512,1024]{1,0:T(8,128)(2,1)} %get-tuple-element.196.refs_2_, ...), custom_call_target="tpu_custom_call" | custom-call | flops 1024 | bytes 1024 | tf_op jit(solution)/shard_map/pallas_call | solution.py:877
  144.0 4.3 %shard_map.371 = bf16[1024,1024]{1,0:T(8,128)(2,1)} custom-call(bf16[1024,1024]{1,0:T(8,128)(2,1)} %get-tuple-element.210.refs_0_, bf16[1024,1024]{1,0:T(8,128)(2,1)} %collective-permute-done.20.refs_1_), custom_call_target="tpu_custom_call" | custom-call | flops 1024 | bytes 1024 | tf_op jit(solution)/shard_map/pallas_call | solution.py:877
  148.3 1.9 collective-permute-start.23
  150.2 23.2 %shard_map.372 = (f32[2,3,256]{2,1,0:T(4,128)}, bf16[1024,1024]{1,0:T(8,128)(2,1)}, bf16[1024,1024]{1,0:T(8,128)(2,1)}, bf16[512,1024]{1,0:T(8,128)(2,1)}, f32[8,1024]{1,0:T(8,128)}) custom-call(s32[1]{0:T(128)} %dynamic_slice.22.refs_0_, s32[1]{0:T(128)} %bitcast.refs_1_.refs_0_, bf16[512,1024]{1,0:T(8,128)(2,1)} %get-tuple-element.196.refs_2_, ...), custom_call_target="tpu_custom_call" | custom-call | flops 1024 | bytes 1024 | tf_op jit(solution)/shard_map/pallas_call | solution.py:877
  173.4 4.3 %shard_map.373 = bf16[1024,1024]{1,0:T(8,128)(2,1)} custom-call(bf16[1024,1024]{1,0:T(8,128)(2,1)} %get-tuple-element.217.refs_0_, bf16[1024,1024]{1,0:T(8,128)(2,1)} %collective-permute-done.21.refs_1_), custom_call_target="tpu_custom_call" | custom-call | flops 1024 | bytes 1024 | tf_op jit(solution)/shard_map/pallas_call | solution.py:877
  179.2 21.4 %shard_map.374 = (f32[512,512]{1,0:T(8,128)}, bf16[6,1024]{1,0:T(8,128)(2,1)}, bf16[512,1024]{1,0:T(8,128)(2,1)}, bf16[512,1024]{1,0:T(8,128)(2,1)}, bf16[512,10...) custom-call(s32[2]{0:T(128)} %pad_add_fusion.refs_0_.own_ref, bf16[512,1024]{1,0:T(8,128)(2,1)} %get-tuple-element.219.refs_1_, ...), custom_call_target="tpu_custom_call" | custom-call | flops 1024 | bytes 1024 | tf_op jit(solution)/shard_map/pallas_call | solution.py:877
  201.2 4.2 shard_map.375
  205.3 1.7 collective-permute-start.27
  207.1 2.6 shard_map.376
  209.7 21.0 %collective-permute-done.27.refs_2_.refs_4_ = bf16[512,1024]{1,0:T(8,128)(2,1)} collective-permute-done((bf16[512,1024]{1,0:T(8,128)(2,1)}, bf16[512,1024]{1,0:T(8,128)(2,1)}, u32[]{:S(2)}, u32[]{:S(2)}) %collective-permute-start.27) | collective-permute-done | bytes 1048608 | tf_op jit(solution)/shard_map/ppermute | solution.py:895
  230.8 2.8 shard_map.377
  233.5 1.8 collective-permute-start.28
  237.0 9.9 %collective-permute-done.28.refs_2_.refs_4_ = bf16[256,1024]{1,0:T(8,128)(2,1)} collective-permute-done((bf16[256,1024]{1,0:T(8,128)(2,1)}, bf16[256,1024]{1,0:T(8,128)(2,1)}, u32[]{:S(2)}, u32[]{:S(2)}) %collective-permute-start.28) | collective-permute-done | bytes 524320 | tf_op jit(solution)/shard_map/ppermute | solution.py:895
  247.0 2.1 shard_map.378
  249.1 4.2 shard_map.379
  255.0 2.6 collective-permute-start.29
  257.6 10.1 %collective-permute-done.29.refs_1_ = bf16[128,1024]{1,0:T(8,128)(2,1)S(1)} collective-permute-done((bf16[128,1024]{1,0:T(8,128)(2,1)S(1)}, bf16[128,1024]{1,0:T(8,128)(2,1)S(1)}, u32[]{:S(2)}, u32[]{:S(2)}) %collective-permute-start.29) | collective-permute-done | bytes 262176 | tf_op jit(solution)/shard_map/ppermute | solution.py:895
  268.4 1.8 shard_map.380.refs_0_
  270.2 3.3 shard_map.381
  274.0 5.0 %collective-permute-done.33.refs_2_.refs_4_ = bf16[512,1024]{1,0:T(8,128)(2,1)} collective-permute-done((bf16[512,1024]{1,0:T(8,128)(2,1)}, bf16[512,1024]{1,0:T(8,128)(2,1)}, u32[]{:S(2)}, u32[]{:S(2)}) %collective-permute-start.33) | collective-permute-done | bytes 1048608 | tf_op jit(solution)/shard_map/ppermute | solution.py:895
  278.9 2.8 shard_map.382
  283.7 3.8 collective-permute-done.37.refs_1_
  289.0 2.1 shard_map.383
  292.5 3.3 all-to-all-start.1
  297.8 6.6 %collective-permute-done.38.refs_2_ = bf16[128,1024]{1,0:T(8,128)(2,1)} collective-permute-done((bf16[128,1024]{1,0:T(8,128)(2,1)S(1)}, bf16[128,1024]{1,0:T(8,128)(2,1)}, u32[]{:S(2)}, u32[]{:S(2)}) %collective-permute-start.38) | collective-permute-done | bytes 262176 | tf_op jit(solution)/shard_map/ppermute | solution.py:895
  310.0 2.1 shard_map.384
  312.2 3.6 collective-permute-done.36.refs_2_.refs_4_
  315.8 3.5 collective-permute-start.35
  320.0 1.9 shard_map.385
  321.9 4.4 %shard_map.386 = (f32[1024,512]{1,0:T(8,128)}, f32[512,1024]{1,0:T(8,128)}) custom-call(s32[8]{0:T(128)} %stack.98.starts_ref, bf16[128,1024]{1,0:T(8,128)(2,1)} %shard_map.380.refs_0_, bf16[128,1024]{1,0:T(8,128)(2,1)} %collective-permute-done.37.refs_1_, bf16[128,1024]{1,0:T(8,128)(2,1)} %collective-permute-done.38.refs_2_, ...), custom_call_target="tpu_custom_call" | custom-call | flops 1024 | bytes 1024 | tf_op jit(solution)/shard_map/pallas_call | solution.py:877
  326.2 4.1 collective-permute-done.35.refs_1_
  330.3 1.8 shard_map.387.refs_0_
  332.8 3.9 all-to-all-start.2
  336.6 3.0 collective-permute-start.44
  340.9 9.6 %collective-permute-done.48.refs_1_ = bf16[128,1024]{1,0:T(8,128)(2,1)S(1)} collective-permute-done((bf16[128,1024]{1,0:T(8,128)(2,1)}, bf16[128,1024]{1,0:T(8,128)(2,1)S(1)}, u32[]{:S(2)}, u32[]{:S(2)}) %collective-permute-start.48) | collective-permute-done | bytes 262176 | tf_op jit(solution)/shard_map/ppermute | solution.py:895
  357.7 4.2 %collective-permute-done.45.refs_1_ = bf16[64,1024]{1,0:T(8,128)(2,1)S(1)} collective-permute-done((bf16[64,1024]{1,0:T(8,128)(2,1)}, bf16[64,1024]{1,0:T(8,128)(2,1)S(1)}, u32[]{:S(2)}, u32[]{:S(2)}) %collective-permute-start.45) | collective-permute-done | bytes 131104 | tf_op jit(solution)/shard_map/ppermute | solution.py:895
  367.3 4.1 collective-permute-done.47.refs_3_
  371.4 5.0 %collective-permute-done.53.refs_6_ = bf16[128,1024]{1,0:T(8,128)(2,1)} collective-permute-done((bf16[128,1024]{1,0:T(8,128)(2,1)}, bf16[128,1024]{1,0:T(8,128)(2,1)}, u32[]{:S(2)}, u32[]{:S(2)}) %collective-permute-start.53) | collective-permute-done | bytes 262176 | tf_op jit(solution)/shard_map/ppermute | solution.py:895
  376.5 2.8 collective-permute-done.54.refs_7_
  379.3 2.6 shard_map.389.refs_0_
  385.1 4.4 %shard_map.390 = (f32[3,1024,256]{2,1,0:T(8,128)}, f32[256,1024]{1,0:T(8,128)}) custom-call(s32[8]{0:T(128)} %stack.98.starts_ref, bf16[128,1024]{1,0:T(8,128)(2,1)} %shard_map.387.refs_0_, bf16[128,1024]{1,0:T(8,128)(2,1)} %copy-done.8, bf16[128,1024]{1,0:T(8,128)(2,1)} %collective-permute-done.49.refs_2_, ...), custom_call_target="tpu_custom_call" | custom-call | flops 1024 | bytes 1024 | tf_op jit(solution)/shard_map/pallas_call | solution.py:877
  389.6 3.4 collective-permute-done.56.refs_2_
  395.1 1.8 collective-permute-done.55.refs_1_
  396.9 8.8 %collective-permute-done.57.refs_3_ = bf16[256,1024]{1,0:T(8,128)(2,1)} collective-permute-done((bf16[256,1024]{1,0:T(8,128)(2,1)}, bf16[256,1024]{1,0:T(8,128)(2,1)}, u32[]{:S(2)}, u32[]{:S(2)}) %collective-permute-start.57) | collective-permute-done | bytes 524320 | tf_op jit(solution)/shard_map/ppermute | solution.py:895
  409.6 6.2 %shard_map.391 = (f32[712,1024]{1,0:T(8,128)}, f32[512,1024]{1,0:T(8,128)}, f32[1024,512]{1,0:T(8,128)}, f32[7,512]{1,0:T(8,128)}, f32[3,512]{1,0:T(4,128)}, /*i...) custom-call(s32[8]{0:T(128)} %stack.107.starts_ref, ...), custom_call_target="tpu_custom_call" | custom-call | flops 1024 | bytes 1024 | tf_op jit(solution)/shard_map/pallas_call | solution.py:877
  418.9 3.7 fusion.2
  (189 shorter events, 63.4 us)
Async XLA Ops:
  2.9 34.4 %collective-permute-start = (bf16[3,512,256]{2,1,0:T(8,128)(2,1)}, bf16[3,512,256]{2,1,0:T(8,128)(2,1)}, u32[]{:S(2)}, u32[]{:S(2)}) collective-permute-start(bf16[3,512,256]{2,1,0:T(8,128)(2,1)} %constant_dynamic-slice_fusion.4), channel_id=1, source_target_pairs={{0,2},{1,3},{2,0},{3,1},{4,6},{5,7},{6,4},{7,5},{8,10},{9,11},{10,... | collective-permute-start | bytes 2359304 | tf_op jit(solution)/shard_map/ppermute | solution.py:895
  7.6 35.6 %collective-permute-start.1 = (bf16[128,1024]{1,0:T(8,128)(2,1)}, bf16[128,1024]{1,0:T(8,128)(2,1)S(1)}, u32[]{:S(2)}, u32[]{:S(2)}) collective-permute-start(bf16[128,1024]{1,0:T(8,128)(2,1)} %constant_dynamic-slice_fusion.3), channel_id=1, source_target_pairs={{0,2},{1,3},{2,0},{3,1},{4,6},{5,7},{6,4},{7,5},{8,10},{9,11},{10,... | collective-permute-start | bytes 786440 | tf_op jit(solution)/shard_map/ppermute | solution.py:895
  26.9 10.4 %all-to-all-start = ((bf16[4,2,1408]{2,1,0:T(2,128)(2,1)}), bf16[4,2,1408]{2,1,0:T(2,128)(2,1)S(1)}, u32[]{:S(2)}, u32[]{:S(2)}) async-start(bf16[4,2,1408]{2,1,0:T(2,128)(2,1)} %reshape.189), calls=%async_computation | async-start | bytes 45056 | tf_op jit(solution)/shard_map/all_to_all | solution.py:1175
  30.4 12.8 %collective-permute-start.3 = (bf16[3,1024,256]{2,1,0:T(8,128)(2,1)}, bf16[3,1024,256]{2,1,0:T(8,128)(2,1)}, u32[]{:S(2)}, u32[]{:S(2)}) collective-permute-start(bf16[3,1024,256]{2,1,0:T(8,128)(2,1)} %refs_13_.4), channel_id=1, source_target_pairs={{0,1},{1,0},{2,3},{3,2},{4,5},{5,4},{6,7},{7,6},{8,9},{9,8},{10,11... | collective-permute-start | bytes 4718600 | tf_op jit(solution)/shard_map/ppermute | solution.py:895
  31.0 12.3 %collective-permute-start.4 = (bf16[256,1024]{1,0:T(8,128)(2,1)}, bf16[256,1024]{1,0:T(8,128)(2,1)}, u32[]{:S(2)}, u32[]{:S(2)}) collective-permute-start(bf16[256,1024]{1,0:T(8,128)(2,1)} %refs_15_.2), channel_id=1, source_target_pairs={{0,1},{1,0},{2,3},{3,2},{4,5},{5,4},{6,7},{7,6},{8,9},{9,8},{10,11... | collective-permute-start | bytes 1572872 | tf_op jit(solution)/shard_map/ppermute | solution.py:895
  37.3 20.4 %collective-permute-start.2 = (bf16[3,512,256]{2,1,0:T(8,128)(2,1)}, bf16[3,512,256]{2,1,0:T(8,128)(2,1)}, u32[]{:S(2)}, u32[]{:S(2)}) collective-permute-start(bf16[3,512,256]{2,1,0:T(8,128)(2,1)} %collective-permute-done.refs_8_.refs_14_), channel_id=1, source_target_pairs={{0,4},{4,0},{8,12},{12,8},{16,20},{20,16},{24,28},{28,24},{1,5},{5... | collective-permute-start | bytes 2359304 | tf_op jit(solution)/shard_map/ppermute | solution.py:895
  41.2 25.3 %collective-permute-start.11 = (bf16[256,1024]{1,0:T(8,128)(2,1)}, bf16[256,1024]{1,0:T(8,128)(2,1)}, u32[]{:S(2)}, u32[]{:S(2)}) collective-permute-start(bf16[256,1024]{1,0:T(8,128)(2,1)} %constant_dynamic-slice_fusion.1), channel_id=1, source_target_pairs={{0,2},{1,3},{2,0},{3,1},{4,6},{5,7},{6,4},{7,5},{8,10},{9,11},{10,... | collective-permute-start | bytes 1572872 | tf_op jit(solution)/shard_map/ppermute | solution.py:895
  43.2 23.8 %collective-permute-start.10 = (bf16[512,512]{1,0:T(8,128)(2,1)}, bf16[512,512]{1,0:T(8,128)(2,1)}, u32[]{:S(2)}, u32[]{:S(2)}) collective-permute-start(bf16[512,512]{1,0:T(8,128)(2,1)} %constant_dynamic-slice_fusion.2), channel_id=1, source_target_pairs={{0,2},{1,3},{2,0},{3,1},{4,6},{5,7},{6,4},{7,5},{8,10},{9,11},{10,... | collective-permute-start | bytes 1572872 | tf_op jit(solution)/shard_map/ppermute | solution.py:895
  57.8 13.9 %collective-permute-start.5 = (bf16[3,512,256]{2,1,0:T(8,128)(2,1)}, bf16[3,512,256]{2,1,0:T(8,128)(2,1)}, u32[]{:S(2)}, u32[]{:S(2)}) collective-permute-start(bf16[3,512,256]{2,1,0:T(8,128)(2,1)} %collective-permute-done.refs_8_.refs_14_), channel_id=1, source_target_pairs={{0,1},{1,0},{2,3},{3,2},{4,5},{5,4},{6,7},{7,6},{8,9},{9,8},{10,11... | collective-permute-start | bytes 2359304 | tf_op jit(solution)/shard_map/ppermute | solution.py:895
  57.8 8.7 %collective-permute-start.7 = (bf16[128,1024]{1,0:T(8,128)(2,1)S(1)}, bf16[128,1024]{1,0:T(8,128)(2,1)S(1)}, u32[]{:S(2)}, u32[]{:S(2)}) collective-permute-start(bf16[128,1024]{1,0:T(8,128)(2,1)S(1)} %collective-permute-done.1.refs_12_.refs_18_), channel_id=1, source_target_pairs={{0,4},{4,0},{8,12},{12,8},{16,20},{20,16},{24,28},{28,24},{1,5},{5... | collective-permute-start | bytes 786440 | tf_op jit(solution)/shard_map/ppermute | solution.py:895
  59.5 35.2 %collective-permute-start.15 = (bf16[1024,512]{1,0:T(8,128)(2,1)}, bf16[1024,512]{1,0:T(8,128)(2,1)}, u32[]{:S(2)}, u32[]{:S(2)}) collective-permute-start(bf16[1024,512]{1,0:T(8,128)(2,1)} %refs_13_.3), channel_id=1, source_target_pairs={{0,1},{1,0},{2,3},{3,2},{4,5},{5,4},{6,7},{7,6},{8,9},{9,8},{10,11... | collective-permute-start | bytes 3145736 | tf_op jit(solution)/shard_map/ppermute | solution.py:895
  66.5 5.7 %collective-permute-start.6 = (bf16[3,512,256]{2,1,0:T(8,128)(2,1)}, bf16[3,512,256]{2,1,0:T(8,128)(2,1)}, u32[]{:S(2)}, u32[]{:S(2)}) collective-permute-start(bf16[3,512,256]{2,1,0:T(8,128)(2,1)} %collective-permute-done.2.refs_9_.refs_15_), channel_id=1, source_target_pairs={{0,1},{1,0},{2,3},{3,2},{4,5},{5,4},{6,7},{7,6},{8,9},{9,8},{10,11... | collective-permute-start | bytes 2359304 | tf_op jit(solution)/shard_map/ppermute | solution.py:895
  66.5 2.6 collective-permute-start.8
  67.0 3.9 collective-permute-start.9
  69.2 20.9 %collective-permute-start.16 = (bf16[256,1024]{1,0:T(8,128)(2,1)}, bf16[256,1024]{1,0:T(8,128)(2,1)}, u32[]{:S(2)}, u32[]{:S(2)}) collective-permute-start(bf16[256,1024]{1,0:T(8,128)(2,1)} %collective-permute-done.11.refs_16_), channel_id=1, source_target_pairs={{0,4},{4,0},{8,12},{12,8},{16,20},{20,16},{24,28},{28,24},{1,5},{5... | collective-permute-start | bytes 1572872 | tf_op jit(solution)/shard_map/ppermute | solution.py:895
  70.9 23.8 %collective-permute-start.12 = (bf16[512,512]{1,0:T(8,128)(2,1)}, bf16[512,512]{1,0:T(8,128)(2,1)}, u32[]{:S(2)}, u32[]{:S(2)}) collective-permute-start(bf16[512,512]{1,0:T(8,128)(2,1)} %collective-permute-done.10.refs_10_), channel_id=1, source_target_pairs={{0,4},{4,0},{8,12},{12,8},{16,20},{20,16},{24,28},{28,24},{1,5},{5... | collective-permute-start | bytes 1572872 | tf_op jit(solution)/shard_map/ppermute | solution.py:895
  71.6 24.2 %collective-permute-start.19 = (bf16[512,1024]{1,0:T(8,128)(2,1)}, bf16[512,1024]{1,0:T(8,128)(2,1)}, u32[]{:S(2)}, u32[]{:S(2)}) collective-permute-start(bf16[512,1024]{1,0:T(8,128)(2,1)} %refs_19_.1), channel_id=1, source_target_pairs={{0,1},{1,0},{2,3},{3,2},{4,5},{5,4},{6,7},{7,6},{8,9},{9,8},{10,11... | collective-permute-start | bytes 3145736 | tf_op jit(solution)/shard_map/ppermute | solution.py:895
  90.0 5.8 %collective-permute-start.17 = (bf16[256,1024]{1,0:T(8,128)(2,1)}, bf16[256,1024]{1,0:T(8,128)(2,1)S(1)}, u32[]{:S(2)}, u32[]{:S(2)}) collective-permute-start(bf16[256,1024]{1,0:T(8,128)(2,1)} %collective-permute-done.11.refs_16_), channel_id=1, source_target_pairs={{0,1},{1,0},{2,3},{3,2},{4,5},{5,4},{6,7},{7,6},{8,9},{9,8},{10,11... | collective-permute-start | bytes 1572872 | tf_op jit(solution)/shard_map/ppermute | solution.py:895
  90.6 5.2 %collective-permute-start.18 = (bf16[256,1024]{1,0:T(8,128)(2,1)}, bf16[256,1024]{1,0:T(8,128)(2,1)}, u32[]{:S(2)}, u32[]{:S(2)}) collective-permute-start(bf16[256,1024]{1,0:T(8,128)(2,1)} %collective-permute-done.16.refs_17_), channel_id=1, source_target_pairs={{0,1},{1,0},{2,3},{3,2},{4,5},{5,4},{6,7},{7,6},{8,9},{9,8},{10,11... | collective-permute-start | bytes 1572872 | tf_op jit(solution)/shard_map/ppermute | solution.py:895
  94.7 3.0 collective-permute-start.14
  123.1 20.9 %collective-permute-start.20 = (bf16[1024,1024]{1,0:T(8,128)(2,1)}, bf16[1024,1024]{1,0:T(8,128)(2,1)}, u32[]{:S(2)}, u32[]{:S(2)}) collective-permute-start(bf16[1024,1024]{1,0:T(8,128)(2,1)} %get-tuple-element.209), channel_id=1, source_target_pairs={{0,1},{1,0},{2,3},{3,2},{4,5},{5,4},{6,7},{7,6},{8,9},{9,8},{10,11... | collective-permute-start | bytes 6291464 | tf_op jit(solution)/shard_map/ppermute | solution.py:895
  143.5 29.9 %collective-permute-start.21 = (bf16[1024,1024]{1,0:T(8,128)(2,1)}, bf16[1024,1024]{1,0:T(8,128)(2,1)}, u32[]{:S(2)}, u32[]{:S(2)}) collective-permute-start(bf16[1024,1024]{1,0:T(8,128)(2,1)} %get-tuple-element.216), channel_id=1, source_target_pairs={{0,1},{1,0},{2,3},{3,2},{4,5},{5,4},{6,7},{7,6},{8,9},{9,8},{10,11... | collective-permute-start | bytes 6291464 | tf_op jit(solution)/shard_map/ppermute | solution.py:895
  143.9 57.3 %collective-permute-start.24 = (bf16[1024,1024]{1,0:T(8,128)(2,1)}, bf16[1024,1024]{1,0:T(8,128)(2,1)}, u32[]{:S(2)}, u32[]{:S(2)}) collective-permute-start(bf16[1024,1024]{1,0:T(8,128)(2,1)} %get-tuple-element.236), channel_id=1, source_target_pairs={{0,1},{1,0},{2,3},{3,2},{4,5},{5,4},{6,7},{7,6},{8,9},{9,8},{10,11... | collective-permute-start | bytes 6291464 | tf_op jit(solution)/shard_map/ppermute | solution.py:895
  148.3 52.8 %collective-permute-start.23 = (bf16[1024,1024]{1,0:T(8,128)(2,1)}, bf16[1024,1024]{1,0:T(8,128)(2,1)}, u32[]{:S(2)}, u32[]{:S(2)}) collective-permute-start(bf16[1024,1024]{1,0:T(8,128)(2,1)} %shard_map.371), channel_id=1, source_target_pairs={{0,2},{1,3},{2,0},{3,1},{4,6},{5,7},{6,4},{7,5},{8,10},{9,11},{10,... | collective-permute-start | bytes 6291464 | tf_op jit(solution)/shard_map/ppermute | solution.py:895
  177.7 71.4 %collective-permute-start.30 = (bf16[1024,1024]{1,0:T(8,128)(2,1)}, bf16[1024,1024]{1,0:T(8,128)(2,1)}, u32[]{:S(2)}, u32[]{:S(2)}) collective-permute-start(bf16[1024,1024]{1,0:T(8,128)(2,1)} %shard_map.373), channel_id=1, source_target_pairs={{0,2},{1,3},{2,0},{3,1},{4,6},{5,7},{6,4},{7,5},{8,10},{9,11},{10,... | collective-permute-start | bytes 6291464 | tf_op jit(solution)/shard_map/ppermute | solution.py:895
  177.9 71.2 %collective-permute-start.31 = (bf16[1024,1024]{1,0:T(8,128)(2,1)}, bf16[1024,1024]{1,0:T(8,128)(2,1)}, u32[]{:S(2)}, u32[]{:S(2)}) collective-permute-start(bf16[1024,1024]{1,0:T(8,128)(2,1)} %get-tuple-element.254), channel_id=1, source_target_pairs={{0,1},{1,0},{2,3},{3,2},{4,5},{5,4},{6,7},{7,6},{8,9},{9,8},{10,11... | collective-permute-start | bytes 6291464 | tf_op jit(solution)/shard_map/ppermute | solution.py:895
  200.6 6.5 %collective-permute-start.22 = (bf16[512,1024]{1,0:T(8,128)(2,1)}, bf16[512,1024]{1,0:T(8,128)(2,1)}, u32[]{:S(2)}, u32[]{:S(2)}) collective-permute-start(bf16[512,1024]{1,0:T(8,128)(2,1)} %get-tuple-element.234), channel_id=1, source_target_pairs={{0,1},{1,0},{2,3},{3,2},{4,5},{5,4},{6,7},{7,6},{8,9},{9,8},{10,11... | collective-permute-start | bytes 3145736 | tf_op jit(solution)/shard_map/ppermute | solution.py:895
  205.3 25.4 %collective-permute-start.27 = (bf16[512,1024]{1,0:T(8,128)(2,1)}, bf16[512,1024]{1,0:T(8,128)(2,1)}, u32[]{:S(2)}, u32[]{:S(2)}) collective-permute-start(bf16[512,1024]{1,0:T(8,128)(2,1)} %get-tuple-element.244), channel_id=1, source_target_pairs={{0,4},{4,0},{8,12},{12,8},{16,20},{20,16},{24,28},{28,24},{1,5},{5... | collective-permute-start | bytes 3145736 | tf_op jit(solution)/shard_map/ppermute | solution.py:895
  233.5 13.4 %collective-permute-start.28 = (bf16[256,1024]{1,0:T(8,128)(2,1)}, bf16[256,1024]{1,0:T(8,128)(2,1)}, u32[]{:S(2)}, u32[]{:S(2)}) collective-permute-start(bf16[256,1024]{1,0:T(8,128)(2,1)} %get-tuple-element.248), channel_id=1, source_target_pairs={{0,8},{4,12},{8,0},{12,4},{16,24},{20,28},{24,16},{28,20},{1,9},{5... | collective-permute-start | bytes 1572872 | tf_op jit(solution)/shard_map/ppermute | solution.py:895
  235.4 34.8 %collective-permute-start.26 = (bf16[512,1024]{1,0:T(8,128)(2,1)}, bf16[512,1024]{1,0:T(8,128)(2,1)}, u32[]{:S(2)}, u32[]{:S(2)}) collective-permute-start(bf16[512,1024]{1,0:T(8,128)(2,1)} %get-tuple-element.243), channel_id=1, source_target_pairs={{0,1},{1,0},{2,3},{3,2},{4,5},{5,4},{6,7},{7,6},{8,9},{9,8},{10,11... | collective-permute-start | bytes 3145736 | tf_op jit(solution)/shard_map/ppermute | solution.py:895
  235.4 34.8 %collective-permute-start.25 = (bf16[512,1024]{1,0:T(8,128)(2,1)}, bf16[512,1024]{1,0:T(8,128)(2,1)}, u32[]{:S(2)}, u32[]{:S(2)}) collective-permute-start(bf16[512,1024]{1,0:T(8,128)(2,1)} %shard_map.376), channel_id=1, source_target_pairs={{0,2},{1,3},{2,0},{3,1},{4,6},{5,7},{6,4},{7,5},{8,10},{9,11},{10,... | collective-permute-start | bytes 3145736 | tf_op jit(solution)/shard_map/ppermute | solution.py:895
  253.3 25.6 %collective-permute-start.33 = (bf16[512,1024]{1,0:T(8,128)(2,1)}, bf16[512,1024]{1,0:T(8,128)(2,1)}, u32[]{:S(2)}, u32[]{:S(2)}) collective-permute-start(bf16[512,1024]{1,0:T(8,128)(2,1)} %get-tuple-element.266), channel_id=1, source_target_pairs={{0,4},{4,0},{8,12},{12,8},{16,20},{20,16},{24,28},{28,24},{1,5},{5... | collective-permute-start | bytes 3145736 | tf_op jit(solution)/shard_map/ppermute | solution.py:895
  255.0 12.7 %collective-permute-start.29 = (bf16[128,1024]{1,0:T(8,128)(2,1)S(1)}, bf16[128,1024]{1,0:T(8,128)(2,1)S(1)}, u32[]{:S(2)}, u32[]{:S(2)}) collective-permute-start(bf16[128,1024]{1,0:T(8,128)(2,1)S(1)} %copy-done.19), channel_id=1, source_target_pairs={{0,16},{4,20},{8,24},{12,28},{16,0},{20,4},{24,8},{28,12},{1,17},{... | collective-permute-start | bytes 786440 | tf_op jit(solution)/shard_map/ppermute | solution.py:895
  273.5 14.7 %collective-permute-start.32 = (bf16[256,1024]{1,0:T(8,128)(2,1)}, bf16[256,1024]{1,0:T(8,128)(2,1)S(1)}, u32[]{:S(2)}, u32[]{:S(2)}) collective-permute-start(bf16[256,1024]{1,0:T(8,128)(2,1)} %get-tuple-element.265), channel_id=1, source_target_pairs={{0,4},{4,0},{8,12},{12,8},{16,20},{20,16},{24,28},{28,24},{1,5},{5... | collective-permute-start | bytes 1572872 | tf_op jit(solution)/shard_map/ppermute | solution.py:895
  274.0 13.5 %collective-permute-start.37 = (bf16[128,1024]{1,0:T(8,128)(2,1)S(1)}, bf16[128,1024]{1,0:T(8,128)(2,1)}, u32[]{:S(2)}, u32[]{:S(2)}) collective-permute-start(bf16[128,1024]{1,0:T(8,128)(2,1)S(1)} %copy-done.2), channel_id=1, source_target_pairs={{0,16},{4,20},{8,24},{12,28},{16,0},{20,4},{24,8},{28,12},{1,17},{... | collective-permute-start | bytes 786440 | tf_op jit(solution)/shard_map/ppermute | solution.py:895
  281.7 27.3 %collective-permute-start.34 = (bf16[256,1024]{1,0:T(8,128)(2,1)}, bf16[256,1024]{1,0:T(8,128)(2,1)}, u32[]{:S(2)}, u32[]{:S(2)}) collective-permute-start(bf16[256,1024]{1,0:T(8,128)(2,1)} %get-tuple-element.274), channel_id=1, source_target_pairs={{0,8},{4,12},{8,0},{12,4},{16,24},{20,28},{24,16},{28,20},{1,9},{5... | collective-permute-start | bytes 1572872 | tf_op jit(solution)/shard_map/ppermute | solution.py:895
  283.1 21.3 %collective-permute-start.38 = (bf16[128,1024]{1,0:T(8,128)(2,1)S(1)}, bf16[128,1024]{1,0:T(8,128)(2,1)}, u32[]{:S(2)}, u32[]{:S(2)}) collective-permute-start(bf16[128,1024]{1,0:T(8,128)(2,1)S(1)} %copy-done.2), channel_id=1, source_target_pairs={{0,8},{4,12},{8,0},{12,4},{16,24},{20,28},{24,16},{28,20},{1,9},{5... | collective-permute-start | bytes 786440 | tf_op jit(solution)/shard_map/ppermute | solution.py:895
  287.5 19.9 %collective-permute-start.39 = (bf16[128,1024]{1,0:T(8,128)(2,1)}, bf16[128,1024]{1,0:T(8,128)(2,1)}, u32[]{:S(2)}, u32[]{:S(2)}) collective-permute-start(bf16[128,1024]{1,0:T(8,128)(2,1)} %collective-permute-done.37.refs_1_), channel_id=1, source_target_pairs={{0,8},{4,12},{8,0},{12,4},{16,24},{20,28},{24,16},{28,20},{1,9},{5... | collective-permute-start | bytes 786440 | tf_op jit(solution)/shard_map/ppermute | solution.py:895
  292.5 16.5 %all-to-all-start.1 = ((bf16[4,2,768]{2,1,0:T(2,128)(2,1)}), bf16[4,2,768]{2,1,0:T(2,128)(2,1)S(1)}, u32[]{:S(2)}, u32[]{:S(2)}) async-start(bf16[4,2,768]{2,1,0:T(2,128)(2,1)} %reshape.191), calls=%async_computation.1 | async-start | bytes 24576 | tf_op jit(solution)/shard_map/all_to_all | solution.py:1430
  295.7 26.1 %collective-permute-start.40 = (bf16[128,1024]{1,0:T(8,128)(2,1)S(1)}, bf16[128,1024]{1,0:T(8,128)(2,1)}, u32[]{:S(2)}, u32[]{:S(2)}) collective-permute-start(bf16[128,1024]{1,0:T(8,128)(2,1)S(1)} %copy-done.2), channel_id=1, source_target_pairs={{0,4},{4,0},{8,12},{12,8},{16,20},{20,16},{24,28},{28,24},{1,5},{5... | collective-permute-start | bytes 786440 | tf_op jit(solution)/shard_map/ppermute | solution.py:895
  297.4 24.5 %collective-permute-start.41 = (bf16[128,1024]{1,0:T(8,128)(2,1)}, bf16[128,1024]{1,0:T(8,128)(2,1)}, u32[]{:S(2)}, u32[]{:S(2)}) collective-permute-start(bf16[128,1024]{1,0:T(8,128)(2,1)} %collective-permute-done.37.refs_1_), channel_id=1, source_target_pairs={{0,4},{4,0},{8,12},{12,8},{16,20},{20,16},{24,28},{28,24},{1,5},{5... | collective-permute-start | bytes 786440 | tf_op jit(solution)/shard_map/ppermute | solution.py:895
  304.4 17.4 %collective-permute-start.42 = (bf16[128,1024]{1,0:T(8,128)(2,1)}, bf16[128,1024]{1,0:T(8,128)(2,1)}, u32[]{:S(2)}, u32[]{:S(2)}) collective-permute-start(bf16[128,1024]{1,0:T(8,128)(2,1)} %collective-permute-done.38.refs_2_), channel_id=1, source_target_pairs={{0,4},{4,0},{8,12},{12,8},{16,20},{20,16},{24,28},{28,24},{1,5},{5... | collective-permute-start | bytes 786440 | tf_op jit(solution)/shard_map/ppermute | solution.py:895
  307.4 14.4 %collective-permute-start.43 = (bf16[128,1024]{1,0:T(8,128)(2,1)}, bf16[128,1024]{1,0:T(8,128)(2,1)}, u32[]{:S(2)}, u32[]{:S(2)}) collective-permute-start(bf16[128,1024]{1,0:T(8,128)(2,1)} %collective-permute-done.39.refs_3_), channel_id=1, source_target_pairs={{0,4},{4,0},{8,12},{12,8},{16,20},{20,16},{24,28},{28,24},{1,5},{5... | collective-permute-start | bytes 786440 | tf_op jit(solution)/shard_map/ppermute | solution.py:895
  309.0 6.8 %collective-permute-start.36 = (bf16[128,1024]{1,0:T(8,128)(2,1)}, bf16[128,1024]{1,0:T(8,128)(2,1)}, u32[]{:S(2)}, u32[]{:S(2)}) collective-permute-start(bf16[128,1024]{1,0:T(8,128)(2,1)} %get-tuple-element.279), channel_id=1, source_target_pairs={{0,8},{4,12},{8,0},{12,4},{16,24},{20,28},{24,16},{28,20},{1,9},{5... | collective-permute-start | bytes 786440 | tf_op jit(solution)/shard_map/ppermute | solution.py:895
  315.8 14.6 %collective-permute-start.35 = (bf16[128,1024]{1,0:T(8,128)(2,1)}, bf16[128,1024]{1,0:T(8,128)(2,1)}, u32[]{:S(2)}, u32[]{:S(2)}) collective-permute-start(bf16[128,1024]{1,0:T(8,128)(2,1)} %get-tuple-element.278), channel_id=1, source_target_pairs={{0,16},{4,20},{8,24},{12,28},{16,0},{20,4},{24,8},{28,12},{1,17},{... | collective-permute-start | bytes 786440 | tf_op jit(solution)/shard_map/ppermute | solution.py:895
  332.1 18.3 %collective-permute-start.48 = (bf16[128,1024]{1,0:T(8,128)(2,1)}, bf16[128,1024]{1,0:T(8,128)(2,1)S(1)}, u32[]{:S(2)}, u32[]{:S(2)}) collective-permute-start(bf16[128,1024]{1,0:T(8,128)(2,1)} %shard_map.387.refs_0_), channel_id=1, source_target_pairs={{0,16},{4,20},{8,24},{12,28},{16,0},{20,4},{24,8},{28,12},{1,17},{... | collective-permute-start | bytes 786440 | tf_op jit(solution)/shard_map/ppermute | solution.py:895
  332.8 17.7 %all-to-all-start.2 = ((bf16[4,4,1024]{2,1,0:T(4,128)(2,1)}), bf16[4,4,1024]{2,1,0:T(4,128)(2,1)}, u32[]{:S(2)}, u32[]{:S(2)}) async-start(bf16[4,4,1024]{2,1,0:T(4,128)(2,1)} %broadcast_in_dim.51), calls=%async_computation.2 | async-start | bytes 65536 | tf_op jit(solution)/shard_map/all_to_all | solution.py:1436
  336.6 15.2 %collective-permute-start.44 = (bf16[64,1024]{1,0:T(8,128)(2,1)}, bf16[64,1024]{1,0:T(8,128)(2,1)S(1)}, u32[]{:S(2)}, u32[]{:S(2)}) collective-permute-start(bf16[64,1024]{1,0:T(8,128)(2,1)} %get-tuple-element.295), channel_id=1, source_target_pairs={{0,16},{4,20},{8,24},{12,28},{16,0},{20,4},{24,8},{28,12},{1,17},{... | collective-permute-start | bytes 393224 | tf_op jit(solution)/shard_map/ppermute | solution.py:895
  339.7 23.8 %collective-permute-start.49 = (bf16[128,1024]{1,0:T(8,128)(2,1)}, bf16[128,1024]{1,0:T(8,128)(2,1)}, u32[]{:S(2)}, u32[]{:S(2)}) collective-permute-start(bf16[128,1024]{1,0:T(8,128)(2,1)} %shard_map.387.refs_0_), channel_id=1, source_target_pairs={{0,8},{4,12},{8,0},{12,4},{16,24},{20,28},{24,16},{28,20},{1,9},{5... | collective-permute-start | bytes 786440 | tf_op jit(solution)/shard_map/ppermute | solution.py:895
  350.5 13.5 %collective-permute-start.50 = (bf16[128,1024]{1,0:T(8,128)(2,1)S(1)}, bf16[128,1024]{1,0:T(8,128)(2,1)}, u32[]{:S(2)}, u32[]{:S(2)}) collective-permute-start(bf16[128,1024]{1,0:T(8,128)(2,1)S(1)} %collective-permute-done.48.refs_1_), channel_id=1, source_target_pairs={{0,8},{4,12},{8,0},{12,4},{16,24},{20,28},{24,16},{28,20},{1,9},{5... | collective-permute-start | bytes 786440 | tf_op jit(solution)/shard_map/ppermute | solution.py:895
  354.2 7.8 %collective-permute-start.45 = (bf16[64,1024]{1,0:T(8,128)(2,1)}, bf16[64,1024]{1,0:T(8,128)(2,1)S(1)}, u32[]{:S(2)}, u32[]{:S(2)}) collective-permute-start(bf16[64,1024]{1,0:T(8,128)(2,1)} %shard_map.388.refs_0_), channel_id=1, source_target_pairs={{0,16},{4,20},{8,24},{12,28},{16,0},{20,4},{24,8},{28,12},{1,17},{... | collective-permute-start | bytes 393224 | tf_op jit(solution)/shard_map/ppermute | solution.py:895
  354.6 12.7 %collective-permute-start.51 = (bf16[128,1024]{1,0:T(8,128)(2,1)}, bf16[128,1024]{1,0:T(8,128)(2,1)}, u32[]{:S(2)}, u32[]{:S(2)}) collective-permute-start(bf16[128,1024]{1,0:T(8,128)(2,1)} %shard_map.387.refs_0_), channel_id=1, source_target_pairs={{0,4},{4,0},{8,12},{12,8},{16,20},{20,16},{24,28},{28,24},{1,5},{5... | collective-permute-start | bytes 786440 | tf_op jit(solution)/shard_map/ppermute | solution.py:895
  356.1 9.8 %collective-permute-start.46 = (bf16[64,1024]{1,0:T(8,128)(2,1)}, bf16[64,1024]{1,0:T(8,128)(2,1)}, u32[]{:S(2)}, u32[]{:S(2)}) collective-permute-start(bf16[64,1024]{1,0:T(8,128)(2,1)} %shard_map.388.refs_0_), channel_id=1, source_target_pairs={{0,8},{4,12},{8,0},{12,4},{16,24},{20,28},{24,16},{28,20},{1,9},{5... | collective-permute-start | bytes 393224 | tf_op jit(solution)/shard_map/ppermute | solution.py:895
  362.0 9.4 %collective-permute-start.52 = (bf16[128,1024]{1,0:T(8,128)(2,1)S(1)}, bf16[128,1024]{1,0:T(8,128)(2,1)}, u32[]{:S(2)}, u32[]{:S(2)}) collective-permute-start(bf16[128,1024]{1,0:T(8,128)(2,1)S(1)} %collective-permute-done.48.refs_1_), channel_id=1, source_target_pairs={{0,4},{4,0},{8,12},{12,8},{16,20},{20,16},{24,28},{28,24},{1,5},{5... | collective-permute-start | bytes 786440 | tf_op jit(solution)/shard_map/ppermute | solution.py:895
  363.5 13.0 %collective-permute-start.53 = (bf16[128,1024]{1,0:T(8,128)(2,1)}, bf16[128,1024]{1,0:T(8,128)(2,1)}, u32[]{:S(2)}, u32[]{:S(2)}) collective-permute-start(bf16[128,1024]{1,0:T(8,128)(2,1)} %collective-permute-done.49.refs_2_), channel_id=1, source_target_pairs={{0,4},{4,0},{8,12},{12,8},{16,20},{20,16},{24,28},{28,24},{1,5},{5... | collective-permute-start | bytes 786440 | tf_op jit(solution)/shard_map/ppermute | solution.py:895
  364.0 15.3 %collective-permute-start.54 = (bf16[128,1024]{1,0:T(8,128)(2,1)}, bf16[128,1024]{1,0:T(8,128)(2,1)}, u32[]{:S(2)}, u32[]{:S(2)}) collective-permute-start(bf16[128,1024]{1,0:T(8,128)(2,1)} %collective-permute-done.50.refs_3_), channel_id=1, source_target_pairs={{0,4},{4,0},{8,12},{12,8},{16,20},{20,16},{24,28},{28,24},{1,5},{5... | collective-permute-start | bytes 786440 | tf_op jit(solution)/shard_map/ppermute | solution.py:895
  365.9 5.5 %collective-permute-start.47 = (bf16[64,1024]{1,0:T(8,128)(2,1)S(1)}, bf16[64,1024]{1,0:T(8,128)(2,1)}, u32[]{:S(2)}, u32[]{:S(2)}) collective-permute-start(bf16[64,1024]{1,0:T(8,128)(2,1)S(1)} %collective-permute-done.45.refs_1_), channel_id=1, source_target_pairs={{0,8},{4,12},{8,0},{12,4},{16,24},{20,28},{24,16},{28,20},{1,9},{5... | collective-permute-start | bytes 393224 | tf_op jit(solution)/shard_map/ppermute | solution.py:895
  381.9 11.2 %collective-permute-start.56 = (bf16[256,1024]{1,0:T(8,128)(2,1)}, bf16[256,1024]{1,0:T(8,128)(2,1)}, u32[]{:S(2)}, u32[]{:S(2)}) collective-permute-start(bf16[256,1024]{1,0:T(8,128)(2,1)} %shard_map.389.refs_0_), channel_id=1, source_target_pairs={{0,2},{1,3},{2,0},{3,1},{4,6},{5,7},{6,4},{7,5},{8,10},{9,11},{10,... | collective-permute-start | bytes 1572872 | tf_op jit(solution)/shard_map/ppermute | solution.py:895
  383.6 13.4 %collective-permute-start.55 = (bf16[256,1024]{1,0:T(8,128)(2,1)}, bf16[256,1024]{1,0:T(8,128)(2,1)}, u32[]{:S(2)}, u32[]{:S(2)}) collective-permute-start(bf16[256,1024]{1,0:T(8,128)(2,1)} %shard_map.389.refs_0_), channel_id=1, source_target_pairs={{0,4},{4,0},{8,12},{12,8},{16,20},{20,16},{24,28},{28,24},{1,5},{5... | collective-permute-start | bytes 1572872 | tf_op jit(solution)/shard_map/ppermute | solution.py:895
  393.0 12.7 %collective-permute-start.57 = (bf16[256,1024]{1,0:T(8,128)(2,1)}, bf16[256,1024]{1,0:T(8,128)(2,1)}, u32[]{:S(2)}, u32[]{:S(2)}) collective-permute-start(bf16[256,1024]{1,0:T(8,128)(2,1)} %collective-permute-done.56.refs_2_), channel_id=1, source_target_pairs={{0,4},{4,0},{8,12},{12,8},{16,20},{20,16},{24,28},{28,24},{1,5},{5... | collective-permute-start | bytes 1572872 | tf_op jit(solution)/shard_map/ppermute | solution.py:895
  394.6 15.0 %collective-permute-start.58 = (bf16[256,1024]{1,0:T(8,128)(2,1)}, bf16[256,1024]{1,0:T(8,128)(2,1)}, u32[]{:S(2)}, u32[]{:S(2)}) collective-permute-start(bf16[256,1024]{1,0:T(8,128)(2,1)} %shard_map.389.refs_0_), channel_id=1, source_target_pairs={{0,1},{1,0},{2,3},{3,2},{4,5},{5,4},{6,7},{7,6},{8,9},{9,8},{10,11... | collective-permute-start | bytes 1572872 | tf_op jit(solution)/shard_map/ppermute | solution.py:895
  394.6 15.0 %collective-permute-start.60 = (bf16[256,1024]{1,0:T(8,128)(2,1)}, bf16[256,1024]{1,0:T(8,128)(2,1)}, u32[]{:S(2)}, u32[]{:S(2)}) collective-permute-start(bf16[256,1024]{1,0:T(8,128)(2,1)} %collective-permute-done.56.refs_2_), channel_id=1, source_target_pairs={{0,1},{1,0},{2,3},{3,2},{4,5},{5,4},{6,7},{7,6},{8,9},{9,8},{10,11... | collective-permute-start | bytes 1572872 | tf_op jit(solution)/shard_map/ppermute | solution.py:895
  396.9 12.7 %collective-permute-start.59 = (bf16[256,1024]{1,0:T(8,128)(2,1)}, bf16[256,1024]{1,0:T(8,128)(2,1)}, u32[]{:S(2)}, u32[]{:S(2)}) collective-permute-start(bf16[256,1024]{1,0:T(8,128)(2,1)} %collective-permute-done.55.refs_1_), channel_id=1, source_target_pairs={{0,1},{1,0},{2,3},{3,2},{4,5},{5,4},{6,7},{7,6},{8,9},{9,8},{10,11... | collective-permute-start | bytes 1572872 | tf_op jit(solution)/shard_map/ppermute | solution.py:895
  405.7 3.9 collective-permute-start.61
  (22 other events, 194.5 us)

commit v5 on v3

--- a/solution.py
+++ b/solution.py
@@ -815,11 +815,11 @@
         copy.wait()
 
 
-def text_unpack(count, group, starts_ref, own_ref, *refs):
+def text_unpack(count, group, utterances, starts_ref, own_ref, *refs):
     pieces = refs[:count]
     project_ref, in_ref, out_ref, taps_ref, bias_ref, gain_ref = refs[count : count + 6]
-    hidden_ref, frame_ref, qkv_bias_ref, up_bias_ref, mods_ref = refs[count + 6 : count + 11]
-    stack_ref, sems, lines_ref = refs[count + 11 :]
+    hidden_ref, frame_ref, qkv_bias_ref, up_bias_ref = refs[count + 6 : count + 10]
+    mod_ref, mod_bias_ref, stack_ref, sems, lines_ref = refs[count + 10 :]
     bring(starts_ref, pieces, stack_ref, sems)
     own = own_ref[0]
     wide = in_ref.shape[0]
@@ -834,7 +834,27 @@
     out_ref[wide:, :] = stack_ref[2 * wide : 3 * wide, wide:].astype(F32)
     lines_ref[...] = stack_ref[small_at : small_at + small_rows(group), :].astype(F32)
     mods_at = small_at + small_rows(group)
-    mods_ref[...] = stack_ref[mods_at : mods_at + mods_ref.shape[0], :]
+    mods = stack_ref[mods_at : mods_at + 8 * utterances, :].astype(F32)
+    mods = mods.reshape(utterances, 8, mods.shape[1])
+    place = lax.broadcasted_iota(jnp.int32, mods.shape, 1)
+
+    def block_rows(at):
+        return jnp.sum(jnp.where(place == at, mods, 0.0), axis=1)
+
+    active = block_rows(6).astype(BF16)
+    unit = mod_ref.shape[1] // 3
+    share = mods.shape[2] // unit
+    for at in range(3):
+        index = own * 3 + at
+        line = block_rows(index // share)
+        piece = line[:, 0:unit]
+        for other in range(1, share):
+            piece = jnp.where(
+                index % share == other, line[:, other * unit : (other + 1) * unit], piece
+            )
+        cut = slice(at * unit, (at + 1) * unit)
+        mod_bias_ref[:, cut] = jnp.sum(piece, axis=0, keepdims=True)
+        mod_ref[:, cut] = inner_rows(active, piece.astype(BF16))
 
     def half(at):
         return lines_ref[at // 2 : at // 2 + 1, (at % 2) * wide : (at % 2 + 1) * wide]
@@ -1195,6 +1215,11 @@
             for fetch in fetches[2:]:
                 fetch.share(normed)
                 fetch.core(0, normed)
+            own_index = jnp.stack([own, own_data * group + own]).astype(jnp.int32)
+            own_active = lax.dynamic_index_in_dim(activated_low, own, 0)
+            before, own_index, own_active = lax.optimization_barrier(
+                (before, own_index, own_active)
+            )
             (before,) = after([before], *[fetch.slots[2][0] for fetch in fetches[2:]])
         chosen = range(turn * parts, (turn + 1) * parts)
         qkv_here = [fetches[0].slots[slot] for slot in chosen]
@@ -1339,8 +1364,6 @@
     stack_rows = 3 * text_width + mels
     stack_rows += -stack_rows % 16 + small_rows(group) + 8 * group * data
     stack_rows += -stack_rows % (16 * group * data)
-    own_index = jnp.stack([own, own_data * group + own]).astype(jnp.int32)
-    own_active = lax.dynamic_index_in_dim(activated_low, own, 0)
     results = run_kernel(
         partial(text_backward, group),
         1,
@@ -1435,7 +1458,7 @@
             token = member.step(token)
 
     weight_up, weight_down = unpack(ffn_unpack, ffn_data, ff_in, ff_out, attn_data.pieces[0])
-    text_half = text_data.half(weight_up, *list(attn_data.pieces.values())[1:])
+    text_half = text_data.half(weight_up, *list(attn_data.pieces.values())[1:-2])
     weight_qkv, weight_out = unpack(attn_unpack, attn_data, qkv_weight, out_weight, text_half)
     text_halves = {0: [text_half]}
     for slot in range(2, group, 2):
@@ -1465,25 +1488,20 @@
         (3, width),
         (1, units),
     )
-    mods_shape = (8 * group * data, model_width)
+    mods_shape = mod_weight.shape
     unpacked = run_kernel(
-        partial(text_unpack, len(text_pieces), group),
+        partial(text_unpack, len(text_pieces), group, group * data),
         1,
         [(SMEM, jnp.stack(text_starts).astype(jnp.int32)), (SMEM, own_index)]
         + [(ANY, member) for member in text_pieces],
         [(whole(shape), shape, F32) for shape in unpacked]
-        + [(whole(mods_shape), mods_shape, BF16)],
+        + [(whole(shape), shape, F32) for shape in (mods_shape, (1, columns))],
         [
             pltpu.VMEM((stack_rows, model_width), BF16),
             semaphores(len(text_pieces), 1),
             pltpu.VMEM((small_rows(group), model_width), F32),
         ],
     )
-    seen = unpacked[10].reshape(group * data, 8, model_width)
-    grad_mod_all = seen[:, :6].reshape(group * data, 6 * model_width)
-    grad_mod_all = lax.dynamic_slice_in_dim(grad_mod_all, own * columns, columns, axis=1)
-    grad_mod_weight = inner_rows(seen[:, 6], grad_mod_all)
-    grad_mod_bias = jnp.sum(grad_mod_all.astype(F32), axis=0)
     return (
         output,
         grad_text,
@@ -1496,8 +1514,8 @@
         unpacked[2],
         unpacked[0],
         unpacked[7],
-        grad_mod_weight,
-        grad_mod_bias,
+        unpacked[10],
+        unpacked[11][0],
         weight_qkv,
         unpacked[8],
         weight_out,

time: 425 us -> 421 us (level)
  waiting for transfers between devices: 116 us -> 123 us
  starting transfers between devices: 64.5 us -> 60.2 us
    ppermute x62, waiting for transfers between devices: 116 us -> 121 us  [swap(): lax.ppermute(array, axis, [(at, at ^ bit) for at in range(lax.axis_size(a...]
    ppermute x62, starting transfers between devices: 53.9 us -> 49.6 us  [swap(): lax.ppermute(array, axis, [(at, at ^ bit) for at in range(lax.axis_size(a...]
  transfers between devices with their start and end apart: 65 -> 65, of which waited for: 24 -> 27; matrix products, arithmetic and copies ran while one was open for 7% -> 7% of each run, Pallas kernels for 38% -> 38%
where the time goes in v5:
time: 421 us; the launch traced here: 417 us
  Pallas kernels  195 us (46%)
  waiting for transfers between devices  123 us (29%)
  starting transfers between devices  60.2 us (14%)
  local copies, waits for them, and re-layouts  22.2 us (5%)
  other arithmetic  11.4 us (3%)
    pallas_call x26, Pallas kernels, run_kernel(): pl.pallas_call(kernel, grid=(parts,), in_specs=[spec for spec, _ in input...  195 us
    ppermute x62, waiting for transfers between devices, swap(): lax.ppermute(array, axis, [(at, at ^ bit) for at in range(lax.axis_size(a...  121 us
    ppermute x62, starting transfers between devices, swap(): lax.ppermute(array, axis, [(at, at ^ bit) for at in range(lax.axis_size(a...  49.6 us
  transfers between devices with their start and end apart: 65, of which 27 were waited for; matrix products, arithmetic and copies ran while one was open for 7% of the time, Pallas kernels for 38%

profile of v5, /device:TPU:0, one launch (start us, length us, event | category | flops | bytes accessed | tf_op | source)
XLA Modules:
  0.0 416.8 jit_solution(8870973998056308577)
XLA Ops:
  0.7 1.8 constant_dynamic-slice_fusion.3
  2.5 3.0 collective-permute-start.1
  5.5 2.1 constant_dynamic-slice_fusion.4
  9.5 1.7 copy.61
  13.6 1.8 pad_maximum_fusion.mel_ref.refs_3_
  15.3 9.7 %shard_map.366 = (bf16[512,512]{1,0:T(8,128)(2,1)}, f32[512,1024]{1,0:T(8,128)}, f32[8,1024]{1,0:T(8,128)}, bf16[512,1024]{1,0:T(8,128)(2,1)}, bf16[512,512]{1,0:T(8,128)(2,1)}, /*index=5*/f32[512,1024]{1,0:T(8,128)}) custom-call(bf16[512,512]{1,0:T(8,128)(2,1)} %refs_2_.1, bf16[512,200]{1,0:T(8,128)(2,1)} %pad_maximum_fusion.mel_ref.refs_3_, ...), custom_call_target="tpu_custom_call" | custom-call | flops 1024 | bytes 1024 | tf_op jit(solution)/shard_map/pallas_call | solution.py:897
  27.4 3.5 all-to-all-start
  30.9 1.9 constant_dynamic-slice_fusion.1
  32.8 1.9 constant_dynamic-slice_fusion
  34.7 1.8 fusion.1
  37.1 1.8 collective-permute-start.2
  40.8 2.0 collective-permute-start.10
  42.9 14.4 %shard_map.367 = (bf16[2,512,256]{2,1,0:T(8,128)(2,1)}, bf16[2,512,256]{2,1,0:T(8,128)(2,1)}, bf16[2,512,256]{2,1,0:T(8,128)(2,1)}, bf16[2,512,256]{2,1,0:T(8,12...) custom-call(s32[1]{0:T(128)} %dynamic_slice.19.refs_0_, s32[1]{0:T(128)} %bitcast.refs_1_.refs_0_, ...), custom_call_target="tpu_custom_call" | custom-call | flops 1024 | bytes 1024 | tf_op jit(solution)/shard_map/pallas_call | solution.py:897
  57.5 1.7 collective-permute-start.7
  59.4 6.8 %collective-permute-done.7.refs_13_.refs_19_ = bf16[128,1024]{1,0:T(8,128)(2,1)S(1)} collective-permute-done((bf16[128,1024]{1,0:T(8,128)(2,1)S(1)}, bf16[128,1024]{1,0:T(8,128)(2,1)S(1)}, u32[]{:S(2)}, u32[]{:S(2)}) %collective-permute-start.7) | collective-permute-done | bytes 262176 | tf_op jit(solution)/shard_map/ppermute | solution.py:915
  66.8 2.1 collective-permute-done.8.refs_14_.refs_16_
  68.8 1.7 collective-permute-start.16
  73.1 17.9 %shard_map.368 = (bf16[2,512,256]{2,1,0:T(8,128)(2,1)}, bf16[2,512,256]{2,1,0:T(8,128)(2,1)}, bf16[2,512,256]{2,1,0:T(8,128)(2,1)}, bf16[2,512,256]{2,1,0:T(8,12...) custom-call(s32[1]{0:T(128)} %dynamic_slice.19.refs_0_, ...), custom_call_target="tpu_custom_call" | custom-call | flops 1024 | bytes 1024 | tf_op jit(solution)/shard_map/pallas_call | solution.py:897
  91.1 3.3 collective-permute-done.12.refs_11_
  98.9 25.5 %shard_map.369 = (f32[4,1,512]{2,1,0:T(1,128)}, f32[8,1024]{1,0:T(8,128)}, bf16[1024,1024]{1,0:T(8,128)(2,1)}, bf16[1024,1024]{1,0:T(8,128)(2,1)}, bf16[1024,102...) custom-call(s32[1]{0:T(128)} %bitcast.refs_1_.refs_0_, ...), custom_call_target="tpu_custom_call" | custom-call | flops 1024 | bytes 1024 | tf_op jit(solution)/shard_map/pallas_call | solution.py:897
  124.5 20.1 %shard_map.370 = (f32[2,3,256]{2,1,0:T(4,128)}, bf16[1024,1024]{1,0:T(8,128)(2,1)}, bf16[1024,1024]{1,0:T(8,128)(2,1)}, f32[512,1024]{1,0:T(8,128)}) custom-call(s32[1]{0:T(128)} %dynamic_slice.19.refs_0_, s32[1]{0:T(128)} %bitcast.refs_1_.refs_0_, bf16[512,1024]{1,0:T(8,128)(2,1)} %get-tuple-element.202.refs_2_, ...), custom_call_target="tpu_custom_call" | custom-call | flops 1024 | bytes 1024 | tf_op jit(solution)/shard_map/pallas_call | solution.py:897
  145.2 4.3 %shard_map.371 = bf16[1024,1024]{1,0:T(8,128)(2,1)} custom-call(bf16[1024,1024]{1,0:T(8,128)(2,1)} %get-tuple-element.216.refs_0_, bf16[1024,1024]{1,0:T(8,128)(2,1)} %collective-permute-done.20.refs_1_), custom_call_target="tpu_custom_call" | custom-call | flops 1024 | bytes 1024 | tf_op jit(solution)/shard_map/pallas_call | solution.py:897
  149.5 1.9 collective-permute-start.23
  151.4 23.2 %shard_map.372 = (f32[2,3,256]{2,1,0:T(4,128)}, bf16[1024,1024]{1,0:T(8,128)(2,1)}, bf16[1024,1024]{1,0:T(8,128)(2,1)}, bf16[512,1024]{1,0:T(8,128)(2,1)}, f32[8,1024]{1,0:T(8,128)}) custom-call(s32[1]{0:T(128)} %dynamic_slice.19.refs_0_, s32[1]{0:T(128)} %bitcast.refs_1_.refs_0_, bf16[512,1024]{1,0:T(8,128)(2,1)} %get-tuple-element.202.refs_2_, ...), custom_call_target="tpu_custom_call" | custom-call | flops 1024 | bytes 1024 | tf_op jit(solution)/shard_map/pallas_call | solution.py:897
  174.7 4.3 %shard_map.373 = bf16[1024,1024]{1,0:T(8,128)(2,1)} custom-call(bf16[1024,1024]{1,0:T(8,128)(2,1)} %get-tuple-element.223.refs_0_, bf16[1024,1024]{1,0:T(8,128)(2,1)} %collective-permute-done.21.refs_1_), custom_call_target="tpu_custom_call" | custom-call | flops 1024 | bytes 1024 | tf_op jit(solution)/shard_map/pallas_call | solution.py:897
  179.3 21.4 %shard_map.374 = (f32[512,512]{1,0:T(8,128)}, bf16[6,1024]{1,0:T(8,128)(2,1)}, bf16[512,1024]{1,0:T(8,128)(2,1)}, bf16[512,1024]{1,0:T(8,128)(2,1)}, bf16[512,10...) custom-call(s32[2]{0:T(128)} %pad_add_fusion.refs_0_.own_ref, bf16[512,1024]{1,0:T(8,128)(2,1)} %get-tuple-element.225.refs_1_, ...), custom_call_target="tpu_custom_call" | custom-call | flops 1024 | bytes 1024 | tf_op jit(solution)/shard_map/pallas_call | solution.py:897
  201.0 4.2 %shard_map.375 = (bf16[512,1024]{1,0:T(8,128)(2,1)}, bf16[512,1024]{1,0:T(8,128)(2,1)}) custom-call(s32[1]{0:T(128)} %bitcast.refs_1_.refs_0_, bf16[1024,1024]{1,0:T(8,128)(2,1)} %get-tuple-element.244.refs_1_.refs_4_, bf16[1024,1024]{1,0:T(8,128)(2,1)} %collective-permute-done.23.refs_2_.refs_5_, ...), custom_call_target="tpu_custom_call" | custom-call | flops 1024 | bytes 1024 | tf_op jit(solution)/shard_map/pallas_call | solution.py:897
  206.9 2.6 shard_map.376
  209.5 1.7 collective-permute-start.25
  211.2 19.7 %collective-permute-done.27.refs_2_.refs_4_ = bf16[512,1024]{1,0:T(8,128)(2,1)} collective-permute-done((bf16[512,1024]{1,0:T(8,128)(2,1)}, bf16[512,1024]{1,0:T(8,128)(2,1)}, u32[]{:S(2)}, u32[]{:S(2)}) %collective-permute-start.27) | collective-permute-done | bytes 1048608 | tf_op jit(solution)/shard_map/ppermute | solution.py:915
  230.9 2.8 shard_map.377
  233.7 9.6 %collective-permute-done.29.refs_2_.refs_5_ = bf16[1024,1024]{1,0:T(8,128)(2,1)} collective-permute-done((bf16[1024,1024]{1,0:T(8,128)(2,1)}, bf16[1024,1024]{1,0:T(8,128)(2,1)}, u32[]{:S(2)}, u32[]{:S(2)}) %collective-permute-start.29) | collective-permute-done | bytes 2097184 | tf_op jit(solution)/shard_map/ppermute | solution.py:915
  243.2 4.2 %shard_map.378 = (bf16[512,1024]{1,0:T(8,128)(2,1)}, bf16[512,1024]{1,0:T(8,128)(2,1)}) custom-call(s32[1]{0:T(128)} %bitcast.refs_1_.refs_0_, bf16[1024,1024]{1,0:T(8,128)(2,1)} %get-tuple-element.258.refs_1_.refs_4_, bf16[1024,1024]{1,0:T(8,128)(2,1)} %collective-permute-done.29.refs_2_.refs_5_, ...), custom_call_target="tpu_custom_call" | custom-call | flops 1024 | bytes 1024 | tf_op jit(solution)/shard_map/pallas_call | solution.py:897
  247.4 1.7 collective-permute-start.33
  250.7 11.3 %collective-permute-done.28.refs_2_.refs_4_ = bf16[256,1024]{1,0:T(8,128)(2,1)} collective-permute-done((bf16[256,1024]{1,0:T(8,128)(2,1)}, bf16[256,1024]{1,0:T(8,128)(2,1)}, u32[]{:S(2)}, u32[]{:S(2)}) %collective-permute-start.28) | collective-permute-done | bytes 524320 | tf_op jit(solution)/shard_map/ppermute | solution.py:915
  262.0 2.1 shard_map.379
  265.3 3.2 shard_map.380
  270.1 2.6 collective-permute-start.32
  272.9 2.8 shard_map.381
  277.3 7.2 %collective-permute-done.32.refs_1_ = bf16[128,1024]{1,0:T(8,128)(2,1)S(1)} collective-permute-done((bf16[128,1024]{1,0:T(8,128)(2,1)}, bf16[128,1024]{1,0:T(8,128)(2,1)S(1)}, u32[]{:S(2)}, u32[]{:S(2)}) %collective-permute-start.32) | collective-permute-done | bytes 262176 | tf_op jit(solution)/shard_map/ppermute | solution.py:915
  285.1 1.8 shard_map.382.refs_0_
  287.7 2.1 shard_map.383
  291.2 3.3 all-to-all-start.1
  294.5 4.0 collective-permute-start.36
  299.5 2.1 shard_map.384
  301.7 3.6 collective-permute-start.42
  305.4 5.0 %collective-permute-done.41.refs_1_ = bf16[128,1024]{1,0:T(8,128)(2,1)} collective-permute-done((bf16[128,1024]{1,0:T(8,128)(2,1)S(1)}, bf16[128,1024]{1,0:T(8,128)(2,1)}, u32[]{:S(2)}, u32[]{:S(2)}) %collective-permute-start.41) | collective-permute-done | bytes 262176 | tf_op jit(solution)/shard_map/ppermute | solution.py:915
  311.4 1.9 shard_map.385
  314.3 7.2 %collective-permute-done.35.refs_1_ = bf16[128,1024]{1,0:T(8,128)(2,1)S(1)} collective-permute-done((bf16[128,1024]{1,0:T(8,128)(2,1)}, bf16[128,1024]{1,0:T(8,128)(2,1)S(1)}, u32[]{:S(2)}, u32[]{:S(2)}) %collective-permute-start.35) | collective-permute-done | bytes 262176 | tf_op jit(solution)/shard_map/ppermute | solution.py:915
  322.2 1.8 shard_map.386.refs_0_
  324.7 3.9 all-to-all-start.2
  333.9 1.7 shard_map.387.refs_0_
  336.4 1.7 collective-permute-done.46.refs_6_
  338.6 5.1 %collective-permute-done.45.refs_5_ = bf16[128,1024]{1,0:T(8,128)(2,1)} collective-permute-done((bf16[128,1024]{1,0:T(8,128)(2,1)}, bf16[128,1024]{1,0:T(8,128)(2,1)}, u32[]{:S(2)}, u32[]{:S(2)}) %collective-permute-start.45) | collective-permute-done | bytes 262176 | tf_op jit(solution)/shard_map/ppermute | solution.py:915
  343.7 5.6 %collective-permute-done.47.refs_7_ = bf16[128,1024]{1,0:T(8,128)(2,1)} collective-permute-done((bf16[128,1024]{1,0:T(8,128)(2,1)}, bf16[128,1024]{1,0:T(8,128)(2,1)}, u32[]{:S(2)}, u32[]{:S(2)}) %collective-permute-start.47) | collective-permute-done | bytes 262176 | tf_op jit(solution)/shard_map/ppermute | solution.py:915
  351.1 5.1 %collective-permute-done.38.refs_1_ = bf16[64,1024]{1,0:T(8,128)(2,1)} collective-permute-done((bf16[64,1024]{1,0:T(8,128)(2,1)}, bf16[64,1024]{1,0:T(8,128)(2,1)}, u32[]{:S(2)}, u32[]{:S(2)}) %collective-permute-start.38) | collective-permute-done | bytes 131104 | tf_op jit(solution)/shard_map/ppermute | solution.py:915
  357.5 4.4 %shard_map.388 = (f32[1024,512]{1,0:T(8,128)}, f32[512,1024]{1,0:T(8,128)}) custom-call(s32[8]{0:T(128)} %stack.112.starts_ref, bf16[128,1024]{1,0:T(8,128)(2,1)} %shard_map.382.refs_0_, bf16[128,1024]{1,0:T(8,128)(2,1)} %collective-permute-done.41.refs_1_, bf16[128,1024]{1,0:T(8,128)(2,1)} %collective-permute-done.42.refs_2_, ...), custom_call_target="tpu_custom_call" | custom-call | flops 1024 | bytes 1024 | tf_op jit(solution)/shard_map/pallas_call | solution.py:897
  363.4 2.6 shard_map.389.refs_0_
  370.1 6.2 %collective-permute-done.55.refs_6_ = bf16[128,1024]{1,0:T(8,128)(2,1)S(1)} collective-permute-done((bf16[128,1024]{1,0:T(8,128)(2,1)}, bf16[128,1024]{1,0:T(8,128)(2,1)S(1)}, u32[]{:S(2)}, u32[]{:S(2)}) %collective-permute-start.55) | collective-permute-done | bytes 262176 | tf_op jit(solution)/shard_map/ppermute | solution.py:915
  376.2 5.6 %collective-permute-done.56.refs_7_ = bf16[128,1024]{1,0:T(8,128)(2,1)S(1)} collective-permute-done((bf16[128,1024]{1,0:T(8,128)(2,1)}, bf16[128,1024]{1,0:T(8,128)(2,1)S(1)}, u32[]{:S(2)}, u32[]{:S(2)}) %collective-permute-start.56) | collective-permute-done | bytes 262176 | tf_op jit(solution)/shard_map/ppermute | solution.py:915
  382.6 4.4 %shard_map.390 = (f32[3,1024,256]{2,1,0:T(8,128)}, f32[256,1024]{1,0:T(8,128)}) custom-call(s32[8]{0:T(128)} %stack.112.starts_ref, bf16[128,1024]{1,0:T(8,128)(2,1)} %shard_map.386.refs_0_, bf16[128,1024]{1,0:T(8,128)(2,1)} %collective-permute-done.48.refs_1_, bf16[128,1024]{1,0:T(8,128)(2,1)} %collective-permute-done.49.refs_2_, ...), custom_call_target="tpu_custom_call" | custom-call | flops 1024 | bytes 1024 | tf_op jit(solution)/shard_map/pallas_call | solution.py:897
  388.9 4.3 %collective-permute-done.53.refs_1_ = bf16[256,1024]{1,0:T(8,128)(2,1)} collective-permute-done((bf16[256,1024]{1,0:T(8,128)(2,1)}, bf16[256,1024]{1,0:T(8,128)(2,1)}, u32[]{:S(2)}, u32[]{:S(2)}) %collective-permute-start.53) | collective-permute-done | bytes 524320 | tf_op jit(solution)/shard_map/ppermute | solution.py:915
  393.2 8.4 %collective-permute-done.57.refs_3_ = bf16[256,1024]{1,0:T(8,128)(2,1)} collective-permute-done((bf16[256,1024]{1,0:T(8,128)(2,1)}, bf16[256,1024]{1,0:T(8,128)(2,1)}, u32[]{:S(2)}, u32[]{:S(2)}) %collective-permute-start.57) | collective-permute-done | bytes 524320 | tf_op jit(solution)/shard_map/ppermute | solution.py:915
  405.5 9.8 %shard_map.391 = (f32[712,1024]{1,0:T(8,128)}, f32[512,1024]{1,0:T(8,128)}, f32[1024,512]{1,0:T(8,128)}, f32[7,512]{1,0:T(8,128)}, f32[3,512]{1,0:T(4,128)}, /*i...) custom-call(s32[8]{0:T(128)} %stack.98.starts_ref, ...), custom_call_target="tpu_custom_call" | custom-call | flops 1024 | bytes 1024 | tf_op jit(solution)/shard_map/pallas_call | solution.py:897
  (190 shorter events, 54.3 us)
Async XLA Ops:
  2.5 40.3 %collective-permute-start.1 = (bf16[128,1024]{1,0:T(8,128)(2,1)}, bf16[128,1024]{1,0:T(8,128)(2,1)S(1)}, u32[]{:S(2)}, u32[]{:S(2)}) collective-permute-start(bf16[128,1024]{1,0:T(8,128)(2,1)} %constant_dynamic-slice_fusion.3), channel_id=1, source_target_pairs={{0,2},{1,3},{2,0},{3,1},{4,6},{5,7},{6,4},{7,5},{8,10},{9,11},{10,... | collective-permute-start | bytes 786440 | tf_op jit(solution)/shard_map/ppermute | solution.py:915
  5.5 37.4 %collective-permute-start.4 = (bf16[256,1024]{1,0:T(8,128)(2,1)}, bf16[256,1024]{1,0:T(8,128)(2,1)}, u32[]{:S(2)}, u32[]{:S(2)}) collective-permute-start(bf16[256,1024]{1,0:T(8,128)(2,1)} %refs_15_.2), channel_id=1, source_target_pairs={{0,1},{1,0},{2,3},{3,2},{4,5},{5,4},{6,7},{7,6},{8,9},{9,8},{10,11... | collective-permute-start | bytes 1572872 | tf_op jit(solution)/shard_map/ppermute | solution.py:915
  7.6 29.6 %collective-permute-start = (bf16[3,512,256]{2,1,0:T(8,128)(2,1)}, bf16[3,512,256]{2,1,0:T(8,128)(2,1)}, u32[]{:S(2)}, u32[]{:S(2)}) collective-permute-start(bf16[3,512,256]{2,1,0:T(8,128)(2,1)} %constant_dynamic-slice_fusion.4), channel_id=1, source_target_pairs={{0,2},{1,3},{2,0},{3,1},{4,6},{5,7},{6,4},{7,5},{8,10},{9,11},{10,... | collective-permute-start | bytes 2359304 | tf_op jit(solution)/shard_map/ppermute | solution.py:915
  7.6 35.3 %collective-permute-start.3 = (bf16[3,1024,256]{2,1,0:T(8,128)(2,1)}, bf16[3,1024,256]{2,1,0:T(8,128)(2,1)}, u32[]{:S(2)}, u32[]{:S(2)}) collective-permute-start(bf16[3,1024,256]{2,1,0:T(8,128)(2,1)} %refs_13_.4), channel_id=1, source_target_pairs={{0,1},{1,0},{2,3},{3,2},{4,5},{5,4},{6,7},{7,6},{8,9},{9,8},{10,11... | collective-permute-start | bytes 4718600 | tf_op jit(solution)/shard_map/ppermute | solution.py:915
  27.4 9.7 %all-to-all-start = ((bf16[4,2,1408]{2,1,0:T(2,128)(2,1)}), bf16[4,2,1408]{2,1,0:T(2,128)(2,1)S(1)}, u32[]{:S(2)}, u32[]{:S(2)}) async-start(bf16[4,2,1408]{2,1,0:T(2,128)(2,1)} %reshape.182), calls=%async_computation | async-start | bytes 45056 | tf_op jit(solution)/shard_map/all_to_all | solution.py:1195
  37.1 20.3 %collective-permute-start.2 = (bf16[3,512,256]{2,1,0:T(8,128)(2,1)}, bf16[3,512,256]{2,1,0:T(8,128)(2,1)}, u32[]{:S(2)}, u32[]{:S(2)}) collective-permute-start(bf16[3,512,256]{2,1,0:T(8,128)(2,1)} %collective-permute-done.refs_8_.refs_14_), channel_id=1, source_target_pairs={{0,4},{4,0},{8,12},{12,8},{16,20},{20,16},{24,28},{28,24},{1,5},{5... | collective-permute-start | bytes 2359304 | tf_op jit(solution)/shard_map/ppermute | solution.py:915
  40.8 25.3 %collective-permute-start.10 = (bf16[512,512]{1,0:T(8,128)(2,1)}, bf16[512,512]{1,0:T(8,128)(2,1)}, u32[]{:S(2)}, u32[]{:S(2)}) collective-permute-start(bf16[512,512]{1,0:T(8,128)(2,1)} %constant_dynamic-slice_fusion.1), channel_id=1, source_target_pairs={{0,2},{1,3},{2,0},{3,1},{4,6},{5,7},{6,4},{7,5},{8,10},{9,11},{10,... | collective-permute-start | bytes 1572872 | tf_op jit(solution)/shard_map/ppermute | solution.py:915
  42.8 23.9 %collective-permute-start.11 = (bf16[256,1024]{1,0:T(8,128)(2,1)}, bf16[256,1024]{1,0:T(8,128)(2,1)}, u32[]{:S(2)}, u32[]{:S(2)}) collective-permute-start(bf16[256,1024]{1,0:T(8,128)(2,1)} %constant_dynamic-slice_fusion), channel_id=1, source_target_pairs={{0,2},{1,3},{2,0},{3,1},{4,6},{5,7},{6,4},{7,5},{8,10},{9,11},{10,... | collective-permute-start | bytes 1572872 | tf_op jit(solution)/shard_map/ppermute | solution.py:915
  57.4 13.8 %collective-permute-start.5 = (bf16[3,512,256]{2,1,0:T(8,128)(2,1)}, bf16[3,512,256]{2,1,0:T(8,128)(2,1)}, u32[]{:S(2)}, u32[]{:S(2)}) collective-permute-start(bf16[3,512,256]{2,1,0:T(8,128)(2,1)} %collective-permute-done.refs_8_.refs_14_), channel_id=1, source_target_pairs={{0,1},{1,0},{2,3},{3,2},{4,5},{5,4},{6,7},{7,6},{8,9},{9,8},{10,11... | collective-permute-start | bytes 2359304 | tf_op jit(solution)/shard_map/ppermute | solution.py:915
  57.5 8.7 %collective-permute-start.7 = (bf16[128,1024]{1,0:T(8,128)(2,1)S(1)}, bf16[128,1024]{1,0:T(8,128)(2,1)S(1)}, u32[]{:S(2)}, u32[]{:S(2)}) collective-permute-start(bf16[128,1024]{1,0:T(8,128)(2,1)S(1)} %collective-permute-done.1.refs_12_.refs_18_), channel_id=1, source_target_pairs={{0,4},{4,0},{8,12},{12,8},{16,20},{20,16},{24,28},{28,24},{1,5},{5... | collective-permute-start | bytes 786440 | tf_op jit(solution)/shard_map/ppermute | solution.py:915
  59.2 35.7 %collective-permute-start.15 = (bf16[1024,512]{1,0:T(8,128)(2,1)}, bf16[1024,512]{1,0:T(8,128)(2,1)}, u32[]{:S(2)}, u32[]{:S(2)}) collective-permute-start(bf16[1024,512]{1,0:T(8,128)(2,1)} %refs_13_.3), channel_id=1, source_target_pairs={{0,1},{1,0},{2,3},{3,2},{4,5},{5,4},{6,7},{7,6},{8,9},{9,8},{10,11... | collective-permute-start | bytes 3145736 | tf_op jit(solution)/shard_map/ppermute | solution.py:915
  66.2 7.0 %collective-permute-start.6 = (bf16[3,512,256]{2,1,0:T(8,128)(2,1)}, bf16[3,512,256]{2,1,0:T(8,128)(2,1)}, u32[]{:S(2)}, u32[]{:S(2)}) collective-permute-start(bf16[3,512,256]{2,1,0:T(8,128)(2,1)} %collective-permute-done.2.refs_9_.refs_15_), channel_id=1, source_target_pairs={{0,1},{1,0},{2,3},{3,2},{4,5},{5,4},{6,7},{7,6},{8,9},{9,8},{10,11... | collective-permute-start | bytes 2359304 | tf_op jit(solution)/shard_map/ppermute | solution.py:915
  66.7 3.9 collective-permute-start.9
  68.8 22.2 %collective-permute-start.16 = (bf16[256,1024]{1,0:T(8,128)(2,1)}, bf16[256,1024]{1,0:T(8,128)(2,1)}, u32[]{:S(2)}, u32[]{:S(2)}) collective-permute-start(bf16[256,1024]{1,0:T(8,128)(2,1)} %collective-permute-done.11.refs_16_), channel_id=1, source_target_pairs={{0,4},{4,0},{8,12},{12,8},{16,20},{20,16},{24,28},{28,24},{1,5},{5... | collective-permute-start | bytes 1572872 | tf_op jit(solution)/shard_map/ppermute | solution.py:915
  70.6 23.8 %collective-permute-start.12 = (bf16[512,512]{1,0:T(8,128)(2,1)}, bf16[512,512]{1,0:T(8,128)(2,1)}, u32[]{:S(2)}, u32[]{:S(2)}) collective-permute-start(bf16[512,512]{1,0:T(8,128)(2,1)} %collective-permute-done.10.refs_10_), channel_id=1, source_target_pairs={{0,4},{4,0},{8,12},{12,8},{16,20},{20,16},{24,28},{28,24},{1,5},{5... | collective-permute-start | bytes 1572872 | tf_op jit(solution)/shard_map/ppermute | solution.py:915
  71.3 24.7 %collective-permute-start.19 = (bf16[512,1024]{1,0:T(8,128)(2,1)}, bf16[512,1024]{1,0:T(8,128)(2,1)}, u32[]{:S(2)}, u32[]{:S(2)}) collective-permute-start(bf16[512,1024]{1,0:T(8,128)(2,1)} %refs_19_.1), channel_id=1, source_target_pairs={{0,1},{1,0},{2,3},{3,2},{4,5},{5,4},{6,7},{7,6},{8,9},{9,8},{10,11... | collective-permute-start | bytes 3145736 | tf_op jit(solution)/shard_map/ppermute | solution.py:915
  94.4 2.8 collective-permute-start.13
  94.4 3.0 collective-permute-start.14
  94.9 3.2 collective-permute-start.17
  94.9 4.0 collective-permute-start.18
  124.3 20.9 %collective-permute-start.20 = (bf16[1024,1024]{1,0:T(8,128)(2,1)}, bf16[1024,1024]{1,0:T(8,128)(2,1)}, u32[]{:S(2)}, u32[]{:S(2)}) collective-permute-start(bf16[1024,1024]{1,0:T(8,128)(2,1)} %get-tuple-element.215), channel_id=1, source_target_pairs={{0,1},{1,0},{2,3},{3,2},{4,5},{5,4},{6,7},{7,6},{8,9},{9,8},{10,11... | collective-permute-start | bytes 6291464 | tf_op jit(solution)/shard_map/ppermute | solution.py:915
  144.6 30.1 %collective-permute-start.21 = (bf16[1024,1024]{1,0:T(8,128)(2,1)}, bf16[1024,1024]{1,0:T(8,128)(2,1)}, u32[]{:S(2)}, u32[]{:S(2)}) collective-permute-start(bf16[1024,1024]{1,0:T(8,128)(2,1)} %get-tuple-element.222), channel_id=1, source_target_pairs={{0,1},{1,0},{2,3},{3,2},{4,5},{5,4},{6,7},{7,6},{8,9},{9,8},{10,11... | collective-permute-start | bytes 6291464 | tf_op jit(solution)/shard_map/ppermute | solution.py:915
  145.1 55.9 %collective-permute-start.24 = (bf16[1024,1024]{1,0:T(8,128)(2,1)}, bf16[1024,1024]{1,0:T(8,128)(2,1)}, u32[]{:S(2)}, u32[]{:S(2)}) collective-permute-start(bf16[1024,1024]{1,0:T(8,128)(2,1)} %get-tuple-element.243), channel_id=1, source_target_pairs={{0,1},{1,0},{2,3},{3,2},{4,5},{5,4},{6,7},{7,6},{8,9},{9,8},{10,11... | collective-permute-start | bytes 6291464 | tf_op jit(solution)/shard_map/ppermute | solution.py:915
  149.5 51.5 %collective-permute-start.23 = (bf16[1024,1024]{1,0:T(8,128)(2,1)}, bf16[1024,1024]{1,0:T(8,128)(2,1)}, u32[]{:S(2)}, u32[]{:S(2)}) collective-permute-start(bf16[1024,1024]{1,0:T(8,128)(2,1)} %shard_map.371), channel_id=1, source_target_pairs={{0,2},{1,3},{2,0},{3,1},{4,6},{5,7},{6,4},{7,5},{8,10},{9,11},{10,... | collective-permute-start | bytes 6291464 | tf_op jit(solution)/shard_map/ppermute | solution.py:915
  174.6 59.1 %collective-permute-start.30 = (bf16[1024,1024]{1,0:T(8,128)(2,1)}, bf16[1024,1024]{1,0:T(8,128)(2,1)}, u32[]{:S(2)}, u32[]{:S(2)}) collective-permute-start(bf16[1024,1024]{1,0:T(8,128)(2,1)} %get-tuple-element.257), channel_id=1, source_target_pairs={{0,1},{1,0},{2,3},{3,2},{4,5},{5,4},{6,7},{7,6},{8,9},{9,8},{10,11... | collective-permute-start | bytes 6291464 | tf_op jit(solution)/shard_map/ppermute | solution.py:915
  179.0 64.2 %collective-permute-start.29 = (bf16[1024,1024]{1,0:T(8,128)(2,1)}, bf16[1024,1024]{1,0:T(8,128)(2,1)}, u32[]{:S(2)}, u32[]{:S(2)}) collective-permute-start(bf16[1024,1024]{1,0:T(8,128)(2,1)} %shard_map.373), channel_id=1, source_target_pairs={{0,2},{1,3},{2,0},{3,1},{4,6},{5,7},{6,4},{7,5},{8,10},{9,11},{10,... | collective-permute-start | bytes 6291464 | tf_op jit(solution)/shard_map/ppermute | solution.py:915
  200.8 6.1 %collective-permute-start.22 = (bf16[512,1024]{1,0:T(8,128)(2,1)}, bf16[512,1024]{1,0:T(8,128)(2,1)}, u32[]{:S(2)}, u32[]{:S(2)}) collective-permute-start(bf16[512,1024]{1,0:T(8,128)(2,1)} %get-tuple-element.241), channel_id=1, source_target_pairs={{0,1},{1,0},{2,3},{3,2},{4,5},{5,4},{6,7},{7,6},{8,9},{9,8},{10,11... | collective-permute-start | bytes 3145736 | tf_op jit(solution)/shard_map/ppermute | solution.py:915
  205.2 25.7 %collective-permute-start.27 = (bf16[512,1024]{1,0:T(8,128)(2,1)}, bf16[512,1024]{1,0:T(8,128)(2,1)}, u32[]{:S(2)}, u32[]{:S(2)}) collective-permute-start(bf16[512,1024]{1,0:T(8,128)(2,1)} %get-tuple-element.251), channel_id=1, source_target_pairs={{0,4},{4,0},{8,12},{12,8},{16,20},{20,16},{24,28},{28,24},{1,5},{5... | collective-permute-start | bytes 3145736 | tf_op jit(solution)/shard_map/ppermute | solution.py:915
  206.8 57.3 %collective-permute-start.26 = (bf16[512,1024]{1,0:T(8,128)(2,1)}, bf16[512,1024]{1,0:T(8,128)(2,1)}, u32[]{:S(2)}, u32[]{:S(2)}) collective-permute-start(bf16[512,1024]{1,0:T(8,128)(2,1)} %get-tuple-element.250), channel_id=1, source_target_pairs={{0,1},{1,0},{2,3},{3,2},{4,5},{5,4},{6,7},{7,6},{8,9},{9,8},{10,11... | collective-permute-start | bytes 3145736 | tf_op jit(solution)/shard_map/ppermute | solution.py:915
  209.5 55.8 %collective-permute-start.25 = (bf16[512,1024]{1,0:T(8,128)(2,1)}, bf16[512,1024]{1,0:T(8,128)(2,1)}, u32[]{:S(2)}, u32[]{:S(2)}) collective-permute-start(bf16[512,1024]{1,0:T(8,128)(2,1)} %shard_map.376), channel_id=1, source_target_pairs={{0,2},{1,3},{2,0},{3,1},{4,6},{5,7},{6,4},{7,5},{8,10},{9,11},{10,... | collective-permute-start | bytes 3145736 | tf_op jit(solution)/shard_map/ppermute | solution.py:915
  247.4 25.5 %collective-permute-start.33 = (bf16[512,1024]{1,0:T(8,128)(2,1)}, bf16[512,1024]{1,0:T(8,128)(2,1)}, u32[]{:S(2)}, u32[]{:S(2)}) collective-permute-start(bf16[512,1024]{1,0:T(8,128)(2,1)} %get-tuple-element.271), channel_id=1, source_target_pairs={{0,4},{4,0},{8,12},{12,8},{16,20},{20,16},{24,28},{28,24},{1,5},{5... | collective-permute-start | bytes 3145736 | tf_op jit(solution)/shard_map/ppermute | solution.py:915
  249.1 12.9 %collective-permute-start.28 = (bf16[256,1024]{1,0:T(8,128)(2,1)}, bf16[256,1024]{1,0:T(8,128)(2,1)}, u32[]{:S(2)}, u32[]{:S(2)}) collective-permute-start(bf16[256,1024]{1,0:T(8,128)(2,1)} %get-tuple-element.255), channel_id=1, source_target_pairs={{0,8},{4,12},{8,0},{12,4},{16,24},{20,28},{24,16},{28,20},{1,9},{5... | collective-permute-start | bytes 1572872 | tf_op jit(solution)/shard_map/ppermute | solution.py:915
  268.5 18.4 %collective-permute-start.31 = (bf16[256,1024]{1,0:T(8,128)(2,1)}, bf16[256,1024]{1,0:T(8,128)(2,1)S(1)}, u32[]{:S(2)}, u32[]{:S(2)}) collective-permute-start(bf16[256,1024]{1,0:T(8,128)(2,1)} %get-tuple-element.269), channel_id=1, source_target_pairs={{0,4},{4,0},{8,12},{12,8},{16,20},{20,16},{24,28},{28,24},{1,5},{5... | collective-permute-start | bytes 1572872 | tf_op jit(solution)/shard_map/ppermute | solution.py:915
  270.1 14.3 %collective-permute-start.32 = (bf16[128,1024]{1,0:T(8,128)(2,1)}, bf16[128,1024]{1,0:T(8,128)(2,1)S(1)}, u32[]{:S(2)}, u32[]{:S(2)}) collective-permute-start(bf16[128,1024]{1,0:T(8,128)(2,1)} %get-tuple-element.270), channel_id=1, source_target_pairs={{0,16},{4,20},{8,24},{12,28},{16,0},{20,4},{24,8},{28,12},{1,17},{... | collective-permute-start | bytes 786440 | tf_op jit(solution)/shard_map/ppermute | solution.py:915
  275.7 23.8 %collective-permute-start.34 = (bf16[256,1024]{1,0:T(8,128)(2,1)}, bf16[256,1024]{1,0:T(8,128)(2,1)}, u32[]{:S(2)}, u32[]{:S(2)}) collective-permute-start(bf16[256,1024]{1,0:T(8,128)(2,1)} %get-tuple-element.281), channel_id=1, source_target_pairs={{0,8},{4,12},{8,0},{12,4},{16,24},{20,28},{24,16},{28,20},{1,9},{5... | collective-permute-start | bytes 1572872 | tf_op jit(solution)/shard_map/ppermute | solution.py:915
  291.2 7.4 %all-to-all-start.1 = ((bf16[4,2,768]{2,1,0:T(2,128)(2,1)}), bf16[4,2,768]{2,1,0:T(2,128)(2,1)S(1)}, u32[]{:S(2)}, u32[]{:S(2)}) async-start(bf16[4,2,768]{2,1,0:T(2,128)(2,1)} %reshape.184), calls=%async_computation.1 | async-start | bytes 24576 | tf_op jit(solution)/shard_map/all_to_all | solution.py:1448
  294.5 15.9 %collective-permute-start.41 = (bf16[128,1024]{1,0:T(8,128)(2,1)S(1)}, bf16[128,1024]{1,0:T(8,128)(2,1)}, u32[]{:S(2)}, u32[]{:S(2)}) collective-permute-start(bf16[128,1024]{1,0:T(8,128)(2,1)S(1)} %copy-done.2), channel_id=1, source_target_pairs={{0,16},{4,20},{8,24},{12,28},{16,0},{20,4},{24,8},{28,12},{1,17},{... | collective-permute-start | bytes 786440 | tf_op jit(solution)/shard_map/ppermute | solution.py:915
  294.5 16.8 %collective-permute-start.36 = (bf16[128,1024]{1,0:T(8,128)(2,1)}, bf16[128,1024]{1,0:T(8,128)(2,1)}, u32[]{:S(2)}, u32[]{:S(2)}) collective-permute-start(bf16[128,1024]{1,0:T(8,128)(2,1)} %get-tuple-element.286), channel_id=1, source_target_pairs={{0,8},{4,12},{8,0},{12,4},{16,24},{20,28},{24,16},{28,20},{1,9},{5... | collective-permute-start | bytes 786440 | tf_op jit(solution)/shard_map/ppermute | solution.py:915
  301.6 19.9 %collective-permute-start.35 = (bf16[128,1024]{1,0:T(8,128)(2,1)}, bf16[128,1024]{1,0:T(8,128)(2,1)S(1)}, u32[]{:S(2)}, u32[]{:S(2)}) collective-permute-start(bf16[128,1024]{1,0:T(8,128)(2,1)} %get-tuple-element.285), channel_id=1, source_target_pairs={{0,16},{4,20},{8,24},{12,28},{16,0},{20,4},{24,8},{28,12},{1,17},{... | collective-permute-start | bytes 786440 | tf_op jit(solution)/shard_map/ppermute | solution.py:915
  301.7 26.8 %collective-permute-start.42 = (bf16[128,1024]{1,0:T(8,128)(2,1)S(1)}, bf16[128,1024]{1,0:T(8,128)(2,1)}, u32[]{:S(2)}, u32[]{:S(2)}) collective-permute-start(bf16[128,1024]{1,0:T(8,128)(2,1)S(1)} %copy-done.2), channel_id=1, source_target_pairs={{0,8},{4,12},{8,0},{12,4},{16,24},{20,28},{24,16},{28,20},{1,9},{5... | collective-permute-start | bytes 786440 | tf_op jit(solution)/shard_map/ppermute | solution.py:915
  310.4 20.3 %collective-permute-start.43 = (bf16[128,1024]{1,0:T(8,128)(2,1)}, bf16[128,1024]{1,0:T(8,128)(2,1)}, u32[]{:S(2)}, u32[]{:S(2)}) collective-permute-start(bf16[128,1024]{1,0:T(8,128)(2,1)} %collective-permute-done.41.refs_1_), channel_id=1, source_target_pairs={{0,8},{4,12},{8,0},{12,4},{16,24},{20,28},{24,16},{28,20},{1,9},{5... | collective-permute-start | bytes 786440 | tf_op jit(solution)/shard_map/ppermute | solution.py:915
  313.2 17.9 %collective-permute-start.37 = (bf16[64,1024]{1,0:T(8,128)(2,1)}, bf16[64,1024]{1,0:T(8,128)(2,1)S(1)}, u32[]{:S(2)}, u32[]{:S(2)}) collective-permute-start(bf16[64,1024]{1,0:T(8,128)(2,1)} %get-tuple-element.293), channel_id=1, source_target_pairs={{0,16},{4,20},{8,24},{12,28},{16,0},{20,4},{24,8},{28,12},{1,17},{... | collective-permute-start | bytes 393224 | tf_op jit(solution)/shard_map/ppermute | solution.py:915
  313.8 21.8 %collective-permute-start.44 = (bf16[128,1024]{1,0:T(8,128)(2,1)S(1)}, bf16[128,1024]{1,0:T(8,128)(2,1)}, u32[]{:S(2)}, u32[]{:S(2)}) collective-permute-start(bf16[128,1024]{1,0:T(8,128)(2,1)S(1)} %copy-done.2), channel_id=1, source_target_pairs={{0,4},{4,0},{8,12},{12,8},{16,20},{20,16},{24,28},{28,24},{1,5},{5... | collective-permute-start | bytes 786440 | tf_op jit(solution)/shard_map/ppermute | solution.py:915
  324.7 7.9 %all-to-all-start.2 = ((bf16[4,4,1024]{2,1,0:T(4,128)(2,1)}), bf16[4,4,1024]{2,1,0:T(4,128)(2,1)}, u32[]{:S(2)}, u32[]{:S(2)}) async-start(bf16[4,4,1024]{2,1,0:T(4,128)(2,1)} %broadcast_in_dim.51), calls=%async_computation.2 | async-start | bytes 65536 | tf_op jit(solution)/shard_map/all_to_all | solution.py:1454
  328.5 9.5 %collective-permute-start.46 = (bf16[128,1024]{1,0:T(8,128)(2,1)}, bf16[128,1024]{1,0:T(8,128)(2,1)}, u32[]{:S(2)}, u32[]{:S(2)}) collective-permute-start(bf16[128,1024]{1,0:T(8,128)(2,1)} %collective-permute-done.42.refs_2_), channel_id=1, source_target_pairs={{0,4},{4,0},{8,12},{12,8},{16,20},{20,16},{24,28},{28,24},{1,5},{5... | collective-permute-start | bytes 786440 | tf_op jit(solution)/shard_map/ppermute | solution.py:915
  329.2 14.5 %collective-permute-start.45 = (bf16[128,1024]{1,0:T(8,128)(2,1)}, bf16[128,1024]{1,0:T(8,128)(2,1)}, u32[]{:S(2)}, u32[]{:S(2)}) collective-permute-start(bf16[128,1024]{1,0:T(8,128)(2,1)} %collective-permute-done.41.refs_1_), channel_id=1, source_target_pairs={{0,4},{4,0},{8,12},{12,8},{16,20},{20,16},{24,28},{28,24},{1,5},{5... | collective-permute-start | bytes 786440 | tf_op jit(solution)/shard_map/ppermute | solution.py:915
  330.7 18.6 %collective-permute-start.47 = (bf16[128,1024]{1,0:T(8,128)(2,1)}, bf16[128,1024]{1,0:T(8,128)(2,1)}, u32[]{:S(2)}, u32[]{:S(2)}) collective-permute-start(bf16[128,1024]{1,0:T(8,128)(2,1)} %collective-permute-done.43.refs_3_), channel_id=1, source_target_pairs={{0,4},{4,0},{8,12},{12,8},{16,20},{20,16},{24,28},{28,24},{1,5},{5... | collective-permute-start | bytes 786440 | tf_op jit(solution)/shard_map/ppermute | solution.py:915
  331.2 18.1 %collective-permute-start.48 = (bf16[128,1024]{1,0:T(8,128)(2,1)}, bf16[128,1024]{1,0:T(8,128)(2,1)}, u32[]{:S(2)}, u32[]{:S(2)}) collective-permute-start(bf16[128,1024]{1,0:T(8,128)(2,1)} %shard_map.386.refs_0_), channel_id=1, source_target_pairs={{0,16},{4,20},{8,24},{12,28},{16,0},{20,4},{24,8},{28,12},{1,17},{... | collective-permute-start | bytes 786440 | tf_op jit(solution)/shard_map/ppermute | solution.py:915
  335.6 14.2 %collective-permute-start.39 = (bf16[64,1024]{1,0:T(8,128)(2,1)}, bf16[64,1024]{1,0:T(8,128)(2,1)S(1)}, u32[]{:S(2)}, u32[]{:S(2)}) collective-permute-start(bf16[64,1024]{1,0:T(8,128)(2,1)} %shard_map.387.refs_0_), channel_id=1, source_target_pairs={{0,8},{4,12},{8,0},{12,4},{16,24},{20,28},{24,16},{28,20},{1,9},{5... | collective-permute-start | bytes 393224 | tf_op jit(solution)/shard_map/ppermute | solution.py:915
  338.1 23.8 %collective-permute-start.51 = (bf16[128,1024]{1,0:T(8,128)(2,1)}, bf16[128,1024]{1,0:T(8,128)(2,1)S(1)}, u32[]{:S(2)}, u32[]{:S(2)}) collective-permute-start(bf16[128,1024]{1,0:T(8,128)(2,1)} %shard_map.386.refs_0_), channel_id=1, source_target_pairs={{0,4},{4,0},{8,12},{12,8},{16,20},{20,16},{24,28},{28,24},{1,5},{5... | collective-permute-start | bytes 786440 | tf_op jit(solution)/shard_map/ppermute | solution.py:915
  343.7 18.2 %collective-permute-start.49 = (bf16[128,1024]{1,0:T(8,128)(2,1)}, bf16[128,1024]{1,0:T(8,128)(2,1)}, u32[]{:S(2)}, u32[]{:S(2)}) collective-permute-start(bf16[128,1024]{1,0:T(8,128)(2,1)} %shard_map.386.refs_0_), channel_id=1, source_target_pairs={{0,8},{4,12},{8,0},{12,4},{16,24},{20,28},{24,16},{28,20},{1,9},{5... | collective-permute-start | bytes 786440 | tf_op jit(solution)/shard_map/ppermute | solution.py:915
  349.3 6.9 %collective-permute-start.38 = (bf16[64,1024]{1,0:T(8,128)(2,1)}, bf16[64,1024]{1,0:T(8,128)(2,1)}, u32[]{:S(2)}, u32[]{:S(2)}) collective-permute-start(bf16[64,1024]{1,0:T(8,128)(2,1)} %shard_map.387.refs_0_), channel_id=1, source_target_pairs={{0,16},{4,20},{8,24},{12,28},{16,0},{20,4},{24,8},{28,12},{1,17},{... | collective-permute-start | bytes 393224 | tf_op jit(solution)/shard_map/ppermute | solution.py:915
  349.3 14.1 %collective-permute-start.52 = (bf16[128,1024]{1,0:T(8,128)(2,1)}, bf16[128,1024]{1,0:T(8,128)(2,1)}, u32[]{:S(2)}, u32[]{:S(2)}) collective-permute-start(bf16[128,1024]{1,0:T(8,128)(2,1)} %collective-permute-done.48.refs_1_), channel_id=1, source_target_pairs={{0,4},{4,0},{8,12},{12,8},{16,20},{20,16},{24,28},{28,24},{1,5},{5... | collective-permute-start | bytes 786440 | tf_op jit(solution)/shard_map/ppermute | solution.py:915
  349.8 13.6 %collective-permute-start.50 = (bf16[128,1024]{1,0:T(8,128)(2,1)}, bf16[128,1024]{1,0:T(8,128)(2,1)}, u32[]{:S(2)}, u32[]{:S(2)}) collective-permute-start(bf16[128,1024]{1,0:T(8,128)(2,1)} %collective-permute-done.48.refs_1_), channel_id=1, source_target_pairs={{0,8},{4,12},{8,0},{12,4},{16,24},{20,28},{24,16},{28,20},{1,9},{5... | collective-permute-start | bytes 786440 | tf_op jit(solution)/shard_map/ppermute | solution.py:915
  356.2 7.2 %collective-permute-start.40 = (bf16[64,1024]{1,0:T(8,128)(2,1)}, bf16[64,1024]{1,0:T(8,128)(2,1)}, u32[]{:S(2)}, u32[]{:S(2)}) collective-permute-start(bf16[64,1024]{1,0:T(8,128)(2,1)} %collective-permute-done.38.refs_1_), channel_id=1, source_target_pairs={{0,8},{4,12},{8,0},{12,4},{16,24},{20,28},{24,16},{28,20},{1,9},{5... | collective-permute-start | bytes 393224 | tf_op jit(solution)/shard_map/ppermute | solution.py:915
  366.0 21.0 %collective-permute-start.54 = (bf16[256,1024]{1,0:T(8,128)(2,1)}, bf16[256,1024]{1,0:T(8,128)(2,1)}, u32[]{:S(2)}, u32[]{:S(2)}) collective-permute-start(bf16[256,1024]{1,0:T(8,128)(2,1)} %shard_map.389.refs_0_), channel_id=1, source_target_pairs={{0,2},{1,3},{2,0},{3,1},{4,6},{5,7},{6,4},{7,5},{8,10},{9,11},{10,... | collective-permute-start | bytes 1572872 | tf_op jit(solution)/shard_map/ppermute | solution.py:915
  366.8 9.5 %collective-permute-start.55 = (bf16[128,1024]{1,0:T(8,128)(2,1)}, bf16[128,1024]{1,0:T(8,128)(2,1)S(1)}, u32[]{:S(2)}, u32[]{:S(2)}) collective-permute-start(bf16[128,1024]{1,0:T(8,128)(2,1)} %collective-permute-done.49.refs_2_), channel_id=1, source_target_pairs={{0,4},{4,0},{8,12},{12,8},{16,20},{20,16},{24,28},{28,24},{1,5},{5... | collective-permute-start | bytes 786440 | tf_op jit(solution)/shard_map/ppermute | solution.py:915
  368.0 13.8 %collective-permute-start.56 = (bf16[128,1024]{1,0:T(8,128)(2,1)}, bf16[128,1024]{1,0:T(8,128)(2,1)S(1)}, u32[]{:S(2)}, u32[]{:S(2)}) collective-permute-start(bf16[128,1024]{1,0:T(8,128)(2,1)} %collective-permute-done.50.refs_3_), channel_id=1, source_target_pairs={{0,4},{4,0},{8,12},{12,8},{16,20},{20,16},{24,28},{28,24},{1,5},{5... | collective-permute-start | bytes 786440 | tf_op jit(solution)/shard_map/ppermute | solution.py:915
  368.8 24.4 %collective-permute-start.53 = (bf16[256,1024]{1,0:T(8,128)(2,1)}, bf16[256,1024]{1,0:T(8,128)(2,1)}, u32[]{:S(2)}, u32[]{:S(2)}) collective-permute-start(bf16[256,1024]{1,0:T(8,128)(2,1)} %shard_map.389.refs_0_), channel_id=1, source_target_pairs={{0,4},{4,0},{8,12},{12,8},{16,20},{20,16},{24,28},{28,24},{1,5},{5... | collective-permute-start | bytes 1572872 | tf_op jit(solution)/shard_map/ppermute | solution.py:915
  387.0 14.6 %collective-permute-start.57 = (bf16[256,1024]{1,0:T(8,128)(2,1)}, bf16[256,1024]{1,0:T(8,128)(2,1)}, u32[]{:S(2)}, u32[]{:S(2)}) collective-permute-start(bf16[256,1024]{1,0:T(8,128)(2,1)} %collective-permute-done.54.refs_2_), channel_id=1, source_target_pairs={{0,4},{4,0},{8,12},{12,8},{16,20},{20,16},{24,28},{28,24},{1,5},{5... | collective-permute-start | bytes 1572872 | tf_op jit(solution)/shard_map/ppermute | solution.py:915
  388.3 17.1 %collective-permute-start.58 = (bf16[256,1024]{1,0:T(8,128)(2,1)}, bf16[256,1024]{1,0:T(8,128)(2,1)}, u32[]{:S(2)}, u32[]{:S(2)}) collective-permute-start(bf16[256,1024]{1,0:T(8,128)(2,1)} %shard_map.389.refs_0_), channel_id=1, source_target_pairs={{0,1},{1,0},{2,3},{3,2},{4,5},{5,4},{6,7},{7,6},{8,9},{9,8},{10,11... | collective-permute-start | bytes 1572872 | tf_op jit(solution)/shard_map/ppermute | solution.py:915
  388.4 17.1 %collective-permute-start.60 = (bf16[256,1024]{1,0:T(8,128)(2,1)}, bf16[256,1024]{1,0:T(8,128)(2,1)}, u32[]{:S(2)}, u32[]{:S(2)}) collective-permute-start(bf16[256,1024]{1,0:T(8,128)(2,1)} %collective-permute-done.54.refs_2_), channel_id=1, source_target_pairs={{0,1},{1,0},{2,3},{3,2},{4,5},{5,4},{6,7},{7,6},{8,9},{9,8},{10,11... | collective-permute-start | bytes 1572872 | tf_op jit(solution)/shard_map/ppermute | solution.py:915
  393.2 12.2 %collective-permute-start.59 = (bf16[256,1024]{1,0:T(8,128)(2,1)}, bf16[256,1024]{1,0:T(8,128)(2,1)}, u32[]{:S(2)}, u32[]{:S(2)}) collective-permute-start(bf16[256,1024]{1,0:T(8,128)(2,1)} %collective-permute-done.53.refs_1_), channel_id=1, source_target_pairs={{0,1},{1,0},{2,3},{3,2},{4,5},{5,4},{6,7},{7,6},{8,9},{9,8},{10,11... | collective-permute-start | bytes 1572872 | tf_op jit(solution)/shard_map/ppermute | solution.py:915
  401.6 3.8 collective-permute-start.61
  (24 other events, 187.1 us)

commit v6 on v5

--- a/solution.py
+++ b/solution.py
@@ -1464,10 +1464,10 @@
     for slot in range(2, group, 2):
         bit = low_bit(slot)
         text_halves[slot] = [swap(text_halves[slot - bit][0], "heads", bit)]
-        text_halves[slot] = list(after(text_halves[slot], weight_qkv))
     for slot in range(0, group, 2):
         text_halves[slot].append(swap(text_halves[slot][0], "dp", 1))
-        text_halves[slot + 1] = [swap(piece, "heads", 1) for piece in text_halves[slot]]
+        pieces = after(text_halves[slot], weight_qkv) if slot else text_halves[slot]
+        text_halves[slot + 1] = [swap(piece, "heads", 1) for piece in pieces]
     slot_rows = stack_rows // group
     text_pieces, text_starts = [], []
     for slot, pieces in text_halves.items():

time: 421 us -> 428 us (1.017)
  waiting for transfers between devices: 123 us -> 129 us
    ppermute x62, waiting for transfers between devices: 121 us -> 128 us  [swap(): lax.ppermute(array, axis, [(at, at ^ bit) for at in range(lax.axis_size(a...]
  transfers between devices with their start and end apart: 65 -> 65, of which waited for: 27 -> 26; matrix products, arithmetic and copies ran while one was open for 7% -> 7% of each run, Pallas kernels for 38% -> 37%
where the time goes in v6:
time: 428 us; the launch traced here: 423 us
  Pallas kernels  195 us (46%)
  waiting for transfers between devices  129 us (30%)
  starting transfers between devices  60 us (14%)
  local copies, waits for them, and re-layouts  22.2 us (5%)
  other arithmetic  11.4 us (3%)
    pallas_call x26, Pallas kernels, run_kernel(): pl.pallas_call(kernel, grid=(parts,), in_specs=[spec for spec, _ in input...  195 us
    ppermute x62, waiting for transfers between devices, swap(): lax.ppermute(array, axis, [(at, at ^ bit) for at in range(lax.axis_size(a...  128 us
    ppermute x62, starting transfers between devices, swap(): lax.ppermute(array, axis, [(at, at ^ bit) for at in range(lax.axis_size(a...  49.4 us
  transfers between devices with their start and end apart: 65, of which 26 were waited for; matrix products, arithmetic and copies ran while one was open for 7% of the time, Pallas kernels for 37%

profile of v6, /device:TPU:0, one launch (start us, length us, event | category | flops | bytes accessed | tf_op | source)
XLA Modules:
  0.0 423.3 jit_solution(14764984857458035982)
XLA Ops:
  0.7 1.8 constant_dynamic-slice_fusion.3
  2.5 3.0 collective-permute-start.1
  5.5 2.1 constant_dynamic-slice_fusion.4
  9.5 1.7 copy.61
  13.6 1.8 pad_maximum_fusion.mel_ref.refs_3_
  15.3 9.7 %shard_map.366 = (bf16[512,512]{1,0:T(8,128)(2,1)}, f32[512,1024]{1,0:T(8,128)}, f32[8,1024]{1,0:T(8,128)}, bf16[512,1024]{1,0:T(8,128)(2,1)}, bf16[512,512]{1,0:T(8,128)(2,1)}, /*index=5*/f32[512,1024]{1,0:T(8,128)}) custom-call(bf16[512,512]{1,0:T(8,128)(2,1)} %refs_2_.1, bf16[512,200]{1,0:T(8,128)(2,1)} %pad_maximum_fusion.mel_ref.refs_3_, ...), custom_call_target="tpu_custom_call" | custom-call | flops 1024 | bytes 1024 | tf_op jit(solution)/shard_map/pallas_call | solution.py:897
  27.4 3.5 all-to-all-start
  30.9 1.9 constant_dynamic-slice_fusion.1
  32.8 1.9 constant_dynamic-slice_fusion
  34.7 1.8 fusion.1
  37.1 1.8 collective-permute-start.2
  40.8 2.0 collective-permute-start.10
  42.9 14.4 %shard_map.367 = (bf16[2,512,256]{2,1,0:T(8,128)(2,1)}, bf16[2,512,256]{2,1,0:T(8,128)(2,1)}, bf16[2,512,256]{2,1,0:T(8,128)(2,1)}, bf16[2,512,256]{2,1,0:T(8,12...) custom-call(s32[1]{0:T(128)} %dynamic_slice.19.refs_0_, s32[1]{0:T(128)} %bitcast.refs_1_.refs_0_, ...), custom_call_target="tpu_custom_call" | custom-call | flops 1024 | bytes 1024 | tf_op jit(solution)/shard_map/pallas_call | solution.py:897
  57.5 1.7 collective-permute-start.7
  59.4 6.8 %collective-permute-done.7.refs_13_.refs_19_ = bf16[128,1024]{1,0:T(8,128)(2,1)S(1)} collective-permute-done((bf16[128,1024]{1,0:T(8,128)(2,1)S(1)}, bf16[128,1024]{1,0:T(8,128)(2,1)S(1)}, u32[]{:S(2)}, u32[]{:S(2)}) %collective-permute-start.7) | collective-permute-done | bytes 262176 | tf_op jit(solution)/shard_map/ppermute | solution.py:915
  66.8 2.1 collective-permute-done.8.refs_14_.refs_16_
  68.8 1.7 collective-permute-start.16
  73.1 17.9 %shard_map.368 = (bf16[2,512,256]{2,1,0:T(8,128)(2,1)}, bf16[2,512,256]{2,1,0:T(8,128)(2,1)}, bf16[2,512,256]{2,1,0:T(8,128)(2,1)}, bf16[2,512,256]{2,1,0:T(8,12...) custom-call(s32[1]{0:T(128)} %dynamic_slice.19.refs_0_, ...), custom_call_target="tpu_custom_call" | custom-call | flops 1024 | bytes 1024 | tf_op jit(solution)/shard_map/pallas_call | solution.py:897
  91.1 3.3 collective-permute-done.12.refs_11_
  98.9 25.5 %shard_map.369 = (f32[4,1,512]{2,1,0:T(1,128)}, f32[8,1024]{1,0:T(8,128)}, bf16[1024,1024]{1,0:T(8,128)(2,1)}, bf16[1024,1024]{1,0:T(8,128)(2,1)}, bf16[1024,102...) custom-call(s32[1]{0:T(128)} %bitcast.refs_1_.refs_0_, ...), custom_call_target="tpu_custom_call" | custom-call | flops 1024 | bytes 1024 | tf_op jit(solution)/shard_map/pallas_call | solution.py:897
  124.5 20.1 %shard_map.370 = (f32[2,3,256]{2,1,0:T(4,128)}, bf16[1024,1024]{1,0:T(8,128)(2,1)}, bf16[1024,1024]{1,0:T(8,128)(2,1)}, f32[512,1024]{1,0:T(8,128)}) custom-call(s32[1]{0:T(128)} %dynamic_slice.19.refs_0_, s32[1]{0:T(128)} %bitcast.refs_1_.refs_0_, bf16[512,1024]{1,0:T(8,128)(2,1)} %get-tuple-element.203.refs_2_, ...), custom_call_target="tpu_custom_call" | custom-call | flops 1024 | bytes 1024 | tf_op jit(solution)/shard_map/pallas_call | solution.py:897
  145.2 4.3 %shard_map.371 = bf16[1024,1024]{1,0:T(8,128)(2,1)} custom-call(bf16[1024,1024]{1,0:T(8,128)(2,1)} %get-tuple-element.217.refs_0_, bf16[1024,1024]{1,0:T(8,128)(2,1)} %collective-permute-done.20.refs_1_), custom_call_target="tpu_custom_call" | custom-call | flops 1024 | bytes 1024 | tf_op jit(solution)/shard_map/pallas_call | solution.py:897
  149.5 1.9 collective-permute-start.23
  151.4 23.2 %shard_map.372 = (f32[2,3,256]{2,1,0:T(4,128)}, bf16[1024,1024]{1,0:T(8,128)(2,1)}, bf16[1024,1024]{1,0:T(8,128)(2,1)}, bf16[512,1024]{1,0:T(8,128)(2,1)}, f32[8,1024]{1,0:T(8,128)}) custom-call(s32[1]{0:T(128)} %dynamic_slice.19.refs_0_, s32[1]{0:T(128)} %bitcast.refs_1_.refs_0_, bf16[512,1024]{1,0:T(8,128)(2,1)} %get-tuple-element.203.refs_2_, ...), custom_call_target="tpu_custom_call" | custom-call | flops 1024 | bytes 1024 | tf_op jit(solution)/shard_map/pallas_call | solution.py:897
  174.7 4.3 %shard_map.373 = bf16[1024,1024]{1,0:T(8,128)(2,1)} custom-call(bf16[1024,1024]{1,0:T(8,128)(2,1)} %get-tuple-element.224.refs_0_, bf16[1024,1024]{1,0:T(8,128)(2,1)} %collective-permute-done.21.refs_1_), custom_call_target="tpu_custom_call" | custom-call | flops 1024 | bytes 1024 | tf_op jit(solution)/shard_map/pallas_call | solution.py:897
  179.3 21.4 %shard_map.374 = (f32[512,512]{1,0:T(8,128)}, bf16[6,1024]{1,0:T(8,128)(2,1)}, bf16[512,1024]{1,0:T(8,128)(2,1)}, bf16[512,1024]{1,0:T(8,128)(2,1)}, bf16[512,10...) custom-call(s32[2]{0:T(128)} %pad_add_fusion.refs_0_.own_ref, bf16[512,1024]{1,0:T(8,128)(2,1)} %get-tuple-element.226.refs_1_, ...), custom_call_target="tpu_custom_call" | custom-call | flops 1024 | bytes 1024 | tf_op jit(solution)/shard_map/pallas_call | solution.py:897
  201.0 4.2 shard_map.375
  205.2 1.6 collective-permute-start.27
  206.9 2.6 shard_map.376
  209.5 1.7 collective-permute-start.25
  211.2 19.7 %collective-permute-done.27.refs_2_.refs_4_ = bf16[512,1024]{1,0:T(8,128)(2,1)} collective-permute-done((bf16[512,1024]{1,0:T(8,128)(2,1)}, bf16[512,1024]{1,0:T(8,128)(2,1)}, u32[]{:S(2)}, u32[]{:S(2)}) %collective-permute-start.27) | collective-permute-done | bytes 1048608 | tf_op jit(solution)/shard_map/ppermute | solution.py:915
  230.9 2.8 shard_map.377
  233.7 9.6 %collective-permute-done.29.refs_2_.refs_5_ = bf16[1024,1024]{1,0:T(8,128)(2,1)} collective-permute-done((bf16[1024,1024]{1,0:T(8,128)(2,1)}, bf16[1024,1024]{1,0:T(8,128)(2,1)}, u32[]{:S(2)}, u32[]{:S(2)}) %collective-permute-start.29) | collective-permute-done | bytes 2097184 | tf_op jit(solution)/shard_map/ppermute | solution.py:915
  243.2 4.2 shard_map.378
  247.4 1.7 collective-permute-start.33
  250.7 11.3 %collective-permute-done.28.refs_2_.refs_4_ = bf16[256,1024]{1,0:T(8,128)(2,1)} collective-permute-done((bf16[256,1024]{1,0:T(8,128)(2,1)}, bf16[256,1024]{1,0:T(8,128)(2,1)}, u32[]{:S(2)}, u32[]{:S(2)}) %collective-permute-start.28) | collective-permute-done | bytes 524320 | tf_op jit(solution)/shard_map/ppermute | solution.py:915
  262.0 2.1 shard_map.379
  265.3 3.2 shard_map.380
  270.1 2.6 collective-permute-start.32
  272.9 2.8 shard_map.381
  277.3 7.2 %collective-permute-done.32.refs_1_ = bf16[128,1024]{1,0:T(8,128)(2,1)S(1)} collective-permute-done((bf16[128,1024]{1,0:T(8,128)(2,1)}, bf16[128,1024]{1,0:T(8,128)(2,1)S(1)}, u32[]{:S(2)}, u32[]{:S(2)}) %collective-permute-start.32) | collective-permute-done | bytes 262176 | tf_op jit(solution)/shard_map/ppermute | solution.py:915
  285.1 1.8 shard_map.382.refs_0_
  287.7 2.1 shard_map.383
  291.2 3.3 all-to-all-start.1
  294.5 4.0 collective-permute-start.36
  299.5 2.1 shard_map.384
  301.7 3.6 collective-permute-start.42
  305.4 5.0 %collective-permute-done.41.refs_1_ = bf16[128,1024]{1,0:T(8,128)(2,1)} collective-permute-done((bf16[128,1024]{1,0:T(8,128)(2,1)S(1)}, bf16[128,1024]{1,0:T(8,128)(2,1)}, u32[]{:S(2)}, u32[]{:S(2)}) %collective-permute-start.41) | collective-permute-done | bytes 262176 | tf_op jit(solution)/shard_map/ppermute | solution.py:915
  311.4 1.9 shard_map.385
  314.3 7.2 %collective-permute-done.35.refs_1_ = bf16[128,1024]{1,0:T(8,128)(2,1)S(1)} collective-permute-done((bf16[128,1024]{1,0:T(8,128)(2,1)}, bf16[128,1024]{1,0:T(8,128)(2,1)S(1)}, u32[]{:S(2)}, u32[]{:S(2)}) %collective-permute-start.35) | collective-permute-done | bytes 262176 | tf_op jit(solution)/shard_map/ppermute | solution.py:915
  322.2 1.8 shard_map.386.refs_0_
  324.7 3.9 all-to-all-start.2
  333.9 1.7 shard_map.387.refs_0_
  336.4 1.7 collective-permute-done.46.refs_6_
  338.6 5.1 %collective-permute-done.45.refs_5_ = bf16[128,1024]{1,0:T(8,128)(2,1)} collective-permute-done((bf16[128,1024]{1,0:T(8,128)(2,1)}, bf16[128,1024]{1,0:T(8,128)(2,1)}, u32[]{:S(2)}, u32[]{:S(2)}) %collective-permute-start.45) | collective-permute-done | bytes 262176 | tf_op jit(solution)/shard_map/ppermute | solution.py:915
  343.7 5.6 %collective-permute-done.47.refs_7_ = bf16[128,1024]{1,0:T(8,128)(2,1)} collective-permute-done((bf16[128,1024]{1,0:T(8,128)(2,1)}, bf16[128,1024]{1,0:T(8,128)(2,1)}, u32[]{:S(2)}, u32[]{:S(2)}) %collective-permute-start.47) | collective-permute-done | bytes 262176 | tf_op jit(solution)/shard_map/ppermute | solution.py:915
  351.1 5.1 %collective-permute-done.38.refs_1_ = bf16[64,1024]{1,0:T(8,128)(2,1)} collective-permute-done((bf16[64,1024]{1,0:T(8,128)(2,1)}, bf16[64,1024]{1,0:T(8,128)(2,1)}, u32[]{:S(2)}, u32[]{:S(2)}) %collective-permute-start.38) | collective-permute-done | bytes 131104 | tf_op jit(solution)/shard_map/ppermute | solution.py:915
  357.4 4.4 %shard_map.388 = (f32[1024,512]{1,0:T(8,128)}, f32[512,1024]{1,0:T(8,128)}) custom-call(s32[8]{0:T(128)} %stack.112.starts_ref, bf16[128,1024]{1,0:T(8,128)(2,1)} %shard_map.382.refs_0_, bf16[128,1024]{1,0:T(8,128)(2,1)} %collective-permute-done.41.refs_1_, bf16[128,1024]{1,0:T(8,128)(2,1)} %collective-permute-done.42.refs_2_, ...), custom_call_target="tpu_custom_call" | custom-call | flops 1024 | bytes 1024 | tf_op jit(solution)/shard_map/pallas_call | solution.py:897
  363.4 2.6 shard_map.389.refs_0_
  368.0 11.0 %collective-permute-done.54.refs_2_ = bf16[256,1024]{1,0:T(8,128)(2,1)} collective-permute-done((bf16[256,1024]{1,0:T(8,128)(2,1)}, bf16[256,1024]{1,0:T(8,128)(2,1)}, u32[]{:S(2)}, u32[]{:S(2)}) %collective-permute-start.54) | collective-permute-done | bytes 524320 | tf_op jit(solution)/shard_map/ppermute | solution.py:915
  382.1 17.3 %collective-permute-done.58.refs_6_ = bf16[128,1024]{1,0:T(8,128)(2,1)S(1)} collective-permute-done((bf16[128,1024]{1,0:T(8,128)(2,1)}, bf16[128,1024]{1,0:T(8,128)(2,1)S(1)}, u32[]{:S(2)}, u32[]{:S(2)}) %collective-permute-start.58) | collective-permute-done | bytes 262176 | tf_op jit(solution)/shard_map/ppermute | solution.py:915
  399.4 2.8 collective-permute-done.59.refs_7_
  403.0 4.4 %shard_map.390 = (f32[3,1024,256]{2,1,0:T(8,128)}, f32[256,1024]{1,0:T(8,128)}) custom-call(s32[8]{0:T(128)} %stack.112.starts_ref, bf16[128,1024]{1,0:T(8,128)(2,1)} %shard_map.386.refs_0_, bf16[128,1024]{1,0:T(8,128)(2,1)} %collective-permute-done.48.refs_1_, bf16[128,1024]{1,0:T(8,128)(2,1)} %collective-permute-done.49.refs_2_, ...), custom_call_target="tpu_custom_call" | custom-call | flops 1024 | bytes 1024 | tf_op jit(solution)/shard_map/pallas_call | solution.py:897
  411.9 9.8 %shard_map.391 = (f32[712,1024]{1,0:T(8,128)}, f32[512,1024]{1,0:T(8,128)}, f32[1024,512]{1,0:T(8,128)}, f32[7,512]{1,0:T(8,128)}, f32[3,512]{1,0:T(4,128)}, /*i...) custom-call(s32[8]{0:T(128)} %stack.98.starts_ref, ...), custom_call_target="tpu_custom_call" | custom-call | flops 1024 | bytes 1024 | tf_op jit(solution)/shard_map/pallas_call | solution.py:897
  (190 shorter events, 52.6 us)
Async XLA Ops:
  2.5 40.3 %collective-permute-start.1 = (bf16[128,1024]{1,0:T(8,128)(2,1)}, bf16[128,1024]{1,0:T(8,128)(2,1)S(1)}, u32[]{:S(2)}, u32[]{:S(2)}) collective-permute-start(bf16[128,1024]{1,0:T(8,128)(2,1)} %constant_dynamic-slice_fusion.3), channel_id=1, source_target_pairs={{0,2},{1,3},{2,0},{3,1},{4,6},{5,7},{6,4},{7,5},{8,10},{9,11},{10,... | collective-permute-start | bytes 786440 | tf_op jit(solution)/shard_map/ppermute | solution.py:915
  5.5 37.4 %collective-permute-start.4 = (bf16[256,1024]{1,0:T(8,128)(2,1)}, bf16[256,1024]{1,0:T(8,128)(2,1)}, u32[]{:S(2)}, u32[]{:S(2)}) collective-permute-start(bf16[256,1024]{1,0:T(8,128)(2,1)} %refs_15_.2), channel_id=1, source_target_pairs={{0,1},{1,0},{2,3},{3,2},{4,5},{5,4},{6,7},{7,6},{8,9},{9,8},{10,11... | collective-permute-start | bytes 1572872 | tf_op jit(solution)/shard_map/ppermute | solution.py:915
  7.6 29.6 %collective-permute-start = (bf16[3,512,256]{2,1,0:T(8,128)(2,1)}, bf16[3,512,256]{2,1,0:T(8,128)(2,1)}, u32[]{:S(2)}, u32[]{:S(2)}) collective-permute-start(bf16[3,512,256]{2,1,0:T(8,128)(2,1)} %constant_dynamic-slice_fusion.4), channel_id=1, source_target_pairs={{0,2},{1,3},{2,0},{3,1},{4,6},{5,7},{6,4},{7,5},{8,10},{9,11},{10,... | collective-permute-start | bytes 2359304 | tf_op jit(solution)/shard_map/ppermute | solution.py:915
  7.6 35.3 %collective-permute-start.3 = (bf16[3,1024,256]{2,1,0:T(8,128)(2,1)}, bf16[3,1024,256]{2,1,0:T(8,128)(2,1)}, u32[]{:S(2)}, u32[]{:S(2)}) collective-permute-start(bf16[3,1024,256]{2,1,0:T(8,128)(2,1)} %refs_13_.4), channel_id=1, source_target_pairs={{0,1},{1,0},{2,3},{3,2},{4,5},{5,4},{6,7},{7,6},{8,9},{9,8},{10,11... | collective-permute-start | bytes 4718600 | tf_op jit(solution)/shard_map/ppermute | solution.py:915
  27.4 9.7 %all-to-all-start = ((bf16[4,2,1408]{2,1,0:T(2,128)(2,1)}), bf16[4,2,1408]{2,1,0:T(2,128)(2,1)S(1)}, u32[]{:S(2)}, u32[]{:S(2)}) async-start(bf16[4,2,1408]{2,1,0:T(2,128)(2,1)} %reshape.182), calls=%async_computation | async-start | bytes 45056 | tf_op jit(solution)/shard_map/all_to_all | solution.py:1195
  37.1 20.3 %collective-permute-start.2 = (bf16[3,512,256]{2,1,0:T(8,128)(2,1)}, bf16[3,512,256]{2,1,0:T(8,128)(2,1)}, u32[]{:S(2)}, u32[]{:S(2)}) collective-permute-start(bf16[3,512,256]{2,1,0:T(8,128)(2,1)} %collective-permute-done.refs_8_.refs_14_), channel_id=1, source_target_pairs={{0,4},{4,0},{8,12},{12,8},{16,20},{20,16},{24,28},{28,24},{1,5},{5... | collective-permute-start | bytes 2359304 | tf_op jit(solution)/shard_map/ppermute | solution.py:915
  40.8 25.3 %collective-permute-start.10 = (bf16[512,512]{1,0:T(8,128)(2,1)}, bf16[512,512]{1,0:T(8,128)(2,1)}, u32[]{:S(2)}, u32[]{:S(2)}) collective-permute-start(bf16[512,512]{1,0:T(8,128)(2,1)} %constant_dynamic-slice_fusion.1), channel_id=1, source_target_pairs={{0,2},{1,3},{2,0},{3,1},{4,6},{5,7},{6,4},{7,5},{8,10},{9,11},{10,... | collective-permute-start | bytes 1572872 | tf_op jit(solution)/shard_map/ppermute | solution.py:915
  42.8 23.9 %collective-permute-start.11 = (bf16[256,1024]{1,0:T(8,128)(2,1)}, bf16[256,1024]{1,0:T(8,128)(2,1)}, u32[]{:S(2)}, u32[]{:S(2)}) collective-permute-start(bf16[256,1024]{1,0:T(8,128)(2,1)} %constant_dynamic-slice_fusion), channel_id=1, source_target_pairs={{0,2},{1,3},{2,0},{3,1},{4,6},{5,7},{6,4},{7,5},{8,10},{9,11},{10,... | collective-permute-start | bytes 1572872 | tf_op jit(solution)/shard_map/ppermute | solution.py:915
  57.4 13.8 %collective-permute-start.5 = (bf16[3,512,256]{2,1,0:T(8,128)(2,1)}, bf16[3,512,256]{2,1,0:T(8,128)(2,1)}, u32[]{:S(2)}, u32[]{:S(2)}) collective-permute-start(bf16[3,512,256]{2,1,0:T(8,128)(2,1)} %collective-permute-done.refs_8_.refs_14_), channel_id=1, source_target_pairs={{0,1},{1,0},{2,3},{3,2},{4,5},{5,4},{6,7},{7,6},{8,9},{9,8},{10,11... | collective-permute-start | bytes 2359304 | tf_op jit(solution)/shard_map/ppermute | solution.py:915
  57.5 8.7 %collective-permute-start.7 = (bf16[128,1024]{1,0:T(8,128)(2,1)S(1)}, bf16[128,1024]{1,0:T(8,128)(2,1)S(1)}, u32[]{:S(2)}, u32[]{:S(2)}) collective-permute-start(bf16[128,1024]{1,0:T(8,128)(2,1)S(1)} %collective-permute-done.1.refs_12_.refs_18_), channel_id=1, source_target_pairs={{0,4},{4,0},{8,12},{12,8},{16,20},{20,16},{24,28},{28,24},{1,5},{5... | collective-permute-start | bytes 786440 | tf_op jit(solution)/shard_map/ppermute | solution.py:915
  59.2 35.7 %collective-permute-start.15 = (bf16[1024,512]{1,0:T(8,128)(2,1)}, bf16[1024,512]{1,0:T(8,128)(2,1)}, u32[]{:S(2)}, u32[]{:S(2)}) collective-permute-start(bf16[1024,512]{1,0:T(8,128)(2,1)} %refs_13_.3), channel_id=1, source_target_pairs={{0,1},{1,0},{2,3},{3,2},{4,5},{5,4},{6,7},{7,6},{8,9},{9,8},{10,11... | collective-permute-start | bytes 3145736 | tf_op jit(solution)/shard_map/ppermute | solution.py:915
  66.2 7.0 %collective-permute-start.6 = (bf16[3,512,256]{2,1,0:T(8,128)(2,1)}, bf16[3,512,256]{2,1,0:T(8,128)(2,1)}, u32[]{:S(2)}, u32[]{:S(2)}) collective-permute-start(bf16[3,512,256]{2,1,0:T(8,128)(2,1)} %collective-permute-done.2.refs_9_.refs_15_), channel_id=1, source_target_pairs={{0,1},{1,0},{2,3},{3,2},{4,5},{5,4},{6,7},{7,6},{8,9},{9,8},{10,11... | collective-permute-start | bytes 2359304 | tf_op jit(solution)/shard_map/ppermute | solution.py:915
  66.7 3.9 collective-permute-start.9
  68.8 22.2 %collective-permute-start.16 = (bf16[256,1024]{1,0:T(8,128)(2,1)}, bf16[256,1024]{1,0:T(8,128)(2,1)}, u32[]{:S(2)}, u32[]{:S(2)}) collective-permute-start(bf16[256,1024]{1,0:T(8,128)(2,1)} %collective-permute-done.11.refs_16_), channel_id=1, source_target_pairs={{0,4},{4,0},{8,12},{12,8},{16,20},{20,16},{24,28},{28,24},{1,5},{5... | collective-permute-start | bytes 1572872 | tf_op jit(solution)/shard_map/ppermute | solution.py:915
  70.6 23.8 %collective-permute-start.12 = (bf16[512,512]{1,0:T(8,128)(2,1)}, bf16[512,512]{1,0:T(8,128)(2,1)}, u32[]{:S(2)}, u32[]{:S(2)}) collective-permute-start(bf16[512,512]{1,0:T(8,128)(2,1)} %collective-permute-done.10.refs_10_), channel_id=1, source_target_pairs={{0,4},{4,0},{8,12},{12,8},{16,20},{20,16},{24,28},{28,24},{1,5},{5... | collective-permute-start | bytes 1572872 | tf_op jit(solution)/shard_map/ppermute | solution.py:915
  71.3 24.7 %collective-permute-start.19 = (bf16[512,1024]{1,0:T(8,128)(2,1)}, bf16[512,1024]{1,0:T(8,128)(2,1)}, u32[]{:S(2)}, u32[]{:S(2)}) collective-permute-start(bf16[512,1024]{1,0:T(8,128)(2,1)} %refs_19_.1), channel_id=1, source_target_pairs={{0,1},{1,0},{2,3},{3,2},{4,5},{5,4},{6,7},{7,6},{8,9},{9,8},{10,11... | collective-permute-start | bytes 3145736 | tf_op jit(solution)/shard_map/ppermute | solution.py:915
  94.4 2.8 collective-permute-start.13
  94.4 3.0 collective-permute-start.14
  94.9 3.2 collective-permute-start.17
  94.9 4.0 collective-permute-start.18
  124.3 20.9 %collective-permute-start.20 = (bf16[1024,1024]{1,0:T(8,128)(2,1)}, bf16[1024,1024]{1,0:T(8,128)(2,1)}, u32[]{:S(2)}, u32[]{:S(2)}) collective-permute-start(bf16[1024,1024]{1,0:T(8,128)(2,1)} %get-tuple-element.216), channel_id=1, source_target_pairs={{0,1},{1,0},{2,3},{3,2},{4,5},{5,4},{6,7},{7,6},{8,9},{9,8},{10,11... | collective-permute-start | bytes 6291464 | tf_op jit(solution)/shard_map/ppermute | solution.py:915
  144.6 30.1 %collective-permute-start.21 = (bf16[1024,1024]{1,0:T(8,128)(2,1)}, bf16[1024,1024]{1,0:T(8,128)(2,1)}, u32[]{:S(2)}, u32[]{:S(2)}) collective-permute-start(bf16[1024,1024]{1,0:T(8,128)(2,1)} %get-tuple-element.223), channel_id=1, source_target_pairs={{0,1},{1,0},{2,3},{3,2},{4,5},{5,4},{6,7},{7,6},{8,9},{9,8},{10,11... | collective-permute-start | bytes 6291464 | tf_op jit(solution)/shard_map/ppermute | solution.py:915
  145.1 55.9 %collective-permute-start.24 = (bf16[1024,1024]{1,0:T(8,128)(2,1)}, bf16[1024,1024]{1,0:T(8,128)(2,1)}, u32[]{:S(2)}, u32[]{:S(2)}) collective-permute-start(bf16[1024,1024]{1,0:T(8,128)(2,1)} %get-tuple-element.244), channel_id=1, source_target_pairs={{0,1},{1,0},{2,3},{3,2},{4,5},{5,4},{6,7},{7,6},{8,9},{9,8},{10,11... | collective-permute-start | bytes 6291464 | tf_op jit(solution)/shard_map/ppermute | solution.py:915
  149.5 51.5 %collective-permute-start.23 = (bf16[1024,1024]{1,0:T(8,128)(2,1)}, bf16[1024,1024]{1,0:T(8,128)(2,1)}, u32[]{:S(2)}, u32[]{:S(2)}) collective-permute-start(bf16[1024,1024]{1,0:T(8,128)(2,1)} %shard_map.371), channel_id=1, source_target_pairs={{0,2},{1,3},{2,0},{3,1},{4,6},{5,7},{6,4},{7,5},{8,10},{9,11},{10,... | collective-permute-start | bytes 6291464 | tf_op jit(solution)/shard_map/ppermute | solution.py:915
  174.6 59.1 %collective-permute-start.30 = (bf16[1024,1024]{1,0:T(8,128)(2,1)}, bf16[1024,1024]{1,0:T(8,128)(2,1)}, u32[]{:S(2)}, u32[]{:S(2)}) collective-permute-start(bf16[1024,1024]{1,0:T(8,128)(2,1)} %get-tuple-element.258), channel_id=1, source_target_pairs={{0,1},{1,0},{2,3},{3,2},{4,5},{5,4},{6,7},{7,6},{8,9},{9,8},{10,11... | collective-permute-start | bytes 6291464 | tf_op jit(solution)/shard_map/ppermute | solution.py:915
  179.0 64.2 %collective-permute-start.29 = (bf16[1024,1024]{1,0:T(8,128)(2,1)}, bf16[1024,1024]{1,0:T(8,128)(2,1)}, u32[]{:S(2)}, u32[]{:S(2)}) collective-permute-start(bf16[1024,1024]{1,0:T(8,128)(2,1)} %shard_map.373), channel_id=1, source_target_pairs={{0,2},{1,3},{2,0},{3,1},{4,6},{5,7},{6,4},{7,5},{8,10},{9,11},{10,... | collective-permute-start | bytes 6291464 | tf_op jit(solution)/shard_map/ppermute | solution.py:915
  200.8 6.1 %collective-permute-start.22 = (bf16[512,1024]{1,0:T(8,128)(2,1)}, bf16[512,1024]{1,0:T(8,128)(2,1)}, u32[]{:S(2)}, u32[]{:S(2)}) collective-permute-start(bf16[512,1024]{1,0:T(8,128)(2,1)} %get-tuple-element.242), channel_id=1, source_target_pairs={{0,1},{1,0},{2,3},{3,2},{4,5},{5,4},{6,7},{7,6},{8,9},{9,8},{10,11... | collective-permute-start | bytes 3145736 | tf_op jit(solution)/shard_map/ppermute | solution.py:915
  205.2 25.7 %collective-permute-start.27 = (bf16[512,1024]{1,0:T(8,128)(2,1)}, bf16[512,1024]{1,0:T(8,128)(2,1)}, u32[]{:S(2)}, u32[]{:S(2)}) collective-permute-start(bf16[512,1024]{1,0:T(8,128)(2,1)} %get-tuple-element.252), channel_id=1, source_target_pairs={{0,4},{4,0},{8,12},{12,8},{16,20},{20,16},{24,28},{28,24},{1,5},{5... | collective-permute-start | bytes 3145736 | tf_op jit(solution)/shard_map/ppermute | solution.py:915
  206.8 57.3 %collective-permute-start.26 = (bf16[512,1024]{1,0:T(8,128)(2,1)}, bf16[512,1024]{1,0:T(8,128)(2,1)}, u32[]{:S(2)}, u32[]{:S(2)}) collective-permute-start(bf16[512,1024]{1,0:T(8,128)(2,1)} %get-tuple-element.251), channel_id=1, source_target_pairs={{0,1},{1,0},{2,3},{3,2},{4,5},{5,4},{6,7},{7,6},{8,9},{9,8},{10,11... | collective-permute-start | bytes 3145736 | tf_op jit(solution)/shard_map/ppermute | solution.py:915
  209.5 55.8 %collective-permute-start.25 = (bf16[512,1024]{1,0:T(8,128)(2,1)}, bf16[512,1024]{1,0:T(8,128)(2,1)}, u32[]{:S(2)}, u32[]{:S(2)}) collective-permute-start(bf16[512,1024]{1,0:T(8,128)(2,1)} %shard_map.376), channel_id=1, source_target_pairs={{0,2},{1,3},{2,0},{3,1},{4,6},{5,7},{6,4},{7,5},{8,10},{9,11},{10,... | collective-permute-start | bytes 3145736 | tf_op jit(solution)/shard_map/ppermute | solution.py:915
  247.4 25.5 %collective-permute-start.33 = (bf16[512,1024]{1,0:T(8,128)(2,1)}, bf16[512,1024]{1,0:T(8,128)(2,1)}, u32[]{:S(2)}, u32[]{:S(2)}) collective-permute-start(bf16[512,1024]{1,0:T(8,128)(2,1)} %get-tuple-element.272), channel_id=1, source_target_pairs={{0,4},{4,0},{8,12},{12,8},{16,20},{20,16},{24,28},{28,24},{1,5},{5... | collective-permute-start | bytes 3145736 | tf_op jit(solution)/shard_map/ppermute | solution.py:915
  249.1 12.9 %collective-permute-start.28 = (bf16[256,1024]{1,0:T(8,128)(2,1)}, bf16[256,1024]{1,0:T(8,128)(2,1)}, u32[]{:S(2)}, u32[]{:S(2)}) collective-permute-start(bf16[256,1024]{1,0:T(8,128)(2,1)} %get-tuple-element.256), channel_id=1, source_target_pairs={{0,8},{4,12},{8,0},{12,4},{16,24},{20,28},{24,16},{28,20},{1,9},{5... | collective-permute-start | bytes 1572872 | tf_op jit(solution)/shard_map/ppermute | solution.py:915
  268.5 18.4 %collective-permute-start.31 = (bf16[256,1024]{1,0:T(8,128)(2,1)}, bf16[256,1024]{1,0:T(8,128)(2,1)S(1)}, u32[]{:S(2)}, u32[]{:S(2)}) collective-permute-start(bf16[256,1024]{1,0:T(8,128)(2,1)} %get-tuple-element.270), channel_id=1, source_target_pairs={{0,4},{4,0},{8,12},{12,8},{16,20},{20,16},{24,28},{28,24},{1,5},{5... | collective-permute-start | bytes 1572872 | tf_op jit(solution)/shard_map/ppermute | solution.py:915
  270.1 14.3 %collective-permute-start.32 = (bf16[128,1024]{1,0:T(8,128)(2,1)}, bf16[128,1024]{1,0:T(8,128)(2,1)S(1)}, u32[]{:S(2)}, u32[]{:S(2)}) collective-permute-start(bf16[128,1024]{1,0:T(8,128)(2,1)} %get-tuple-element.271), channel_id=1, source_target_pairs={{0,16},{4,20},{8,24},{12,28},{16,0},{20,4},{24,8},{28,12},{1,17},{... | collective-permute-start | bytes 786440 | tf_op jit(solution)/shard_map/ppermute | solution.py:915
  275.7 23.8 %collective-permute-start.34 = (bf16[256,1024]{1,0:T(8,128)(2,1)}, bf16[256,1024]{1,0:T(8,128)(2,1)}, u32[]{:S(2)}, u32[]{:S(2)}) collective-permute-start(bf16[256,1024]{1,0:T(8,128)(2,1)} %get-tuple-element.282), channel_id=1, source_target_pairs={{0,8},{4,12},{8,0},{12,4},{16,24},{20,28},{24,16},{28,20},{1,9},{5... | collective-permute-start | bytes 1572872 | tf_op jit(solution)/shard_map/ppermute | solution.py:915
  291.2 7.4 %all-to-all-start.1 = ((bf16[4,2,768]{2,1,0:T(2,128)(2,1)}), bf16[4,2,768]{2,1,0:T(2,128)(2,1)S(1)}, u32[]{:S(2)}, u32[]{:S(2)}) async-start(bf16[4,2,768]{2,1,0:T(2,128)(2,1)} %reshape.184), calls=%async_computation.1 | async-start | bytes 24576 | tf_op jit(solution)/shard_map/all_to_all | solution.py:1448
  294.5 15.9 %collective-permute-start.41 = (bf16[128,1024]{1,0:T(8,128)(2,1)S(1)}, bf16[128,1024]{1,0:T(8,128)(2,1)}, u32[]{:S(2)}, u32[]{:S(2)}) collective-permute-start(bf16[128,1024]{1,0:T(8,128)(2,1)S(1)} %copy-done.2), channel_id=1, source_target_pairs={{0,16},{4,20},{8,24},{12,28},{16,0},{20,4},{24,8},{28,12},{1,17},{... | collective-permute-start | bytes 786440 | tf_op jit(solution)/shard_map/ppermute | solution.py:915
  294.5 16.8 %collective-permute-start.36 = (bf16[128,1024]{1,0:T(8,128)(2,1)}, bf16[128,1024]{1,0:T(8,128)(2,1)}, u32[]{:S(2)}, u32[]{:S(2)}) collective-permute-start(bf16[128,1024]{1,0:T(8,128)(2,1)} %get-tuple-element.287), channel_id=1, source_target_pairs={{0,8},{4,12},{8,0},{12,4},{16,24},{20,28},{24,16},{28,20},{1,9},{5... | collective-permute-start | bytes 786440 | tf_op jit(solution)/shard_map/ppermute | solution.py:915
  301.6 19.9 %collective-permute-start.35 = (bf16[128,1024]{1,0:T(8,128)(2,1)}, bf16[128,1024]{1,0:T(8,128)(2,1)S(1)}, u32[]{:S(2)}, u32[]{:S(2)}) collective-permute-start(bf16[128,1024]{1,0:T(8,128)(2,1)} %get-tuple-element.286), channel_id=1, source_target_pairs={{0,16},{4,20},{8,24},{12,28},{16,0},{20,4},{24,8},{28,12},{1,17},{... | collective-permute-start | bytes 786440 | tf_op jit(solution)/shard_map/ppermute | solution.py:915
  301.7 26.8 %collective-permute-start.42 = (bf16[128,1024]{1,0:T(8,128)(2,1)S(1)}, bf16[128,1024]{1,0:T(8,128)(2,1)}, u32[]{:S(2)}, u32[]{:S(2)}) collective-permute-start(bf16[128,1024]{1,0:T(8,128)(2,1)S(1)} %copy-done.2), channel_id=1, source_target_pairs={{0,8},{4,12},{8,0},{12,4},{16,24},{20,28},{24,16},{28,20},{1,9},{5... | collective-permute-start | bytes 786440 | tf_op jit(solution)/shard_map/ppermute | solution.py:915
  310.4 20.3 %collective-permute-start.43 = (bf16[128,1024]{1,0:T(8,128)(2,1)}, bf16[128,1024]{1,0:T(8,128)(2,1)}, u32[]{:S(2)}, u32[]{:S(2)}) collective-permute-start(bf16[128,1024]{1,0:T(8,128)(2,1)} %collective-permute-done.41.refs_1_), channel_id=1, source_target_pairs={{0,8},{4,12},{8,0},{12,4},{16,24},{20,28},{24,16},{28,20},{1,9},{5... | collective-permute-start | bytes 786440 | tf_op jit(solution)/shard_map/ppermute | solution.py:915
  313.2 17.9 %collective-permute-start.37 = (bf16[64,1024]{1,0:T(8,128)(2,1)}, bf16[64,1024]{1,0:T(8,128)(2,1)S(1)}, u32[]{:S(2)}, u32[]{:S(2)}) collective-permute-start(bf16[64,1024]{1,0:T(8,128)(2,1)} %get-tuple-element.294), channel_id=1, source_target_pairs={{0,16},{4,20},{8,24},{12,28},{16,0},{20,4},{24,8},{28,12},{1,17},{... | collective-permute-start | bytes 393224 | tf_op jit(solution)/shard_map/ppermute | solution.py:915
  313.8 21.8 %collective-permute-start.44 = (bf16[128,1024]{1,0:T(8,128)(2,1)S(1)}, bf16[128,1024]{1,0:T(8,128)(2,1)}, u32[]{:S(2)}, u32[]{:S(2)}) collective-permute-start(bf16[128,1024]{1,0:T(8,128)(2,1)S(1)} %copy-done.2), channel_id=1, source_target_pairs={{0,4},{4,0},{8,12},{12,8},{16,20},{20,16},{24,28},{28,24},{1,5},{5... | collective-permute-start | bytes 786440 | tf_op jit(solution)/shard_map/ppermute | solution.py:915
  324.7 7.9 %all-to-all-start.2 = ((bf16[4,4,1024]{2,1,0:T(4,128)(2,1)}), bf16[4,4,1024]{2,1,0:T(4,128)(2,1)}, u32[]{:S(2)}, u32[]{:S(2)}) async-start(bf16[4,4,1024]{2,1,0:T(4,128)(2,1)} %broadcast_in_dim.51), calls=%async_computation.2 | async-start | bytes 65536 | tf_op jit(solution)/shard_map/all_to_all | solution.py:1454
  328.5 9.5 %collective-permute-start.46 = (bf16[128,1024]{1,0:T(8,128)(2,1)}, bf16[128,1024]{1,0:T(8,128)(2,1)}, u32[]{:S(2)}, u32[]{:S(2)}) collective-permute-start(bf16[128,1024]{1,0:T(8,128)(2,1)} %collective-permute-done.42.refs_2_), channel_id=1, source_target_pairs={{0,4},{4,0},{8,12},{12,8},{16,20},{20,16},{24,28},{28,24},{1,5},{5... | collective-permute-start | bytes 786440 | tf_op jit(solution)/shard_map/ppermute | solution.py:915
  329.2 14.5 %collective-permute-start.45 = (bf16[128,1024]{1,0:T(8,128)(2,1)}, bf16[128,1024]{1,0:T(8,128)(2,1)}, u32[]{:S(2)}, u32[]{:S(2)}) collective-permute-start(bf16[128,1024]{1,0:T(8,128)(2,1)} %collective-permute-done.41.refs_1_), channel_id=1, source_target_pairs={{0,4},{4,0},{8,12},{12,8},{16,20},{20,16},{24,28},{28,24},{1,5},{5... | collective-permute-start | bytes 786440 | tf_op jit(solution)/shard_map/ppermute | solution.py:915
  330.7 18.6 %collective-permute-start.47 = (bf16[128,1024]{1,0:T(8,128)(2,1)}, bf16[128,1024]{1,0:T(8,128)(2,1)}, u32[]{:S(2)}, u32[]{:S(2)}) collective-permute-start(bf16[128,1024]{1,0:T(8,128)(2,1)} %collective-permute-done.43.refs_3_), channel_id=1, source_target_pairs={{0,4},{4,0},{8,12},{12,8},{16,20},{20,16},{24,28},{28,24},{1,5},{5... | collective-permute-start | bytes 786440 | tf_op jit(solution)/shard_map/ppermute | solution.py:915
  331.2 18.1 %collective-permute-start.48 = (bf16[128,1024]{1,0:T(8,128)(2,1)}, bf16[128,1024]{1,0:T(8,128)(2,1)}, u32[]{:S(2)}, u32[]{:S(2)}) collective-permute-start(bf16[128,1024]{1,0:T(8,128)(2,1)} %shard_map.386.refs_0_), channel_id=1, source_target_pairs={{0,16},{4,20},{8,24},{12,28},{16,0},{20,4},{24,8},{28,12},{1,17},{... | collective-permute-start | bytes 786440 | tf_op jit(solution)/shard_map/ppermute | solution.py:915
  335.6 14.2 %collective-permute-start.39 = (bf16[64,1024]{1,0:T(8,128)(2,1)}, bf16[64,1024]{1,0:T(8,128)(2,1)S(1)}, u32[]{:S(2)}, u32[]{:S(2)}) collective-permute-start(bf16[64,1024]{1,0:T(8,128)(2,1)} %shard_map.387.refs_0_), channel_id=1, source_target_pairs={{0,8},{4,12},{8,0},{12,4},{16,24},{20,28},{24,16},{28,20},{1,9},{5... | collective-permute-start | bytes 393224 | tf_op jit(solution)/shard_map/ppermute | solution.py:915
  338.1 23.7 %collective-permute-start.51 = (bf16[128,1024]{1,0:T(8,128)(2,1)}, bf16[128,1024]{1,0:T(8,128)(2,1)S(1)}, u32[]{:S(2)}, u32[]{:S(2)}) collective-permute-start(bf16[128,1024]{1,0:T(8,128)(2,1)} %shard_map.386.refs_0_), channel_id=1, source_target_pairs={{0,4},{4,0},{8,12},{12,8},{16,20},{20,16},{24,28},{28,24},{1,5},{5... | collective-permute-start | bytes 786440 | tf_op jit(solution)/shard_map/ppermute | solution.py:915
  343.7 18.1 %collective-permute-start.49 = (bf16[128,1024]{1,0:T(8,128)(2,1)}, bf16[128,1024]{1,0:T(8,128)(2,1)}, u32[]{:S(2)}, u32[]{:S(2)}) collective-permute-start(bf16[128,1024]{1,0:T(8,128)(2,1)} %shard_map.386.refs_0_), channel_id=1, source_target_pairs={{0,8},{4,12},{8,0},{12,4},{16,24},{20,28},{24,16},{28,20},{1,9},{5... | collective-permute-start | bytes 786440 | tf_op jit(solution)/shard_map/ppermute | solution.py:915
  349.3 6.9 %collective-permute-start.38 = (bf16[64,1024]{1,0:T(8,128)(2,1)}, bf16[64,1024]{1,0:T(8,128)(2,1)}, u32[]{:S(2)}, u32[]{:S(2)}) collective-permute-start(bf16[64,1024]{1,0:T(8,128)(2,1)} %shard_map.387.refs_0_), channel_id=1, source_target_pairs={{0,16},{4,20},{8,24},{12,28},{16,0},{20,4},{24,8},{28,12},{1,17},{... | collective-permute-start | bytes 393224 | tf_op jit(solution)/shard_map/ppermute | solution.py:915
  349.3 14.1 %collective-permute-start.52 = (bf16[128,1024]{1,0:T(8,128)(2,1)}, bf16[128,1024]{1,0:T(8,128)(2,1)}, u32[]{:S(2)}, u32[]{:S(2)}) collective-permute-start(bf16[128,1024]{1,0:T(8,128)(2,1)} %collective-permute-done.48.refs_1_), channel_id=1, source_target_pairs={{0,4},{4,0},{8,12},{12,8},{16,20},{20,16},{24,28},{28,24},{1,5},{5... | collective-permute-start | bytes 786440 | tf_op jit(solution)/shard_map/ppermute | solution.py:915
  349.8 13.6 %collective-permute-start.50 = (bf16[128,1024]{1,0:T(8,128)(2,1)}, bf16[128,1024]{1,0:T(8,128)(2,1)}, u32[]{:S(2)}, u32[]{:S(2)}) collective-permute-start(bf16[128,1024]{1,0:T(8,128)(2,1)} %collective-permute-done.48.refs_1_), channel_id=1, source_target_pairs={{0,8},{4,12},{8,0},{12,4},{16,24},{20,28},{24,16},{28,20},{1,9},{5... | collective-permute-start | bytes 786440 | tf_op jit(solution)/shard_map/ppermute | solution.py:915
  356.2 7.2 %collective-permute-start.40 = (bf16[64,1024]{1,0:T(8,128)(2,1)}, bf16[64,1024]{1,0:T(8,128)(2,1)}, u32[]{:S(2)}, u32[]{:S(2)}) collective-permute-start(bf16[64,1024]{1,0:T(8,128)(2,1)} %collective-permute-done.38.refs_1_), channel_id=1, source_target_pairs={{0,8},{4,12},{8,0},{12,4},{16,24},{20,28},{24,16},{28,20},{1,9},{5... | collective-permute-start | bytes 393224 | tf_op jit(solution)/shard_map/ppermute | solution.py:915
  366.0 13.0 %collective-permute-start.54 = (bf16[256,1024]{1,0:T(8,128)(2,1)}, bf16[256,1024]{1,0:T(8,128)(2,1)}, u32[]{:S(2)}, u32[]{:S(2)}) collective-permute-start(bf16[256,1024]{1,0:T(8,128)(2,1)} %shard_map.389.refs_0_), channel_id=1, source_target_pairs={{0,2},{1,3},{2,0},{3,1},{4,6},{5,7},{6,4},{7,5},{8,10},{9,11},{10,... | collective-permute-start | bytes 1572872 | tf_op jit(solution)/shard_map/ppermute | solution.py:915
  366.8 40.6 %collective-permute-start.53 = (bf16[256,1024]{1,0:T(8,128)(2,1)}, bf16[256,1024]{1,0:T(8,128)(2,1)}, u32[]{:S(2)}, u32[]{:S(2)}) collective-permute-start(bf16[256,1024]{1,0:T(8,128)(2,1)} %shard_map.389.refs_0_), channel_id=1, source_target_pairs={{0,4},{4,0},{8,12},{12,8},{16,20},{20,16},{24,28},{28,24},{1,5},{5... | collective-permute-start | bytes 1572872 | tf_op jit(solution)/shard_map/ppermute | solution.py:915
  379.1 28.4 %collective-permute-start.55 = (bf16[256,1024]{1,0:T(8,128)(2,1)}, bf16[256,1024]{1,0:T(8,128)(2,1)}, u32[]{:S(2)}, u32[]{:S(2)}) collective-permute-start(bf16[256,1024]{1,0:T(8,128)(2,1)} %collective-permute-done.54.refs_2_), channel_id=1, source_target_pairs={{0,4},{4,0},{8,12},{12,8},{16,20},{20,16},{24,28},{28,24},{1,5},{5... | collective-permute-start | bytes 1572872 | tf_op jit(solution)/shard_map/ppermute | solution.py:915
  380.1 19.3 %collective-permute-start.58 = (bf16[128,1024]{1,0:T(8,128)(2,1)}, bf16[128,1024]{1,0:T(8,128)(2,1)S(1)}, u32[]{:S(2)}, u32[]{:S(2)}) collective-permute-start(bf16[128,1024]{1,0:T(8,128)(2,1)} %collective-permute-done.49.refs_2_), channel_id=1, source_target_pairs={{0,4},{4,0},{8,12},{12,8},{16,20},{20,16},{24,28},{28,24},{1,5},{5... | collective-permute-start | bytes 786440 | tf_op jit(solution)/shard_map/ppermute | solution.py:915
  381.1 21.2 %collective-permute-start.59 = (bf16[128,1024]{1,0:T(8,128)(2,1)}, bf16[128,1024]{1,0:T(8,128)(2,1)S(1)}, u32[]{:S(2)}, u32[]{:S(2)}) collective-permute-start(bf16[128,1024]{1,0:T(8,128)(2,1)} %collective-permute-done.50.refs_3_), channel_id=1, source_target_pairs={{0,4},{4,0},{8,12},{12,8},{16,20},{20,16},{24,28},{28,24},{1,5},{5... | collective-permute-start | bytes 786440 | tf_op jit(solution)/shard_map/ppermute | solution.py:915
  382.1 29.8 %collective-permute-start.56 = (bf16[256,1024]{1,0:T(8,128)(2,1)}, bf16[256,1024]{1,0:T(8,128)(2,1)}, u32[]{:S(2)}, u32[]{:S(2)}) collective-permute-start(bf16[256,1024]{1,0:T(8,128)(2,1)} %shard_map.389.refs_0_), channel_id=1, source_target_pairs={{0,1},{1,0},{2,3},{3,2},{4,5},{5,4},{6,7},{7,6},{8,9},{9,8},{10,11... | collective-permute-start | bytes 1572872 | tf_op jit(solution)/shard_map/ppermute | solution.py:915
  407.4 4.5 %collective-permute-start.57 = (bf16[256,1024]{1,0:T(8,128)(2,1)}, bf16[256,1024]{1,0:T(8,128)(2,1)}, u32[]{:S(2)}, u32[]{:S(2)}) collective-permute-start(bf16[256,1024]{1,0:T(8,128)(2,1)} %collective-permute-done.53.refs_1_), channel_id=1, source_target_pairs={{0,1},{1,0},{2,3},{3,2},{4,5},{5,4},{6,7},{7,6},{8,9},{9,8},{10,11... | collective-permute-start | bytes 1572872 | tf_op jit(solution)/shard_map/ppermute | solution.py:915
  407.5 4.4 %collective-permute-start.60 = (bf16[256,1024]{1,0:T(8,128)(2,1)}, bf16[256,1024]{1,0:T(8,128)(2,1)}, u32[]{:S(2)}, u32[]{:S(2)}) collective-permute-start(bf16[256,1024]{1,0:T(8,128)(2,1)} %collective-permute-done.54.refs_2_), channel_id=1, source_target_pairs={{0,1},{1,0},{2,3},{3,2},{4,5},{5,4},{6,7},{7,6},{8,9},{9,8},{10,11... | collective-permute-start | bytes 1572872 | tf_op jit(solution)/shard_map/ppermute | solution.py:915
  408.0 3.9 collective-permute-start.61
  (24 other events, 204.7 us)
